TPU v7x, 32 devices: a whole 2x2x4 slice. The times are simulated.
32 devices in a mesh: batch: 8 (over z, y), proto: 4 (over x, core).
Axes of the slice: x: 2, y: 2, z: 4, core: 2. Of those that a mesh axis runs over, the one named last changes fastest.
Arguments:
- features: bfloat16 [1024, 1536], P('batch'), may hold values from -20 to 20
- w_first: bfloat16 [1536, 4096], P(None, 'proto'), may hold values from -0.15625 to 0.15625
- bn_gain: float32 [4096], P('proto'), may hold values from 0.1 to 1.9
- bn_shift: float32 [4096], P('proto'), may hold values from -3 to 3
- w_second: bfloat16 [4096, 256], P('proto'), may hold values from -1 to 1
- prototypes: bfloat16 [16384, 256], P('proto'), may hold values from -6 to 6
- partner: int32 [1024], P('batch'), may hold values from 0 to 127, as said below
Outputs:
- crop_penalty: float32 [1024], P('batch')
- grad_w1: float32 [1536, 4096], P('batch', 'proto')
- grad_gain: float32 [4096], P('proto')
- grad_shift: float32 [4096], P('proto')
- grad_w2: float32 [4096, 256], P('proto', 'batch')
Inputs may be any that keep to these rules, and one draw needn't show every extreme that they name: partner_i is a crop index within crop i's group of 128 consecutive crops; the partner of partner_i is i, and partner_i is never i.
All inputs are finite; a program needn't handle non-finite values.
Results may differ from a plain program's by a relative error of at most 0.015.
Values sent between devices are 32-bit elements; how exact they have to be, the bound alone decides.
No kernel may reach another device: no remote copies, remote signals or barrier semaphores. Data moves between devices by JAX's collectives and lax.ppermute only.
A program may use at most 64 MiB of HBM per device.

v0:
```python
import jax
import jax.numpy as jnp
from jax import lax
from jax.sharding import PartitionSpec as P

ITERS = 3


balancing_epsilon = 0.05
sharpness_divisor = 0.1
penalty_weighting = 64.0


def proto_sums(values):
    return lax.psum(values, "proto")


def batch_sums(values):
    return lax.psum(values, "batch")


def body(features, w_first, bn_gain, bn_shift, w_second, prototypes, partner):
    f32 = jnp.float32
    highest = lax.Precision.HIGHEST
    crop_rows = features.shape[0]
    crops_all = crop_rows * lax.axis_size("batch")
    pre_act = jnp.dot(features, w_first, preferred_element_type=f32)
    first_moment, second_moment = batch_sums((jnp.sum(pre_act, 0), jnp.sum(pre_act * pre_act, 0)))
    batch_mean = first_moment / crops_all
    batch_var = second_moment / crops_all - batch_mean * batch_mean
    inv_std = lax.rsqrt(batch_var + 1e-05)
    normed = (pre_act - batch_mean) * inv_std
    shifted = bn_gain * normed + bn_shift
    hidden = jnp.maximum(shifted, 0.0).astype(jnp.bfloat16)
    raw_emb = proto_sums(jnp.dot(hidden, w_second, preferred_element_type=f32))
    inv_norm = lax.rsqrt(jnp.sum(raw_emb * raw_emb, 1, keepdims=True) + 1e-06)
    embedded = raw_emb * inv_norm
    emb_low = embedded.astype(jnp.bfloat16)
    proto_float = prototypes.astype(f32)
    unit_protos = (
        proto_float * lax.rsqrt(jnp.sum(proto_float * proto_float, 1, keepdims=True) + 1e-06)
    ).astype(jnp.bfloat16)
    centroid_affinity = lax.dot_general(
        emb_low, unit_protos, (((1,), (1,)), ((), ())), preferred_element_type=f32
    )
    exponent_codes = jnp.exp(centroid_affinity / balancing_epsilon)
    raised_affinity = jnp.exp(centroid_affinity / sharpness_divisor)
    part_total = jnp.sum(raised_affinity, 1)
    scale_rows = jnp.ones((crop_rows,), f32)
    for iteration in range(ITERS):
        col_part = jnp.dot(scale_rows, exponent_codes, precision=highest)
        scale_cols = 1.0 / batch_sums(col_part)
        scale_rows = 1.0 / proto_sums(jnp.dot(exponent_codes, scale_cols, precision=highest))
    partner_codes = jnp.take(exponent_codes, partner, axis=0) * scale_cols
    cross_part = jnp.sum(partner_codes * centroid_affinity, 1)
    partition_total, mismatch_total = proto_sums((part_total, cross_part))
    companion_weighting = jnp.take(scale_rows, partner)
    crop_penalty = (
        jnp.log(partition_total) - companion_weighting * mismatch_total / sharpness_divisor
    )
    desired_assignments = partner_codes * companion_weighting[:, None]
    normalized_likelihood = raised_affinity / partition_total[:, None]
    affinity_derivative = (
        penalty_weighting * (normalized_likelihood - desired_assignments) / sharpness_divisor
    ).astype(jnp.bfloat16)
    emb_grad = proto_sums(jnp.dot(affinity_derivative, unit_protos, preferred_element_type=f32))
    inner_prod = jnp.sum(embedded * emb_grad, 1, keepdims=True)
    raw_grad = ((emb_grad - embedded * inner_prod) * inv_norm).astype(jnp.bfloat16)
    second_local = lax.dot_general(
        hidden, raw_grad, (((0,), (0,)), ((), ())), preferred_element_type=f32
    )
    hidden_grad = lax.dot_general(
        raw_grad, w_second, (((1,), (1,)), ((), ())), preferred_element_type=f32
    )
    bn_grad = jnp.where(shifted > 0, hidden_grad, 0.0)
    grad_shift, grad_gain = batch_sums((jnp.sum(bn_grad, 0), jnp.sum(bn_grad * normed, 0)))
    pre_grad = (
        bn_gain * inv_std * (bn_grad - grad_shift / crops_all - normed * grad_gain / crops_all)
    ).astype(jnp.bfloat16)
    first_local = lax.dot_general(
        features, pre_grad, (((0,), (0,)), ((), ())), preferred_element_type=f32
    )
    grad_w1, grad_w2 = (
        lax.psum_scatter(first_local, "batch", scatter_dimension=0, tiled=True),
        lax.psum_scatter(second_local, "batch", scatter_dimension=1, tiled=True),
    )
    return (crop_penalty, grad_w1, grad_gain, grad_shift, grad_w2)


def solution(mesh):
    return jax.shard_map(
        body,
        mesh=mesh,
        in_specs=(
            P("batch", None),
            P(None, "proto"),
            P("proto"),
            P("proto"),
            P("proto", None),
            P("proto", None),
            P("batch"),
        ),
        out_specs=(P("batch"), P("batch", "proto"), P("proto"), P("proto"), P("proto", "batch")),
        check_vma=False,
    )
```

profile of v0, /device:TPU:0, one launch (start us, length us, event | category | flops | bytes accessed | tf_op | source)
XLA Modules:
  0.0 448.8 jit_solution(5772298387618652179)
XLA Ops:
  7.2 0.0 copy-start
  7.2 0.0 copy-start.7
  7.2 0.0 all-reduce.6.cloned.1.call-start
  7.3 1.8 copy-done
  9.1 2.4 fusion.35
  11.4 23.4 %all-reduce.1 = (f32[1024]{0:T(1024)S(1)}, f32[1024]{0:T(1024)S(1)}) all-reduce(f32[1024]{0:T(1024)S(1)} %get-tuple-element.25, f32[1024]{0:T(1024)S(1)} %get-tuple-element.24), channel_id=1, replica_groups=mesh['batch'=8,'proto'=4] {'batch'}, use_global_device_ids=true, to_apply=%region_3.0 | all-reduce | flops 2048 | bytes 16384 | tf_op jit(solution)/shard_map/psum | solution.py:19
  34.8 2.1 fusion.33
  37.0 0.0 all-reduce.6.cloned.1.call-update
  37.0 0.0 all-reduce.8.cloned.1.call-start
  37.1 2.2 fusion
  39.3 26.5 %all-reduce.6.cloned.1.call-done = f32[128,256]{1,0:T(8,128)} async-done(((f32[128,256]{1,0:T(8,128)}), f32[128,256]{1,0:T(8,128)}) %all-reduce.6.cloned.1.call-update) | async-done | bytes 131088 | tf_op jit(solution)/shard_map/psum | solution.py:15
  65.8 1.0 multiply_reduce_fusion.4
  66.8 4.0 multiply_exponential_fusion
  70.8 1.3 copy-done.1
  72.1 1.3 fusion.21
  73.4 37.1 %psum.102 = f32[4096]{0:T(1024)S(1)} all-reduce(f32[4096]{0:T(1024)S(1)} %bitcast.36), channel_id=1, replica_groups=mesh['batch'=8,'proto'=4] {'batch'}, use_global_device_ids=true, to_apply=%region_9.0 | all-reduce | flops 4096 | bytes 32768 | tf_op jit(solution)/shard_map/psum | solution.py:19
  110.5 3.4 convolution_bitcast_fusion.3
  113.9 5.9 %psum.103 = f32[128]{0:T(128)S(1)} all-reduce(f32[128]{0:T(128)S(1)} %convolution_bitcast_fusion.3), channel_id=1, replica_groups=mesh['batch'=8,'proto'=4] {'proto'}, use_global_device_ids=true, to_apply=%region_10.0 | all-reduce | flops 128 | bytes 1024 | tf_op jit(solution)/shard_map/psum | solution.py:15
  119.8 2.9 fusion.17
  122.6 33.0 %psum.104 = f32[4096]{0:T(1024)S(1)} all-reduce(f32[4096]{0:T(1024)S(1)} %bitcast.33), channel_id=1, replica_groups=mesh['batch'=8,'proto'=4] {'batch'}, use_global_device_ids=true, to_apply=%region_11.0 | all-reduce | flops 4096 | bytes 32768 | tf_op jit(solution)/shard_map/psum | solution.py:19
  155.6 3.4 convolution_bitcast_fusion.2
  159.0 5.7 %psum.105 = f32[128]{0:T(128)S(1)} all-reduce(f32[128]{0:T(128)S(1)} %convolution_bitcast_fusion.2), channel_id=1, replica_groups=mesh['batch'=8,'proto'=4] {'proto'}, use_global_device_ids=true, to_apply=%region_12.0 | all-reduce | flops 128 | bytes 1024 | tf_op jit(solution)/shard_map/psum | solution.py:15
  164.8 2.9 fusion.15
  167.6 33.1 %psum.106 = f32[4096]{0:T(1024)S(1)} all-reduce(f32[4096]{0:T(1024)S(1)} %bitcast.35), channel_id=1, replica_groups=mesh['batch'=8,'proto'=4] {'batch'}, use_global_device_ids=true, to_apply=%region_13.0 | all-reduce | flops 4096 | bytes 32768 | tf_op jit(solution)/shard_map/psum | solution.py:19
  200.8 3.4 convolution_bitcast_fusion.1
  204.2 5.0 %gather_fusion.1 = f32[128,4096]{1,0:T(8,128)} fusion(f32[128,4096]{1,0:T(8,128)} %get-tuple-element.39, s32[1024]{0:T(1024)S(1)} %pad_clamp_fusion), kind=kCustom, calls=%fused_computation.1 | custom fusion | bytes 4194816 | tf_op jit(solution)/shard_map/jit(_take)/gather | solution.py:54
  209.3 2.9 fusion.2
  212.1 5.8 %all-reduce.2 = (f32[128]{0:T(128)S(1)}, f32[128]{0:T(128)S(1)}, f32[128]{0:T(128)S(1)}) all-reduce(f32[128]{0:T(128)S(1)} %convolution_bitcast_fusion.1, f32[128]{0:T(128)S(1)} %get-tuple-element.21, f32[128]{0:T(128)S(1)} %get-tuple-element.20), channel_id=1, replica_groups=mesh['batch'=8,'proto'=4] {'proto'}, use_global_device_ids=true, to_apply=%region_14.15 | all-reduce | flops 384 | bytes 3072 | tf_op jit(solution)/shard_map/psum | solution.py:15
  217.9 1.2 gather_fusion
  219.1 0.5 multiply_subtract_fusion
  219.6 4.7 %fusion.3 = f32[128,256]{1,0:T(8,128)} fusion(f32[128,4096]{1,0:T(8,128)} %copy-done.1, f32[128,4096]{1,0:T(8,128)} %gather_fusion.1, f32[128]{0:T(128)S(1)} %get-tuple-element.34, f32[128]{0:T(128)S(1)} %get-tuple-element.32, f32[4096]{0:T(1024)S(1)} %broadcast_divide_fusion, pred[128]{0:T(512)(128)(4,1)S(1)} %compare_and_fusion, ...), kind=kOutput, calls=%fused_computation.17 | convolution fusion | flops 275775488 | bytes 6456448 | tf_op jit(solution)/shard_map/dot_general | solution.py:66
  224.4 0.0 all-reduce.8.cloned.1.call-update
  224.4 0.0 reduce-scatter.5.cloned.1.call-start
  224.4 27.4 %all-reduce.8.cloned.1.call-done = f32[128,256]{1,0:T(8,128)} async-done(((f32[128,256]{1,0:T(8,128)}), f32[128,256]{1,0:T(8,128)}) %all-reduce.8.cloned.1.call-update) | async-done | bytes 131088 | tf_op jit(solution)/shard_map/psum | solution.py:15
  251.8 1.1 multiply_reduce_fusion.3
  252.9 1.0 multiply_convert_fusion.4
  253.9 0.6 copy-done.4
  254.6 2.5 fusion.32
  257.0 0.0 reduce-scatter.5.cloned.1.call-update
  257.1 0.0 reduce-scatter.7.cloned.1.call-start
  257.1 3.0 fusion.34
  260.1 22.3 %all-reduce = (f32[1024]{0:T(1024)S(1)}, f32[1024]{0:T(1024)}) all-reduce(f32[1024]{0:T(1024)} %get-tuple-element.23, f32[1024]{0:T(1024)} %get-tuple-element.22), channel_id=1, replica_groups=mesh['batch'=8,'proto'=4] {'batch'}, use_global_device_ids=true, to_apply=%region_22.23 | all-reduce | flops 2048 | bytes 16384 | tf_op jit(solution)/shard_map/psum | solution.py:19
  282.4 0.7 broadcast_multiply_fusion
  283.1 4.9 %convolution_bitcast_fusion = f32[1536,1024]{0,1:T(8,128)} fusion(bf16[128,1536]{1,0:T(8,128)(2,1)S(1)} %copy-done.3, f32[128,1024]{1,0:T(8,128)} %get-tuple-element.41, f32[128,1024]{1,0:T(8,128)} %get-tuple-element.38, f32[1024]{0:T(1024)S(1)} %get-tuple-element.26, f32[1024]{0:T(1024)S(1)} %broadcast_multiply_fusion, f32[1024]{0:T(1024)S(1)} %get-tuple-element.35, ...), kind=kOutput, calls=%fused_computation.4 | convolution fusion | flops 403701760 | bytes 7753728 | tf_op jit(solution)/shard_map/dot_general | solution.py:80
  288.0 6.5 %copy.15 = f32[1536,1024]{1,0:T(8,128)} copy(f32[1536,1024]{0,1:T(8,128)} %convolution_bitcast_fusion) | data formatting | bytes 12582912
  294.5 0.0 reduce-scatter.7.cloned.1.call-update
  294.6 26.3 %reduce-scatter.5.cloned.1.call-done = f32[1024,32]{0,1:T(8,128)} async-done(((f32[1024,256]{0,1:T(8,128)}), f32[1024,32]{0,1:T(8,128)}) %reduce-scatter.5.cloned.1.call-update) | async-done | bytes 131088 | tf_op jit(solution)/shard_map/reduce_scatter | solution.py:85
  320.8 121.4 %reduce-scatter.7.cloned.1.call-done = f32[192,1024]{1,0:T(8,128)} async-done(((f32[1536,1024]{1,0:T(8,128)}), f32[192,1024]{1,0:T(8,128)}) %reduce-scatter.7.cloned.1.call-update) | async-done | bytes 786448
  (23 shorter events, 0.1 us)
Async XLA Ops:
  7.2 1.9 copy-start
  7.2 27.6 %copy-start.6 = (f32[1024]{0:T(1024)S(1)}, f32[1024]{0:T(1024)}, u32[]{:S(2)}) copy-start(f32[1024]{0:T(1024)} %param.9) | copy-start | bytes 12292
  7.2 27.6 %copy-start.7 = (f32[1024]{0:T(1024)S(1)}, f32[1024]{0:T(1024)}, u32[]{:S(2)}) copy-start(f32[1024]{0:T(1024)} %param.10) | copy-start | bytes 12292
  7.2 29.8 %copy-start.8 = (s32[128]{0:T(128)S(1)}, s32[128]{0:T(128)}, u32[]{:S(2)}) copy-start(s32[128]{0:T(128)} %param.13) | copy-start | bytes 1540
  7.2 58.6 %all-reduce.6.cloned.1.call-start = ((), (), s32[]{:S(2)}) async-start(), calls=%async_computation.2 | async-start | bytes 262144 | tf_op jit(solution)/shard_map/psum | solution.py:15
  37.0 214.8 %all-reduce.8.cloned.1.call-start = ((), (), s32[]{:S(2)}) async-start(), calls=%async_computation.3 | async-start | bytes 262144 | tf_op jit(solution)/shard_map/psum | solution.py:15
  70.8 1.3 copy-start.1
  219.6 32.2 %copy-start.2 = (f32[128,256]{1,0:T(8,128)S(1)}, f32[128,256]{1,0:T(8,128)}, u32[]{:S(2)}) copy-start(f32[128,256]{1,0:T(8,128)} %all-reduce.6.cloned.1.call-done) | copy-start | bytes 393220
  224.4 96.4 %reduce-scatter.5.cloned.1.call-start = ((), (), s32[]{:S(2)}) async-start(), calls=%async_computation.4 | async-start | bytes 1179648 | tf_op jit(solution)/shard_map/reduce_scatter | solution.py:85
  253.9 0.6 copy-start.4
  254.6 28.5 %copy-start.3 = (bf16[128,1536]{1,0:T(8,128)(2,1)S(1)}, bf16[128,1536]{1,0:T(8,128)(2,1)}, u32[]{:S(2)}) copy-start(bf16[128,1536]{1,0:T(8,128)(2,1)} %param.7) | copy-start | bytes 1179652
  257.1 185.2 %reduce-scatter.7.cloned.1.call-start = ((), (), s32[]{:S(2)}) async-start(), calls=%async_computation.5 | async-start | bytes 7077888
  282.4 5.6 %copy-start.5 = (f32[1024]{0:T(1024)}, f32[1024]{0:T(1024)S(1)}, u32[]{:S(2)}) copy-start(f32[1024]{0:T(1024)S(1)} %get-tuple-element.26) | copy-start | bytes 12292
Sparse Core Ops, SparseCore 0:
  37.1 28.6 all-reduce.5
  224.5 27.2 all-reduce.7
  257.2 63.5 reduce-scatter.4
  325.3 116.9 reduce-scatter.6
where the time goes:
time: 450 us; the launch traced here: 449 us
  waiting for transfers between devices  202 us (45%)
  blocking collectives  166 us (37%)
  matrix products  40.8 us (9%)
  local copies, waits for them, and re-layouts  16.6 us (4%)
  between operations  13.9 us (3%)
  other arithmetic  9.44 us (2%)
    psum x5, blocking collectives, batch_sums(): return lax.psum(values, 'batch')  149 us
    unnamed x5, waiting for transfers between devices  121 us
    psum x2, waiting for transfers between devices, proto_sums(): return lax.psum(values, 'proto')  53.9 us
    reduce_scatter x1, waiting for transfers between devices, body(): lax.psum_scatter(second_local, 'batch', scatter_dimension=1, tiled=True)  26.3 us
    psum x3, blocking collectives, proto_sums(): return lax.psum(values, 'proto')  17.4 us
    unnamed x19, local copies, waits for them, and re-layouts  10.3 us
    dot_general x3, matrix products, body(): jnp.dot(exponent_codes, scale_cols, precision=highest)  10.2 us
  transfers between devices with their start and end apart: 4, of which 4 were waited for; matrix products, arithmetic and copies ran while one was open for 4% of the time, Pallas kernels for 0%

commit v1 on v0

v1 whole, which is shorter than its diff:
```python
import functools

import jax
import jax.numpy as jnp
from jax import lax
from jax.experimental import pallas as pl
from jax.experimental.pallas import tpu as pltpu
from jax.sharding import PartitionSpec as P

ITERS = 3
F32 = jnp.float32
BF16 = jnp.bfloat16
HIGHEST = lax.Precision.HIGHEST

balancing_epsilon = 0.05
sharpness_divisor = 0.1
penalty_weighting = 64.0

VMEM_BYTES = 48 * 1024 * 1024


def stages(n, first):
    out, stride = [], 1
    while stride < n:
        left = n // stride
        radix = first if stride == 1 else (4 if left % 4 == 0 else 2)
        radix = min(radix, left)
        out.append((stride, radix))
        stride *= radix
    return out


def swap(v, axis, mask):
    n = lax.axis_size(axis)
    return lax.ppermute(v, axis, [(i, i ^ mask) for i in range(n)])


def add_parts(parts):
    if len(parts) == 1:
        return parts[0]
    if len(parts) == 2:
        return parts[0] + parts[1]
    return (parts[0] + parts[1]) + (parts[2] + parts[3])


def exchange(v, axis, first):
    n = lax.axis_size(axis)
    if n & (n - 1):
        return [lax.psum(v, axis)]
    parts = [v]
    for stride, radix in stages(n, first):
        v = add_parts(parts)
        parts = [v] + [swap(v, axis, k * stride) for k in range(1, radix)]
    return parts


def batch_parts(v):
    n = lax.axis_size("batch")
    return exchange(v, "batch", 2 if (n.bit_length() - 1) % 2 else 4)


def proto_parts(v):
    return exchange(v, "proto", 2)


def whole(shape):
    return pl.BlockSpec(shape, lambda *_: (0,) * len(shape))


def params(**kw):
    return pltpu.CompilerParams(vmem_limit_bytes=VMEM_BYTES, **kw)


def cost(flops, nbytes, trans=0):
    return pl.CostEstimate(flops=int(flops), bytes_accessed=int(nbytes), transcendentals=int(trans))


def dot(a, b, dims, precision=None):
    return lax.dot_general(a, b, ((dims[0], dims[1]), ((), ())), precision=precision, preferred_element_type=F32)


def eye(n):
    return lax.broadcasted_iota(jnp.int32, (n, n), 0) == lax.broadcasted_iota(jnp.int32, (n, n), 1)


def to_lanes(col):
    n = col.shape[0]
    return jnp.sum(jnp.where(eye(n), col, 0.0), axis=0, keepdims=True)


def to_column(row):
    n = row.shape[1]
    return jnp.sum(jnp.where(eye(n), row, 0.0), axis=1, keepdims=True)


def first_kernel(f_ref, w_ref, pre_ref, mom_ref):
    pre = jnp.dot(f_ref[...], w_ref[...], preferred_element_type=F32)
    pre_ref[...] = pre
    mom_ref[0:1, :] = jnp.sum(pre, axis=0, keepdims=True)
    mom_ref[1:2, :] = jnp.sum(pre * pre, axis=0, keepdims=True)


def first_layer(features, w_first):
    rows, depth = features.shape
    hidden = w_first.shape[1]
    blk = min(256, hidden)
    return pl.pallas_call(
        first_kernel,
        grid=(hidden // blk,),
        in_specs=[whole((rows, depth)), pl.BlockSpec((depth, blk), lambda j: (0, j))],
        out_specs=[pl.BlockSpec((rows, blk), lambda j: (0, j)), pl.BlockSpec((2, blk), lambda j: (0, j))],
        out_shape=[jax.ShapeDtypeStruct((rows, hidden), F32), jax.ShapeDtypeStruct((2, hidden), F32)],
        compiler_params=params(),
        cost_estimate=cost(2 * rows * depth * hidden, 2 * depth * hidden + 4 * rows * hidden),
        name="first_layer",
    )(features, w_first)


def batch_norm(pre, stats, gain, shift):
    normed = (pre - stats[0:1, :]) * stats[1:2, :]
    return normed, gain * normed + shift


def second_kernel(crops_all, n_parts, *refs):
    parts = refs[:n_parts]
    pre_ref, gain_ref, shift_ref, w_ref, emb_ref, stats_ref = refs[n_parts:]
    moments = add_parts([p[...] for p in parts]) / crops_all
    mean = moments[0:1, :]
    var = moments[1:2, :] - mean * mean
    stats_ref[0:1, :] = mean
    stats_ref[1:2, :] = lax.rsqrt(var + 1e-05)
    _, shifted = batch_norm(pre_ref[...], stats_ref[...], gain_ref[...], shift_ref[...])
    low = jnp.maximum(shifted, 0.0).astype(BF16)
    emb_ref[...] = jnp.dot(low, w_ref[...], preferred_element_type=F32)


def second_layer(crops_all, parts, pre, gain, shift, w_second):
    rows, hidden = pre.shape
    width = w_second.shape[1]
    return pl.pallas_call(
        functools.partial(second_kernel, crops_all, len(parts)),
        out_shape=[jax.ShapeDtypeStruct((rows, width), F32), jax.ShapeDtypeStruct((2, hidden), F32)],
        compiler_params=params(),
        cost_estimate=cost(2 * rows * hidden * width, 4 * rows * hidden + 2 * hidden * width),
        name="second_layer",
    )(*parts, pre, gain, shift, w_second)


def unit_kernel(p_ref, u_ref):
    wide = p_ref[...].astype(F32)
    u_ref[...] = (wide * lax.rsqrt(jnp.sum(wide * wide, 1, keepdims=True) + 1e-06)).astype(BF16)


def unit_rows(prototypes):
    rows, width = prototypes.shape
    blk = min(1024, rows)
    return pl.pallas_call(
        unit_kernel,
        grid=(rows // blk,),
        in_specs=[pl.BlockSpec((blk, width), lambda j: (j, 0))],
        out_specs=pl.BlockSpec((blk, width), lambda j: (j, 0)),
        out_shape=jax.ShapeDtypeStruct((rows, width), BF16),
        compiler_params=params(),
        cost_estimate=cost(4 * rows * width, 4 * rows * width),
        name="unit_rows",
    )(prototypes)


def embed(raw):
    inv_norm = lax.rsqrt(jnp.sum(raw * raw, 1, keepdims=True) + 1e-06)
    return raw * inv_norm, inv_norm


def score_kernel(n_parts, *refs):
    parts = refs[:n_parts]
    u_ref, codes_ref, logits_ref, col_ref, denom_ref, total = refs[n_parts:]
    j = pl.program_id(0)
    raw = add_parts([p[...] for p in parts])
    embedded, _ = embed(raw)
    scores = dot(embedded.astype(BF16), u_ref[...], ((1,), (1,)))
    logits = jnp.exp(scores / sharpness_divisor)
    codes = logits * logits
    codes_ref[...] = codes
    logits_ref[...] = logits.astype(BF16)
    col_ref[...] = jnp.sum(codes, axis=0, keepdims=True)

    @pl.when(j == 0)
    def _():
        total[...] = jnp.zeros_like(total)

    total[...] += jnp.sum(logits, axis=1, keepdims=True)

    @pl.when(j == pl.num_programs(0) - 1)
    def _():
        denom_ref[...] = to_lanes(total[...])


def score(parts, units):
    rows, width = parts[0].shape
    protos = units.shape[0]
    blk = min(1024, protos)
    return pl.pallas_call(
        functools.partial(score_kernel, len(parts)),
        grid=(protos // blk,),
        in_specs=[whole((rows, width))] * len(parts) + [pl.BlockSpec((blk, width), lambda j: (j, 0))],
        out_specs=[
            pl.BlockSpec((rows, blk), lambda j: (0, j)),
            pl.BlockSpec((rows, blk), lambda j: (0, j)),
            pl.BlockSpec((1, blk), lambda j: (0, j)),
            whole((1, rows)),
        ],
        out_shape=[
            jax.ShapeDtypeStruct((rows, protos), F32),
            jax.ShapeDtypeStruct((rows, protos), BF16),
            jax.ShapeDtypeStruct((1, protos), F32),
            jax.ShapeDtypeStruct((1, rows), F32),
        ],
        scratch_shapes=[pltpu.VMEM((rows, 1), F32)],
        compiler_params=params(),
        cost_estimate=cost(2 * rows * protos * width, 6 * rows * protos, rows * protos),
        name="score",
    )(*parts, units)


def pack(table, lane_row, out_ref):
    rows, width = table.shape
    out_ref[0:rows, :] = table
    out_ref[rows:, :] = jnp.zeros((8, width), F32)
    out_ref[rows : rows + 1, 0:rows] = lane_row


def logit_kernel(l_ref, u_ref, d_ref, out_ref):
    pack(jnp.dot(l_ref[...], u_ref[...], preferred_element_type=F32), d_ref[...], out_ref)


def logit_sum(logits, units, denom):
    rows, protos = logits.shape
    width = units.shape[1]
    return pl.pallas_call(
        logit_kernel,
        out_shape=jax.ShapeDtypeStruct((rows + 8, width), F32),
        compiler_params=params(),
        cost_estimate=cost(2 * rows * protos * width, 2 * rows * protos + 2 * protos * width),
        name="logit_sum",
    )(logits, units, denom)


def row_kernel(n_parts, *refs):
    parts = refs[:n_parts]
    codes_ref, out_ref = refs[n_parts:]
    scale = 1.0 / add_parts([p[...] for p in parts])
    out_ref[...] = to_lanes(jnp.sum(codes_ref[...] * scale, axis=1, keepdims=True))


def row_pass(parts, codes):
    rows, protos = codes.shape
    return pl.pallas_call(
        functools.partial(row_kernel, len(parts)),
        out_shape=jax.ShapeDtypeStruct((1, rows), F32),
        compiler_params=params(),
        cost_estimate=cost(2 * rows * protos, 4 * rows * protos),
        name="row_pass",
    )(*parts, codes)


def col_kernel(n_parts, *refs):
    parts = refs[:n_parts]
    codes_ref, out_ref = refs[n_parts:]
    scale = to_column(1.0 / add_parts([p[...] for p in parts]))
    out_ref[...] = jnp.sum(codes_ref[...] * scale, axis=0, keepdims=True)


def col_pass(parts, codes):
    rows, protos = codes.shape
    return pl.pallas_call(
        functools.partial(col_kernel, len(parts)),
        out_shape=jax.ShapeDtypeStruct((1, protos), F32),
        compiler_params=params(),
        cost_estimate=cost(2 * rows * protos, 4 * rows * protos),
        name="col_pass",
    )(*parts, codes)


def target_kernel(n_parts, *refs):
    parts = refs[:n_parts]
    codes_ref, u_ref, partner_ref, out_ref = refs[n_parts:]
    rows = codes_ref.shape[0]
    scale = 1.0 / add_parts([p[...] for p in parts])
    weighted = codes_ref[...] * scale
    mass = jnp.sum(weighted, axis=1, keepdims=True)
    table = jnp.dot(weighted.astype(BF16), u_ref[...], preferred_element_type=F32)
    chosen = partner_ref[...] == lax.broadcasted_iota(jnp.int32, (rows, rows), 1)
    moved = dot(jnp.where(chosen, 1.0, 0.0).astype(F32), table, ((1,), (0,)), HIGHEST)
    pack(moved, jnp.sum(jnp.where(chosen, mass, 0.0), axis=0, keepdims=True), out_ref)


def target_sum(parts, codes, units, partner):
    rows, protos = codes.shape
    width = units.shape[1]
    return pl.pallas_call(
        functools.partial(target_kernel, len(parts)),
        out_shape=jax.ShapeDtypeStruct((rows + 8, width), F32),
        compiler_params=params(),
        cost_estimate=cost(2 * rows * protos * width, 4 * rows * protos + 2 * protos * width),
        name="target_sum",
    )(*parts, codes, units, partner)


def loss_kernel(n_raw, n_logit, n_target, *refs):
    raw = add_parts([p[...] for p in refs[:n_raw]])
    refs = refs[n_raw:]
    logit = add_parts([p[...] for p in refs[:n_logit]])
    refs = refs[n_logit:]
    target = add_parts([p[...] for p in refs[:n_target]])
    grad_ref, loss_ref = refs[n_target:]
    rows = raw.shape[0]
    embedded, inv_norm = embed(raw)
    denom_lanes = logit[rows : rows + 1, 0:rows]
    denom = to_column(denom_lanes)
    row_scale = to_column(1.0 / target[rows : rows + 1, 0:rows])
    wanted = target[0:rows, :] * row_scale
    emb_low = embedded.astype(BF16).astype(F32)
    cross = jnp.sum(wanted * emb_low, axis=1, keepdims=True)
    loss_ref[...] = jnp.log(denom_lanes) - to_lanes(cross) / sharpness_divisor
    emb_grad = penalty_weighting * (logit[0:rows, :] / denom - wanted) / sharpness_divisor
    inner = jnp.sum(embedded * emb_grad, 1, keepdims=True)
    grad_ref[...] = (emb_grad - embedded * inner) * inv_norm


def loss_grad(raw_parts, logit_parts, target_parts):
    rows, width = raw_parts[0].shape
    return pl.pallas_call(
        functools.partial(loss_kernel, len(raw_parts), len(logit_parts), len(target_parts)),
        out_shape=[jax.ShapeDtypeStruct((rows, width), F32), jax.ShapeDtypeStruct((1, rows), F32)],
        compiler_params=params(),
        cost_estimate=cost(20 * rows * width, 24 * rows * width),
        name="loss_grad",
    )(*raw_parts, *logit_parts, *target_parts)


def tail_kernel(crops_all, n_feat, n_grad, e_cols, *refs):
    feat_at, grad_at, pre_ref, stats_ref, gain_ref, shift_ref, w_ref = refs[:7]
    refs = refs[7:]
    feats, refs = refs[:n_feat], refs[n_feat:]
    grads, refs = refs[:n_grad], refs[n_grad:]
    w1_ref, w2_ref, gain_grad_ref, shift_grad_ref, feat_all, grad_all, grad_cols = refs

    @pl.when(pl.program_id(0) == 0)
    def _():
        for k in range(n_feat):
            rows = feats[k].shape[0]
            start = pl.multiple_of(feat_at[k] * rows, rows)
            feat_all[pl.ds(start, rows), :] = feats[k][...].astype(BF16)
        for k in range(n_grad):
            rows = grads[k].shape[0]
            start = pl.multiple_of(grad_at[k] * rows, rows)
            grad_all[pl.ds(start, rows), :] = grads[k][...].astype(BF16)
        shape = (grad_cols.shape[0], grad_all.shape[1])
        mine = lax.broadcasted_iota(jnp.int32, shape, 0) + grad_at[n_grad] * e_cols
        chosen = mine == lax.broadcasted_iota(jnp.int32, shape, 1)
        picked = dot(jnp.where(chosen, 1.0, 0.0).astype(BF16), grad_all[...], ((1,), (1,)))
        grad_cols[...] = picked.astype(BF16)

    stats = stats_ref[...]
    gain = gain_ref[...]
    normed, shifted = batch_norm(pre_ref[...], stats, gain, shift_ref[...])
    hidden = jnp.maximum(shifted, 0.0).astype(BF16)
    w2_ref[...] = jnp.dot(grad_cols[...], hidden, preferred_element_type=F32)[0:e_cols, :]
    hidden_grad = dot(grad_all[...], w_ref[...], ((1,), (1,)))
    bn_grad = jnp.where(shifted > 0, hidden_grad, 0.0)
    shift_grad = jnp.sum(bn_grad, axis=0, keepdims=True)
    gain_grad = jnp.sum(bn_grad * normed, axis=0, keepdims=True)
    shift_grad_ref[...] = shift_grad
    gain_grad_ref[...] = gain_grad
    pre_grad = gain * stats[1:2, :] * (bn_grad - shift_grad / crops_all - normed * (gain_grad / crops_all))
    w1_ref[...] = dot(feat_all[...], pre_grad.astype(BF16), ((0,), (0,)))


def tail(pre_all, stats, gain, shift, w_second, feats, feat_at, grads, grad_at, d_cols, e_cols):
    crops_all, hidden = pre_all.shape
    width = w_second.shape[1]
    blk = min(hidden, max(128, 256 * 1024 // crops_all))
    smem = pl.BlockSpec(memory_space=pltpu.SMEM)
    vmem = pl.BlockSpec(memory_space=pltpu.VMEM)

    def cols(n):
        return pl.BlockSpec((n, blk), lambda j: (0, j))

    return pl.pallas_call(
        functools.partial(tail_kernel, crops_all, len(feats), len(grads), e_cols),
        grid=(hidden // blk,),
        in_specs=[smem, smem, cols(crops_all), cols(2), cols(1), cols(1), pl.BlockSpec((blk, width), lambda j: (j, 0))]
        + [vmem] * (len(feats) + len(grads)),
        out_specs=[cols(d_cols), cols(e_cols), cols(1), cols(1)],
        out_shape=[
            jax.ShapeDtypeStruct((d_cols, hidden), F32),
            jax.ShapeDtypeStruct((e_cols, hidden), F32),
            jax.ShapeDtypeStruct((1, hidden), F32),
            jax.ShapeDtypeStruct((1, hidden), F32),
        ],
        scratch_shapes=[
            pltpu.VMEM((crops_all, d_cols), BF16),
            pltpu.VMEM((crops_all, width), BF16),
            pltpu.VMEM((-(-e_cols // 16) * 16, crops_all), BF16),
        ],
        compiler_params=params(),
        cost_estimate=cost(2 * crops_all * hidden * (width + d_cols), 4 * crops_all * hidden),
        name="tail",
    )(feat_at, grad_at, pre_all, stats, gain, shift, w_second, *feats, *grads)


def rotate(v, axis, k):
    n = lax.axis_size(axis)
    return lax.ppermute(v, axis, [(i, (i + k) % n) for i in range(n)])


def body(features, w_first, bn_gain, bn_shift, w_second, prototypes, partner):
    n_batch = lax.axis_size("batch")
    me = lax.axis_index("batch")
    rows, depth = features.shape
    width = w_second.shape[1]
    crops_all = rows * n_batch
    d_cols, e_cols = depth // n_batch, width // n_batch
    small = n_batch <= 8
    gain, shift = bn_gain[None, :], bn_shift[None, :]

    pre, moments = first_layer(features, w_first)
    pre_all = lax.all_gather(pre, "batch", tiled=True)
    moment_parts = batch_parts(moments)
    emb_part, stats = second_layer(crops_all, moment_parts, pre, gain, shift, w_second)
    raw_parts = proto_parts(emb_part)

    by_owner = jnp.swapaxes(features.astype(F32).reshape(rows, n_batch, d_cols), 0, 1)
    by_owner, _ = lax.optimization_barrier((by_owner, emb_part))
    if small:
        feats = [lax.dynamic_index_in_dim(by_owner, me, 0, False)]
        for k in range(1, n_batch):
            piece = lax.dynamic_index_in_dim(by_owner, lax.rem(me + k, n_batch), 0, False)
            feats.append(rotate(piece, "batch", k))
        feat_at = lax.rem(me - jnp.arange(n_batch, dtype=jnp.int32) + n_batch, n_batch)
    else:
        feats = [lax.all_to_all(by_owner, "batch", 0, 0).reshape(crops_all, d_cols)]
        feat_at = jnp.zeros((1,), jnp.int32)

    units = unit_rows(prototypes)
    codes, logits, col_part, denom = score(raw_parts, units)
    logit_parts = proto_parts(logit_sum(logits, units, denom))
    for iteration in range(ITERS - 1):
        row_part = row_pass(batch_parts(col_part), codes)
        col_part = col_pass(proto_parts(row_part), codes)
    target_parts = proto_parts(target_sum(batch_parts(col_part), codes, units, partner[:, None]))
    raw_grad, penalty = loss_grad(raw_parts, logit_parts, target_parts)

    if small:
        grads = [raw_grad] + [rotate(raw_grad, "batch", k) for k in range(1, n_batch)]
        grad_at = lax.rem(me - jnp.arange(n_batch, dtype=jnp.int32) + n_batch, n_batch)
    else:
        grads = [lax.all_gather(raw_grad, "batch", tiled=True)]
        grad_at = jnp.zeros((1,), jnp.int32)
    grad_at = jnp.concatenate([grad_at, me[None].astype(jnp.int32)])
    grad_w1, grad_w2, grad_gain, grad_shift = tail(
        pre_all, stats, gain, shift, w_second, feats, feat_at, grads, grad_at, d_cols, e_cols
    )
    return (penalty[0], grad_w1, grad_gain[0], grad_shift[0], grad_w2.T)


def solution(mesh):
    return jax.shard_map(
        body,
        mesh=mesh,
        in_specs=(
            P("batch", None),
            P(None, "proto"),
            P("proto"),
            P("proto"),
            P("proto", None),
            P("proto", None),
            P("batch"),
        ),
        out_specs=(P("batch"), P("batch", "proto"), P("proto"), P("proto"), P("proto", "batch")),
        check_vma=False,
    )
```

time: 450 us -> 153 us (0.34)
  the two profiles are of different devices: /device:TPU:0 before, /device:TPU:28 now
where the time goes in v1:
time: 153 us
  starting transfers between devices  62.3 us (41%)
  waiting for transfers between devices  51.2 us (33%)
  Pallas kernels  17.2 us (11%)
  between operations  14.4 us (9%)
  local copies, waits for them, and re-layouts  7.61 us (5%)
    ppermute x26, waiting for transfers between devices, swap(): return lax.ppermute(v, axis, [(i, i ^ mask) for i in range(n)])  36.4 us
    ppermute x14, starting transfers between devices, rotate(): return lax.ppermute(v, axis, [(i, (i + k) % n) for i in range(n)])  34.9 us
    ppermute x26, starting transfers between devices, swap(): return lax.ppermute(v, axis, [(i, i ^ mask) for i in range(n)])  27.4 us
    ppermute x14, waiting for transfers between devices, rotate(): return lax.ppermute(v, axis, [(i, (i + k) % n) for i in range(n)])  14.7 us
    pallas_call x1, Pallas kernels, tail(): pl.pallas_call(functools.partial(tail_kernel, crops_all, len(feats), len(...  7.09 us
    unnamed x27, local copies, waits for them, and re-layouts  6.69 us
  transfers between devices with their start and end apart: 41, of which 24 were waited for; matrix products, arithmetic and copies ran while one was open for 1% of the time, Pallas kernels for 5%

profile of v1, /device:TPU:28, one launch (start us, length us, event | category | flops | bytes accessed | tf_op | source)
XLA Modules:
  0.0 153.0 jit_solution(88265420749234425)
XLA Ops:
  7.2 1.9 %copy-done.2 = bf16[1536,1024]{1,0:T(8,128)(2,1)S(1)} copy-done((bf16[1536,1024]{1,0:T(8,128)(2,1)S(1)}, bf16[1536,1024]{1,0:T(8,128)(2,1)}, u32[]{:S(2)}) %copy-start.2) | copy-done | bytes 3145752
  9.1 1.0 copy-done.5
  10.1 2.5 %first_layer.1 = (f32[128,1024]{1,0:T(8,128)}, f32[2,1024]{1,0:T(2,128)S(1)}) custom-call(bf16[128,1536]{1,0:T(8,128)(2,1)S(1)} %copy-done.5, bf16[1536,1024]{1,0:T(8,128)(2,1)S(1)} %copy-done.2), custom_call_target="tpu_custom_call" | custom-call | flops 402653184 | bytes 3670016 | tf_op jit(solution)/shard_map/first_layer/pallas_call | solution.py:107
  13.2 3.1 %collective-permute-done = f32[2,1024]{1,0:T(2,128)S(1)} collective-permute-done((f32[2,1024]{1,0:T(2,128)S(1)}, f32[2,1024]{1,0:T(2,128)S(1)}, u32[]{:S(2)}, u32[]{:S(2)}) %collective-permute-start) | collective-permute-done | bytes 8224 | tf_op jit(solution)/shard_map/ppermute | solution.py:35
  17.1 3.6 %collective-permute-start.3 = (f32[2,1024]{1,0:T(2,128)S(1)}, f32[2,1024]{1,0:T(2,128)S(1)}, u32[]{:S(2)}, u32[]{:S(2)}) collective-permute-start(f32[2,1024]{1,0:T(2,128)S(1)} %add.77.refs_0_), channel_id=1, source_target_pairs={{0,24},{4,28},{8,16},{12,20},{16,8},{20,12},{24,0},{28,4},{1,25},{... | collective-permute-start | bytes 24584 | tf_op jit(solution)/shard_map/ppermute | solution.py:35
  21.4 1.2 collective-permute-done.3.refs_3_
  22.6 1.4 second_layer.1
  24.1 1.3 collective-permute-done.4
  25.4 1.6 %collective-permute-start.5 = (f32[128,256]{1,0:T(8,128)S(1)}, f32[128,256]{1,0:T(8,128)S(1)}, u32[]{:S(2)}, u32[]{:S(2)}) collective-permute-start(f32[128,256]{1,0:T(8,128)S(1)} %add.78.refs_0_), channel_id=1, source_target_pairs={{0,2},{1,3},{2,0},{3,1},{4,6},{5,7},{6,4},{7,5},{8,10},{9,11},{10,... | collective-permute-start | bytes 393224 | tf_op jit(solution)/shard_map/ppermute | solution.py:35
  27.0 0.9 unit_rows.1.refs_2_.u_ref.refs_5_
  27.9 3.1 %collective-permute-done.5.refs_1_ = f32[128,256]{1,0:T(8,128)S(1)} collective-permute-done((f32[128,256]{1,0:T(8,128)S(1)}, f32[128,256]{1,0:T(8,128)S(1)}, u32[]{:S(2)}, u32[]{:S(2)}) %collective-permute-start.5) | collective-permute-done | bytes 131104 | tf_op jit(solution)/shard_map/ppermute | solution.py:35
  31.0 2.2 %score.1 = (f32[128,4096]{1,0:T(8,128)S(1)}, bf16[128,4096]{1,0:T(8,128)(2,1)S(1)}, f32[1,4096]{1,0:T(1,128)S(1)}, f32[1,128]{1,0:T(1,128)S(1)}) custom-call(f32[128,256]{1,0:T(8,128)S(1)} %add.78.refs_0_, f32[128,256]{1,0:T(8,128)S(1)} %collective-permute-done.5.refs_1_, bf16[4096,256]{1,0:T(8,128)(2,1)S(1)} %unit_rows.1.refs_2_.u_ref.refs_5_), custom_call_target="tpu_custom_call" | custom-call | flops 268435456 | bytes 3145728 | tf_op jit(solution)/shard_map/score/pallas_call | solution.py:202
  33.7 3.4 %collective-permute-done.8 = f32[1,4096]{1,0:T(1,128)S(1)} collective-permute-done((f32[1,4096]{1,0:T(1,128)S(1)}, f32[1,4096]{1,0:T(1,128)S(1)}, u32[]{:S(2)}, u32[]{:S(2)}) %collective-permute-start.8) | collective-permute-done | bytes 16416 | tf_op jit(solution)/shard_map/ppermute | solution.py:35
  37.5 3.9 %collective-permute-start.10 = (f32[1,4096]{1,0:T(1,128)S(1)}, f32[1,4096]{1,0:T(1,128)S(1)}, u32[]{:S(2)}, u32[]{:S(2)}) collective-permute-start(f32[1,4096]{1,0:T(1,128)S(1)} %add.80.refs_0_), channel_id=1, source_target_pairs={{0,16},{4,20},{8,24},{12,28},{16,0},{20,4},{24,8},{28,12},{1,17},{... | collective-permute-start | bytes 49160 | tf_op jit(solution)/shard_map/ppermute | solution.py:35
  41.6 1.5 collective-permute-done.10.refs_2_
  43.1 3.8 %collective-permute-done.11.refs_3_ = f32[1,4096]{1,0:T(1,128)S(1)} collective-permute-done((f32[1,4096]{1,0:T(1,128)S(1)}, f32[1,4096]{1,0:T(1,128)S(1)}, u32[]{:S(2)}, u32[]{:S(2)}) %collective-permute-start.11) | collective-permute-done | bytes 16416 | tf_op jit(solution)/shard_map/ppermute | solution.py:35
  47.2 1.1 collective-permute-done.12
  48.3 1.5 collective-permute-start.13
  49.8 2.1 %collective-permute-done.13.refs_1_ = f32[1,128]{1,0:T(1,128)S(1)} collective-permute-done((f32[1,128]{1,0:T(1,128)S(1)}, f32[1,128]{1,0:T(1,128)S(1)}, u32[]{:S(2)}, u32[]{:S(2)}) %collective-permute-start.13) | collective-permute-done | bytes 544 | tf_op jit(solution)/shard_map/ppermute | solution.py:35
  52.8 3.6 %collective-permute-done.14 = f32[1,4096]{1,0:T(1,128)S(1)} collective-permute-done((f32[1,4096]{1,0:T(1,128)S(1)}, f32[1,4096]{1,0:T(1,128)S(1)}, u32[]{:S(2)}, u32[]{:S(2)}) %collective-permute-start.14) | collective-permute-done | bytes 16416 | tf_op jit(solution)/shard_map/ppermute | solution.py:35
  57.2 3.6 %collective-permute-start.17 = (f32[1,4096]{1,0:T(1,128)S(1)}, f32[1,4096]{1,0:T(1,128)S(1)}, u32[]{:S(2)}, u32[]{:S(2)}) collective-permute-start(f32[1,4096]{1,0:T(1,128)S(1)} %add.82.refs_0_), channel_id=1, source_target_pairs={{0,24},{4,28},{8,16},{12,20},{16,8},{20,12},{24,0},{28,4},{1,25},{... | collective-permute-start | bytes 49160 | tf_op jit(solution)/shard_map/ppermute | solution.py:35
  61.3 1.8 %collective-permute-done.16.refs_2_ = f32[1,4096]{1,0:T(1,128)S(1)} collective-permute-done((f32[1,4096]{1,0:T(1,128)S(1)}, f32[1,4096]{1,0:T(1,128)S(1)}, u32[]{:S(2)}, u32[]{:S(2)}) %collective-permute-start.16) | collective-permute-done | bytes 16416 | tf_op jit(solution)/shard_map/ppermute | solution.py:35
  63.7 1.1 collective-permute-done.18
  64.8 1.5 collective-permute-start.19
  66.3 2.1 %collective-permute-done.19.refs_1_ = f32[1,128]{1,0:T(1,128)S(1)} collective-permute-done((f32[1,128]{1,0:T(1,128)S(1)}, f32[1,128]{1,0:T(1,128)S(1)}, u32[]{:S(2)}, u32[]{:S(2)}) %collective-permute-start.19) | collective-permute-done | bytes 544 | tf_op jit(solution)/shard_map/ppermute | solution.py:35
  69.2 1.0 copy.15
  70.3 2.2 %collective-permute-done.20 = f32[1,4096]{1,0:T(1,128)S(1)} collective-permute-done((f32[1,4096]{1,0:T(1,128)S(1)}, f32[1,4096]{1,0:T(1,128)S(1)}, u32[]{:S(2)}, u32[]{:S(2)}) %collective-permute-start.20) | collective-permute-done | bytes 16416 | tf_op jit(solution)/shard_map/ppermute | solution.py:35
  72.5 0.9 collective-permute-start.21
  73.4 3.1 %collective-permute-start.22 = (f32[1,4096]{1,0:T(1,128)S(1)}, f32[1,4096]{1,0:T(1,128)S(1)}, u32[]{:S(2)}, u32[]{:S(2)}) collective-permute-start(f32[1,4096]{1,0:T(1,128)S(1)} %add.84.refs_0_), channel_id=1, source_target_pairs={{0,16},{4,20},{8,24},{12,28},{16,0},{20,4},{24,8},{28,12},{1,17},{... | collective-permute-start | bytes 49160 | tf_op jit(solution)/shard_map/ppermute | solution.py:35
  76.9 1.6 %copy-done.1 = bf16[4096,256]{1,0:T(8,128)(2,1)S(1)} copy-done((bf16[4096,256]{1,0:T(8,128)(2,1)S(1)}, bf16[4096,256]{1,0:T(8,128)(2,1)}, u32[]{:S(2)}) %copy-start.1) | copy-done | bytes 2097176
  78.5 1.2 copy-done.8
  80.3 2.1 %collective-permute-done.23.refs_3_ = f32[1,4096]{1,0:T(1,128)S(1)} collective-permute-done((f32[1,4096]{1,0:T(1,128)S(1)}, f32[1,4096]{1,0:T(1,128)S(1)}, u32[]{:S(2)}, u32[]{:S(2)}) %collective-permute-start.23) | collective-permute-done | bytes 16416 | tf_op jit(solution)/shard_map/ppermute | solution.py:35
  83.5 1.5 collective-permute-start.7
  85.0 1.2 collective-permute-start.25
  86.4 1.5 collective-permute-start.26
  88.5 1.5 collective-permute-done.7.refs_3_
  90.0 2.8 %collective-permute-start.29 = (f32[128,192]{1,0:T(8,128)S(1)}, f32[128,192]{1,0:T(8,128)S(1)}, u32[]{:S(2)}, u32[]{:S(2)}) collective-permute-start(f32[128,192]{1,0:T(8,128)S(1)} %bitcast.26), channel_id=1, source_target_pairs={{0,16},{4,20},{8,24},{12,28},{16,0},{20,4},{24,8},{28,12},{1,17},{... | collective-permute-start | bytes 294920 | tf_op jit(solution)/shard_map/ppermute | solution.py:414
  93.5 1.0 collective-permute-start.33
  95.3 1.2 collective-permute-done.27.refs_9_
  96.5 0.9 collective-permute-start.30
  97.4 11.9 %collective-permute-start.31 = (f32[128,192]{1,0:T(8,128)S(1)}, f32[128,192]{1,0:T(8,128)S(1)}, u32[]{:S(2)}, u32[]{:S(2)}) collective-permute-start(f32[128,192]{1,0:T(8,128)S(1)} %bitcast.31), channel_id=1, source_target_pairs={{0,24},{4,28},{8,0},{12,4},{16,8},{20,12},{24,16},{28,20},{1,25},{... | collective-permute-start | bytes 294920 | tf_op jit(solution)/shard_map/ppermute | solution.py:414
  109.5 8.3 %collective-permute-start.35 = (f32[128,256]{1,0:T(8,128)S(1)}, f32[128,256]{1,0:T(8,128)S(1)}, u32[]{:S(2)}, u32[]{:S(2)}) collective-permute-start(f32[128,256]{1,0:T(8,128)S(1)} %get-tuple-element.30.refs_15_), channel_id=1, source_target_pairs={{0,12},{4,16},{8,20},{12,24},{16,28},{20,0},{24,4},{28,8},{1,13},{... | collective-permute-start | bytes 393224 | tf_op jit(solution)/shard_map/ppermute | solution.py:414
  117.7 1.9 %collective-permute-start.36 = (f32[128,256]{1,0:T(8,128)S(1)}, f32[128,256]{1,0:T(8,128)S(1)}, u32[]{:S(2)}, u32[]{:S(2)}) collective-permute-start(f32[128,256]{1,0:T(8,128)S(1)} %get-tuple-element.30.refs_15_), channel_id=1, source_target_pairs={{0,16},{4,20},{8,24},{12,28},{16,0},{20,4},{24,8},{28,12},{1,17},{... | collective-permute-start | bytes 393224 | tf_op jit(solution)/shard_map/ppermute | solution.py:414
  120.4 2.2 %collective-permute-start.38 = (f32[128,256]{1,0:T(8,128)S(1)}, f32[128,256]{1,0:T(8,128)S(1)}, u32[]{:S(2)}, u32[]{:S(2)}) collective-permute-start(f32[128,256]{1,0:T(8,128)S(1)} %get-tuple-element.30.refs_15_), channel_id=1, source_target_pairs={{0,24},{4,28},{8,0},{12,4},{16,8},{20,12},{24,16},{28,20},{1,25},{... | collective-permute-start | bytes 393224 | tf_op jit(solution)/shard_map/ppermute | solution.py:414
  122.6 3.5 %collective-permute-start.39 = (f32[128,256]{1,0:T(8,128)S(1)}, f32[128,256]{1,0:T(8,128)S(1)}, u32[]{:S(2)}, u32[]{:S(2)}) collective-permute-start(f32[128,256]{1,0:T(8,128)S(1)} %get-tuple-element.30.refs_15_), channel_id=1, source_target_pairs={{0,28},{4,0},{8,4},{12,8},{16,12},{20,16},{24,20},{28,24},{1,29},{... | collective-permute-start | bytes 393224 | tf_op jit(solution)/shard_map/ppermute | solution.py:414
  126.3 6.3 %collective-permute-done.36.refs_19_ = f32[128,256]{1,0:T(8,128)S(1)} collective-permute-done((f32[128,256]{1,0:T(8,128)S(1)}, f32[128,256]{1,0:T(8,128)S(1)}, u32[]{:S(2)}, u32[]{:S(2)}) %collective-permute-start.36) | collective-permute-done | bytes 131104 | tf_op jit(solution)/shard_map/ppermute | solution.py:414
  132.5 6.6 %collective-permute-done.37.refs_20_ = f32[128,256]{1,0:T(8,128)S(1)} collective-permute-done((f32[128,256]{1,0:T(8,128)S(1)}, f32[128,256]{1,0:T(8,128)S(1)}, u32[]{:S(2)}, u32[]{:S(2)}) %collective-permute-start.37) | collective-permute-done | bytes 131104 | tf_op jit(solution)/shard_map/ppermute | solution.py:414
  139.1 7.1 %tail.1 = (f32[192,1024]{1,0:T(8,128)}, f32[32,1024]{1,0:T(8,128)}, f32[1,1024]{1,0:T(1,128)}, f32[1,1024]{1,0:T(1,128)}) custom-call(s32[8]{0:T(128)S(1)} %compare_select_fusion.refs_0_, s32[9]{0:T(128)S(1)} %pad_add_fusion.refs_1_, f32[1024,1024]{1,0:T(8,128)} %all-gather.2.cloned.1.call-done.refs_2_, f32[2,1024]{1,0:T(2,128)S(1)} %get-tuple-element.28.refs_3_, ...), custom_call_target="tpu_custom_call" | custom-call | flops 939524096 | bytes 4194304 | tf_op jit(solution)/shard_map/tail/pallas_call | solution.py:389
  (96 shorter events, 12.7 us)
Async XLA Ops:
  7.2 131.9 %all-gather.2.cloned.1.call-start = ((), (), s32[]{:S(2)}) async-start(), calls=%async_computation | async-start | bytes 4718592 | tf_op jit(solution)/shard_map/all_gather | solution.py:428
  10.1 12.5 %copy-start.9 = (f32[1024]{0:T(1024)S(1)}, f32[1024]{0:T(1024)}, u32[]{:S(2)}) copy-start(f32[1024]{0:T(1024)} %param.9) | copy-start | bytes 12292
  10.1 12.5 %copy-start.10 = (f32[1024]{0:T(1024)S(1)}, f32[1024]{0:T(1024)}, u32[]{:S(2)}) copy-start(f32[1024]{0:T(1024)} %param.10) | copy-start | bytes 12292
  10.1 16.9 %copy-start.4 = (bf16[4096,256]{1,0:T(8,128)(2,1)S(1)}, bf16[4096,256]{1,0:T(8,128)(2,1)}, u32[]{:S(2)}) copy-start(bf16[4096,256]{1,0:T(8,128)(2,1)} %p_ref.1) | copy-start | bytes 6291460
  12.6 3.7 %collective-permute-start = (f32[2,1024]{1,0:T(2,128)S(1)}, f32[2,1024]{1,0:T(2,128)S(1)}, u32[]{:S(2)}, u32[]{:S(2)}) collective-permute-start(f32[2,1024]{1,0:T(2,128)S(1)} %get-tuple-element.20), channel_id=1, source_target_pairs={{0,4},{4,0},{8,12},{12,8},{16,20},{20,16},{24,28},{28,24},{1,5},{5... | collective-permute-start | bytes 24584 | tf_op jit(solution)/shard_map/ppermute | solution.py:35
  16.4 4.4 %collective-permute-start.1 = (f32[2,1024]{1,0:T(2,128)S(1)}, f32[2,1024]{1,0:T(2,128)S(1)}, u32[]{:S(2)}, u32[]{:S(2)}) collective-permute-start(f32[2,1024]{1,0:T(2,128)S(1)} %add.77.refs_0_), channel_id=1, source_target_pairs={{0,8},{4,12},{8,0},{12,4},{16,24},{20,28},{24,16},{28,20},{1,9},{5... | collective-permute-start | bytes 24584 | tf_op jit(solution)/shard_map/ppermute | solution.py:35
  16.8 4.5 %collective-permute-start.2 = (f32[2,1024]{1,0:T(2,128)S(1)}, f32[2,1024]{1,0:T(2,128)S(1)}, u32[]{:S(2)}, u32[]{:S(2)}) collective-permute-start(f32[2,1024]{1,0:T(2,128)S(1)} %add.77.refs_0_), channel_id=1, source_target_pairs={{0,16},{4,20},{8,24},{12,28},{16,0},{20,4},{24,8},{28,12},{1,17},{... | collective-permute-start | bytes 24584 | tf_op jit(solution)/shard_map/ppermute | solution.py:35
  17.1 5.4 %collective-permute-start.3 = (f32[2,1024]{1,0:T(2,128)S(1)}, f32[2,1024]{1,0:T(2,128)S(1)}, u32[]{:S(2)}, u32[]{:S(2)}) collective-permute-start(f32[2,1024]{1,0:T(2,128)S(1)} %add.77.refs_0_), channel_id=1, source_target_pairs={{0,24},{4,28},{8,16},{12,20},{16,8},{20,12},{24,0},{28,4},{1,25},{... | collective-permute-start | bytes 24584 | tf_op jit(solution)/shard_map/ppermute | solution.py:35
  24.0 1.4 collective-permute-start.4
  25.4 5.6 %collective-permute-start.5 = (f32[128,256]{1,0:T(8,128)S(1)}, f32[128,256]{1,0:T(8,128)S(1)}, u32[]{:S(2)}, u32[]{:S(2)}) collective-permute-start(f32[128,256]{1,0:T(8,128)S(1)} %add.78.refs_0_), channel_id=1, source_target_pairs={{0,2},{1,3},{2,0},{3,1},{4,6},{5,7},{6,4},{7,5},{8,10},{9,11},{10,... | collective-permute-start | bytes 393224 | tf_op jit(solution)/shard_map/ppermute | solution.py:35
  27.9 19.2 %copy-start = (bf16[4096,256]{1,0:T(8,128)(2,1)}, bf16[4096,256]{1,0:T(8,128)(2,1)S(1)}, u32[]{:S(2)}) copy-start(bf16[4096,256]{1,0:T(8,128)(2,1)S(1)} %unit_rows.1.refs_2_.u_ref.refs_5_) | copy-start | bytes 6291460
  33.3 18.9 %copy-start.7 = (bf16[128,4096]{1,0:T(8,128)(2,1)}, bf16[128,4096]{1,0:T(8,128)(2,1)S(1)}, u32[]{:S(2)}) copy-start(bf16[128,4096]{1,0:T(8,128)(2,1)S(1)} %get-tuple-element.23.l_ref) | copy-start | bytes 3145732
  33.3 3.8 %collective-permute-start.8 = (f32[1,4096]{1,0:T(1,128)S(1)}, f32[1,4096]{1,0:T(1,128)S(1)}, u32[]{:S(2)}, u32[]{:S(2)}) collective-permute-start(f32[1,4096]{1,0:T(1,128)S(1)} %get-tuple-element.25), channel_id=1, source_target_pairs={{0,4},{4,0},{8,12},{12,8},{16,20},{20,16},{24,28},{28,24},{1,5},{5... | collective-permute-start | bytes 49160 | tf_op jit(solution)/shard_map/ppermute | solution.py:35
  37.1 4.5 %collective-permute-start.9 = (f32[1,4096]{1,0:T(1,128)S(1)}, f32[1,4096]{1,0:T(1,128)S(1)}, u32[]{:S(2)}, u32[]{:S(2)}) collective-permute-start(f32[1,4096]{1,0:T(1,128)S(1)} %add.80.refs_0_), channel_id=1, source_target_pairs={{0,8},{4,12},{8,0},{12,4},{16,24},{20,28},{24,16},{28,20},{1,9},{5... | collective-permute-start | bytes 49160 | tf_op jit(solution)/shard_map/ppermute | solution.py:35
  37.5 5.6 %collective-permute-start.10 = (f32[1,4096]{1,0:T(1,128)S(1)}, f32[1,4096]{1,0:T(1,128)S(1)}, u32[]{:S(2)}, u32[]{:S(2)}) collective-permute-start(f32[1,4096]{1,0:T(1,128)S(1)} %add.80.refs_0_), channel_id=1, source_target_pairs={{0,16},{4,20},{8,24},{12,28},{16,0},{20,4},{24,8},{28,12},{1,17},{... | collective-permute-start | bytes 49160 | tf_op jit(solution)/shard_map/ppermute | solution.py:35
  41.4 5.5 %collective-permute-start.11 = (f32[1,4096]{1,0:T(1,128)S(1)}, f32[1,4096]{1,0:T(1,128)S(1)}, u32[]{:S(2)}, u32[]{:S(2)}) collective-permute-start(f32[1,4096]{1,0:T(1,128)S(1)} %add.80.refs_0_), channel_id=1, source_target_pairs={{0,24},{4,28},{8,16},{12,20},{16,8},{20,12},{24,0},{28,4},{1,25},{... | collective-permute-start | bytes 49160 | tf_op jit(solution)/shard_map/ppermute | solution.py:35
  47.1 1.2 collective-permute-start.12
  48.3 3.5 %collective-permute-start.13 = (f32[1,128]{1,0:T(1,128)S(1)}, f32[1,128]{1,0:T(1,128)S(1)}, u32[]{:S(2)}, u32[]{:S(2)}) collective-permute-start(f32[1,128]{1,0:T(1,128)S(1)} %add.81.refs_0_), channel_id=1, source_target_pairs={{0,2},{1,3},{2,0},{3,1},{4,6},{5,7},{6,4},{7,5},{8,10},{9,11},{10,... | collective-permute-start | bytes 1544 | tf_op jit(solution)/shard_map/ppermute | solution.py:35
  52.2 4.1 %collective-permute-start.14 = (f32[1,4096]{1,0:T(1,128)S(1)}, f32[1,4096]{1,0:T(1,128)S(1)}, u32[]{:S(2)}, u32[]{:S(2)}) collective-permute-start(f32[1,4096]{1,0:T(1,128)S(1)} %col_pass.2), channel_id=1, source_target_pairs={{0,4},{4,0},{8,12},{12,8},{16,20},{20,16},{24,28},{28,24},{1,5},{5... | collective-permute-start | bytes 49160 | tf_op jit(solution)/shard_map/ppermute | solution.py:35
  56.3 12.9 %copy-start.6 = (bf16[128,1536]{1,0:T(8,128)(2,1)S(1)}, bf16[128,1536]{1,0:T(8,128)(2,1)}, u32[]{:S(2)}) copy-start(bf16[128,1536]{1,0:T(8,128)(2,1)} %f_ref.1) | copy-start | bytes 1179652
  56.4 13.8 %copy-start.12 = (s32[128]{0:T(128)S(1)}, s32[128]{0:T(128)}, u32[]{:S(2)}) copy-start(s32[128]{0:T(128)} %param.13) | copy-start | bytes 1540
  56.4 4.9 %collective-permute-start.15 = (f32[1,4096]{1,0:T(1,128)S(1)}, f32[1,4096]{1,0:T(1,128)S(1)}, u32[]{:S(2)}, u32[]{:S(2)}) collective-permute-start(f32[1,4096]{1,0:T(1,128)S(1)} %add.82.refs_0_), channel_id=1, source_target_pairs={{0,8},{4,12},{8,0},{12,4},{16,24},{20,28},{24,16},{28,20},{1,9},{5... | collective-permute-start | bytes 49160 | tf_op jit(solution)/shard_map/ppermute | solution.py:35
  56.4 6.6 %collective-permute-start.16 = (f32[1,4096]{1,0:T(1,128)S(1)}, f32[1,4096]{1,0:T(1,128)S(1)}, u32[]{:S(2)}, u32[]{:S(2)}) collective-permute-start(f32[1,4096]{1,0:T(1,128)S(1)} %add.82.refs_0_), channel_id=1, source_target_pairs={{0,16},{4,20},{8,24},{12,28},{16,0},{20,4},{24,8},{28,12},{1,17},{... | collective-permute-start | bytes 49160 | tf_op jit(solution)/shard_map/ppermute | solution.py:35
  57.2 6.2 %collective-permute-start.17 = (f32[1,4096]{1,0:T(1,128)S(1)}, f32[1,4096]{1,0:T(1,128)S(1)}, u32[]{:S(2)}, u32[]{:S(2)}) collective-permute-start(f32[1,4096]{1,0:T(1,128)S(1)} %add.82.refs_0_), channel_id=1, source_target_pairs={{0,24},{4,28},{8,16},{12,20},{16,8},{20,12},{24,0},{28,4},{1,25},{... | collective-permute-start | bytes 49160 | tf_op jit(solution)/shard_map/ppermute | solution.py:35
  63.6 1.2 collective-permute-start.18
  64.8 3.5 %collective-permute-start.19 = (f32[1,128]{1,0:T(1,128)S(1)}, f32[1,128]{1,0:T(1,128)S(1)}, u32[]{:S(2)}, u32[]{:S(2)}) collective-permute-start(f32[1,128]{1,0:T(1,128)S(1)} %add.83.refs_0_), channel_id=1, source_target_pairs={{0,2},{1,3},{2,0},{3,1},{4,6},{5,7},{6,4},{7,5},{8,10},{9,11},{10,... | collective-permute-start | bytes 1544 | tf_op jit(solution)/shard_map/ppermute | solution.py:35
  68.7 3.8 %collective-permute-start.20 = (f32[1,4096]{1,0:T(1,128)S(1)}, f32[1,4096]{1,0:T(1,128)S(1)}, u32[]{:S(2)}, u32[]{:S(2)}) collective-permute-start(f32[1,4096]{1,0:T(1,128)S(1)} %col_pass.3), channel_id=1, source_target_pairs={{0,4},{4,0},{8,12},{12,8},{16,20},{20,16},{24,28},{28,24},{1,5},{5... | collective-permute-start | bytes 49160 | tf_op jit(solution)/shard_map/ppermute | solution.py:35
  72.5 7.8 %collective-permute-start.21 = (f32[1,4096]{1,0:T(1,128)S(1)}, f32[1,4096]{1,0:T(1,128)S(1)}, u32[]{:S(2)}, u32[]{:S(2)}) collective-permute-start(f32[1,4096]{1,0:T(1,128)S(1)} %add.84.refs_0_), channel_id=1, source_target_pairs={{0,8},{4,12},{8,0},{12,4},{16,24},{20,28},{24,16},{28,20},{1,9},{5... | collective-permute-start | bytes 49160 | tf_op jit(solution)/shard_map/ppermute | solution.py:35
  73.4 6.9 %collective-permute-start.22 = (f32[1,4096]{1,0:T(1,128)S(1)}, f32[1,4096]{1,0:T(1,128)S(1)}, u32[]{:S(2)}, u32[]{:S(2)}) collective-permute-start(f32[1,4096]{1,0:T(1,128)S(1)} %add.84.refs_0_), channel_id=1, source_target_pairs={{0,16},{4,20},{8,24},{12,28},{16,0},{20,4},{24,8},{28,12},{1,17},{... | collective-permute-start | bytes 49160 | tf_op jit(solution)/shard_map/ppermute | solution.py:35
  76.5 6.0 %collective-permute-start.23 = (f32[1,4096]{1,0:T(1,128)S(1)}, f32[1,4096]{1,0:T(1,128)S(1)}, u32[]{:S(2)}, u32[]{:S(2)}) collective-permute-start(f32[1,4096]{1,0:T(1,128)S(1)} %add.84.refs_0_), channel_id=1, source_target_pairs={{0,24},{4,28},{8,16},{12,20},{16,8},{20,12},{24,0},{28,4},{1,25},{... | collective-permute-start | bytes 49160 | tf_op jit(solution)/shard_map/ppermute | solution.py:35
  80.2 3.2 %collective-permute-start.6 = (f32[136,256]{1,0:T(8,128)S(1)}, f32[136,256]{1,0:T(8,128)S(1)}, u32[]{:S(2)}, u32[]{:S(2)}) collective-permute-start(f32[136,256]{1,0:T(8,128)S(1)} %logit_sum.1), channel_id=1, source_target_pairs={{0,1},{1,0},{2,3},{3,2},{4,5},{5,4},{6,7},{7,6},{8,9},{9,8},{10,11... | collective-permute-start | bytes 417800 | tf_op jit(solution)/shard_map/ppermute | solution.py:35
  83.3 1.7 %collective-permute-start.24 = (f32[136,256]{1,0:T(8,128)S(1)}, f32[136,256]{1,0:T(8,128)S(1)}, u32[]{:S(2)}, u32[]{:S(2)}) collective-permute-start(f32[136,256]{1,0:T(8,128)S(1)} %target_sum.1), channel_id=1, source_target_pairs={{0,1},{1,0},{2,3},{3,2},{4,5},{5,4},{6,7},{7,6},{8,9},{9,8},{10,11... | collective-permute-start | bytes 417800 | tf_op jit(solution)/shard_map/ppermute | solution.py:35
  83.5 6.5 %collective-permute-start.7 = (f32[136,256]{1,0:T(8,128)S(1)}, f32[136,256]{1,0:T(8,128)S(1)}, u32[]{:S(2)}, u32[]{:S(2)}) collective-permute-start(f32[136,256]{1,0:T(8,128)S(1)} %add.79.refs_2_), channel_id=1, source_target_pairs={{0,2},{1,3},{2,0},{3,1},{4,6},{5,7},{6,4},{7,5},{8,10},{9,11},{10,... | collective-permute-start | bytes 417800 | tf_op jit(solution)/shard_map/ppermute | solution.py:35
  85.0 7.8 %collective-permute-start.25 = (f32[136,256]{1,0:T(8,128)S(1)}, f32[136,256]{1,0:T(8,128)S(1)}, u32[]{:S(2)}, u32[]{:S(2)}) collective-permute-start(f32[136,256]{1,0:T(8,128)S(1)} %add.85.refs_4_), channel_id=1, source_target_pairs={{0,2},{1,3},{2,0},{3,1},{4,6},{5,7},{6,4},{7,5},{8,10},{9,11},{10,... | collective-permute-start | bytes 417800 | tf_op jit(solution)/shard_map/ppermute | solution.py:35
  86.4 8.1 %collective-permute-start.26 = (f32[128,192]{1,0:T(8,128)S(1)}, f32[128,192]{1,0:T(8,128)S(1)}, u32[]{:S(2)}, u32[]{:S(2)}) collective-permute-start(f32[128,192]{1,0:T(8,128)S(1)} %bitcast.29), channel_id=1, source_target_pairs={{0,4},{4,8},{8,12},{12,16},{16,20},{20,24},{24,28},{28,0},{1,5},{5... | collective-permute-start | bytes 294920 | tf_op jit(solution)/shard_map/ppermute | solution.py:414
  87.9 8.6 %collective-permute-start.27 = (f32[128,192]{1,0:T(8,128)S(1)}, f32[128,192]{1,0:T(8,128)S(1)}, u32[]{:S(2)}, u32[]{:S(2)}) collective-permute-start(f32[128,192]{1,0:T(8,128)S(1)} %bitcast.28), channel_id=1, source_target_pairs={{0,8},{4,12},{8,16},{12,20},{16,24},{20,28},{24,0},{28,4},{1,9},{5... | collective-permute-start | bytes 294920 | tf_op jit(solution)/shard_map/ppermute | solution.py:414
  88.2 9.2 %collective-permute-start.28 = (f32[128,192]{1,0:T(8,128)S(1)}, f32[128,192]{1,0:T(8,128)S(1)}, u32[]{:S(2)}, u32[]{:S(2)}) collective-permute-start(f32[128,192]{1,0:T(8,128)S(1)} %bitcast.27), channel_id=1, source_target_pairs={{0,12},{4,16},{8,20},{12,24},{16,28},{20,0},{24,4},{28,8},{1,13},{... | collective-permute-start | bytes 294920 | tf_op jit(solution)/shard_map/ppermute | solution.py:414
  90.0 19.2 %collective-permute-start.29 = (f32[128,192]{1,0:T(8,128)S(1)}, f32[128,192]{1,0:T(8,128)S(1)}, u32[]{:S(2)}, u32[]{:S(2)}) collective-permute-start(f32[128,192]{1,0:T(8,128)S(1)} %bitcast.26), channel_id=1, source_target_pairs={{0,16},{4,20},{8,24},{12,28},{16,0},{20,4},{24,8},{28,12},{1,17},{... | collective-permute-start | bytes 294920 | tf_op jit(solution)/shard_map/ppermute | solution.py:414
  93.5 26.9 %collective-permute-start.33 = (f32[128,256]{1,0:T(8,128)S(1)}, f32[128,256]{1,0:T(8,128)S(1)}, u32[]{:S(2)}, u32[]{:S(2)}) collective-permute-start(f32[128,256]{1,0:T(8,128)S(1)} %get-tuple-element.30.refs_15_), channel_id=1, source_target_pairs={{0,4},{4,8},{8,12},{12,16},{16,20},{20,24},{24,28},{28,0},{1,5},{5... | collective-permute-start | bytes 393224 | tf_op jit(solution)/shard_map/ppermute | solution.py:414
  94.5 28.1 %collective-permute-start.34 = (f32[128,256]{1,0:T(8,128)S(1)}, f32[128,256]{1,0:T(8,128)S(1)}, u32[]{:S(2)}, u32[]{:S(2)}) collective-permute-start(f32[128,256]{1,0:T(8,128)S(1)} %get-tuple-element.30.refs_15_), channel_id=1, source_target_pairs={{0,8},{4,12},{8,16},{12,20},{16,24},{20,28},{24,0},{28,4},{1,9},{5... | collective-permute-start | bytes 393224 | tf_op jit(solution)/shard_map/ppermute | solution.py:414
  96.5 12.9 %collective-permute-start.30 = (f32[128,192]{1,0:T(8,128)S(1)}, f32[128,192]{1,0:T(8,128)S(1)}, u32[]{:S(2)}, u32[]{:S(2)}) collective-permute-start(f32[128,192]{1,0:T(8,128)S(1)} %bitcast.32), channel_id=1, source_target_pairs={{0,20},{4,24},{8,28},{12,0},{16,4},{20,8},{24,12},{28,16},{1,21},{... | collective-permute-start | bytes 294920 | tf_op jit(solution)/shard_map/ppermute | solution.py:414
  97.4 20.3 %collective-permute-start.31 = (f32[128,192]{1,0:T(8,128)S(1)}, f32[128,192]{1,0:T(8,128)S(1)}, u32[]{:S(2)}, u32[]{:S(2)}) collective-permute-start(f32[128,192]{1,0:T(8,128)S(1)} %bitcast.31), channel_id=1, source_target_pairs={{0,24},{4,28},{8,0},{12,4},{16,8},{20,12},{24,16},{28,20},{1,25},{... | collective-permute-start | bytes 294920 | tf_op jit(solution)/shard_map/ppermute | solution.py:414
  109.3 10.9 %collective-permute-start.32 = (f32[128,192]{1,0:T(8,128)S(1)}, f32[128,192]{1,0:T(8,128)S(1)}, u32[]{:S(2)}, u32[]{:S(2)}) collective-permute-start(f32[128,192]{1,0:T(8,128)S(1)} %bitcast.30), channel_id=1, source_target_pairs={{0,28},{4,0},{8,4},{12,8},{16,12},{20,16},{24,20},{28,24},{1,29},{... | collective-permute-start | bytes 294920 | tf_op jit(solution)/shard_map/ppermute | solution.py:414
  109.5 16.8 %collective-permute-start.35 = (f32[128,256]{1,0:T(8,128)S(1)}, f32[128,256]{1,0:T(8,128)S(1)}, u32[]{:S(2)}, u32[]{:S(2)}) collective-permute-start(f32[128,256]{1,0:T(8,128)S(1)} %get-tuple-element.30.refs_15_), channel_id=1, source_target_pairs={{0,12},{4,16},{8,20},{12,24},{16,28},{20,0},{24,4},{28,8},{1,13},{... | collective-permute-start | bytes 393224 | tf_op jit(solution)/shard_map/ppermute | solution.py:414
  117.7 14.8 %collective-permute-start.36 = (f32[128,256]{1,0:T(8,128)S(1)}, f32[128,256]{1,0:T(8,128)S(1)}, u32[]{:S(2)}, u32[]{:S(2)}) collective-permute-start(f32[128,256]{1,0:T(8,128)S(1)} %get-tuple-element.30.refs_15_), channel_id=1, source_target_pairs={{0,16},{4,20},{8,24},{12,28},{16,0},{20,4},{24,8},{28,12},{1,17},{... | collective-permute-start | bytes 393224 | tf_op jit(solution)/shard_map/ppermute | solution.py:414
  120.2 18.9 %collective-permute-start.37 = (f32[128,256]{1,0:T(8,128)S(1)}, f32[128,256]{1,0:T(8,128)S(1)}, u32[]{:S(2)}, u32[]{:S(2)}) collective-permute-start(f32[128,256]{1,0:T(8,128)S(1)} %get-tuple-element.30.refs_15_), channel_id=1, source_target_pairs={{0,20},{4,24},{8,28},{12,0},{16,4},{20,8},{24,12},{28,16},{1,21},{... | collective-permute-start | bytes 393224 | tf_op jit(solution)/shard_map/ppermute | solution.py:414
  120.4 18.7 %collective-permute-start.38 = (f32[128,256]{1,0:T(8,128)S(1)}, f32[128,256]{1,0:T(8,128)S(1)}, u32[]{:S(2)}, u32[]{:S(2)}) collective-permute-start(f32[128,256]{1,0:T(8,128)S(1)} %get-tuple-element.30.refs_15_), channel_id=1, source_target_pairs={{0,24},{4,28},{8,0},{12,4},{16,8},{20,12},{24,16},{28,20},{1,25},{... | collective-permute-start | bytes 393224 | tf_op jit(solution)/shard_map/ppermute | solution.py:414
  122.6 16.5 %collective-permute-start.39 = (f32[128,256]{1,0:T(8,128)S(1)}, f32[128,256]{1,0:T(8,128)S(1)}, u32[]{:S(2)}, u32[]{:S(2)}) collective-permute-start(f32[128,256]{1,0:T(8,128)S(1)} %get-tuple-element.30.refs_15_), channel_id=1, source_target_pairs={{0,28},{4,0},{8,4},{12,8},{16,12},{20,16},{24,20},{28,24},{1,29},{... | collective-permute-start | bytes 393224 | tf_op jit(solution)/shard_map/ppermute | solution.py:414
  (6 other events, 21.4 us)
Sparse Core Ops, SparseCore 0:
  12.8 73.8 all-gather.1

commit v2 on v1

v2 whole, which is shorter than its diff:
```python
import functools

import jax
import jax.numpy as jnp
from jax import lax
from jax.experimental import pallas as pl
from jax.experimental.pallas import tpu as pltpu
from jax.sharding import PartitionSpec as P

ITERS = 3
F32 = jnp.float32
BF16 = jnp.bfloat16
HIGHEST = lax.Precision.HIGHEST

balancing_epsilon = 0.05
sharpness_divisor = 0.1
penalty_weighting = 64.0


def stages(n, first, stride=1):
    out, radix = [], first
    while stride < n:
        radix = min(radix, n // stride)
        out.append((stride, radix))
        stride *= radix
        radix = 4 if (n // stride) % 4 == 0 else 2
    return out


def swap(v, axis, mask):
    n = lax.axis_size(axis)
    return lax.ppermute(v, axis, [(i, i ^ mask) for i in range(n)])


def add_parts(parts):
    if len(parts) == 4:
        return (parts[0] + parts[1]) + (parts[2] + parts[3])
    return functools.reduce(lambda x, y: x + y, parts)


def exchange(v, axis, first, stride=1):
    n = lax.axis_size(axis)
    parts = [v]
    for step, radix in stages(n, first, stride):
        v = add_parts(parts)
        parts = [v] + [swap(v, axis, k * step) for k in range(1, radix)]
    return parts


def batch_parts(v, stride=1):
    steps = (lax.axis_size("batch") // stride).bit_length() - 1
    return exchange(v, "batch", 2 if steps % 2 else 4, stride)


def proto_parts(v, stride=1):
    return exchange(v, "proto", 2, stride)


def whole(shape):
    return pl.BlockSpec(shape, lambda *_: (0,) * len(shape))


def params(mib=24):
    return pltpu.CompilerParams(vmem_limit_bytes=mib * 1024 * 1024)


def cost(flops, nbytes, trans=0):
    return pl.CostEstimate(flops=int(flops), bytes_accessed=int(nbytes), transcendentals=int(trans))


def dot(a, b, dims, precision=None):
    return lax.dot_general(a, b, ((dims[0], dims[1]), ((), ())), precision=precision, preferred_element_type=F32)


def eye(n):
    return lax.broadcasted_iota(jnp.int32, (n, n), 0) == lax.broadcasted_iota(jnp.int32, (n, n), 1)


def to_lanes(col):
    n = col.shape[0]
    return jnp.sum(jnp.where(eye(n), col, 0.0), axis=0, keepdims=True)


def to_column(row):
    n = row.shape[1]
    return jnp.sum(jnp.where(eye(n), row, 0.0), axis=1, keepdims=True)


def first_kernel(f_hbm, w_hbm, pre_ref, again_ref, mom_ref, f_ref, w_ref, sems):
    depth, hidden = w_ref.shape
    n = sems.shape[0] - 1
    step = depth // n
    copies = [pltpu.make_async_copy(f_hbm, f_ref, sems.at[n])]
    for k in range(n):
        at = pl.ds(k * step, step)
        copies.append(pltpu.make_async_copy(w_hbm.at[at, :], w_ref.at[at, :], sems.at[k]))
    for copy in copies:
        copy.start()
    copies[0].wait()
    for k in range(n):
        copies[k + 1].wait()
        at = slice(k * step, (k + 1) * step)
        part = jnp.dot(f_ref[:, at], w_ref[at, :], preferred_element_type=F32)
        if k == 0:
            pre_ref[...] = part
        else:
            pre_ref[...] += part
    pre = pre_ref[...]
    again_ref[...] = pre
    mom_ref[:, 0:hidden] = jnp.sum(pre, axis=0, keepdims=True)
    mom_ref[:, hidden:] = jnp.sum(pre * pre, axis=0, keepdims=True)


def first_layer(features, w_first):
    rows, depth = features.shape
    hidden = w_first.shape[1]
    steps = 6 if depth % (6 * 128) == 0 else 1
    return pl.pallas_call(
        first_kernel,
        in_specs=[pl.BlockSpec(memory_space=pl.ANY)] * 2,
        out_shape=[jax.ShapeDtypeStruct((rows, hidden), F32)] * 2 + [jax.ShapeDtypeStruct((1, 2 * hidden), F32)],
        scratch_shapes=[
            pltpu.VMEM((rows, depth), BF16),
            pltpu.VMEM((depth, hidden), BF16),
            pltpu.SemaphoreType.DMA((steps + 1,)),
        ],
        compiler_params=params(60),
        cost_estimate=cost(2 * rows * depth * hidden, 2 * depth * hidden + 4 * rows * hidden),
        name="first_layer",
    )(features, w_first)


def batch_norm(pre, stats, gain, shift):
    normed = (pre - stats[0:1, :]) * stats[1:2, :]
    return normed, gain * normed + shift


def second_kernel(crops_all, n_parts, *refs):
    parts = refs[:n_parts]
    pre_ref, gain_ref, shift_ref, w_ref, emb_ref, stats_ref = refs[n_parts:]
    hidden = pre_ref.shape[1]
    moments = add_parts([p[...] for p in parts]) / crops_all
    mean = moments[:, 0:hidden]
    var = moments[:, hidden:] - mean * mean
    stats_ref[0:1, :] = mean
    stats_ref[1:2, :] = lax.rsqrt(var + 1e-05)
    _, shifted = batch_norm(pre_ref[...], stats_ref[...], gain_ref[...], shift_ref[...])
    low = jnp.maximum(shifted, 0.0).astype(BF16)
    emb_ref[...] = jnp.dot(low, w_ref[...], preferred_element_type=F32)


def second_layer(crops_all, parts, pre, gain, shift, w_second):
    rows, hidden = pre.shape
    width = w_second.shape[1]
    return pl.pallas_call(
        functools.partial(second_kernel, crops_all, len(parts)),
        out_shape=[jax.ShapeDtypeStruct((rows, width), F32), jax.ShapeDtypeStruct((2, hidden), F32)],
        compiler_params=params(),
        cost_estimate=cost(2 * rows * hidden * width, 4 * rows * hidden + 2 * hidden * width),
        name="second_layer",
    )(*parts, pre, gain, shift, w_second)


def unit_kernel(p_ref, u_ref):
    wide = p_ref[...].astype(F32)
    u_ref[...] = (wide * lax.rsqrt(jnp.sum(wide * wide, 1, keepdims=True) + 1e-06)).astype(BF16)


def unit_rows(prototypes):
    rows, width = prototypes.shape
    blk = min(1024, rows)
    return pl.pallas_call(
        unit_kernel,
        grid=(rows // blk,),
        in_specs=[pl.BlockSpec((blk, width), lambda j: (j, 0))],
        out_specs=pl.BlockSpec((blk, width), lambda j: (j, 0)),
        out_shape=jax.ShapeDtypeStruct((rows, width), BF16),
        compiler_params=params(),
        cost_estimate=cost(4 * rows * width, 4 * rows * width),
        name="unit_rows",
    )(prototypes)


def embed(raw):
    inv_norm = lax.rsqrt(jnp.sum(raw * raw, 1, keepdims=True) + 1e-06)
    return raw * inv_norm, inv_norm


def embed_kernel(*refs):
    refs[-1][...] = embed(add_parts([p[...] for p in refs[:-1]]))[0]


def embed_rows(parts):
    return pl.pallas_call(
        embed_kernel,
        out_shape=jax.ShapeDtypeStruct(parts[0].shape, F32),
        compiler_params=params(),
        cost_estimate=cost(8 * parts[0].size, 12 * parts[0].size),
        name="embed_rows",
    )(*parts)


def score_kernel(n, *refs):
    pieces, u_ref, codes, col_ref = refs[:n], refs[n], refs[n + 1 : 2 * n + 1], refs[2 * n + 1]
    units = u_ref[...]
    col = 0.0
    for piece, out in zip(pieces, codes):
        code = jnp.exp(dot(piece[...].astype(BF16), units, ((1,), (1,))) / balancing_epsilon)
        out[...] = code
        col = col + jnp.sum(code, axis=0, keepdims=True)
    col_ref[...] = col


def score(pieces, units):
    rows, width = pieces[0].shape
    protos, n = units.shape[0], len(pieces)
    blk = min(1024, protos)
    *codes, col = pl.pallas_call(
        functools.partial(score_kernel, n),
        grid=(protos // blk,),
        in_specs=[whole((rows, width))] * n + [pl.BlockSpec((blk, width), lambda j: (j, 0))],
        out_specs=[pl.BlockSpec((rows, blk), lambda j: (0, j))] * n + [pl.BlockSpec((1, blk), lambda j: (0, j))],
        out_shape=[jax.ShapeDtypeStruct((rows, protos), F32)] * n + [jax.ShapeDtypeStruct((1, protos), F32)],
        compiler_params=params(),
        cost_estimate=cost(2 * n * rows * protos * width, 4 * n * rows * protos, n * rows * protos),
        name="score",
    )(*pieces, units)
    return codes, col


def pack(table, lane_row, out_ref):
    rows, width = table.shape
    out_ref[0:rows, :] = table
    out_ref[rows:, :] = jnp.zeros((8, width), F32)
    out_ref[rows : rows + 1, 0:rows] = lane_row


def logit_kernel(emb_ref, u_ref, out_ref, total, mass):
    j = pl.program_id(0)

    @pl.when(j == 0)
    def _():
        total[...] = jnp.zeros_like(total)
        mass[...] = jnp.zeros_like(mass)

    units = u_ref[...]
    logits = jnp.exp(dot(emb_ref[...].astype(BF16), units, ((1,), (1,))) / sharpness_divisor)
    total[...] += jnp.dot(logits.astype(BF16), units, preferred_element_type=F32)
    mass[...] += jnp.sum(logits, axis=1, keepdims=True)

    @pl.when(j == pl.num_programs(0) - 1)
    def _():
        pack(total[...], to_lanes(mass[...]), out_ref)


def logit_sum(embedded, units):
    rows, width = embedded.shape
    protos = units.shape[0]
    blk = min(1024, protos)
    return pl.pallas_call(
        logit_kernel,
        grid=(protos // blk,),
        in_specs=[whole((rows, width)), pl.BlockSpec((blk, width), lambda j: (j, 0))],
        out_specs=whole((rows + 8, width)),
        out_shape=jax.ShapeDtypeStruct((rows + 8, width), F32),
        scratch_shapes=[pltpu.VMEM((rows, width), F32), pltpu.VMEM((rows, 1), F32)],
        compiler_params=params(),
        cost_estimate=cost(4 * rows * protos * width, 2 * protos * width, rows * protos),
        name="logit_sum",
    )(embedded, units)


def row_kernel(n_parts, *refs):
    parts, codes, out_ref = refs[:n_parts], refs[n_parts:-1], refs[-1]
    scale = 1.0 / add_parts([p[...] for p in parts])
    for k, code in enumerate(codes):
        out_ref[k : k + 1, :] = to_lanes(jnp.sum(code[...] * scale, axis=1, keepdims=True))


def row_pass(parts, codes):
    rows, protos = codes[0].shape
    n = len(codes)
    return pl.pallas_call(
        functools.partial(row_kernel, len(parts)),
        out_shape=jax.ShapeDtypeStruct((n, rows), F32),
        compiler_params=params(),
        cost_estimate=cost(2 * n * rows * protos, 4 * n * rows * protos),
        name="row_pass",
    )(*parts, *codes)


def col_kernel(n_parts, *refs):
    parts, codes, out_ref = refs[:n_parts], refs[n_parts:-1], refs[-1]
    scale = 1.0 / add_parts([p[...] for p in parts])
    total = 0.0
    for k, code in enumerate(codes):
        total = total + jnp.sum(code[...] * to_column(scale[k : k + 1, :]), axis=0, keepdims=True)
    out_ref[...] = total


def col_pass(parts, codes):
    rows, protos = codes[0].shape
    n = len(codes)
    return pl.pallas_call(
        functools.partial(col_kernel, len(parts)),
        out_shape=jax.ShapeDtypeStruct((1, protos), F32),
        compiler_params=params(),
        cost_estimate=cost(2 * n * rows * protos, 4 * n * rows * protos),
        name="col_pass",
    )(*parts, *codes)


def target_kernel(n_parts, halves, *refs):
    parts = refs[:n_parts]
    codes_ref, u_ref, partner_ref, core_ref = refs[n_parts : n_parts + 4]
    outs, table_all, mass_all = refs[n_parts + 4 : -2], refs[-2], refs[-1]
    rows = codes_ref.shape[0]
    scale = 1.0 / add_parts([p[...] for p in parts])
    weighted = codes_ref[...] * scale
    mass = jnp.sum(weighted, axis=1, keepdims=True)
    table = jnp.dot(weighted.astype(BF16), u_ref[...], preferred_element_type=F32)
    chosen = partner_ref[...] == lax.broadcasted_iota(jnp.int32, (rows, rows), 0)
    table_all[...] = dot(jnp.where(chosen, 1.0, 0.0).astype(F32), table, ((1,), (0,)), HIGHEST)
    mass_all[...] = jnp.sum(jnp.where(chosen, to_lanes(mass), 0.0), axis=1, keepdims=True)
    size = rows // halves
    for k in range(halves):
        at = pl.ds(pl.multiple_of((core_ref[2] ^ k) * size, size), size)
        pack(table_all[at, :], to_lanes(mass_all[at, :]), outs[k])


def target_sum(parts, codes, units, partner, core, halves):
    rows, protos = codes.shape
    width = units.shape[1]
    n_vmem = len(parts) + 3
    return pl.pallas_call(
        functools.partial(target_kernel, len(parts), halves),
        in_specs=[pl.BlockSpec(memory_space=pltpu.VMEM)] * n_vmem + [pl.BlockSpec(memory_space=pltpu.SMEM)],
        out_shape=[jax.ShapeDtypeStruct((rows // halves + 8, width), F32)] * halves,
        scratch_shapes=[pltpu.VMEM((rows, width), F32), pltpu.VMEM((rows, 1), F32)],
        compiler_params=params(),
        cost_estimate=cost(2 * rows * protos * width, 4 * rows * protos + 2 * protos * width),
        name="target_sum",
    )(*parts, codes, units, partner, core)


def loss_kernel(n_raw, n_logit, n_target, *refs):
    core_ref, refs = refs[0], refs[1:]
    raws, refs = refs[:n_raw], refs[n_raw:]
    logits, refs = refs[:n_logit], refs[n_logit:]
    target = add_parts([p[...] for p in refs[:n_target]])
    grad_ref, loss_ref = refs[n_target:]
    rows = raws[0].shape[0]
    size = grad_ref.shape[0]
    at = pl.ds(pl.multiple_of(core_ref[2] * size, size), size)
    raw = add_parts([p[at, :] for p in raws])
    logit = add_parts([p[at, :] for p in logits])
    denoms = to_column(add_parts([p[rows : rows + 1, 0:rows] for p in logits]))
    denom = jnp.where(core_ref[2] == 0, denoms[0:size], denoms[rows - size :])
    embedded, inv_norm = embed(raw)
    row_scale = to_column(1.0 / target[size : size + 1, 0:size])
    wanted = target[0:size, :] * row_scale
    emb_low = embedded.astype(BF16).astype(F32)
    cross = jnp.sum(wanted * emb_low, axis=1, keepdims=True)
    loss_ref[...] = to_lanes(jnp.log(denom) - cross / sharpness_divisor)
    emb_grad = penalty_weighting * (logit / denom - wanted) / sharpness_divisor
    inner = jnp.sum(embedded * emb_grad, 1, keepdims=True)
    grad_ref[...] = (emb_grad - embedded * inner) * inv_norm


def loss_grad(raw_parts, logit_parts, target_parts, core):
    width = raw_parts[0].shape[1]
    rows = target_parts[0].shape[0] - 8
    n_vmem = len(raw_parts) + len(logit_parts) + len(target_parts)
    return pl.pallas_call(
        functools.partial(loss_kernel, len(raw_parts), len(logit_parts), len(target_parts)),
        in_specs=[pl.BlockSpec(memory_space=pltpu.SMEM)] + [pl.BlockSpec(memory_space=pltpu.VMEM)] * n_vmem,
        out_shape=[jax.ShapeDtypeStruct((rows, width), F32), jax.ShapeDtypeStruct((1, rows), F32)],
        compiler_params=params(),
        cost_estimate=cost(20 * rows * width, 24 * rows * width),
        name="loss_grad",
    )(core, *raw_parts, *logit_parts, *target_parts)


def pick_kernel(f_ref, at_ref, keep_ref, send_ref):
    n_z, height, rows = keep_ref.shape
    depth = f_ref.shape[1]
    shape = (n_z * height, depth)
    row = lax.broadcasted_iota(jnp.int32, shape, 0)
    col = lax.broadcasted_iota(jnp.int32, shape, 1)
    d_cols = depth // (2 * n_z)
    me, share = at_ref[0], at_ref[1] * height
    for out, y in ((keep_ref, me & 1), (send_ref, (me & 1) ^ 1)):
        first = jnp.zeros(shape, jnp.int32)
        for k in range(n_z):
            owner = (((me >> 1) ^ k) << 1) + y
            first = jnp.where(row >= k * height, owner * d_cols + share - k * height, first)
        chosen = jnp.where(col == first + row, 1.0, 0.0).astype(BF16)
        out[...] = dot(chosen, f_ref[...], ((1,), (1,))).reshape(n_z, height, rows)


def columns_pick(features, at, n_batch, n_proto):
    rows, depth = features.shape
    shape = jax.ShapeDtypeStruct((n_batch // 2, depth // (n_batch * n_proto), rows), F32)
    return pl.pallas_call(
        pick_kernel,
        in_specs=[pl.BlockSpec(memory_space=pltpu.VMEM), pl.BlockSpec(memory_space=pltpu.SMEM)],
        out_shape=[shape, shape],
        compiler_params=params(),
        cost_estimate=cost(2 * depth * depth // n_proto * rows, 8 * rows * depth),
        name="columns_pick",
    )(features, at)


def columns_z(keep, got):
    both = [jnp.stack([keep[k], got[k]]) for k in range(keep.shape[0])]
    return [both[0]] + [swap(both[k], "batch", 2 * k) for k in range(1, len(both))]


def columns_kernel(masks, at_ref, *refs):
    out_ref = refs[-1]
    inner = len(masks) // (len(refs) - 1)
    for k, mask in enumerate(masks):
        _, n_batch, height, rows = refs[k // inner].shape
        row = pl.multiple_of((at_ref[1] ^ mask) * height, height)
        for i in range(n_batch):
            col = pl.multiple_of((at_ref[0] ^ i) * rows, rows)
            out_ref[pl.ds(row, height), pl.ds(col, rows)] = refs[k // inner][k % inner, i].astype(BF16)


def columns_all(own, other, at):
    n_proto = 2 * own.shape[0]
    _, n_batch, height, rows = own.shape
    smem = pl.BlockSpec(memory_space=pltpu.SMEM)
    vmem = pl.BlockSpec(memory_space=pltpu.VMEM)
    return pl.pallas_call(
        functools.partial(columns_kernel, (0, 2, 1, 3)),
        in_specs=[smem, vmem, vmem],
        out_shape=jax.ShapeDtypeStruct((n_proto * height, n_batch * rows), BF16),
        compiler_params=params(),
        cost_estimate=cost(0, 6 * n_proto * height * n_batch * rows),
        name="columns_all",
    )(at, own, other)


def cast_kernel(in_ref, out_ref):
    out_ref[...] = in_ref[...].T.astype(BF16)


def columns_cast(columns):
    return pl.pallas_call(
        cast_kernel,
        out_shape=jax.ShapeDtypeStruct(columns.shape[::-1], BF16),
        compiler_params=params(),
        name="columns_cast",
    )(columns)


def tail_kernel(crops_all, places, e_cols, *refs):
    n_grad = len(places)
    at_ref, pre_ref, cols_ref, stats_ref, gain_ref, shift_ref, w_ref = refs[:7]
    grads, refs = refs[7 : 7 + n_grad], refs[7 + n_grad :]
    w1_ref, w2_ref, gain_grad_ref, shift_grad_ref, grad_all, grad_cols = refs
    width = grad_all.shape[1]

    @pl.when(pl.program_id(0) == 0)
    def _():
        for piece, (masks, flip) in zip(grads, places):
            rows = piece.shape[1]
            for k, mask in enumerate(masks):
                place = 0 if mask is None else ((at_ref[0] ^ mask) << 1) + (at_ref[2] ^ flip)
                grad_all[pl.ds(pl.multiple_of(place * rows, rows), rows), :] = piece[k].astype(BF16)
        shape = (grad_cols.shape[0], width)
        mine = lax.broadcasted_iota(jnp.int32, shape, 0) + at_ref[0] * e_cols
        chosen = jnp.where(mine == lax.broadcasted_iota(jnp.int32, shape, 1), 1.0, 0.0).astype(BF16)
        grad_cols[...] = dot(chosen, grad_all[...], ((1,), (1,))).astype(BF16)

    stats, gain = stats_ref[...], gain_ref[...]
    normed, shifted = batch_norm(pre_ref[...], stats, gain, shift_ref[...])
    hidden = jnp.maximum(shifted, 0.0).astype(BF16)
    w2_ref[...] = jnp.dot(grad_cols[...], hidden, preferred_element_type=F32)[0:e_cols, :]
    hidden_grad = dot(grad_all[...], w_ref[...], ((1,), (1,)))
    bn_grad = jnp.where(shifted > 0, hidden_grad, 0.0)
    shift_grad = jnp.sum(bn_grad, axis=0, keepdims=True)
    gain_grad = jnp.sum(bn_grad * normed, axis=0, keepdims=True)
    shift_grad_ref[...] = shift_grad
    gain_grad_ref[...] = gain_grad
    scale = gain * stats[1:2, :]
    pre_grad = scale * (bn_grad - shift_grad / crops_all - normed * (gain_grad / crops_all))
    w1_ref[...] = jnp.dot(cols_ref[...], pre_grad.astype(BF16), preferred_element_type=F32)


def tail(pre_all, columns, stats, gain, shift, w_second, grads, places, at, e_cols):
    crops_all, hidden = pre_all.shape
    width, d_cols = w_second.shape[1], columns.shape[0]
    blk = min(hidden, max(128, 256 * 1024 // crops_all))
    smem = pl.BlockSpec(memory_space=pltpu.SMEM)
    vmem = pl.BlockSpec(memory_space=pltpu.VMEM)

    def cols(n):
        return pl.BlockSpec((n, blk), lambda j: (0, j))

    return pl.pallas_call(
        functools.partial(tail_kernel, crops_all, places, e_cols),
        grid=(hidden // blk,),
        in_specs=[smem, cols(crops_all), vmem, cols(2), cols(1), cols(1)]
        + [pl.BlockSpec((blk, width), lambda j: (j, 0))]
        + [vmem] * len(grads),
        out_specs=[cols(d_cols), cols(e_cols), cols(1), cols(1)],
        out_shape=[
            jax.ShapeDtypeStruct((d_cols, hidden), F32),
            jax.ShapeDtypeStruct((e_cols, hidden), F32),
            jax.ShapeDtypeStruct((1, hidden), F32),
            jax.ShapeDtypeStruct((1, hidden), F32),
        ],
        scratch_shapes=[
            pltpu.VMEM((crops_all, width), BF16),
            pltpu.VMEM((-(-e_cols // 16) * 16, crops_all), BF16),
        ],
        compiler_params=params(24 if crops_all <= 1024 else 56),
        cost_estimate=cost(2 * crops_all * hidden * (width + d_cols), 4 * crops_all * hidden),
        name="tail",
    )(at, pre_all, columns, stats, gain, shift, w_second, *grads)


def after(value, *others):
    return lax.optimization_barrier((value,) + others)[0]


def body(features, w_first, bn_gain, bn_shift, w_second, prototypes, partner):
    n_batch, n_proto = lax.axis_size("batch"), lax.axis_size("proto")
    me, proto_me = lax.axis_index("batch").astype(jnp.int32), lax.axis_index("proto").astype(jnp.int32)
    rows, depth = features.shape
    width = w_second.shape[1]
    crops_all = rows * n_batch
    d_cols, e_cols = depth // n_batch, width // n_batch
    gain, shift = bn_gain[None, :], bn_shift[None, :]
    short = n_batch == 8 and n_proto == 4 and depth % 512 == 0
    at = jnp.stack([me, proto_me, proto_me & 1 if short else proto_me * 0])

    pre, pre_again, moments = first_layer(features, w_first)
    pre_all = lax.all_gather(pre, "batch", tiled=True)
    moment_parts = batch_parts(moments)
    units = unit_rows(prototypes)
    if short:
        keep, send = columns_pick(after(features, moments), at, n_batch, n_proto)
        moment_parts[0], keep, send, units = lax.optimization_barrier((moment_parts[0], keep, send, units))
    emb_part, stats = second_layer(crops_all, moment_parts, pre_again, gain, shift, w_second)
    raw_parts = proto_parts(emb_part)
    embedded = embed_rows(raw_parts)

    if short:
        partner_emb = swap(embedded, "batch", 1)
        got = swap(after(send, embedded), "batch", 1)
        own_codes, own_col = score([embedded], units)
        partner_emb, own_col = lax.optimization_barrier((partner_emb, own_col))
        more_codes, more_col = score([partner_emb], units)
        codes, col_part = own_codes + more_codes, own_col + more_col
        got = after(got, col_part)
        z_stride = 2
    else:
        codes, col_part = score([embedded], units)
        z_stride = 1
    logit = logit_sum(after(embedded, col_part), units)
    col_parts = batch_parts(col_part, z_stride)
    if short:
        col_parts[0], got, logit = lax.optimization_barrier((col_parts[0], got, logit))
    for iteration in range(ITERS - 1):
        row_part = row_pass(col_parts, codes)
        row_parts = proto_parts(row_part)
        if short and iteration == 0:
            columns = columns_z(after(keep, row_parts[0]), after(got, row_parts[0]))
        col_part = col_pass(row_parts, codes)
        col_parts = batch_parts(col_part, z_stride)
        if iteration == 0:
            logit_parts = proto_parts(after(logit, col_part))
        if short and iteration == 0:
            col_parts[0], *rest = lax.optimization_barrier((col_parts[0], *columns, *logit_parts))
            columns, logit_parts = rest[: len(columns)], rest[len(columns) :]
    if short:
        keep, send = target_sum(col_parts, codes[0], units, partner[None, :], at, 2)
        target_parts = proto_parts(keep + swap(send, "proto", 1), 2)
    else:
        target_parts = proto_parts(target_sum(col_parts, codes[0], units, partner[None, :], at, 1)[0])
    raw_grad, penalty = loss_grad(raw_parts, logit_parts, target_parts, at)

    if short:
        pre_all, *columns = lax.optimization_barrier((pre_all, *columns, raw_grad))[:-1]
        near = jnp.stack([raw_grad] + [swap(raw_grad, "batch", k) for k in (2, 4, 6)])
        columns = jnp.concatenate(columns)[None]
        columns = jnp.concatenate([columns, swap(columns, "proto", 2)])
        columns = columns_all(columns, swap(columns, "proto", 1), at)
        far = swap(near, "batch", 1)
        grads = [near, far, swap(near, "proto", 1), swap(far, "proto", 1)]
        places = [((0, 2, 4, 6), 0), ((1, 3, 5, 7), 0), ((0, 2, 4, 6), 1), ((1, 3, 5, 7), 1)]
        other_penalty = swap(penalty, "proto", 1)
        first = at[2] == 0
        penalty = jnp.concatenate(
            [jnp.where(first, penalty, other_penalty), jnp.where(first, other_penalty, penalty)], axis=1
        )
    else:
        by_owner = jnp.swapaxes(features.astype(F32).reshape(rows, n_batch, d_cols), 0, 1)
        columns = columns_cast(lax.all_to_all(by_owner, "batch", 0, 0).reshape(crops_all, d_cols))
        grads = [lax.all_gather(raw_grad, "batch", tiled=True)[None]]
        places = [((None,), 0)]
    grad_w1, grad_w2, grad_gain, grad_shift = tail(
        pre_all, columns, stats, gain, shift, w_second, grads, places, at, e_cols
    )
    return (penalty[0], grad_w1, grad_gain[0], grad_shift[0], grad_w2.T)


def solution(mesh):
    return jax.shard_map(
        body,
        mesh=mesh,
        in_specs=(
            P("batch", None),
            P(None, "proto"),
            P("proto"),
            P("proto"),
            P("proto", None),
            P("proto", None),
            P("batch"),
        ),
        out_specs=(P("batch"), P("batch", "proto"), P("proto"), P("proto"), P("proto", "batch")),
        check_vma=False,
    )
```

time: 153 us -> 127 us (0.83)
  the two profiles are of different devices: /device:TPU:28 before, /device:TPU:0 now
where the time goes in v2:
time: 127 us
  starting transfers between devices  45.1 us (36%)
  waiting for transfers between devices  42.7 us (34%)
  Pallas kernels  21.7 us (17%)
  between operations  14.4 us (11%)
  local copies, waits for them, and re-layouts  2.24 us (2%)
    ppermute x37, starting transfers between devices, swap(): return lax.ppermute(v, axis, [(i, i ^ mask) for i in range(n)])  45 us
    ppermute x37, waiting for transfers between devices, swap(): return lax.ppermute(v, axis, [(i, i ^ mask) for i in range(n)])  42.6 us
    pallas_call x1, Pallas kernels, tail(): pl.pallas_call(functools.partial(tail_kernel, crops_all, places, e_cols),...  6.37 us
    pallas_call x1, Pallas kernels, first_layer(): pl.pallas_call(first_kernel, in_specs=[pl.BlockSpec(memory_space=pl.ANY)]...  3.37 us
    pallas_call x2, Pallas kernels, score(): pl.pallas_call(functools.partial(score_kernel, n), grid=(protos // blk,),...  2.85 us
  transfers between devices with their start and end apart: 38, of which 23 were waited for; matrix products, arithmetic and copies ran while one was open for 1% of the time, Pallas kernels for 9%

profile of v2, /device:TPU:0, one launch (start us, length us, event | category | flops | bytes accessed | tf_op | source)
XLA Modules:
  0.0 126.9 jit_solution(2677338379693039075)
XLA Ops:
  7.2 3.4 %first_layer.1 = (f32[128,1024]{1,0:T(8,128)}, f32[128,1024]{1,0:T(8,128)}, f32[1,2048]{1,0:T(1,128)}) custom-call(bf16[128,1536]{1,0:T(8,128)(2,1)} %f_ref, bf16[1536,1024]{1,0:T(8,128)(2,1)} %w_hbm.1), custom_call_target="tpu_custom_call" | custom-call | flops 402653184 | bytes 3670016 | tf_op jit(solution)/shard_map/first_layer/pallas_call | solution.py:118
  10.6 3.0 %collective-permute-start = (f32[1,2048]{1,0:T(1,128)}, f32[1,2048]{1,0:T(1,128)S(1)}, u32[]{:S(2)}, u32[]{:S(2)}) collective-permute-start(f32[1,2048]{1,0:T(1,128)} %get-tuple-element.52), channel_id=1, source_target_pairs={{0,4},{4,0},{8,12},{12,8},{16,20},{20,16},{24,28},{28,24},{1,5},{5... | collective-permute-start | bytes 24584 | tf_op jit(solution)/shard_map/ppermute | solution.py:32
  13.8 1.0 unit_rows.1.refs_1_.u_ref.refs_5_
  15.5 2.1 %collective-permute-start.1 = (f32[1,2048]{1,0:T(1,128)S(1)}, f32[1,2048]{1,0:T(1,128)S(1)}, u32[]{:S(2)}, u32[]{:S(2)}) collective-permute-start(f32[1,2048]{1,0:T(1,128)S(1)} %add.21.refs_0_), channel_id=1, source_target_pairs={{0,8},{4,12},{8,0},{12,4},{16,24},{20,28},{24,16},{28,20},{1,9},{5... | collective-permute-start | bytes 24584 | tf_op jit(solution)/shard_map/ppermute | solution.py:32
  17.7 2.6 %collective-permute-start.2 = (f32[1,2048]{1,0:T(1,128)S(1)}, f32[1,2048]{1,0:T(1,128)S(1)}, u32[]{:S(2)}, u32[]{:S(2)}) collective-permute-start(f32[1,2048]{1,0:T(1,128)S(1)} %add.21.refs_0_), channel_id=1, source_target_pairs={{0,16},{4,20},{8,24},{12,28},{16,0},{20,4},{24,8},{28,12},{1,17},{... | collective-permute-start | bytes 24584 | tf_op jit(solution)/shard_map/ppermute | solution.py:32
  20.2 1.0 columns_pick.1
  21.3 0.9 collective-permute-done.2.refs_2_
  22.2 3.7 %collective-permute-done.3.refs_3_ = f32[1,2048]{1,0:T(1,128)S(1)} collective-permute-done((f32[1,2048]{1,0:T(1,128)S(1)}, f32[1,2048]{1,0:T(1,128)S(1)}, u32[]{:S(2)}, u32[]{:S(2)}) %collective-permute-start.3) | collective-permute-done | bytes 8224 | tf_op jit(solution)/shard_map/ppermute | solution.py:32
  26.3 1.3 %collective-permute-done.4 = f32[128,256]{1,0:T(8,128)S(1)} collective-permute-done((f32[128,256]{1,0:T(8,128)S(1)}, f32[128,256]{1,0:T(8,128)S(1)}, u32[]{:S(2)}, u32[]{:S(2)}) %collective-permute-start.4) | collective-permute-done | bytes 131104 | tf_op jit(solution)/shard_map/ppermute | solution.py:32
  27.6 1.6 %collective-permute-start.5 = (f32[128,256]{1,0:T(8,128)S(1)}, f32[128,256]{1,0:T(8,128)S(1)}, u32[]{:S(2)}, u32[]{:S(2)}) collective-permute-start(f32[128,256]{1,0:T(8,128)S(1)} %add.22.refs_0_.refs_1_), channel_id=1, source_target_pairs={{0,2},{1,3},{2,0},{3,1},{4,6},{5,7},{6,4},{7,5},{8,10},{9,11},{10,... | collective-permute-start | bytes 393224 | tf_op jit(solution)/shard_map/ppermute | solution.py:32
  29.2 4.1 %collective-permute-done.5.refs_1_.refs_2_ = f32[128,256]{1,0:T(8,128)S(1)} collective-permute-done((f32[128,256]{1,0:T(8,128)S(1)}, f32[128,256]{1,0:T(8,128)S(1)}, u32[]{:S(2)}, u32[]{:S(2)}) %collective-permute-start.5) | collective-permute-done | bytes 131104 | tf_op jit(solution)/shard_map/ppermute | solution.py:32
  33.4 1.6 %collective-permute-start.6 = (f32[128,256]{1,0:T(8,128)S(1)}, f32[128,256]{1,0:T(8,128)S(1)}, u32[]{:S(2)}, u32[]{:S(2)}) collective-permute-start(f32[128,256]{1,0:T(8,128)S(1)} %embed_rows.1.refs_0_.emb_ref), channel_id=1, source_target_pairs={{0,4},{4,0},{8,12},{12,8},{16,20},{20,16},{24,28},{28,24},{1,5},{5... | collective-permute-start | bytes 393224 | tf_op jit(solution)/shard_map/ppermute | solution.py:32
  35.4 1.4 %score.2 = (f32[128,4096]{1,0:T(8,128)S(1)}, f32[1,4096]{1,0:T(1,128)S(1)}) custom-call(f32[128,256]{1,0:T(8,128)S(1)} %embed_rows.1.refs_0_.emb_ref, bf16[4096,256]{1,0:T(8,128)(2,1)S(1)} %unit_rows.1.refs_1_.u_ref.refs_5_), custom_call_target="tpu_custom_call" | custom-call | flops 268435456 | bytes 2097152 | tf_op jit(solution)/shard_map/score/pallas_call | solution.py:218
  36.9 2.4 %collective-permute-done.6.refs_0_ = f32[128,256]{1,0:T(8,128)S(1)} collective-permute-done((f32[128,256]{1,0:T(8,128)S(1)}, f32[128,256]{1,0:T(8,128)S(1)}, u32[]{:S(2)}, u32[]{:S(2)}) %collective-permute-start.6) | collective-permute-done | bytes 131104 | tf_op jit(solution)/shard_map/ppermute | solution.py:32
  39.3 1.4 %score.3 = (f32[128,4096]{1,0:T(8,128)S(1)}, f32[1,4096]{1,0:T(1,128)S(1)}) custom-call(f32[128,256]{1,0:T(8,128)S(1)} %collective-permute-done.6.refs_0_, bf16[4096,256]{1,0:T(8,128)(2,1)S(1)} %unit_rows.1.refs_1_.u_ref.refs_5_), custom_call_target="tpu_custom_call" | custom-call | flops 268435456 | bytes 2097152 | tf_op jit(solution)/shard_map/score/pallas_call | solution.py:218
  41.3 3.9 %collective-permute-start.10 = (f32[1,4096]{1,0:T(1,128)S(1)}, f32[1,4096]{1,0:T(1,128)S(1)}, u32[]{:S(2)}, u32[]{:S(2)}) collective-permute-start(f32[1,4096]{1,0:T(1,128)S(1)} %add.23.refs_0_), channel_id=1, source_target_pairs={{0,24},{4,28},{8,16},{12,20},{16,8},{20,12},{24,0},{28,4},{1,25},{... | collective-permute-start | bytes 49160 | tf_op jit(solution)/shard_map/ppermute | solution.py:32
  45.2 2.1 %logit_sum.1 = f32[136,256]{1,0:T(8,128)S(1)} custom-call(f32[128,256]{1,0:T(8,128)S(1)} %embed_rows.1.refs_0_.emb_ref, bf16[4096,256]{1,0:T(8,128)(2,1)S(1)} %unit_rows.1.refs_1_.u_ref.refs_5_), custom_call_target="tpu_custom_call" | custom-call | flops 536870912 | bytes 2097152 | tf_op jit(solution)/shard_map/logit_sum/pallas_call | solution.py:260
  47.8 1.1 collective-permute-done.11
  49.0 1.5 %collective-permute-start.12 = (f32[2,128]{1,0:T(2,128)S(1)}, f32[2,128]{1,0:T(2,128)S(1)}, u32[]{:S(2)}, u32[]{:S(2)}) collective-permute-start(f32[2,128]{1,0:T(2,128)S(1)} %add.24.refs_0_), channel_id=1, source_target_pairs={{0,2},{1,3},{2,0},{3,1},{4,6},{5,7},{6,4},{7,5},{8,10},{9,11},{10,... | collective-permute-start | bytes 3080 | tf_op jit(solution)/shard_map/ppermute | solution.py:32
  50.5 2.1 %collective-permute-done.12.refs_1_ = f32[2,128]{1,0:T(2,128)S(1)} collective-permute-done((f32[2,128]{1,0:T(2,128)S(1)}, f32[2,128]{1,0:T(2,128)S(1)}, u32[]{:S(2)}, u32[]{:S(2)}) %collective-permute-start.12) | collective-permute-done | bytes 1056 | tf_op jit(solution)/shard_map/ppermute | solution.py:32
  53.4 3.8 %collective-permute-start.14 = (f32[2,48,128]{2,1,0:T(8,128)S(1)}, f32[2,48,128]{2,1,0:T(8,128)S(1)}, u32[]{:S(2)}, u32[]{:S(2)}) collective-permute-start(f32[2,48,128]{2,1,0:T(8,128)S(1)} %pad_maximum_fusion.4), channel_id=1, source_target_pairs={{0,16},{4,20},{8,24},{12,28},{16,0},{20,4},{24,8},{28,12},{1,17},{... | collective-permute-start | bytes 147464 | tf_op jit(solution)/shard_map/ppermute | solution.py:32
  57.2 1.6 %collective-permute-start.17 = (f32[136,256]{1,0:T(8,128)S(1)}, f32[136,256]{1,0:T(8,128)S(1)}, u32[]{:S(2)}, u32[]{:S(2)}) collective-permute-start(f32[136,256]{1,0:T(8,128)S(1)} %add.25.refs_3_), channel_id=1, source_target_pairs={{0,2},{1,3},{2,0},{3,1},{4,6},{5,7},{6,4},{7,5},{8,10},{9,11},{10,... | collective-permute-start | bytes 417800 | tf_op jit(solution)/shard_map/ppermute | solution.py:32
  59.5 2.1 %collective-permute-done.13 = f32[2,48,128]{2,1,0:T(8,128)S(1)} collective-permute-done((f32[2,48,128]{2,1,0:T(8,128)S(1)}, f32[2,48,128]{2,1,0:T(8,128)S(1)}, u32[]{:S(2)}, u32[]{:S(2)}) %collective-permute-start.13) | collective-permute-done | bytes 49184 | tf_op jit(solution)/shard_map/ppermute | solution.py:32
  61.6 1.6 %collective-permute-start.19 = (f32[1,4096]{1,0:T(1,128)S(1)}, f32[1,4096]{1,0:T(1,128)S(1)}, u32[]{:S(2)}, u32[]{:S(2)}) collective-permute-start(f32[1,4096]{1,0:T(1,128)S(1)} %col_pass.2.refs_0_), channel_id=1, source_target_pairs={{0,16},{4,20},{8,24},{12,28},{16,0},{20,4},{24,8},{28,12},{1,17},{... | collective-permute-start | bytes 49160 | tf_op jit(solution)/shard_map/ppermute | solution.py:32
  63.2 5.1 %collective-permute-start.20 = (f32[1,4096]{1,0:T(1,128)S(1)}, f32[1,4096]{1,0:T(1,128)S(1)}, u32[]{:S(2)}, u32[]{:S(2)}) collective-permute-start(f32[1,4096]{1,0:T(1,128)S(1)} %col_pass.2.refs_0_), channel_id=1, source_target_pairs={{0,24},{4,28},{8,16},{12,20},{16,8},{20,12},{24,0},{28,4},{1,25},{... | collective-permute-start | bytes 49160 | tf_op jit(solution)/shard_map/ppermute | solution.py:32
  68.3 1.1 collective-permute-done.19.refs_2_
  69.4 0.9 collective-permute-done.20.refs_3_
  70.8 1.1 collective-permute-done.21
  72.7 2.9 %collective-permute-done.22.refs_1_ = f32[2,128]{1,0:T(2,128)S(1)} collective-permute-done((f32[2,128]{1,0:T(2,128)S(1)}, f32[2,128]{1,0:T(2,128)S(1)}, u32[]{:S(2)}, u32[]{:S(2)}) %collective-permute-start.22) | collective-permute-done | bytes 1056 | tf_op jit(solution)/shard_map/ppermute | solution.py:32
  76.1 1.9 %collective-permute-start.23 = (f32[1,4096]{1,0:T(1,128)S(1)}, f32[1,4096]{1,0:T(1,128)S(1)}, u32[]{:S(2)}, u32[]{:S(2)}) collective-permute-start(f32[1,4096]{1,0:T(1,128)S(1)} %col_pass.3.refs_0_), channel_id=1, source_target_pairs={{0,8},{4,12},{8,0},{12,4},{16,24},{20,28},{24,16},{28,20},{1,9},{5... | collective-permute-start | bytes 49160 | tf_op jit(solution)/shard_map/ppermute | solution.py:32
  78.0 2.6 %collective-permute-start.24 = (f32[1,4096]{1,0:T(1,128)S(1)}, f32[1,4096]{1,0:T(1,128)S(1)}, u32[]{:S(2)}, u32[]{:S(2)}) collective-permute-start(f32[1,4096]{1,0:T(1,128)S(1)} %col_pass.3.refs_0_), channel_id=1, source_target_pairs={{0,16},{4,20},{8,24},{12,28},{16,0},{20,4},{24,8},{28,12},{1,17},{... | collective-permute-start | bytes 49160 | tf_op jit(solution)/shard_map/ppermute | solution.py:32
  80.6 0.8 collective-permute-start.25
  81.6 2.1 %collective-permute-done.24.refs_2_ = f32[1,4096]{1,0:T(1,128)S(1)} collective-permute-done((f32[1,4096]{1,0:T(1,128)S(1)}, f32[1,4096]{1,0:T(1,128)S(1)}, u32[]{:S(2)}, u32[]{:S(2)}) %collective-permute-start.24) | collective-permute-done | bytes 16416 | tf_op jit(solution)/shard_map/ppermute | solution.py:32
  83.7 2.7 %collective-permute-done.25.refs_3_ = f32[1,4096]{1,0:T(1,128)S(1)} collective-permute-done((f32[1,4096]{1,0:T(1,128)S(1)}, f32[1,4096]{1,0:T(1,128)S(1)}, u32[]{:S(2)}, u32[]{:S(2)}) %collective-permute-start.25) | collective-permute-done | bytes 16416 | tf_op jit(solution)/shard_map/ppermute | solution.py:32
  86.5 1.4 %target_sum.1 = (f32[72,256]{1,0:T(8,128)S(1)}, f32[72,256]{1,0:T(8,128)S(1)}) custom-call(f32[1,4096]{1,0:T(1,128)S(1)} %col_pass.3.refs_0_, f32[1,4096]{1,0:T(1,128)S(1)} %collective-permute-done.23.refs_1_, f32[1,4096]{1,0:T(1,128)S(1)} %collective-permute-done.24.refs_2_, f32[1,4096]{1,0:T(1,128)S(1)} %collective-permute-done.25.refs_3_, ...), custom_call_target="tpu_custom_call" | custom-call | flops 268435456 | bytes 4194304 | tf_op jit(solution)/shard_map/target_sum/pallas_call | solution.py:335
  88.0 1.3 collective-permute-done.26
  89.3 1.0 collective-permute-start.27
  90.3 3.4 %collective-permute-done.27.refs_6_ = f32[72,256]{1,0:T(8,128)S(1)} collective-permute-done((f32[72,256]{1,0:T(8,128)S(1)}, f32[72,256]{1,0:T(8,128)S(1)}, u32[]{:S(2)}, u32[]{:S(2)}) %collective-permute-start.27) | collective-permute-done | bytes 73760 | tf_op jit(solution)/shard_map/ppermute | solution.py:32
  94.5 1.1 collective-permute-start.33
  95.6 1.4 %collective-permute-start.32 = (f32[64,256]{1,0:T(8,128)S(1)}, f32[64,256]{1,0:T(8,128)S(1)}, u32[]{:S(2)}, u32[]{:S(2)}) collective-permute-start(f32[64,256]{1,0:T(8,128)S(1)} %get-tuple-element.88), channel_id=1, source_target_pairs={{0,16},{4,20},{8,24},{12,28},{16,0},{20,4},{24,8},{28,12},{1,17},{... | collective-permute-start | bytes 196616 | tf_op jit(solution)/shard_map/ppermute | solution.py:32
  97.0 2.0 %collective-permute-start.31 = (f32[64,256]{1,0:T(8,128)S(1)}, f32[64,256]{1,0:T(8,128)S(1)}, u32[]{:S(2)}, u32[]{:S(2)}) collective-permute-start(f32[64,256]{1,0:T(8,128)S(1)} %get-tuple-element.88), channel_id=1, source_target_pairs={{0,8},{4,12},{8,0},{12,4},{16,24},{20,28},{24,16},{28,20},{1,9},{5... | collective-permute-start | bytes 196616 | tf_op jit(solution)/shard_map/ppermute | solution.py:32
  98.9 1.0 collective-permute-start.29
  100.0 0.9 collective-permute-done.33
  100.9 1.8 %collective-permute-done.32 = f32[64,256]{1,0:T(8,128)S(1)} collective-permute-done((f32[64,256]{1,0:T(8,128)S(1)}, f32[64,256]{1,0:T(8,128)S(1)}, u32[]{:S(2)}, u32[]{:S(2)}) %collective-permute-start.32) | collective-permute-done | bytes 65568 | tf_op jit(solution)/shard_map/ppermute | solution.py:32
  102.8 1.2 collective-permute-start.34
  105.3 4.6 %collective-permute-done.34.refs_8_ = f32[4,64,256]{2,1,0:T(8,128)S(1)} collective-permute-done((f32[4,64,256]{2,1,0:T(8,128)S(1)}, f32[4,64,256]{2,1,0:T(8,128)S(1)}, u32[]{:S(2)}, u32[]{:S(2)}) %collective-permute-start.34) | collective-permute-done | bytes 262176 | tf_op jit(solution)/shard_map/ppermute | solution.py:32
  111.5 2.2 %copy-done = f32[1024,1024]{1,0:T(8,128)S(1)} copy-done((f32[1024,1024]{1,0:T(8,128)S(1)}, f32[1024,1024]{1,0:T(8,128)}, u32[]{:S(2)}) %copy-start) | copy-done | bytes 4194328
  113.7 6.4 %tail.1 = (f32[192,1024]{1,0:T(8,128)}, f32[32,1024]{1,0:T(8,128)}, f32[1,1024]{1,0:T(1,128)}, f32[1,1024]{1,0:T(1,128)}) custom-call(s32[3]{0:T(128)S(1)} %pad_add_fusion.at_ref.refs_7_.refs_0_, f32[1024,1024]{1,0:T(8,128)S(1)} %copy-done, bf16[192,1024]{1,0:T(8,128)(2,1)S(1)} %columns_all.1.refs_2_, f32[2,1024]{1,0:T(2,128)S(1)} %get-tuple-element.94.refs_3_, ...), custom_call_target="tpu_custom_call" | custom-call | flops 939524096 | bytes 4194304 | tf_op jit(solution)/shard_map/tail/pallas_call | solution.py:502
  (81 shorter events, 10.3 us)
Async XLA Ops:
  7.2 6.6 %copy-start.2 = (bf16[4096,256]{1,0:T(8,128)(2,1)S(1)}, bf16[4096,256]{1,0:T(8,128)(2,1)}, u32[]{:S(2)}) copy-start(bf16[4096,256]{1,0:T(8,128)(2,1)} %p_ref.1) | copy-start | bytes 6291460
  7.2 91.7 %all-gather.2.cloned.1.call-start = ((), (), s32[]{:S(2)}) async-start(), calls=%async_computation | async-start | bytes 4718592 | tf_op jit(solution)/shard_map/all_gather | solution.py:541
  10.6 4.9 %collective-permute-start = (f32[1,2048]{1,0:T(1,128)}, f32[1,2048]{1,0:T(1,128)S(1)}, u32[]{:S(2)}, u32[]{:S(2)}) collective-permute-start(f32[1,2048]{1,0:T(1,128)} %get-tuple-element.52), channel_id=1, source_target_pairs={{0,4},{4,0},{8,12},{12,8},{16,20},{20,16},{24,28},{28,24},{1,5},{5... | collective-permute-start | bytes 24584 | tf_op jit(solution)/shard_map/ppermute | solution.py:32
  13.7 1.8 %copy-start.8 = (f32[1,2048]{1,0:T(1,128)S(1)}, f32[1,2048]{1,0:T(1,128)}, u32[]{:S(2)}) copy-start(f32[1,2048]{1,0:T(1,128)} %get-tuple-element.52) | copy-start | bytes 24580
  13.7 6.5 %copy-start.4 = (bf16[128,1536]{1,0:T(8,128)(2,1)S(1)}, bf16[128,1536]{1,0:T(8,128)(2,1)}, u32[]{:S(2)}) copy-start(bf16[128,1536]{1,0:T(8,128)(2,1)} %f_ref) | copy-start | bytes 1179652
  13.7 12.2 %copy-start.1 = (bf16[1024,256]{1,0:T(8,128)(2,1)S(1)}, bf16[1024,256]{1,0:T(8,128)(2,1)}, u32[]{:S(2)}) copy-start(bf16[1024,256]{1,0:T(8,128)(2,1)} %refs_6_.1) | copy-start | bytes 1572868
  13.7 12.2 %copy-start.3 = (f32[128,1024]{1,0:T(8,128)S(1)}, f32[128,1024]{1,0:T(8,128)}, u32[]{:S(2)}) copy-start(f32[128,1024]{1,0:T(8,128)} %get-tuple-element.57.refs_4_) | copy-start | bytes 1572868
  13.8 12.2 %copy-start.5 = (f32[1024]{0:T(1024)S(1)}, f32[1024]{0:T(1024)}, u32[]{:S(2)}) copy-start(f32[1024]{0:T(1024)} %param.9) | copy-start | bytes 12292
  13.8 12.1 %copy-start.6 = (f32[1024]{0:T(1024)S(1)}, f32[1024]{0:T(1024)}, u32[]{:S(2)}) copy-start(f32[1024]{0:T(1024)} %param.10) | copy-start | bytes 12292
  15.5 5.7 %collective-permute-start.1 = (f32[1,2048]{1,0:T(1,128)S(1)}, f32[1,2048]{1,0:T(1,128)S(1)}, u32[]{:S(2)}, u32[]{:S(2)}) collective-permute-start(f32[1,2048]{1,0:T(1,128)S(1)} %add.21.refs_0_), channel_id=1, source_target_pairs={{0,8},{4,12},{8,0},{12,4},{16,24},{20,28},{24,16},{28,20},{1,9},{5... | collective-permute-start | bytes 24584 | tf_op jit(solution)/shard_map/ppermute | solution.py:32
  17.7 4.5 %collective-permute-start.2 = (f32[1,2048]{1,0:T(1,128)S(1)}, f32[1,2048]{1,0:T(1,128)S(1)}, u32[]{:S(2)}, u32[]{:S(2)}) collective-permute-start(f32[1,2048]{1,0:T(1,128)S(1)} %add.21.refs_0_), channel_id=1, source_target_pairs={{0,16},{4,20},{8,24},{12,28},{16,0},{20,4},{24,8},{28,12},{1,17},{... | collective-permute-start | bytes 24584 | tf_op jit(solution)/shard_map/ppermute | solution.py:32
  20.2 5.7 %collective-permute-start.3 = (f32[1,2048]{1,0:T(1,128)S(1)}, f32[1,2048]{1,0:T(1,128)S(1)}, u32[]{:S(2)}, u32[]{:S(2)}) collective-permute-start(f32[1,2048]{1,0:T(1,128)S(1)} %add.21.refs_0_), channel_id=1, source_target_pairs={{0,24},{4,28},{8,16},{12,20},{16,8},{20,12},{24,0},{28,4},{1,25},{... | collective-permute-start | bytes 24584 | tf_op jit(solution)/shard_map/ppermute | solution.py:32
  26.2 1.4 %collective-permute-start.4 = (f32[128,256]{1,0:T(8,128)S(1)}, f32[128,256]{1,0:T(8,128)S(1)}, u32[]{:S(2)}, u32[]{:S(2)}) collective-permute-start(f32[128,256]{1,0:T(8,128)S(1)} %get-tuple-element.58), channel_id=1, source_target_pairs={{0,1},{1,0},{2,3},{3,2},{4,5},{5,4},{6,7},{7,6},{8,9},{9,8},{10,11... | collective-permute-start | bytes 393224 | tf_op jit(solution)/shard_map/ppermute | solution.py:32
  27.6 5.6 %collective-permute-start.5 = (f32[128,256]{1,0:T(8,128)S(1)}, f32[128,256]{1,0:T(8,128)S(1)}, u32[]{:S(2)}, u32[]{:S(2)}) collective-permute-start(f32[128,256]{1,0:T(8,128)S(1)} %add.22.refs_0_.refs_1_), channel_id=1, source_target_pairs={{0,2},{1,3},{2,0},{3,1},{4,6},{5,7},{6,4},{7,5},{8,10},{9,11},{10,... | collective-permute-start | bytes 393224 | tf_op jit(solution)/shard_map/ppermute | solution.py:32
  33.4 5.9 %collective-permute-start.6 = (f32[128,256]{1,0:T(8,128)S(1)}, f32[128,256]{1,0:T(8,128)S(1)}, u32[]{:S(2)}, u32[]{:S(2)}) collective-permute-start(f32[128,256]{1,0:T(8,128)S(1)} %embed_rows.1.refs_0_.emb_ref), channel_id=1, source_target_pairs={{0,4},{4,0},{8,12},{12,8},{16,20},{20,16},{24,28},{28,24},{1,5},{5... | collective-permute-start | bytes 393224 | tf_op jit(solution)/shard_map/ppermute | solution.py:32
  34.9 12.4 %collective-permute-start.7 = (f32[4,48,128]{2,1,0:T(8,128)S(1)}, f32[4,48,128]{2,1,0:T(8,128)S(1)}, u32[]{:S(2)}, u32[]{:S(2)}) collective-permute-start(f32[4,48,128]{2,1,0:T(8,128)S(1)} %get-tuple-element.65), channel_id=1, source_target_pairs={{0,4},{4,0},{8,12},{12,8},{16,20},{20,16},{24,28},{28,24},{1,5},{5... | collective-permute-start | bytes 294920 | tf_op jit(solution)/shard_map/ppermute | solution.py:32
  40.8 6.6 %collective-permute-start.8 = (f32[1,4096]{1,0:T(1,128)S(1)}, f32[1,4096]{1,0:T(1,128)S(1)}, u32[]{:S(2)}, u32[]{:S(2)}) collective-permute-start(f32[1,4096]{1,0:T(1,128)S(1)} %add.23.refs_0_), channel_id=1, source_target_pairs={{0,8},{4,12},{8,0},{12,4},{16,24},{20,28},{24,16},{28,20},{1,9},{5... | collective-permute-start | bytes 49160 | tf_op jit(solution)/shard_map/ppermute | solution.py:32
  40.8 6.5 %collective-permute-start.9 = (f32[1,4096]{1,0:T(1,128)S(1)}, f32[1,4096]{1,0:T(1,128)S(1)}, u32[]{:S(2)}, u32[]{:S(2)}) collective-permute-start(f32[1,4096]{1,0:T(1,128)S(1)} %add.23.refs_0_), channel_id=1, source_target_pairs={{0,16},{4,20},{8,24},{12,28},{16,0},{20,4},{24,8},{28,12},{1,17},{... | collective-permute-start | bytes 49160 | tf_op jit(solution)/shard_map/ppermute | solution.py:32
  41.3 6.1 %collective-permute-start.10 = (f32[1,4096]{1,0:T(1,128)S(1)}, f32[1,4096]{1,0:T(1,128)S(1)}, u32[]{:S(2)}, u32[]{:S(2)}) collective-permute-start(f32[1,4096]{1,0:T(1,128)S(1)} %add.23.refs_0_), channel_id=1, source_target_pairs={{0,24},{4,28},{8,16},{12,20},{16,8},{20,12},{24,0},{28,4},{1,25},{... | collective-permute-start | bytes 49160 | tf_op jit(solution)/shard_map/ppermute | solution.py:32
  47.8 1.2 collective-permute-start.11
  49.0 3.6 %collective-permute-start.12 = (f32[2,128]{1,0:T(2,128)S(1)}, f32[2,128]{1,0:T(2,128)S(1)}, u32[]{:S(2)}, u32[]{:S(2)}) collective-permute-start(f32[2,128]{1,0:T(2,128)S(1)} %add.24.refs_0_), channel_id=1, source_target_pairs={{0,2},{1,3},{2,0},{3,1},{4,6},{5,7},{6,4},{7,5},{8,10},{9,11},{10,... | collective-permute-start | bytes 3080 | tf_op jit(solution)/shard_map/ppermute | solution.py:32
  53.1 4.1 %collective-permute-start.16 = (f32[136,256]{1,0:T(8,128)S(1)}, f32[136,256]{1,0:T(8,128)S(1)}, u32[]{:S(2)}, u32[]{:S(2)}) collective-permute-start(f32[136,256]{1,0:T(8,128)S(1)} %logit_sum.1), channel_id=1, source_target_pairs={{0,1},{1,0},{2,3},{3,2},{4,5},{5,4},{6,7},{7,6},{8,9},{9,8},{10,11... | collective-permute-start | bytes 417800 | tf_op jit(solution)/shard_map/ppermute | solution.py:32
  53.2 8.4 %collective-permute-start.13 = (f32[2,48,128]{2,1,0:T(8,128)S(1)}, f32[2,48,128]{2,1,0:T(8,128)S(1)}, u32[]{:S(2)}, u32[]{:S(2)}) collective-permute-start(f32[2,48,128]{2,1,0:T(8,128)S(1)} %pad_maximum_fusion.3), channel_id=1, source_target_pairs={{0,8},{4,12},{8,0},{12,4},{16,24},{20,28},{24,16},{28,20},{1,9},{5... | collective-permute-start | bytes 147464 | tf_op jit(solution)/shard_map/ppermute | solution.py:32
  53.4 9.8 %collective-permute-start.14 = (f32[2,48,128]{2,1,0:T(8,128)S(1)}, f32[2,48,128]{2,1,0:T(8,128)S(1)}, u32[]{:S(2)}, u32[]{:S(2)}) collective-permute-start(f32[2,48,128]{2,1,0:T(8,128)S(1)} %pad_maximum_fusion.4), channel_id=1, source_target_pairs={{0,16},{4,20},{8,24},{12,28},{16,0},{20,4},{24,8},{28,12},{1,17},{... | collective-permute-start | bytes 147464 | tf_op jit(solution)/shard_map/ppermute | solution.py:32
  57.2 11.1 %collective-permute-start.17 = (f32[136,256]{1,0:T(8,128)S(1)}, f32[136,256]{1,0:T(8,128)S(1)}, u32[]{:S(2)}, u32[]{:S(2)}) collective-permute-start(f32[136,256]{1,0:T(8,128)S(1)} %add.25.refs_3_), channel_id=1, source_target_pairs={{0,2},{1,3},{2,0},{3,1},{4,6},{5,7},{6,4},{7,5},{8,10},{9,11},{10,... | collective-permute-start | bytes 417800 | tf_op jit(solution)/shard_map/ppermute | solution.py:32
  58.8 9.5 %collective-permute-start.15 = (f32[2,48,128]{2,1,0:T(8,128)S(1)}, f32[2,48,128]{2,1,0:T(8,128)S(1)}, u32[]{:S(2)}, u32[]{:S(2)}) collective-permute-start(f32[2,48,128]{2,1,0:T(8,128)S(1)} %pad_maximum_fusion.5), channel_id=1, source_target_pairs={{0,24},{4,28},{8,16},{12,20},{16,8},{20,12},{24,0},{28,4},{1,25},{... | collective-permute-start | bytes 147464 | tf_op jit(solution)/shard_map/ppermute | solution.py:32
  59.5 8.8 %collective-permute-start.18 = (f32[1,4096]{1,0:T(1,128)S(1)}, f32[1,4096]{1,0:T(1,128)S(1)}, u32[]{:S(2)}, u32[]{:S(2)}) collective-permute-start(f32[1,4096]{1,0:T(1,128)S(1)} %col_pass.2.refs_0_), channel_id=1, source_target_pairs={{0,8},{4,12},{8,0},{12,4},{16,24},{20,28},{24,16},{28,20},{1,9},{5... | collective-permute-start | bytes 49160 | tf_op jit(solution)/shard_map/ppermute | solution.py:32
  61.6 7.9 %collective-permute-start.19 = (f32[1,4096]{1,0:T(1,128)S(1)}, f32[1,4096]{1,0:T(1,128)S(1)}, u32[]{:S(2)}, u32[]{:S(2)}) collective-permute-start(f32[1,4096]{1,0:T(1,128)S(1)} %col_pass.2.refs_0_), channel_id=1, source_target_pairs={{0,16},{4,20},{8,24},{12,28},{16,0},{20,4},{24,8},{28,12},{1,17},{... | collective-permute-start | bytes 49160 | tf_op jit(solution)/shard_map/ppermute | solution.py:32
  63.2 7.2 %collective-permute-start.20 = (f32[1,4096]{1,0:T(1,128)S(1)}, f32[1,4096]{1,0:T(1,128)S(1)}, u32[]{:S(2)}, u32[]{:S(2)}) collective-permute-start(f32[1,4096]{1,0:T(1,128)S(1)} %col_pass.2.refs_0_), channel_id=1, source_target_pairs={{0,24},{4,28},{8,16},{12,20},{16,8},{20,12},{24,0},{28,4},{1,25},{... | collective-permute-start | bytes 49160 | tf_op jit(solution)/shard_map/ppermute | solution.py:32
  70.8 1.2 collective-permute-start.21
  72.0 14.5 %copy-start.7 = (s32[128]{0:T(128)S(1)}, s32[128]{0:T(128)}, u32[]{:S(2)}) copy-start(s32[128]{0:T(128)} %param.13) | copy-start | bytes 1540
  72.0 3.6 %collective-permute-start.22 = (f32[2,128]{1,0:T(2,128)S(1)}, f32[2,128]{1,0:T(2,128)S(1)}, u32[]{:S(2)}, u32[]{:S(2)}) collective-permute-start(f32[2,128]{1,0:T(2,128)S(1)} %add.26.refs_0_), channel_id=1, source_target_pairs={{0,2},{1,3},{2,0},{3,1},{4,6},{5,7},{6,4},{7,5},{8,10},{9,11},{10,... | collective-permute-start | bytes 3080 | tf_op jit(solution)/shard_map/ppermute | solution.py:32
  76.1 5.5 %collective-permute-start.23 = (f32[1,4096]{1,0:T(1,128)S(1)}, f32[1,4096]{1,0:T(1,128)S(1)}, u32[]{:S(2)}, u32[]{:S(2)}) collective-permute-start(f32[1,4096]{1,0:T(1,128)S(1)} %col_pass.3.refs_0_), channel_id=1, source_target_pairs={{0,8},{4,12},{8,0},{12,4},{16,24},{20,28},{24,16},{28,20},{1,9},{5... | collective-permute-start | bytes 49160 | tf_op jit(solution)/shard_map/ppermute | solution.py:32
  78.0 5.8 %collective-permute-start.24 = (f32[1,4096]{1,0:T(1,128)S(1)}, f32[1,4096]{1,0:T(1,128)S(1)}, u32[]{:S(2)}, u32[]{:S(2)}) collective-permute-start(f32[1,4096]{1,0:T(1,128)S(1)} %col_pass.3.refs_0_), channel_id=1, source_target_pairs={{0,16},{4,20},{8,24},{12,28},{16,0},{20,4},{24,8},{28,12},{1,17},{... | collective-permute-start | bytes 49160 | tf_op jit(solution)/shard_map/ppermute | solution.py:32
  80.6 5.9 %collective-permute-start.25 = (f32[1,4096]{1,0:T(1,128)S(1)}, f32[1,4096]{1,0:T(1,128)S(1)}, u32[]{:S(2)}, u32[]{:S(2)}) collective-permute-start(f32[1,4096]{1,0:T(1,128)S(1)} %col_pass.3.refs_0_), channel_id=1, source_target_pairs={{0,24},{4,28},{8,16},{12,20},{16,8},{20,12},{24,0},{28,4},{1,25},{... | collective-permute-start | bytes 49160 | tf_op jit(solution)/shard_map/ppermute | solution.py:32
  87.9 1.3 %collective-permute-start.26 = (f32[72,256]{1,0:T(8,128)S(1)}, f32[72,256]{1,0:T(8,128)S(1)}, u32[]{:S(2)}, u32[]{:S(2)}) collective-permute-start(f32[72,256]{1,0:T(8,128)S(1)} %get-tuple-element.81), channel_id=1, source_target_pairs={{0,1},{1,0},{2,3},{3,2},{4,5},{5,4},{6,7},{7,6},{8,9},{9,8},{10,11... | collective-permute-start | bytes 221192 | tf_op jit(solution)/shard_map/ppermute | solution.py:32
  89.3 4.4 %collective-permute-start.27 = (f32[72,256]{1,0:T(8,128)S(1)}, f32[72,256]{1,0:T(8,128)S(1)}, u32[]{:S(2)}, u32[]{:S(2)}) collective-permute-start(f32[72,256]{1,0:T(8,128)S(1)} %add.27.refs_5_), channel_id=1, source_target_pairs={{0,2},{1,3},{2,0},{3,1},{4,6},{5,7},{6,4},{7,5},{8,10},{9,11},{10,... | collective-permute-start | bytes 221192 | tf_op jit(solution)/shard_map/ppermute | solution.py:32
  94.5 6.4 %collective-permute-start.33 = (f32[64,256]{1,0:T(8,128)S(1)}, f32[64,256]{1,0:T(8,128)S(1)}, u32[]{:S(2)}, u32[]{:S(2)}) collective-permute-start(f32[64,256]{1,0:T(8,128)S(1)} %get-tuple-element.88), channel_id=1, source_target_pairs={{0,24},{4,28},{8,16},{12,20},{16,8},{20,12},{24,0},{28,4},{1,25},{... | collective-permute-start | bytes 196616 | tf_op jit(solution)/shard_map/ppermute | solution.py:32
  95.6 7.1 %collective-permute-start.32 = (f32[64,256]{1,0:T(8,128)S(1)}, f32[64,256]{1,0:T(8,128)S(1)}, u32[]{:S(2)}, u32[]{:S(2)}) collective-permute-start(f32[64,256]{1,0:T(8,128)S(1)} %get-tuple-element.88), channel_id=1, source_target_pairs={{0,16},{4,20},{8,24},{12,28},{16,0},{20,4},{24,8},{28,12},{1,17},{... | collective-permute-start | bytes 196616 | tf_op jit(solution)/shard_map/ppermute | solution.py:32
  97.0 5.8 %collective-permute-start.31 = (f32[64,256]{1,0:T(8,128)S(1)}, f32[64,256]{1,0:T(8,128)S(1)}, u32[]{:S(2)}, u32[]{:S(2)}) collective-permute-start(f32[64,256]{1,0:T(8,128)S(1)} %get-tuple-element.88), channel_id=1, source_target_pairs={{0,8},{4,12},{8,0},{12,4},{16,24},{20,28},{24,16},{28,20},{1,9},{5... | collective-permute-start | bytes 196616 | tf_op jit(solution)/shard_map/ppermute | solution.py:32
  98.9 5.7 %collective-permute-start.29 = (f32[1,8,48,128]{3,2,1,0:T(8,128)S(1)}, f32[1,8,48,128]{3,2,1,0:T(8,128)S(1)}, u32[]{:S(2)}, u32[]{:S(2)}) collective-permute-start(f32[1,8,48,128]{3,2,1,0:T(8,128)S(1)} %maximum_bitcast_fusion), channel_id=1, source_target_pairs={{0,2},{1,3},{2,0},{3,1},{4,6},{5,7},{6,4},{7,5},{8,10},{9,11},{10,... | collective-permute-start | bytes 589832 | tf_op jit(solution)/shard_map/ppermute | solution.py:32
  102.8 7.2 %collective-permute-start.34 = (f32[4,64,256]{2,1,0:T(8,128)S(1)}, f32[4,64,256]{2,1,0:T(8,128)S(1)}, u32[]{:S(2)}, u32[]{:S(2)}) collective-permute-start(f32[4,64,256]{2,1,0:T(8,128)S(1)} %pad_maximum_fusion.1.refs_7_), channel_id=1, source_target_pairs={{0,4},{4,0},{8,12},{12,8},{16,20},{20,16},{24,28},{28,24},{1,5},{5... | collective-permute-start | bytes 786440 | tf_op jit(solution)/shard_map/ppermute | solution.py:32
  104.7 5.9 %collective-permute-start.30 = (f32[2,8,48,128]{3,2,1,0:T(8,128)S(1)}, f32[2,8,48,128]{3,2,1,0:T(8,128)S(1)}, u32[]{:S(2)}, u32[]{:S(2)}) collective-permute-start(f32[2,8,48,128]{3,2,1,0:T(8,128)S(1)} %pad_maximum_fusion.refs_0_), channel_id=1, source_target_pairs={{0,1},{1,0},{2,3},{3,2},{4,5},{5,4},{6,7},{7,6},{8,9},{9,8},{10,11... | collective-permute-start | bytes 1179656 | tf_op jit(solution)/shard_map/ppermute | solution.py:32
  104.8 5.2 %collective-permute-start.28 = (f32[1,64]{1,0:T(1,128)S(1)}, f32[1,64]{1,0:T(1,128)S(1)}, u32[]{:S(2)}, u32[]{:S(2)}) collective-permute-start(f32[1,64]{1,0:T(1,128)S(1)} %get-tuple-element.82), channel_id=1, source_target_pairs={{0,1},{1,0},{2,3},{3,2},{4,5},{5,4},{6,7},{7,6},{8,9},{9,8},{10,11... | collective-permute-start | bytes 776 | tf_op jit(solution)/shard_map/ppermute | solution.py:32
  105.3 5.9 %collective-permute-start.35 = (f32[4,64,256]{2,1,0:T(8,128)S(1)}, f32[4,64,256]{2,1,0:T(8,128)S(1)}, u32[]{:S(2)}, u32[]{:S(2)}) collective-permute-start(f32[4,64,256]{2,1,0:T(8,128)S(1)} %pad_maximum_fusion.1.refs_7_), channel_id=1, source_target_pairs={{0,1},{1,0},{2,3},{3,2},{4,5},{5,4},{6,7},{7,6},{8,9},{9,8},{10,11... | collective-permute-start | bytes 786440 | tf_op jit(solution)/shard_map/ppermute | solution.py:32
  109.9 1.5 %collective-permute-start.36 = (f32[4,64,256]{2,1,0:T(8,128)S(1)}, f32[4,64,256]{2,1,0:T(8,128)S(1)}, u32[]{:S(2)}, u32[]{:S(2)}) collective-permute-start(f32[4,64,256]{2,1,0:T(8,128)S(1)} %collective-permute-done.34.refs_8_), channel_id=1, source_target_pairs={{0,1},{1,0},{2,3},{3,2},{4,5},{5,4},{6,7},{7,6},{8,9},{9,8},{10,11... | collective-permute-start | bytes 786440 | tf_op jit(solution)/shard_map/ppermute | solution.py:32
  111.5 2.2 %copy-start = (f32[1024,1024]{1,0:T(8,128)S(1)}, f32[1024,1024]{1,0:T(8,128)}, u32[]{:S(2)}) copy-start(f32[1024,1024]{1,0:T(8,128)} %all-gather.2.cloned.1.call-done.refs_1_) | copy-start | bytes 12582916
Sparse Core Ops, SparseCore 0:
  10.7 81.2 all-gather.1

commit v3 on v2

--- a/solution.py
+++ b/solution.py
@@ -107,24 +107,28 @@
             pre_ref[...] += part
     pre = pre_ref[...]
     again_ref[...] = pre
-    mom_ref[:, 0:hidden] = jnp.sum(pre, axis=0, keepdims=True)
-    mom_ref[:, hidden:] = jnp.sum(pre * pre, axis=0, keepdims=True)
-
-
-def first_layer(features, w_first):
+    first = jnp.sum(pre, axis=0, keepdims=True)
+    second = jnp.sum(pre * pre, axis=0, keepdims=True)
+    for k in range(mom_ref.shape[0]):
+        mom_ref[k, :, 0:hidden] = first
+        mom_ref[k, :, hidden:] = second
+
+
+def first_layer(features, w_first, spread):
     rows, depth = features.shape
     hidden = w_first.shape[1]
     steps = 6 if depth % (6 * 128) == 0 else 1
     return pl.pallas_call(
         first_kernel,
         in_specs=[pl.BlockSpec(memory_space=pl.ANY)] * 2,
-        out_shape=[jax.ShapeDtypeStruct((rows, hidden), F32)] * 2 + [jax.ShapeDtypeStruct((1, 2 * hidden), F32)],
+        out_shape=[jax.ShapeDtypeStruct((rows, hidden), F32)] * 2
+        + [jax.ShapeDtypeStruct((spread, 1, 2 * hidden), F32)],
         scratch_shapes=[
             pltpu.VMEM((rows, depth), BF16),
             pltpu.VMEM((depth, hidden), BF16),
             pltpu.SemaphoreType.DMA((steps + 1,)),
         ],
-        compiler_params=params(60),
+        compiler_params=params(52),
         cost_estimate=cost(2 * rows * depth * hidden, 2 * depth * hidden + 4 * rows * hidden),
         name="first_layer",
     )(features, w_first)
@@ -139,7 +143,7 @@
     parts = refs[:n_parts]
     pre_ref, gain_ref, shift_ref, w_ref, emb_ref, stats_ref = refs[n_parts:]
     hidden = pre_ref.shape[1]
-    moments = add_parts([p[...] for p in parts]) / crops_all
+    moments = add_parts([p[k] for p in parts for k in range(p.shape[0])]) / crops_all
     mean = moments[:, 0:hidden]
     var = moments[:, hidden:] - mean * mean
     stats_ref[0:1, :] = mean
@@ -200,32 +204,61 @@
     )(*parts)
 
 
+def put_blocks(out_ref, row, value):
+    for k in range(value.shape[1] // 128):
+        out_ref[row + k : row + k + 1, :] = value[:, k * 128 : (k + 1) * 128]
+
+
 def score_kernel(n, *refs):
-    pieces, u_ref, codes, col_ref = refs[:n], refs[n], refs[n + 1 : 2 * n + 1], refs[2 * n + 1]
-    units = u_ref[...]
-    col = 0.0
-    for piece, out in zip(pieces, codes):
-        code = jnp.exp(dot(piece[...].astype(BF16), units, ((1,), (1,))) / balancing_epsilon)
-        out[...] = code
-        col = col + jnp.sum(code, axis=0, keepdims=True)
-    col_ref[...] = col
-
-
-def score(pieces, units):
-    rows, width = pieces[0].shape
-    protos, n = units.shape[0], len(pieces)
+    piece, u_ref = refs[:2]
+    code_ref, col_ref = refs[-2:] if n == 0 else refs[4:6]
+    j = pl.program_id(0)
+    code = jnp.exp(dot(piece[...].astype(BF16), u_ref[...], ((1,), (1,))) / balancing_epsilon)
+    code_ref[...] = code
+    put_blocks(col_ref, 0, jnp.sum(code, axis=0, keepdims=True))
+    if n:
+        col_ref[...] += refs[2][...]
+        size = col_ref.shape[0]
+        at = pl.ds(pl.multiple_of(j * size, size), size)
+        for k, out in enumerate(refs[6:]):
+            out[at, :] = col_ref[...]
+
+            @pl.when(j == 0)
+            def _():
+                out[out.shape[0] - refs[3].shape[1] :, :] = refs[3][k + 1]
+
+
+def score(piece, units, more=None):
+    rows, width = piece.shape
+    protos = units.shape[0]
     blk = min(1024, protos)
-    *codes, col = pl.pallas_call(
+    lines, step = protos // 128, blk // 128
+    by_step = pl.BlockSpec((step, 128), lambda j: (j, 0))
+    in_specs = [whole((rows, width)), pl.BlockSpec((blk, width), lambda j: (j, 0))]
+    out_specs = [pl.BlockSpec((rows, blk), lambda j: (0, j)), by_step]
+    out_shape = [jax.ShapeDtypeStruct((rows, protos), F32), jax.ShapeDtypeStruct((lines, 128), F32)]
+    n, extra = 0, ()
+    if more is not None:
+        n, extra = more[1].shape[0] - 1, more
+        sent = (lines + more[1].shape[1], 128)
+        in_specs += [by_step, whole(more[1].shape)]
+        out_specs += [whole(sent)] * n
+        out_shape += [jax.ShapeDtypeStruct(sent, F32)] * n
+    return pl.pallas_call(
         functools.partial(score_kernel, n),
         grid=(protos // blk,),
-        in_specs=[whole((rows, width))] * n + [pl.BlockSpec((blk, width), lambda j: (j, 0))],
-        out_specs=[pl.BlockSpec((rows, blk), lambda j: (0, j))] * n + [pl.BlockSpec((1, blk), lambda j: (0, j))],
-        out_shape=[jax.ShapeDtypeStruct((rows, protos), F32)] * n + [jax.ShapeDtypeStruct((1, protos), F32)],
-        compiler_params=params(),
-        cost_estimate=cost(2 * n * rows * protos * width, 4 * n * rows * protos, n * rows * protos),
+        in_specs=in_specs,
+        out_specs=out_specs,
+        out_shape=out_shape,
+        compiler_params=params(),
+        cost_estimate=cost(2 * rows * protos * width, 4 * rows * protos, rows * protos),
         name="score",
-    )(*pieces, units)
-    return codes, col
+    )(piece, units, *extra)
+
+
+def col_scale(parts):
+    lines = parts[0].shape[0]
+    return 1.0 / add_parts([p[0:lines, :] for p in parts])
 
 
 def pack(table, lane_row, out_ref):
@@ -272,9 +305,12 @@
 
 def row_kernel(n_parts, *refs):
     parts, codes, out_ref = refs[:n_parts], refs[n_parts:-1], refs[-1]
-    scale = 1.0 / add_parts([p[...] for p in parts])
+    scale = col_scale(parts)
     for k, code in enumerate(codes):
-        out_ref[k : k + 1, :] = to_lanes(jnp.sum(code[...] * scale, axis=1, keepdims=True))
+        total = 0.0
+        for j in range(scale.shape[0]):
+            total = total + code[:, j * 128 : (j + 1) * 128] * scale[j : j + 1, :]
+        out_ref[k : k + 1, :] = to_lanes(jnp.sum(total, axis=1, keepdims=True))
 
 
 def row_pass(parts, codes):
@@ -289,46 +325,59 @@
     )(*parts, *codes)
 
 
-def col_kernel(n_parts, *refs):
-    parts, codes, out_ref = refs[:n_parts], refs[n_parts:-1], refs[-1]
+def col_kernel(n_parts, n_codes, *refs):
+    parts, codes, refs = refs[:n_parts], refs[n_parts : n_parts + n_codes], refs[n_parts + n_codes :]
     scale = 1.0 / add_parts([p[...] for p in parts])
     total = 0.0
     for k, code in enumerate(codes):
         total = total + jnp.sum(code[...] * to_column(scale[k : k + 1, :]), axis=0, keepdims=True)
-    out_ref[...] = total
-
-
-def col_pass(parts, codes):
+    if len(refs) == 1:
+        put_blocks(refs[0], 0, total)
+    else:
+        put_blocks(refs[1], 0, total)
+        for k, out in enumerate(refs[2:]):
+            out[0 : refs[1].shape[0], :] = refs[1][...]
+            out[refs[1].shape[0] :, :] = refs[0][k + 1]
+
+
+def col_pass(parts, codes, columns=None):
     rows, protos = codes[0].shape
     n = len(codes)
-    return pl.pallas_call(
-        functools.partial(col_kernel, len(parts)),
-        out_shape=jax.ShapeDtypeStruct((1, protos), F32),
+    lines = protos // 128
+    extra = () if columns is None else (columns,)
+    shapes = [(lines, 128)] + [(lines + c.shape[1], 128) for c in extra for _ in range(c.shape[0] - 1)]
+    return pl.pallas_call(
+        functools.partial(col_kernel, len(parts), n),
+        out_shape=[jax.ShapeDtypeStruct(shape, F32) for shape in shapes],
         compiler_params=params(),
         cost_estimate=cost(2 * n * rows * protos, 4 * n * rows * protos),
         name="col_pass",
-    )(*parts, *codes)
+    )(*parts, *codes, *extra)
 
 
 def target_kernel(n_parts, halves, *refs):
     parts = refs[:n_parts]
-    codes_ref, u_ref, partner_ref, core_ref = refs[n_parts : n_parts + 4]
-    outs, table_all, mass_all = refs[n_parts + 4 : -2], refs[-2], refs[-1]
+    codes_ref, u_ref, partner_ref, at_ref = refs[n_parts : n_parts + 4]
+    outs, table_all, mass_all, low = refs[n_parts + 4 : -3], refs[-3], refs[-2], refs[-1]
     rows = codes_ref.shape[0]
-    scale = 1.0 / add_parts([p[...] for p in parts])
-    weighted = codes_ref[...] * scale
-    mass = jnp.sum(weighted, axis=1, keepdims=True)
-    table = jnp.dot(weighted.astype(BF16), u_ref[...], preferred_element_type=F32)
+    scale = col_scale(parts)
+    total = 0.0
+    for j in range(scale.shape[0]):
+        weighted = codes_ref[:, j * 128 : (j + 1) * 128] * scale[j : j + 1, :]
+        low[:, j * 128 : (j + 1) * 128] = weighted.astype(BF16)
+        total = total + weighted
+    mass = jnp.sum(total, axis=1, keepdims=True)
+    table = jnp.dot(low[...], u_ref[...], preferred_element_type=F32)
     chosen = partner_ref[...] == lax.broadcasted_iota(jnp.int32, (rows, rows), 0)
     table_all[...] = dot(jnp.where(chosen, 1.0, 0.0).astype(F32), table, ((1,), (0,)), HIGHEST)
     mass_all[...] = jnp.sum(jnp.where(chosen, to_lanes(mass), 0.0), axis=1, keepdims=True)
     size = rows // halves
     for k in range(halves):
-        at = pl.ds(pl.multiple_of((core_ref[2] ^ k) * size, size), size)
+        at = pl.ds(pl.multiple_of((at_ref[2] ^ k) * size, size), size)
         pack(table_all[at, :], to_lanes(mass_all[at, :]), outs[k])
 
 
-def target_sum(parts, codes, units, partner, core, halves):
+def target_sum(parts, codes, units, partner, at, halves):
     rows, protos = codes.shape
     width = units.shape[1]
     n_vmem = len(parts) + 3
@@ -336,11 +385,15 @@
         functools.partial(target_kernel, len(parts), halves),
         in_specs=[pl.BlockSpec(memory_space=pltpu.VMEM)] * n_vmem + [pl.BlockSpec(memory_space=pltpu.SMEM)],
         out_shape=[jax.ShapeDtypeStruct((rows // halves + 8, width), F32)] * halves,
-        scratch_shapes=[pltpu.VMEM((rows, width), F32), pltpu.VMEM((rows, 1), F32)],
+        scratch_shapes=[
+            pltpu.VMEM((rows, width), F32),
+            pltpu.VMEM((rows, 1), F32),
+            pltpu.VMEM((rows, protos), BF16),
+        ],
         compiler_params=params(),
         cost_estimate=cost(2 * rows * protos * width, 4 * rows * protos + 2 * protos * width),
         name="target_sum",
-    )(*parts, codes, units, partner, core)
+    )(*parts, codes, units, partner, at)
 
 
 def loss_kernel(n_raw, n_logit, n_target, *refs):
@@ -411,9 +464,23 @@
     )(features, at)
 
 
-def columns_z(keep, got):
-    both = [jnp.stack([keep[k], got[k]]) for k in range(keep.shape[0])]
-    return [both[0]] + [swap(both[k], "batch", 2 * k) for k in range(1, len(both))]
+def join_kernel(n_z, keep_ref, got_ref, *refs):
+    out_ref, height = refs[-1], keep_ref.shape[1]
+    out_ref[0, 0] = keep_ref[0]
+    out_ref[0, 1] = got_ref[0]
+    for k in range(2 * n_z - 2):
+        out_ref[0, 2 + k] = refs[k][refs[k].shape[0] - height :, :]
+
+
+def columns_join(keep, got, first, second):
+    n_z, height, rows = keep.shape
+    return pl.pallas_call(
+        functools.partial(join_kernel, n_z),
+        out_shape=jax.ShapeDtypeStruct((1, 2 * n_z, height, rows), F32),
+        compiler_params=params(),
+        cost_estimate=cost(0, 16 * n_z * height * rows),
+        name="columns_join",
+    )(keep, got, *[m for pair in zip(first, second) for m in pair])
 
 
 def columns_kernel(masks, at_ref, *refs):
@@ -423,8 +490,7 @@
         _, n_batch, height, rows = refs[k // inner].shape
         row = pl.multiple_of((at_ref[1] ^ mask) * height, height)
         for i in range(n_batch):
-            col = pl.multiple_of((at_ref[0] ^ i) * rows, rows)
-            out_ref[pl.ds(row, height), pl.ds(col, rows)] = refs[k // inner][k % inner, i].astype(BF16)
+            out_ref[at_ref[0] ^ i, pl.ds(row, height), :] = refs[k // inner][k % inner, i].astype(BF16)
 
 
 def columns_all(own, other, at):
@@ -435,7 +501,7 @@
     return pl.pallas_call(
         functools.partial(columns_kernel, (0, 2, 1, 3)),
         in_specs=[smem, vmem, vmem],
-        out_shape=jax.ShapeDtypeStruct((n_proto * height, n_batch * rows), BF16),
+        out_shape=jax.ShapeDtypeStruct((n_batch, n_proto * height, rows), BF16),
         compiler_params=params(),
         cost_estimate=cost(0, 6 * n_proto * height * n_batch * rows),
         name="columns_all",
@@ -455,21 +521,137 @@
     )(columns)
 
 
-def tail_kernel(crops_all, places, e_cols, *refs):
-    n_grad = len(places)
+def tail_step(refs, w1_ref, w2_ref, sums_ref, grad_all):
+    at_ref, pre_ref, cols_ref, stats, gain, shift, w_ref, grads, masks = refs
+    k = pl.program_id(0)
+    block = at_ref[0] ^ (2 * k + masks[0])
+    size = pre_ref.shape[1] // 2
+    for flip, piece in enumerate(grads):
+        place = pl.multiple_of((at_ref[2] ^ flip) * size, size)
+        grad_all[pl.ds(place, size), :] = piece[k]
+    grad = grad_all[...].astype(BF16)
+    e_rows = w2_ref.shape[0]
+    shape = (e_rows, grad.shape[1])
+    mine = lax.broadcasted_iota(jnp.int32, shape, 0) + at_ref[0] * (grad.shape[1] // masks[1])
+    chosen = jnp.where(mine == lax.broadcasted_iota(jnp.int32, shape, 1), 1.0, 0.0).astype(BF16)
+    picked = dot(chosen, grad, ((1,), (1,))).astype(BF16)
+    normed, shifted = batch_norm(pre_ref[block], stats, gain, shift)
+    hidden_grad = dot(grad, w_ref[...], ((1,), (1,)))
+    bn_grad = jnp.where(shifted > 0, hidden_grad, 0.0)
+    sums_ref[0, pl.ds(block, 1), :] = jnp.sum(bn_grad, axis=0, keepdims=True)
+    sums_ref[1, pl.ds(block, 1), :] = jnp.sum(bn_grad * normed, axis=0, keepdims=True)
+    hidden = jnp.maximum(shifted, 0.0).astype(BF16)
+    w2_ref[...] += jnp.dot(picked, hidden, preferred_element_type=F32)
+    w1_ref[...] += jnp.dot(cols_ref[block], bn_grad.astype(BF16), preferred_element_type=F32)
+
+
+def near_kernel(masks, *refs):
     at_ref, pre_ref, cols_ref, stats_ref, gain_ref, shift_ref, w_ref = refs[:7]
-    grads, refs = refs[7 : 7 + n_grad], refs[7 + n_grad :]
-    w1_ref, w2_ref, gain_grad_ref, shift_grad_ref, grad_all, grad_cols = refs
-    width = grad_all.shape[1]
+    grads, (w1_ref, w2_ref, sums_ref, grad_all) = refs[7:9], refs[9:]
 
     @pl.when(pl.program_id(0) == 0)
     def _():
-        for piece, (masks, flip) in zip(grads, places):
-            rows = piece.shape[1]
-            for k, mask in enumerate(masks):
-                place = 0 if mask is None else ((at_ref[0] ^ mask) << 1) + (at_ref[2] ^ flip)
-                grad_all[pl.ds(pl.multiple_of(place * rows, rows), rows), :] = piece[k].astype(BF16)
-        shape = (grad_cols.shape[0], width)
+        w1_ref[...] = jnp.zeros_like(w1_ref)
+        w2_ref[...] = jnp.zeros_like(w2_ref)
+        sums_ref[...] = jnp.zeros_like(sums_ref)
+
+    ins = (at_ref, pre_ref, cols_ref, stats_ref[...], gain_ref[...], shift_ref[...], w_ref, grads, masks)
+    tail_step(ins, w1_ref, w2_ref, sums_ref, grad_all)
+
+
+def far_kernel(crops_all, e_cols, masks, *refs):
+    at_ref, pre_ref, cols_ref, stats_ref, gain_ref, shift_ref, w_ref = refs[:7]
+    grads, (near_w1, near_w2, near_sums, flat_ref, total_ref) = refs[7:9], refs[9:14]
+    w1_ref, w2_ref, gain_grad_ref, shift_grad_ref, grad_all, sums, w2_all = refs[14:]
+
+    @pl.when(pl.program_id(0) == 0)
+    def _():
+        w1_ref[...] = near_w1[...]
+        w2_all[...] = near_w2[...]
+        sums[...] = near_sums[...]
+
+    stats, gain = stats_ref[...], gain_ref[...]
+    ins = (at_ref, pre_ref, cols_ref, stats, gain, shift_ref[...], w_ref, grads, masks)
+    tail_step(ins, w1_ref, w2_all, sums, grad_all)
+
+    @pl.when(pl.program_id(0) == pl.num_programs(0) - 1)
+    def _():
+        w2_ref[...] = w2_all[0:e_cols, :]
+        shift_grad = jnp.sum(sums[0], axis=0, keepdims=True)
+        gain_grad = jnp.sum(sums[1], axis=0, keepdims=True)
+        shift_grad_ref[...] = shift_grad
+        gain_grad_ref[...] = gain_grad
+        flat = total_ref[...] * (shift_grad / crops_all) + flat_ref[...] * (gain_grad / crops_all)
+        w1_ref[...] = gain * stats[1:2, :] * (w1_ref[...] - flat)
+
+
+def tail_call(kernel, odd, outs, scratch, at, pre_all, columns, stats, gain, shift, w_second, grads, more, name):
+    n_batch, unit, hidden = pre_all.shape
+    width = w_second.shape[1]
+    crops = n_batch * unit // 2
+    return pl.pallas_call(
+        functools.partial(kernel, (odd, n_batch)),
+        grid_spec=pltpu.PrefetchScalarGridSpec(
+            num_scalar_prefetch=1,
+            grid=(n_batch // 2,),
+            in_specs=[pl.BlockSpec(memory_space=pltpu.VMEM)] * (6 + len(grads) + len(more)),
+            out_specs=[whole(n) for n in outs],
+            scratch_shapes=[pltpu.VMEM((unit, width), F32)] + [pltpu.VMEM(n, F32) for n in scratch],
+        ),
+        out_shape=[jax.ShapeDtypeStruct(n, F32) for n in outs],
+        compiler_params=params(20),
+        cost_estimate=cost(2 * crops * hidden * (width + 256), 4 * crops * hidden),
+        name=name,
+    )(at, pre_all, columns, stats, gain, shift, w_second, *grads, *more)
+
+
+def flat_kernel(pre_hbm, cols_ref, stats_ref, gain_ref, shift_ref, pre_ref, flat_ref, total_ref, sems):
+    n_batch = pre_ref.shape[0]
+    copies = [pltpu.make_async_copy(pre_hbm.at[k], pre_ref.at[k], sems.at[k]) for k in range(n_batch)]
+    for copy in copies:
+        copy.start()
+    stats, gain, shift = stats_ref[...], gain_ref[...], shift_ref[...]
+    total = 0.0
+    for k in range(n_batch):
+        total = total + jnp.sum(cols_ref[k].astype(F32), axis=1, keepdims=True)
+        copies[k].wait()
+        normed, _ = batch_norm(pre_ref[k], stats, gain, shift)
+        part = jnp.dot(cols_ref[k], normed.astype(BF16), preferred_element_type=F32)
+        if k == 0:
+            flat_ref[...] = part
+        else:
+            flat_ref[...] += part
+    total_ref[...] = total
+
+
+def flat_sums(pre_all, columns, stats, gain, shift):
+    n_batch, unit, hidden = pre_all.shape
+    d_cols = columns.shape[1]
+    vmem = pl.BlockSpec(memory_space=pltpu.VMEM)
+    return pl.pallas_call(
+        flat_kernel,
+        in_specs=[pl.BlockSpec(memory_space=pltpu.HBM)] + [vmem] * 4,
+        out_specs=[vmem] * 3,
+        out_shape=[
+            jax.ShapeDtypeStruct((n_batch, unit, hidden), F32),
+            jax.ShapeDtypeStruct((d_cols, hidden), F32),
+            jax.ShapeDtypeStruct((d_cols, 1), F32),
+        ],
+        scratch_shapes=[pltpu.SemaphoreType.DMA((n_batch,))],
+        compiler_params=params(20),
+        cost_estimate=cost(2 * n_batch * unit * hidden * d_cols, 4 * n_batch * unit * hidden),
+        name="flat_sums",
+    )(pre_all, columns, stats, gain, shift)
+
+
+def whole_tail_kernel(crops_all, e_cols, *refs):
+    at_ref, pre_ref, cols_ref, stats_ref, gain_ref, shift_ref, w_ref, raw_ref = refs[:8]
+    w1_ref, w2_ref, gain_grad_ref, shift_grad_ref, grad_all, grad_cols = refs[8:]
+
+    @pl.when(pl.program_id(0) == 0)
+    def _():
+        grad_all[...] = raw_ref[...].astype(BF16)
+        shape = (grad_cols.shape[0], grad_all.shape[1])
         mine = lax.broadcasted_iota(jnp.int32, shape, 0) + at_ref[0] * e_cols
         chosen = jnp.where(mine == lax.broadcasted_iota(jnp.int32, shape, 1), 1.0, 0.0).astype(BF16)
         grad_cols[...] = dot(chosen, grad_all[...], ((1,), (1,))).astype(BF16)
@@ -489,7 +671,7 @@
     w1_ref[...] = jnp.dot(cols_ref[...], pre_grad.astype(BF16), preferred_element_type=F32)
 
 
-def tail(pre_all, columns, stats, gain, shift, w_second, grads, places, at, e_cols):
+def whole_tail(pre_all, columns, stats, gain, shift, w_second, raw, at, e_cols):
     crops_all, hidden = pre_all.shape
     width, d_cols = w_second.shape[1], columns.shape[0]
     blk = min(hidden, max(128, 256 * 1024 // crops_all))
@@ -500,26 +682,20 @@
         return pl.BlockSpec((n, blk), lambda j: (0, j))
 
     return pl.pallas_call(
-        functools.partial(tail_kernel, crops_all, places, e_cols),
+        functools.partial(whole_tail_kernel, crops_all, e_cols),
         grid=(hidden // blk,),
         in_specs=[smem, cols(crops_all), vmem, cols(2), cols(1), cols(1)]
-        + [pl.BlockSpec((blk, width), lambda j: (j, 0))]
-        + [vmem] * len(grads),
+        + [pl.BlockSpec((blk, width), lambda j: (j, 0)), vmem],
         out_specs=[cols(d_cols), cols(e_cols), cols(1), cols(1)],
-        out_shape=[
-            jax.ShapeDtypeStruct((d_cols, hidden), F32),
-            jax.ShapeDtypeStruct((e_cols, hidden), F32),
-            jax.ShapeDtypeStruct((1, hidden), F32),
-            jax.ShapeDtypeStruct((1, hidden), F32),
-        ],
+        out_shape=[jax.ShapeDtypeStruct((n, hidden), F32) for n in (d_cols, e_cols, 1, 1)],
         scratch_shapes=[
             pltpu.VMEM((crops_all, width), BF16),
             pltpu.VMEM((-(-e_cols // 16) * 16, crops_all), BF16),
         ],
-        compiler_params=params(24 if crops_all <= 1024 else 56),
+        compiler_params=params(58),
         cost_estimate=cost(2 * crops_all * hidden * (width + d_cols), 4 * crops_all * hidden),
-        name="tail",
-    )(at, pre_all, columns, stats, gain, shift, w_second, *grads)
+        name="whole_tail",
+    )(at, pre_all, columns, stats, gain, shift, w_second, raw)
 
 
 def after(value, *others):
@@ -537,74 +713,90 @@
     short = n_batch == 8 and n_proto == 4 and depth % 512 == 0
     at = jnp.stack([me, proto_me, proto_me & 1 if short else proto_me * 0])
 
-    pre, pre_again, moments = first_layer(features, w_first)
+    pre, pre_again, moments = first_layer(features, w_first, n_batch if short else 1)
     pre_all = lax.all_gather(pre, "batch", tiled=True)
-    moment_parts = batch_parts(moments)
+    moment_parts = [lax.all_to_all(moments, "batch", 0, 0)] if short else batch_parts(moments)
     units = unit_rows(prototypes)
-    if short:
-        keep, send = columns_pick(after(features, moments), at, n_batch, n_proto)
-        moment_parts[0], keep, send, units = lax.optimization_barrier((moment_parts[0], keep, send, units))
     emb_part, stats = second_layer(crops_all, moment_parts, pre_again, gain, shift, w_second)
     raw_parts = proto_parts(emb_part)
+    if short:
+        keep, send = columns_pick(after(features, emb_part), at, n_batch, n_proto)
+        raw_parts[0], keep, send, units = lax.optimization_barrier((raw_parts[0], keep, send, units))
     embedded = embed_rows(raw_parts)
 
     if short:
         partner_emb = swap(embedded, "batch", 1)
-        got = swap(after(send, embedded), "batch", 1)
-        own_codes, own_col = score([embedded], units)
-        partner_emb, own_col = lax.optimization_barrier((partner_emb, own_col))
-        more_codes, more_col = score([partner_emb], units)
-        codes, col_part = own_codes + more_codes, own_col + more_col
-        got = after(got, col_part)
-        z_stride = 2
+        own_codes, own_col = score(embedded, units)
+        logit = logit_sum(embedded, units)
+        partner_emb, own_col, logit = lax.optimization_barrier((partner_emb, own_col, logit))
+        more_codes, *cols = score(partner_emb, units, (own_col, keep))
+        codes = [own_codes, more_codes]
     else:
-        codes, col_part = score([embedded], units)
-        z_stride = 1
-    logit = logit_sum(after(embedded, col_part), units)
-    col_parts = batch_parts(col_part, z_stride)
+        codes, *cols = score(embedded, units)
+        codes = [codes]
+        logit = logit_sum(embedded, units)
+    moved = []
+    for iteration in range(ITERS):
+        if short and iteration < 2:
+            moved.append([swap(c, "batch", 2 * k + 2) for k, c in enumerate(cols[1:])])
+            col_parts = [cols[0]] + moved[-1]
+        else:
+            col_parts = batch_parts(cols[0], 2 if short else 1)
+        if iteration == 0:
+            logit = logit + swap(after(logit, cols[0]), "proto", 1)
+            col_parts[0], logit = lax.optimization_barrier((col_parts[0], logit))
+            if short:
+                got = swap(after(send, cols[0]), "batch", 1)
+                col_parts[0], got = lax.optimization_barrier((col_parts[0], got))
+        if iteration == 1:
+            logit_parts = proto_parts(after(logit, cols[0]), 2)
+            col_parts[0], *logit_parts = lax.optimization_barrier((col_parts[0], *logit_parts))
+        if short and iteration == 2:
+            columns = columns_join(after(keep, cols[0]), got, *moved)
+            columns = [columns, swap(columns, "proto", 2)]
+            col_parts[0], *columns = lax.optimization_barrier((col_parts[0], *columns))
+        if iteration < ITERS - 1:
+            row_parts = proto_parts(row_pass(col_parts, codes))
+            cols = col_pass(row_parts, codes, got if short and iteration == 0 else None)
     if short:
-        col_parts[0], got, logit = lax.optimization_barrier((col_parts[0], got, logit))
-    for iteration in range(ITERS - 1):
-        row_part = row_pass(col_parts, codes)
-        row_parts = proto_parts(row_part)
-        if short and iteration == 0:
-            columns = columns_z(after(keep, row_parts[0]), after(got, row_parts[0]))
-        col_part = col_pass(row_parts, codes)
-        col_parts = batch_parts(col_part, z_stride)
-        if iteration == 0:
-            logit_parts = proto_parts(after(logit, col_part))
-        if short and iteration == 0:
-            col_parts[0], *rest = lax.optimization_barrier((col_parts[0], *columns, *logit_parts))
-            columns, logit_parts = rest[: len(columns)], rest[len(columns) :]
-    if short:
-        keep, send = target_sum(col_parts, codes[0], units, partner[None, :], at, 2)
-        target_parts = proto_parts(keep + swap(send, "proto", 1), 2)
+        mine, send = target_sum(col_parts, codes[0], units, partner[None, :], at, 2)
+        target_parts = proto_parts(mine + swap(send, "proto", 1), 2)
     else:
         target_parts = proto_parts(target_sum(col_parts, codes[0], units, partner[None, :], at, 1)[0])
     raw_grad, penalty = loss_grad(raw_parts, logit_parts, target_parts, at)
 
     if short:
-        pre_all, *columns = lax.optimization_barrier((pre_all, *columns, raw_grad))[:-1]
+        columns = after(jnp.concatenate(columns), raw_grad)
+        columns = columns_all(columns, swap(columns, "proto", 1), at)
+        pre_all = after(pre_all, raw_grad)
         near = jnp.stack([raw_grad] + [swap(raw_grad, "batch", k) for k in (2, 4, 6)])
-        columns = jnp.concatenate(columns)[None]
-        columns = jnp.concatenate([columns, swap(columns, "proto", 2)])
-        columns = columns_all(columns, swap(columns, "proto", 1), at)
-        far = swap(near, "batch", 1)
-        grads = [near, far, swap(near, "proto", 1), swap(far, "proto", 1)]
-        places = [((0, 2, 4, 6), 0), ((1, 3, 5, 7), 0), ((0, 2, 4, 6), 1), ((1, 3, 5, 7), 1)]
         other_penalty = swap(penalty, "proto", 1)
         first = at[2] == 0
         penalty = jnp.concatenate(
             [jnp.where(first, penalty, other_penalty), jnp.where(first, other_penalty, penalty)], axis=1
         )
+        ins = (at, pre_all.reshape(n_batch, rows, -1), columns, stats, gain, shift, w_second)
+        e_rows, hidden = -(-e_cols // 16) * 16, w_second.shape[0]
+        table = (2, n_batch, hidden)
+        pre_near, *flat = flat_sums(*ins[1:-1])
+        ins = (at, pre_near) + ins[2:]
+        far = swap(near, "batch", 1)
+        half = tail_call(
+            near_kernel, 0, [(d_cols, hidden), (e_rows, hidden), table], [], *ins, [near, swap(near, "proto", 1)], [], "tail_near"
+        )
+        far, penalty, *half = lax.optimization_barrier((far, penalty, *half, *flat))
+        grad_w1, grad_w2, grad_gain, grad_shift = tail_call(
+            functools.partial(far_kernel, crops_all, e_cols), 1,
+            [(d_cols, hidden), (e_cols, hidden), (1, hidden), (1, hidden)], [table, (e_rows, hidden)],
+            *ins, [far, swap(far, "proto", 1)], half, "tail_far",
+        )
     else:
         by_owner = jnp.swapaxes(features.astype(F32).reshape(rows, n_batch, d_cols), 0, 1)
         columns = columns_cast(lax.all_to_all(by_owner, "batch", 0, 0).reshape(crops_all, d_cols))
-        grads = [lax.all_gather(raw_grad, "batch", tiled=True)[None]]
-        places = [((None,), 0)]
-    grad_w1, grad_w2, grad_gain, grad_shift = tail(
-        pre_all, columns, stats, gain, shift, w_second, grads, places, at, e_cols
-    )
+        raw_all = lax.all_gather(raw_grad, "batch", tiled=True)
+        grad_w1, grad_w2, grad_gain, grad_shift = whole_tail(
+            pre_all, columns, stats, gain, shift, w_second, raw_all, at, e_cols
+        )
     return (penalty[0], grad_w1, grad_gain[0], grad_shift[0], grad_w2.T)
 
 

time: 127 us -> 120 us (0.945)
  starting transfers between devices: 45.1 us -> 29.5 us
  blocking collectives: 0 us -> 14.1 us
  waiting for transfers between devices: 42.7 us -> 34.1 us
  Pallas kernels: 21.7 us -> 23.6 us
    ppermute x37 -> x30, starting transfers between devices: 45 us -> 29.4 us  [swap(): return lax.ppermute(v, axis, [(i, i ^ mask) for i in range(n)])]
    all_to_all x0 -> x1, blocking collectives: none -> 14.1 us  [body(): lax.all_to_all(moments, 'batch', 0, 0)]
    ppermute x37 -> x30, waiting for transfers between devices: 42.6 us -> 34.1 us  [swap(): return lax.ppermute(v, axis, [(i, i ^ mask) for i in range(n)])]
    pallas_call x3 -> x6, Pallas kernels: 7.51 us -> 9.44 us  [the longest x2 6.6 us: tail_call(): pl.pallas_call(functools.partial(kernel, (odd, n_batch)), grid_spec=pltpu...]
    unnamed x18 -> x16, local copies, waits for them, and re-layouts: 2.22 us -> 3.35 us
  transfers between devices with their start and end apart: 38 -> 31, of which waited for: 23 -> 19; matrix products, arithmetic and copies ran while one was open for 1% -> 1% of each run, Pallas kernels for 9% -> 14%
where the time goes in v3:
time: 120 us
  waiting for transfers between devices  34.1 us (28%)
  starting transfers between devices  29.5 us (25%)
  Pallas kernels  23.6 us (20%)
  between operations  14.3 us (12%)
  blocking collectives  14.1 us (12%)
  local copies, waits for them, and re-layouts  3.35 us (3%)
    ppermute x30, waiting for transfers between devices, swap(): return lax.ppermute(v, axis, [(i, i ^ mask) for i in range(n)])  34.1 us
    ppermute x30, starting transfers between devices, swap(): return lax.ppermute(v, axis, [(i, i ^ mask) for i in range(n)])  29.4 us
    all_to_all x1, blocking collectives, body(): lax.all_to_all(moments, 'batch', 0, 0)  14.1 us
    pallas_call x2, Pallas kernels, tail_call(): pl.pallas_call(functools.partial(kernel, (odd, n_batch)), grid_spec=pltpu...  6.6 us
    unnamed x16, local copies, waits for them, and re-layouts  3.35 us
    pallas_call x1, Pallas kernels, first_layer(): pl.pallas_call(first_kernel, in_specs=[pl.BlockSpec(memory_space=pl.ANY)]...  3.11 us
    pallas_call x2, Pallas kernels, score(): pl.pallas_call(functools.partial(score_kernel, n), grid=(protos // blk,),...  2.97 us
  transfers between devices with their start and end apart: 31, of which 19 were waited for; matrix products, arithmetic and copies ran while one was open for 1% of the time, Pallas kernels for 14%

profile of v3, /device:TPU:0, one launch (start us, length us, event | category | flops | bytes accessed | tf_op | source)
XLA Modules:
  0.0 119.7 jit_solution(18139766500140367522)
XLA Ops:
  7.2 1.1 copy-done.3
  8.4 3.1 %first_layer.1 = (f32[128,1024]{1,0:T(8,128)}, f32[128,1024]{1,0:T(8,128)S(1)}, f32[8,1,2048]{2,1,0:T(1,128)S(1)}) custom-call(bf16[128,1536]{1,0:T(8,128)(2,1)S(1)} %copy-done.3, bf16[1536,1024]{1,0:T(8,128)(2,1)} %w_hbm.1), custom_call_target="tpu_custom_call" | custom-call | flops 402653184 | bytes 3670016 | tf_op jit(solution)/shard_map/first_layer/pallas_call | solution.py:121
  11.5 14.1 %all_to_all.5.refs_0_ = f32[8,1,2048]{2,1,0:T(1,128)S(1)} all-to-all(f32[8,1,2048]{2,1,0:T(1,128)S(1)} %get-tuple-element.68), channel_id=1, replica_groups=mesh['batch'=8,'proto'=4] {'batch'}, dimensions={0} | all-to-all | bytes 131072 | tf_op jit(solution)/shard_map/all_to_all | solution.py:718
  26.0 1.3 %collective-permute-done = f32[128,256]{1,0:T(8,128)S(1)} collective-permute-done((f32[128,256]{1,0:T(8,128)S(1)}, f32[128,256]{1,0:T(8,128)S(1)}, u32[]{:S(2)}, u32[]{:S(2)}) %collective-permute-start) | collective-permute-done | bytes 131104 | tf_op jit(solution)/shard_map/ppermute | solution.py:32
  27.3 1.6 %collective-permute-start.1 = (f32[128,256]{1,0:T(8,128)S(1)}, f32[128,256]{1,0:T(8,128)S(1)}, u32[]{:S(2)}, u32[]{:S(2)}) collective-permute-start(f32[128,256]{1,0:T(8,128)S(1)} %add.15.refs_0_.refs_1_), channel_id=1, source_target_pairs={{0,2},{1,3},{2,0},{3,1},{4,6},{5,7},{6,4},{7,5},{8,10},{9,11},{10,... | collective-permute-start | bytes 393224 | tf_op jit(solution)/shard_map/ppermute | solution.py:32
  28.9 0.9 unit_rows.1.refs_1_.u_ref.refs_5_
  29.9 1.0 columns_pick.1
  30.9 2.0 %collective-permute-done.1.refs_1_.refs_2_ = f32[128,256]{1,0:T(8,128)S(1)} collective-permute-done((f32[128,256]{1,0:T(8,128)S(1)}, f32[128,256]{1,0:T(8,128)S(1)}, u32[]{:S(2)}, u32[]{:S(2)}) %collective-permute-start.1) | collective-permute-done | bytes 131104 | tf_op jit(solution)/shard_map/ppermute | solution.py:32
  33.4 1.4 %score.2 = (f32[128,4096]{1,0:T(8,128)S(1)}, f32[32,128]{1,0:T(8,128)S(1)}) custom-call(f32[128,256]{1,0:T(8,128)S(1)} %embed_rows.1.refs_0_.emb_ref, bf16[4096,256]{1,0:T(8,128)(2,1)S(1)} %unit_rows.1.refs_1_.u_ref.refs_5_), custom_call_target="tpu_custom_call" | custom-call | flops 268435456 | bytes 2097152 | tf_op jit(solution)/shard_map/score/pallas_call | solution.py:247
  34.9 2.1 %logit_sum.1 = f32[136,256]{1,0:T(8,128)S(1)} custom-call(f32[128,256]{1,0:T(8,128)S(1)} %embed_rows.1.refs_0_.emb_ref, bf16[4096,256]{1,0:T(8,128)(2,1)S(1)} %unit_rows.1.refs_1_.u_ref.refs_5_), custom_call_target="tpu_custom_call" | custom-call | flops 536870912 | bytes 2097152 | tf_op jit(solution)/shard_map/logit_sum/pallas_call | solution.py:293
  37.0 1.1 collective-permute-done.2.refs_0_
  38.1 1.5 %score.3 = (f32[128,4096]{1,0:T(8,128)S(1)}, f32[32,128]{1,0:T(8,128)S(1)}, f32[80,128]{1,0:T(8,128)S(1)}, f32[80,128]{1,0:T(8,128)S(1)}, f32[80,128]{1,0:T(8,128)S(1)}) custom-call(f32[128,256]{1,0:T(8,128)S(1)} %collective-permute-done.2.refs_0_, bf16[4096,256]{1,0:T(8,128)(2,1)S(1)} %unit_rows.1.refs_1_.u_ref.refs_5_, ...), custom_call_target="tpu_custom_call" | custom-call | flops 268435456 | bytes 2097152 | tf_op jit(solution)/shard_map/score/pallas_call | solution.py:247
  39.7 0.7 collective-permute-start.4
  40.9 0.7 collective-permute-start.6
  41.6 3.2 %collective-permute-start.7 = (f32[80,128]{1,0:T(8,128)S(1)}, f32[80,128]{1,0:T(8,128)S(1)}, u32[]{:S(2)}, u32[]{:S(2)}) collective-permute-start(f32[80,128]{1,0:T(8,128)S(1)} %get-tuple-element.89), channel_id=1, source_target_pairs={{0,24},{4,28},{8,16},{12,20},{16,8},{20,12},{24,0},{28,4},{1,25},{... | collective-permute-start | bytes 122888 | tf_op jit(solution)/shard_map/ppermute | solution.py:32
  44.9 2.6 %collective-permute-done.6.refs_2_ = f32[80,128]{1,0:T(8,128)S(1)} collective-permute-done((f32[80,128]{1,0:T(8,128)S(1)}, f32[80,128]{1,0:T(8,128)S(1)}, u32[]{:S(2)}, u32[]{:S(2)}) %collective-permute-start.6) | collective-permute-done | bytes 40992 | tf_op jit(solution)/shard_map/ppermute | solution.py:32
  48.0 1.1 collective-permute-done.8
  49.1 1.5 %collective-permute-start.9 = (f32[2,128]{1,0:T(2,128)S(1)}, f32[2,128]{1,0:T(2,128)S(1)}, u32[]{:S(2)}, u32[]{:S(2)}) collective-permute-start(f32[2,128]{1,0:T(2,128)S(1)} %add.17.refs_0_), channel_id=1, source_target_pairs={{0,2},{1,3},{2,0},{3,1},{4,6},{5,7},{6,4},{7,5},{8,10},{9,11},{10,... | collective-permute-start | bytes 3080 | tf_op jit(solution)/shard_map/ppermute | solution.py:32
  50.6 2.1 %collective-permute-done.9.refs_1_ = f32[2,128]{1,0:T(2,128)S(1)} collective-permute-done((f32[2,128]{1,0:T(2,128)S(1)}, f32[2,128]{1,0:T(2,128)S(1)}, u32[]{:S(2)}, u32[]{:S(2)}) %collective-permute-start.9) | collective-permute-done | bytes 1056 | tf_op jit(solution)/shard_map/ppermute | solution.py:32
  53.3 1.6 %collective-permute-start.10 = (f32[136,256]{1,0:T(8,128)S(1)}, f32[136,256]{1,0:T(8,128)S(1)}, u32[]{:S(2)}, u32[]{:S(2)}) collective-permute-start(f32[136,256]{1,0:T(8,128)S(1)} %add.16.refs_3_), channel_id=1, source_target_pairs={{0,2},{1,3},{2,0},{3,1},{4,6},{5,7},{6,4},{7,5},{8,10},{9,11},{10,... | collective-permute-start | bytes 417800 | tf_op jit(solution)/shard_map/ppermute | solution.py:32
  54.8 1.0 collective-permute-start.11
  55.8 2.7 %collective-permute-start.12 = (f32[80,128]{1,0:T(8,128)S(1)}, f32[80,128]{1,0:T(8,128)S(1)}, u32[]{:S(2)}, u32[]{:S(2)}) collective-permute-start(f32[80,128]{1,0:T(8,128)S(1)} %get-tuple-element.100), channel_id=1, source_target_pairs={{0,16},{4,20},{8,24},{12,28},{16,0},{20,4},{24,8},{28,12},{1,17},{... | collective-permute-start | bytes 122888 | tf_op jit(solution)/shard_map/ppermute | solution.py:32
  58.5 0.7 collective-permute-start.13
  59.2 1.6 %collective-permute-done.11.refs_1_ = f32[80,128]{1,0:T(8,128)S(1)} collective-permute-done((f32[80,128]{1,0:T(8,128)S(1)}, f32[80,128]{1,0:T(8,128)S(1)}, u32[]{:S(2)}, u32[]{:S(2)}) %collective-permute-start.11) | collective-permute-done | bytes 40992 | tf_op jit(solution)/shard_map/ppermute | solution.py:32
  60.8 4.4 %collective-permute-done.12.refs_2_.refs_3_ = f32[80,128]{1,0:T(8,128)S(1)} collective-permute-done((f32[80,128]{1,0:T(8,128)S(1)}, f32[80,128]{1,0:T(8,128)S(1)}, u32[]{:S(2)}, u32[]{:S(2)}) %collective-permute-start.12) | collective-permute-done | bytes 40992 | tf_op jit(solution)/shard_map/ppermute | solution.py:32
  65.8 1.1 collective-permute-done.14
  67.4 3.1 %collective-permute-done.15.refs_1_ = f32[2,128]{1,0:T(2,128)S(1)} collective-permute-done((f32[2,128]{1,0:T(2,128)S(1)}, f32[2,128]{1,0:T(2,128)S(1)}, u32[]{:S(2)}, u32[]{:S(2)}) %collective-permute-start.15) | collective-permute-done | bytes 1056 | tf_op jit(solution)/shard_map/ppermute | solution.py:32
  71.6 3.1 %collective-permute-start.17 = (f32[32,128]{1,0:T(8,128)S(1)}, f32[32,128]{1,0:T(8,128)S(1)}, u32[]{:S(2)}, u32[]{:S(2)}) collective-permute-start(f32[32,128]{1,0:T(8,128)S(1)} %col_pass.3.refs_0_), channel_id=1, source_target_pairs={{0,8},{4,12},{8,0},{12,4},{16,24},{20,28},{24,16},{28,20},{1,9},{5... | collective-permute-start | bytes 49160 | tf_op jit(solution)/shard_map/ppermute | solution.py:32
  74.7 1.0 collective-permute-start.18
  75.6 1.5 %collective-permute-start.19 = (f32[32,128]{1,0:T(8,128)S(1)}, f32[32,128]{1,0:T(8,128)S(1)}, u32[]{:S(2)}, u32[]{:S(2)}) collective-permute-start(f32[32,128]{1,0:T(8,128)S(1)} %col_pass.3.refs_0_), channel_id=1, source_target_pairs={{0,24},{4,28},{8,16},{12,20},{16,8},{20,12},{24,0},{28,4},{1,25},{... | collective-permute-start | bytes 49160 | tf_op jit(solution)/shard_map/ppermute | solution.py:32
  77.4 3.6 %collective-permute-done.18.refs_2_ = f32[32,128]{1,0:T(8,128)S(1)} collective-permute-done((f32[32,128]{1,0:T(8,128)S(1)}, f32[32,128]{1,0:T(8,128)S(1)}, u32[]{:S(2)}, u32[]{:S(2)}) %collective-permute-start.18) | collective-permute-done | bytes 16416 | tf_op jit(solution)/shard_map/ppermute | solution.py:32
  81.5 1.5 %target_sum.1 = (f32[72,256]{1,0:T(8,128)S(1)}, f32[72,256]{1,0:T(8,128)S(1)}) custom-call(f32[32,128]{1,0:T(8,128)S(1)} %col_pass.3.refs_0_, f32[32,128]{1,0:T(8,128)S(1)} %collective-permute-done.17.refs_1_, f32[32,128]{1,0:T(8,128)S(1)} %collective-permute-done.18.refs_2_, f32[32,128]{1,0:T(8,128)S(1)} %collective-permute-done.19.refs_3_, ...), custom_call_target="tpu_custom_call" | custom-call | flops 268435456 | bytes 4194304 | tf_op jit(solution)/shard_map/target_sum/pallas_call | solution.py:384
  83.1 1.3 %collective-permute-done.20 = f32[72,256]{1,0:T(8,128)S(1)} collective-permute-done((f32[72,256]{1,0:T(8,128)S(1)}, f32[72,256]{1,0:T(8,128)S(1)}, u32[]{:S(2)}, u32[]{:S(2)}) %collective-permute-start.20) | collective-permute-done | bytes 73760 | tf_op jit(solution)/shard_map/ppermute | solution.py:32
  84.4 1.3 %collective-permute-start.21 = (f32[72,256]{1,0:T(8,128)S(1)}, f32[72,256]{1,0:T(8,128)S(1)}, u32[]{:S(2)}, u32[]{:S(2)}) collective-permute-start(f32[72,256]{1,0:T(8,128)S(1)} %add.19.refs_5_), channel_id=1, source_target_pairs={{0,2},{1,3},{2,0},{3,1},{4,6},{5,7},{6,4},{7,5},{8,10},{9,11},{10,... | collective-permute-start | bytes 221192 | tf_op jit(solution)/shard_map/ppermute | solution.py:32
  85.7 3.1 %collective-permute-done.21.refs_6_ = f32[72,256]{1,0:T(8,128)S(1)} collective-permute-done((f32[72,256]{1,0:T(8,128)S(1)}, f32[72,256]{1,0:T(8,128)S(1)}, u32[]{:S(2)}, u32[]{:S(2)}) %collective-permute-start.21) | collective-permute-done | bytes 73760 | tf_op jit(solution)/shard_map/ppermute | solution.py:32
  88.8 0.7 loss_grad.1
  89.6 0.7 collective-permute-start.22
  90.3 1.5 %collective-permute-start.23 = (f32[64,256]{1,0:T(8,128)S(1)}, f32[64,256]{1,0:T(8,128)S(1)}, u32[]{:S(2)}, u32[]{:S(2)}) collective-permute-start(f32[64,256]{1,0:T(8,128)S(1)} %get-tuple-element.106), channel_id=1, source_target_pairs={{0,16},{4,20},{8,24},{12,28},{16,0},{20,4},{24,8},{28,12},{1,17},{... | collective-permute-start | bytes 196616 | tf_op jit(solution)/shard_map/ppermute | solution.py:32
  91.8 2.2 %collective-permute-start.24 = (f32[64,256]{1,0:T(8,128)S(1)}, f32[64,256]{1,0:T(8,128)S(1)}, u32[]{:S(2)}, u32[]{:S(2)}) collective-permute-start(f32[64,256]{1,0:T(8,128)S(1)} %get-tuple-element.106), channel_id=1, source_target_pairs={{0,24},{4,28},{8,16},{12,20},{16,8},{20,12},{24,0},{28,4},{1,25},{... | collective-permute-start | bytes 196616 | tf_op jit(solution)/shard_map/ppermute | solution.py:32
  94.6 2.6 %collective-permute-done.23 = f32[64,256]{1,0:T(8,128)S(1)} collective-permute-done((f32[64,256]{1,0:T(8,128)S(1)}, f32[64,256]{1,0:T(8,128)S(1)}, u32[]{:S(2)}, u32[]{:S(2)}) %collective-permute-start.23) | collective-permute-done | bytes 65568 | tf_op jit(solution)/shard_map/ppermute | solution.py:32
  97.2 0.7 collective-permute-done.24
  98.0 1.5 %collective-permute-start.25 = (f32[4,64,256]{2,1,0:T(8,128)S(1)}, f32[4,64,256]{2,1,0:T(8,128)S(1)}, u32[]{:S(2)}, u32[]{:S(2)}) collective-permute-start(f32[4,64,256]{2,1,0:T(8,128)S(1)} %pad_maximum_fusion.1.refs_7_), channel_id=1, source_target_pairs={{0,4},{4,0},{8,12},{12,8},{16,20},{20,16},{24,28},{28,24},{1,5},{5... | collective-permute-start | bytes 786440 | tf_op jit(solution)/shard_map/ppermute | solution.py:32
  99.5 0.6 pad_maximum_fusion.2
  100.8 2.2 %copy-done.1 = f32[1024,1024]{1,0:T(8,128)S(1)} copy-done((f32[1024,1024]{1,0:T(8,128)S(1)}, f32[1024,1024]{1,0:T(8,128)}, u32[]{:S(2)}) %copy-start.1) | copy-done | bytes 4194328
  102.9 1.7 %flat_sums.1 = (f32[8,128,1024]{2,1,0:T(8,128)S(1)}, f32[192,1024]{1,0:T(8,128)S(1)}, f32[192,1]{1,0:T(8,128)S(1)}) custom-call(f32[8,128,1024]{2,1,0:T(8,128)S(1)} %bitcast.15, bf16[8,192,128]{2,1,0:T(8,128)(2,1)S(1)} %columns_all.1.cols_ref.refs_2_, f32[2,1024]{1,0:T(2,128)S(1)} %get-tuple-element.113.stats_ref.refs_3_, f32[1,1024]{1,0:T(1,128)S(1)} %bitcast.18, ...), custom_call_target="tpu_custom_call" | custom-call | flops 402653184 | bytes 4194304 | tf_op jit(solution)/shard_map/flat_sums/pallas_call | solution.py:631
  104.7 2.7 %tail_near.1 = (f32[192,1024]{1,0:T(8,128)S(1)}, f32[32,1024]{1,0:T(8,128)S(1)}, f32[2,8,1024]{2,1,0:T(8,128)S(1)}) custom-call(s32[3]{0:T(128)S(1)} %pad_add_fusion.at_ref.refs_7_.refs_0_, f32[8,128,1024]{2,1,0:T(8,128)S(1)} %get-tuple-element.114.refs_1_, bf16[8,192,128]{2,1,0:T(8,128)(2,1)S(1)} %columns_all.1.cols_ref.refs_2_, ...), custom_call_target="tpu_custom_call" | custom-call | flops 536870912 | bytes 2097152 | tf_op jit(solution)/shard_map/tail_near/pallas_call | solution.py:592
  107.7 1.4 %collective-permute-done.29.refs_8_ = f32[4,64,256]{2,1,0:T(8,128)S(1)} collective-permute-done((f32[4,64,256]{2,1,0:T(8,128)S(1)}, f32[4,64,256]{2,1,0:T(8,128)S(1)}, u32[]{:S(2)}, u32[]{:S(2)}) %collective-permute-start.29) | collective-permute-done | bytes 262176 | tf_op jit(solution)/shard_map/ppermute | solution.py:32
  109.0 3.9 %tail_far.1 = (f32[192,1024]{1,0:T(8,128)}, f32[32,1024]{1,0:T(8,128)}, f32[1,1024]{1,0:T(1,128)}, f32[1,1024]{1,0:T(1,128)}) custom-call(s32[3]{0:T(128)S(1)} %pad_add_fusion.at_ref.refs_7_.refs_0_, f32[8,128,1024]{2,1,0:T(8,128)S(1)} %get-tuple-element.114.refs_1_, bf16[8,192,128]{2,1,0:T(8,128)(2,1)S(1)} %columns_all.1.cols_ref.refs_2_, ...), custom_call_target="tpu_custom_call" | custom-call | flops 536870912 | bytes 2097152 | tf_op jit(solution)/shard_map/tail_far/pallas_call | solution.py:592
  (61 shorter events, 7.1 us)
Async XLA Ops:
  7.2 18.5 %copy-start = (bf16[1024,256]{1,0:T(8,128)(2,1)S(1)}, bf16[1024,256]{1,0:T(8,128)(2,1)}, u32[]{:S(2)}) copy-start(bf16[1024,256]{1,0:T(8,128)(2,1)} %refs_6_.3) | copy-start | bytes 1572868
  7.2 21.7 %copy-start.2 = (bf16[4096,256]{1,0:T(8,128)(2,1)S(1)}, bf16[4096,256]{1,0:T(8,128)(2,1)}, u32[]{:S(2)}) copy-start(bf16[4096,256]{1,0:T(8,128)(2,1)} %p_ref.1) | copy-start | bytes 6291460
  7.2 93.5 %all-gather.2.cloned.1.call-start = ((), (), s32[]{:S(2)}) async-start(), calls=%async_computation.1 | async-start | bytes 4718592 | tf_op jit(solution)/shard_map/all_gather | solution.py:717
  7.2 1.1 copy-start.3
  8.4 17.2 %copy-start.5 = (f32[1024]{0:T(1024)S(1)}, f32[1024]{0:T(1024)}, u32[]{:S(2)}) copy-start(f32[1024]{0:T(1024)} %param.9) | copy-start | bytes 12292
  8.4 17.2 %copy-start.6 = (f32[1024]{0:T(1024)S(1)}, f32[1024]{0:T(1024)}, u32[]{:S(2)}) copy-start(f32[1024]{0:T(1024)} %param.10) | copy-start | bytes 12292
  25.9 1.4 %collective-permute-start = (f32[128,256]{1,0:T(8,128)S(1)}, f32[128,256]{1,0:T(8,128)S(1)}, u32[]{:S(2)}, u32[]{:S(2)}) collective-permute-start(f32[128,256]{1,0:T(8,128)S(1)} %get-tuple-element.70), channel_id=1, source_target_pairs={{0,1},{1,0},{2,3},{3,2},{4,5},{5,4},{6,7},{7,6},{8,9},{9,8},{10,11... | collective-permute-start | bytes 393224 | tf_op jit(solution)/shard_map/ppermute | solution.py:32
  27.3 5.6 %collective-permute-start.1 = (f32[128,256]{1,0:T(8,128)S(1)}, f32[128,256]{1,0:T(8,128)S(1)}, u32[]{:S(2)}, u32[]{:S(2)}) collective-permute-start(f32[128,256]{1,0:T(8,128)S(1)} %add.15.refs_0_.refs_1_), channel_id=1, source_target_pairs={{0,2},{1,3},{2,0},{3,1},{4,6},{5,7},{6,4},{7,5},{8,10},{9,11},{10,... | collective-permute-start | bytes 393224 | tf_op jit(solution)/shard_map/ppermute | solution.py:32
  28.9 1.0 copy-start.4
  33.1 5.0 %collective-permute-start.2 = (f32[128,256]{1,0:T(8,128)S(1)}, f32[128,256]{1,0:T(8,128)S(1)}, u32[]{:S(2)}, u32[]{:S(2)}) collective-permute-start(f32[128,256]{1,0:T(8,128)S(1)} %embed_rows.1.refs_0_.emb_ref), channel_id=1, source_target_pairs={{0,4},{4,0},{8,12},{12,8},{16,20},{20,16},{24,28},{28,24},{1,5},{5... | collective-permute-start | bytes 393224 | tf_op jit(solution)/shard_map/ppermute | solution.py:32
  39.6 5.2 %collective-permute-start.3 = (f32[136,256]{1,0:T(8,128)S(1)}, f32[136,256]{1,0:T(8,128)S(1)}, u32[]{:S(2)}, u32[]{:S(2)}) collective-permute-start(f32[136,256]{1,0:T(8,128)S(1)} %logit_sum.1), channel_id=1, source_target_pairs={{0,1},{1,0},{2,3},{3,2},{4,5},{5,4},{6,7},{7,6},{8,9},{9,8},{10,11... | collective-permute-start | bytes 417800 | tf_op jit(solution)/shard_map/ppermute | solution.py:32
  39.7 5.2 %collective-permute-start.4 = (f32[4,48,128]{2,1,0:T(8,128)S(1)}, f32[4,48,128]{2,1,0:T(8,128)S(1)}, u32[]{:S(2)}, u32[]{:S(2)}) collective-permute-start(f32[4,48,128]{2,1,0:T(8,128)S(1)} %get-tuple-element.85), channel_id=1, source_target_pairs={{0,4},{4,0},{8,12},{12,8},{16,20},{20,16},{24,28},{28,24},{1,5},{5... | collective-permute-start | bytes 294920 | tf_op jit(solution)/shard_map/ppermute | solution.py:32
  40.5 4.5 %collective-permute-start.5 = (f32[80,128]{1,0:T(8,128)S(1)}, f32[80,128]{1,0:T(8,128)S(1)}, u32[]{:S(2)}, u32[]{:S(2)}) collective-permute-start(f32[80,128]{1,0:T(8,128)S(1)} %get-tuple-element.87), channel_id=1, source_target_pairs={{0,8},{4,12},{8,0},{12,4},{16,24},{20,28},{24,16},{28,20},{1,9},{5... | collective-permute-start | bytes 122888 | tf_op jit(solution)/shard_map/ppermute | solution.py:32
  40.9 6.6 %collective-permute-start.6 = (f32[80,128]{1,0:T(8,128)S(1)}, f32[80,128]{1,0:T(8,128)S(1)}, u32[]{:S(2)}, u32[]{:S(2)}) collective-permute-start(f32[80,128]{1,0:T(8,128)S(1)} %get-tuple-element.88), channel_id=1, source_target_pairs={{0,16},{4,20},{8,24},{12,28},{16,0},{20,4},{24,8},{28,12},{1,17},{... | collective-permute-start | bytes 122888 | tf_op jit(solution)/shard_map/ppermute | solution.py:32
  41.6 5.9 %collective-permute-start.7 = (f32[80,128]{1,0:T(8,128)S(1)}, f32[80,128]{1,0:T(8,128)S(1)}, u32[]{:S(2)}, u32[]{:S(2)}) collective-permute-start(f32[80,128]{1,0:T(8,128)S(1)} %get-tuple-element.89), channel_id=1, source_target_pairs={{0,24},{4,28},{8,16},{12,20},{16,8},{20,12},{24,0},{28,4},{1,25},{... | collective-permute-start | bytes 122888 | tf_op jit(solution)/shard_map/ppermute | solution.py:32
  47.9 1.2 %collective-permute-start.8 = (f32[2,128]{1,0:T(2,128)S(1)}, f32[2,128]{1,0:T(2,128)S(1)}, u32[]{:S(2)}, u32[]{:S(2)}) collective-permute-start(f32[2,128]{1,0:T(2,128)S(1)} %row_pass.2), channel_id=1, source_target_pairs={{0,1},{1,0},{2,3},{3,2},{4,5},{5,4},{6,7},{7,6},{8,9},{9,8},{10,11... | collective-permute-start | bytes 3080 | tf_op jit(solution)/shard_map/ppermute | solution.py:32
  49.1 3.6 %collective-permute-start.9 = (f32[2,128]{1,0:T(2,128)S(1)}, f32[2,128]{1,0:T(2,128)S(1)}, u32[]{:S(2)}, u32[]{:S(2)}) collective-permute-start(f32[2,128]{1,0:T(2,128)S(1)} %add.17.refs_0_), channel_id=1, source_target_pairs={{0,2},{1,3},{2,0},{3,1},{4,6},{5,7},{6,4},{7,5},{8,10},{9,11},{10,... | collective-permute-start | bytes 3080 | tf_op jit(solution)/shard_map/ppermute | solution.py:32
  53.3 5.9 %collective-permute-start.10 = (f32[136,256]{1,0:T(8,128)S(1)}, f32[136,256]{1,0:T(8,128)S(1)}, u32[]{:S(2)}, u32[]{:S(2)}) collective-permute-start(f32[136,256]{1,0:T(8,128)S(1)} %add.16.refs_3_), channel_id=1, source_target_pairs={{0,2},{1,3},{2,0},{3,1},{4,6},{5,7},{6,4},{7,5},{8,10},{9,11},{10,... | collective-permute-start | bytes 417800 | tf_op jit(solution)/shard_map/ppermute | solution.py:32
  54.8 6.0 %collective-permute-start.11 = (f32[80,128]{1,0:T(8,128)S(1)}, f32[80,128]{1,0:T(8,128)S(1)}, u32[]{:S(2)}, u32[]{:S(2)}) collective-permute-start(f32[80,128]{1,0:T(8,128)S(1)} %get-tuple-element.99), channel_id=1, source_target_pairs={{0,8},{4,12},{8,0},{12,4},{16,24},{20,28},{24,16},{28,20},{1,9},{5... | collective-permute-start | bytes 122888 | tf_op jit(solution)/shard_map/ppermute | solution.py:32
  55.8 9.5 %collective-permute-start.12 = (f32[80,128]{1,0:T(8,128)S(1)}, f32[80,128]{1,0:T(8,128)S(1)}, u32[]{:S(2)}, u32[]{:S(2)}) collective-permute-start(f32[80,128]{1,0:T(8,128)S(1)} %get-tuple-element.100), channel_id=1, source_target_pairs={{0,16},{4,20},{8,24},{12,28},{16,0},{20,4},{24,8},{28,12},{1,17},{... | collective-permute-start | bytes 122888 | tf_op jit(solution)/shard_map/ppermute | solution.py:32
  58.5 6.7 %collective-permute-start.13 = (f32[80,128]{1,0:T(8,128)S(1)}, f32[80,128]{1,0:T(8,128)S(1)}, u32[]{:S(2)}, u32[]{:S(2)}) collective-permute-start(f32[80,128]{1,0:T(8,128)S(1)} %get-tuple-element.101), channel_id=1, source_target_pairs={{0,24},{4,28},{8,16},{12,20},{16,8},{20,12},{24,0},{28,4},{1,25},{... | collective-permute-start | bytes 122888 | tf_op jit(solution)/shard_map/ppermute | solution.py:32
  65.7 1.2 %collective-permute-start.14 = (f32[2,128]{1,0:T(2,128)S(1)}, f32[2,128]{1,0:T(2,128)S(1)}, u32[]{:S(2)}, u32[]{:S(2)}) collective-permute-start(f32[2,128]{1,0:T(2,128)S(1)} %row_pass.3), channel_id=1, source_target_pairs={{0,1},{1,0},{2,3},{3,2},{4,5},{5,4},{6,7},{7,6},{8,9},{9,8},{10,11... | collective-permute-start | bytes 3080 | tf_op jit(solution)/shard_map/ppermute | solution.py:32
  66.9 14.6 %copy-start.7 = (s32[128]{0:T(128)S(1)}, s32[128]{0:T(128)}, u32[]{:S(2)}) copy-start(s32[128]{0:T(128)} %param.13) | copy-start | bytes 1540
  66.9 3.6 %collective-permute-start.15 = (f32[2,128]{1,0:T(2,128)S(1)}, f32[2,128]{1,0:T(2,128)S(1)}, u32[]{:S(2)}, u32[]{:S(2)}) collective-permute-start(f32[2,128]{1,0:T(2,128)S(1)} %add.18.refs_0_), channel_id=1, source_target_pairs={{0,2},{1,3},{2,0},{3,1},{4,6},{5,7},{6,4},{7,5},{8,10},{9,11},{10,... | collective-permute-start | bytes 3080 | tf_op jit(solution)/shard_map/ppermute | solution.py:32
  71.1 6.3 %collective-permute-start.16 = (f32[1,8,48,128]{3,2,1,0:T(8,128)S(1)}, f32[1,8,48,128]{3,2,1,0:T(8,128)S(1)}, u32[]{:S(2)}, u32[]{:S(2)}) collective-permute-start(f32[1,8,48,128]{3,2,1,0:T(8,128)S(1)} %columns_join.1), channel_id=1, source_target_pairs={{0,2},{1,3},{2,0},{3,1},{4,6},{5,7},{6,4},{7,5},{8,10},{9,11},{10,... | collective-permute-start | bytes 589832 | tf_op jit(solution)/shard_map/ppermute | solution.py:32
  71.6 5.8 %collective-permute-start.17 = (f32[32,128]{1,0:T(8,128)S(1)}, f32[32,128]{1,0:T(8,128)S(1)}, u32[]{:S(2)}, u32[]{:S(2)}) collective-permute-start(f32[32,128]{1,0:T(8,128)S(1)} %col_pass.3.refs_0_), channel_id=1, source_target_pairs={{0,8},{4,12},{8,0},{12,4},{16,24},{20,28},{24,16},{28,20},{1,9},{5... | collective-permute-start | bytes 49160 | tf_op jit(solution)/shard_map/ppermute | solution.py:32
  74.7 6.3 %collective-permute-start.18 = (f32[32,128]{1,0:T(8,128)S(1)}, f32[32,128]{1,0:T(8,128)S(1)}, u32[]{:S(2)}, u32[]{:S(2)}) collective-permute-start(f32[32,128]{1,0:T(8,128)S(1)} %col_pass.3.refs_0_), channel_id=1, source_target_pairs={{0,16},{4,20},{8,24},{12,28},{16,0},{20,4},{24,8},{28,12},{1,17},{... | collective-permute-start | bytes 49160 | tf_op jit(solution)/shard_map/ppermute | solution.py:32
  75.6 5.9 %collective-permute-start.19 = (f32[32,128]{1,0:T(8,128)S(1)}, f32[32,128]{1,0:T(8,128)S(1)}, u32[]{:S(2)}, u32[]{:S(2)}) collective-permute-start(f32[32,128]{1,0:T(8,128)S(1)} %col_pass.3.refs_0_), channel_id=1, source_target_pairs={{0,24},{4,28},{8,16},{12,20},{16,8},{20,12},{24,0},{28,4},{1,25},{... | collective-permute-start | bytes 49160 | tf_op jit(solution)/shard_map/ppermute | solution.py:32
  83.0 1.3 %collective-permute-start.20 = (f32[72,256]{1,0:T(8,128)S(1)}, f32[72,256]{1,0:T(8,128)S(1)}, u32[]{:S(2)}, u32[]{:S(2)}) collective-permute-start(f32[72,256]{1,0:T(8,128)S(1)} %get-tuple-element.105), channel_id=1, source_target_pairs={{0,1},{1,0},{2,3},{3,2},{4,5},{5,4},{6,7},{7,6},{8,9},{9,8},{10,11... | collective-permute-start | bytes 221192 | tf_op jit(solution)/shard_map/ppermute | solution.py:32
  84.4 4.4 %collective-permute-start.21 = (f32[72,256]{1,0:T(8,128)S(1)}, f32[72,256]{1,0:T(8,128)S(1)}, u32[]{:S(2)}, u32[]{:S(2)}) collective-permute-start(f32[72,256]{1,0:T(8,128)S(1)} %add.19.refs_5_), channel_id=1, source_target_pairs={{0,2},{1,3},{2,0},{3,1},{4,6},{5,7},{6,4},{7,5},{8,10},{9,11},{10,... | collective-permute-start | bytes 221192 | tf_op jit(solution)/shard_map/ppermute | solution.py:32
  89.6 5.1 %collective-permute-start.22 = (f32[64,256]{1,0:T(8,128)S(1)}, f32[64,256]{1,0:T(8,128)S(1)}, u32[]{:S(2)}, u32[]{:S(2)}) collective-permute-start(f32[64,256]{1,0:T(8,128)S(1)} %get-tuple-element.106), channel_id=1, source_target_pairs={{0,8},{4,12},{8,0},{12,4},{16,24},{20,28},{24,16},{28,20},{1,9},{5... | collective-permute-start | bytes 196616 | tf_op jit(solution)/shard_map/ppermute | solution.py:32
  90.3 7.0 %collective-permute-start.23 = (f32[64,256]{1,0:T(8,128)S(1)}, f32[64,256]{1,0:T(8,128)S(1)}, u32[]{:S(2)}, u32[]{:S(2)}) collective-permute-start(f32[64,256]{1,0:T(8,128)S(1)} %get-tuple-element.106), channel_id=1, source_target_pairs={{0,16},{4,20},{8,24},{12,28},{16,0},{20,4},{24,8},{28,12},{1,17},{... | collective-permute-start | bytes 196616 | tf_op jit(solution)/shard_map/ppermute | solution.py:32
  91.8 6.2 %collective-permute-start.24 = (f32[64,256]{1,0:T(8,128)S(1)}, f32[64,256]{1,0:T(8,128)S(1)}, u32[]{:S(2)}, u32[]{:S(2)}) collective-permute-start(f32[64,256]{1,0:T(8,128)S(1)} %get-tuple-element.106), channel_id=1, source_target_pairs={{0,24},{4,28},{8,16},{12,20},{16,8},{20,12},{24,0},{28,4},{1,25},{... | collective-permute-start | bytes 196616 | tf_op jit(solution)/shard_map/ppermute | solution.py:32
  94.0 6.1 %collective-permute-start.27 = (f32[2,8,48,128]{3,2,1,0:T(8,128)S(1)}, f32[2,8,48,128]{3,2,1,0:T(8,128)S(1)}, u32[]{:S(2)}, u32[]{:S(2)}) collective-permute-start(f32[2,8,48,128]{3,2,1,0:T(8,128)S(1)} %pad_maximum_fusion.refs_0_), channel_id=1, source_target_pairs={{0,1},{1,0},{2,3},{3,2},{4,5},{5,4},{6,7},{7,6},{8,9},{9,8},{10,11... | collective-permute-start | bytes 1179656 | tf_op jit(solution)/shard_map/ppermute | solution.py:32
  94.1 5.4 %collective-permute-start.26 = (f32[1,64]{1,0:T(1,128)S(1)}, f32[1,64]{1,0:T(1,128)S(1)}, u32[]{:S(2)}, u32[]{:S(2)}) collective-permute-start(f32[1,64]{1,0:T(1,128)S(1)} %get-tuple-element.107), channel_id=1, source_target_pairs={{0,1},{1,0},{2,3},{3,2},{4,5},{5,4},{6,7},{7,6},{8,9},{9,8},{10,11... | collective-permute-start | bytes 776 | tf_op jit(solution)/shard_map/ppermute | solution.py:32
  98.0 6.7 %collective-permute-start.28 = (f32[4,64,256]{2,1,0:T(8,128)S(1)}, f32[4,64,256]{2,1,0:T(8,128)S(1)}, u32[]{:S(2)}, u32[]{:S(2)}) collective-permute-start(f32[4,64,256]{2,1,0:T(8,128)S(1)} %pad_maximum_fusion.1.refs_7_), channel_id=1, source_target_pairs={{0,1},{1,0},{2,3},{3,2},{4,5},{5,4},{6,7},{7,6},{8,9},{9,8},{10,11... | collective-permute-start | bytes 786440 | tf_op jit(solution)/shard_map/ppermute | solution.py:32
  98.0 9.4 %collective-permute-start.25 = (f32[4,64,256]{2,1,0:T(8,128)S(1)}, f32[4,64,256]{2,1,0:T(8,128)S(1)}, u32[]{:S(2)}, u32[]{:S(2)}) collective-permute-start(f32[4,64,256]{2,1,0:T(8,128)S(1)} %pad_maximum_fusion.1.refs_7_), channel_id=1, source_target_pairs={{0,4},{4,0},{8,12},{12,8},{16,20},{20,16},{24,28},{28,24},{1,5},{5... | collective-permute-start | bytes 786440 | tf_op jit(solution)/shard_map/ppermute | solution.py:32
  100.7 2.2 %copy-start.1 = (f32[1024,1024]{1,0:T(8,128)S(1)}, f32[1024,1024]{1,0:T(8,128)}, u32[]{:S(2)}) copy-start(f32[1024,1024]{1,0:T(8,128)} %all-gather.2.cloned.1.call-done) | copy-start | bytes 12582916
  107.4 1.6 %collective-permute-start.29 = (f32[4,64,256]{2,1,0:T(8,128)S(1)}, f32[4,64,256]{2,1,0:T(8,128)S(1)}, u32[]{:S(2)}, u32[]{:S(2)}) collective-permute-start(f32[4,64,256]{2,1,0:T(8,128)S(1)} %collective-permute-done.25.refs_7_), channel_id=1, source_target_pairs={{0,1},{1,0},{2,3},{3,2},{4,5},{5,4},{6,7},{7,6},{8,9},{9,8},{10,11... | collective-permute-start | bytes 786440 | tf_op jit(solution)/shard_map/ppermute | solution.py:32
Sparse Core Ops, SparseCore 0:
  11.6 79.4 all-gather.1

commit v4 on v3

--- a/solution.py
+++ b/solution.py
@@ -54,6 +54,10 @@
 
 def proto_parts(v, stride=1):
     return exchange(v, "proto", 2, stride)
+
+
+def proto_small(v):
+    return exchange(v, "proto", 4 if lax.axis_size("proto") == 4 else 2)
 
 
 def whole(shape):
@@ -521,84 +525,76 @@
     )(columns)
 
 
-def tail_step(refs, w1_ref, w2_ref, sums_ref, grad_all):
-    at_ref, pre_ref, cols_ref, stats, gain, shift, w_ref, grads, masks = refs
-    k = pl.program_id(0)
-    block = at_ref[0] ^ (2 * k + masks[0])
-    size = pre_ref.shape[1] // 2
-    for flip, piece in enumerate(grads):
-        place = pl.multiple_of((at_ref[2] ^ flip) * size, size)
-        grad_all[pl.ds(place, size), :] = piece[k]
-    grad = grad_all[...].astype(BF16)
-    e_rows = w2_ref.shape[0]
-    shape = (e_rows, grad.shape[1])
-    mine = lax.broadcasted_iota(jnp.int32, shape, 0) + at_ref[0] * (grad.shape[1] // masks[1])
-    chosen = jnp.where(mine == lax.broadcasted_iota(jnp.int32, shape, 1), 1.0, 0.0).astype(BF16)
-    picked = dot(chosen, grad, ((1,), (1,))).astype(BF16)
-    normed, shifted = batch_norm(pre_ref[block], stats, gain, shift)
-    hidden_grad = dot(grad, w_ref[...], ((1,), (1,)))
-    bn_grad = jnp.where(shifted > 0, hidden_grad, 0.0)
-    sums_ref[0, pl.ds(block, 1), :] = jnp.sum(bn_grad, axis=0, keepdims=True)
-    sums_ref[1, pl.ds(block, 1), :] = jnp.sum(bn_grad * normed, axis=0, keepdims=True)
-    hidden = jnp.maximum(shifted, 0.0).astype(BF16)
-    w2_ref[...] += jnp.dot(picked, hidden, preferred_element_type=F32)
-    w1_ref[...] += jnp.dot(cols_ref[block], bn_grad.astype(BF16), preferred_element_type=F32)
-
-
-def near_kernel(masks, *refs):
-    at_ref, pre_ref, cols_ref, stats_ref, gain_ref, shift_ref, w_ref = refs[:7]
-    grads, (w1_ref, w2_ref, sums_ref, grad_all) = refs[7:9], refs[9:]
-
-    @pl.when(pl.program_id(0) == 0)
-    def _():
-        w1_ref[...] = jnp.zeros_like(w1_ref)
-        w2_ref[...] = jnp.zeros_like(w2_ref)
-        sums_ref[...] = jnp.zeros_like(sums_ref)
-
-    ins = (at_ref, pre_ref, cols_ref, stats_ref[...], gain_ref[...], shift_ref[...], w_ref, grads, masks)
-    tail_step(ins, w1_ref, w2_ref, sums_ref, grad_all)
-
-
-def far_kernel(crops_all, e_cols, masks, *refs):
-    at_ref, pre_ref, cols_ref, stats_ref, gain_ref, shift_ref, w_ref = refs[:7]
-    grads, (near_w1, near_w2, near_sums, flat_ref, total_ref) = refs[7:9], refs[9:14]
-    w1_ref, w2_ref, gain_grad_ref, shift_grad_ref, grad_all, sums, w2_all = refs[14:]
-
-    @pl.when(pl.program_id(0) == 0)
-    def _():
-        w1_ref[...] = near_w1[...]
-        w2_all[...] = near_w2[...]
-        sums[...] = near_sums[...]
-
-    stats, gain = stats_ref[...], gain_ref[...]
-    ins = (at_ref, pre_ref, cols_ref, stats, gain, shift_ref[...], w_ref, grads, masks)
-    tail_step(ins, w1_ref, w2_all, sums, grad_all)
-
-    @pl.when(pl.program_id(0) == pl.num_programs(0) - 1)
-    def _():
-        w2_ref[...] = w2_all[0:e_cols, :]
-        shift_grad = jnp.sum(sums[0], axis=0, keepdims=True)
-        gain_grad = jnp.sum(sums[1], axis=0, keepdims=True)
-        shift_grad_ref[...] = shift_grad
-        gain_grad_ref[...] = gain_grad
-        flat = total_ref[...] * (shift_grad / crops_all) + flat_ref[...] * (gain_grad / crops_all)
-        w1_ref[...] = gain * stats[1:2, :] * (w1_ref[...] - flat)
-
-
-def tail_call(kernel, odd, outs, scratch, at, pre_all, columns, stats, gain, shift, w_second, grads, more, name):
+def tail_half(refs, grads, odd, n_batch, sums_ref, grad_all, low_all, cols_all):
+    at_ref, pre_ref, cols_ref, stats, gain, shift, w_ref = refs
+    unit, width = pre_ref.shape[1], grad_all.shape[1]
+    size, n = unit // 2, n_batch // 2
+    e_rows = 16 * (-(-(width // n_batch) // 16))
+    for k in range(n):
+        for flip in range(2):
+            place = pl.multiple_of(k * unit + (at_ref[2] ^ flip) * size, size)
+            grad_all[pl.ds(place, size), :] = grads[flip][k].astype(BF16)
+    mine = lax.broadcasted_iota(jnp.int32, (e_rows, width), 0) + at_ref[0] * (width // n_batch)
+    chosen = jnp.where(mine == lax.broadcasted_iota(jnp.int32, (e_rows, width), 1), 1.0, 0.0).astype(BF16)
+    w2 = 0.0
+    for k in range(n):
+        rows = slice(k * unit, (k + 1) * unit)
+        block = at_ref[0] ^ (2 * k + odd)
+        normed, shifted = batch_norm(pre_ref[block], stats, gain, shift)
+        grad = grad_all[rows, :]
+        picked = dot(chosen, grad, ((1,), (1,))).astype(BF16)
+        hidden = jnp.maximum(shifted, 0.0).astype(BF16)
+        w2 = w2 + jnp.dot(picked, hidden, preferred_element_type=F32)
+        hidden_grad = dot(grad, w_ref[...], ((1,), (1,)))
+        bn_grad = jnp.where(shifted > 0, hidden_grad, 0.0)
+        sums_ref[0, pl.ds(block, 1), :] = jnp.sum(bn_grad, axis=0, keepdims=True)
+        sums_ref[1, pl.ds(block, 1), :] = jnp.sum(bn_grad * normed, axis=0, keepdims=True)
+        low_all[rows, :] = bn_grad.astype(BF16)
+        cols_all[:, rows] = cols_ref[block]
+    return jnp.dot(cols_all[...], low_all[...], preferred_element_type=F32), w2
+
+
+def near_kernel(n_batch, n_grads, *refs):
+    ins, refs = refs[:7], refs[7:]
+    grads, (w1_ref, w2_ref, sums_ref, *scratch) = refs[:2], refs[2:]
+    sums_ref[...] = jnp.zeros_like(sums_ref)
+    ins = ins[:3] + tuple(r[...] for r in ins[3:6]) + ins[6:]
+    w1_ref[...], w2_ref[...] = tail_half(ins, grads, 0, n_batch, sums_ref, *scratch)
+
+
+def far_kernel(crops_all, n_batch, n_grads, *refs):
+    ins, refs = refs[:7], refs[7:]
+    grads, refs = (refs[: n_grads // 2], refs[n_grads // 2 : n_grads]), refs[n_grads:]
+    near_w1, near_w2, near_sums, flat_ref, total_ref = refs[:5]
+    w1_ref, w2_ref, gain_grad_ref, shift_grad_ref, sums, *scratch = refs[5:]
+    ins = ins[:3] + tuple(r[...] for r in ins[3:6]) + ins[6:]
+    stats, gain = ins[3:5]
+    sums[...] = near_sums[...]
+    w1, w2 = tail_half(ins, [half[0] for half in grads], 1, n_batch, sums, *scratch)
+    w2_ref[...] = (near_w2[...] + w2)[0 : w2_ref.shape[0], :]
+    shift_grad = jnp.sum(sums[0], axis=0, keepdims=True)
+    gain_grad = jnp.sum(sums[1], axis=0, keepdims=True)
+    shift_grad_ref[...] = shift_grad
+    gain_grad_ref[...] = gain_grad
+    flat = total_ref[...] * (shift_grad / crops_all) + flat_ref[...] * (gain_grad / crops_all)
+    w1_ref[...] = gain * stats[1:2, :] * (near_w1[...] + w1 - flat)
+
+
+def tail_call(kernel, outs, scratch, at, pre_all, columns, stats, gain, shift, w_second, grads, more, name):
     n_batch, unit, hidden = pre_all.shape
-    width = w_second.shape[1]
+    width, d_cols = w_second.shape[1], columns.shape[1]
     crops = n_batch * unit // 2
-    return pl.pallas_call(
-        functools.partial(kernel, (odd, n_batch)),
-        grid_spec=pltpu.PrefetchScalarGridSpec(
-            num_scalar_prefetch=1,
-            grid=(n_batch // 2,),
-            in_specs=[pl.BlockSpec(memory_space=pltpu.VMEM)] * (6 + len(grads) + len(more)),
-            out_specs=[whole(n) for n in outs],
-            scratch_shapes=[pltpu.VMEM((unit, width), F32)] + [pltpu.VMEM(n, F32) for n in scratch],
-        ),
+    vmem = pl.BlockSpec(memory_space=pltpu.VMEM)
+    return pl.pallas_call(
+        functools.partial(kernel, n_batch, len(grads)),
+        in_specs=[pl.BlockSpec(memory_space=pltpu.SMEM)] + [vmem] * (6 + len(grads) + len(more)),
         out_shape=[jax.ShapeDtypeStruct(n, F32) for n in outs],
+        scratch_shapes=[pltpu.VMEM(n, F32) for n in scratch]
+        + [
+            pltpu.VMEM((crops, width), BF16),
+            pltpu.VMEM((crops, hidden), BF16),
+            pltpu.VMEM((d_cols, crops), BF16),
+        ],
         compiler_params=params(20),
         cost_estimate=cost(2 * crops * hidden * (width + 256), 4 * crops * hidden),
         name=name,
@@ -729,7 +725,9 @@
         own_codes, own_col = score(embedded, units)
         logit = logit_sum(embedded, units)
         partner_emb, own_col, logit = lax.optimization_barrier((partner_emb, own_col, logit))
+        logit = logit + swap(logit, "proto", 1)
         more_codes, *cols = score(partner_emb, units, (own_col, keep))
+        cols[0], logit = lax.optimization_barrier((cols[0], logit))
         codes = [own_codes, more_codes]
     else:
         codes, *cols = score(embedded, units)
@@ -743,33 +741,35 @@
         else:
             col_parts = batch_parts(cols[0], 2 if short else 1)
         if iteration == 0:
-            logit = logit + swap(after(logit, cols[0]), "proto", 1)
-            col_parts[0], logit = lax.optimization_barrier((col_parts[0], logit))
-            if short:
-                got = swap(after(send, cols[0]), "batch", 1)
-                col_parts[0], got = lax.optimization_barrier((col_parts[0], got))
-        if iteration == 1:
-            logit_parts = proto_parts(after(logit, cols[0]), 2)
+            logit_parts = proto_parts(logit, 2 if short else 1)
             col_parts[0], *logit_parts = lax.optimization_barrier((col_parts[0], *logit_parts))
+        if short and iteration == 0:
+            got = swap(after(send, cols[0]), "batch", 1)
+            col_parts[0], got = lax.optimization_barrier((col_parts[0], got))
         if short and iteration == 2:
             columns = columns_join(after(keep, cols[0]), got, *moved)
             columns = [columns, swap(columns, "proto", 2)]
             col_parts[0], *columns = lax.optimization_barrier((col_parts[0], *columns))
         if iteration < ITERS - 1:
-            row_parts = proto_parts(row_pass(col_parts, codes))
+            row_parts = proto_small(row_pass(col_parts, codes))
             cols = col_pass(row_parts, codes, got if short and iteration == 0 else None)
     if short:
-        mine, send = target_sum(col_parts, codes[0], units, partner[None, :], at, 2)
-        target_parts = proto_parts(mine + swap(send, "proto", 1), 2)
+        own_half, send = target_sum(col_parts, codes[0], units, partner[None, :], at, 2)
+        columns = after(jnp.concatenate(columns), own_half)
+        own_half = own_half + swap(send, "proto", 1)
+        columns = [columns, swap(columns, "proto", 1)]
+        target_parts = proto_parts(own_half, 2)
+        target_parts[0], *columns = lax.optimization_barrier((target_parts[0], *columns))
     else:
         target_parts = proto_parts(target_sum(col_parts, codes[0], units, partner[None, :], at, 1)[0])
     raw_grad, penalty = loss_grad(raw_parts, logit_parts, target_parts, at)
 
     if short:
-        columns = after(jnp.concatenate(columns), raw_grad)
-        columns = columns_all(columns, swap(columns, "proto", 1), at)
+        columns = columns_all(*(after(c, raw_grad) for c in columns), at)
         pre_all = after(pre_all, raw_grad)
-        near = jnp.stack([raw_grad] + [swap(raw_grad, "batch", k) for k in (2, 4, 6)])
+        near = [raw_grad] + [swap(raw_grad, "batch", k) for k in (2, 4, 6)]
+        near = jnp.stack(near)
+        far = swap(near, "batch", 1)
         other_penalty = swap(penalty, "proto", 1)
         first = at[2] == 0
         penalty = jnp.concatenate(
@@ -780,14 +780,13 @@
         table = (2, n_batch, hidden)
         pre_near, *flat = flat_sums(*ins[1:-1])
         ins = (at, pre_near) + ins[2:]
-        far = swap(near, "batch", 1)
         half = tail_call(
-            near_kernel, 0, [(d_cols, hidden), (e_rows, hidden), table], [], *ins, [near, swap(near, "proto", 1)], [], "tail_near"
+            near_kernel, [(d_cols, hidden), (e_rows, hidden), table], [], *ins, [near, swap(near, "proto", 1)], [], "tail_near"
         )
         far, penalty, *half = lax.optimization_barrier((far, penalty, *half, *flat))
         grad_w1, grad_w2, grad_gain, grad_shift = tail_call(
-            functools.partial(far_kernel, crops_all, e_cols), 1,
-            [(d_cols, hidden), (e_cols, hidden), (1, hidden), (1, hidden)], [table, (e_rows, hidden)],
+            functools.partial(far_kernel, crops_all),
+            [(d_cols, hidden), (e_cols, hidden), (1, hidden), (1, hidden)], [table],
             *ins, [far, swap(far, "proto", 1)], half, "tail_far",
         )
     else:

time: 120 us -> 119 us (level)
  waiting for transfers between devices: 34.1 us -> 32 us
  starting transfers between devices: 29.5 us -> 31.3 us
    ppermute x30 -> x32, waiting for transfers between devices: 34.1 us -> 32 us  [swap(): return lax.ppermute(v, axis, [(i, i ^ mask) for i in range(n)])]
    ppermute x30 -> x32, starting transfers between devices: 29.4 us -> 31.2 us  [swap(): return lax.ppermute(v, axis, [(i, i ^ mask) for i in range(n)])]
  transfers between devices with their start and end apart: 31 -> 33, of which waited for: 19 -> 18; matrix products, arithmetic and copies ran while one was open for 1% -> 1% of each run, Pallas kernels for 14% -> 14%
where the time goes in v4:
time: 119 us
  waiting for transfers between devices  32 us (27%)
  starting transfers between devices  31.3 us (26%)
  Pallas kernels  22.9 us (19%)
  between operations  14.3 us (12%)
  blocking collectives  14.1 us (12%)
  local copies, waits for them, and re-layouts  3.35 us (3%)
    ppermute x32, waiting for transfers between devices, swap(): return lax.ppermute(v, axis, [(i, i ^ mask) for i in range(n)])  32 us
    ppermute x32, starting transfers between devices, swap(): return lax.ppermute(v, axis, [(i, i ^ mask) for i in range(n)])  31.2 us
    all_to_all x1, blocking collectives, body(): lax.all_to_all(moments, 'batch', 0, 0)  14.1 us
    pallas_call x2, Pallas kernels, tail_call(): pl.pallas_call(functools.partial(kernel, n_batch, len(grads)), in_specs=[...  5.84 us
    unnamed x16, local copies, waits for them, and re-layouts  3.35 us
    pallas_call x1, Pallas kernels, first_layer(): pl.pallas_call(first_kernel, in_specs=[pl.BlockSpec(memory_space=pl.ANY)]...  3.11 us
    pallas_call x2, Pallas kernels, score(): pl.pallas_call(functools.partial(score_kernel, n), grid=(protos // blk,),...  2.97 us
  transfers between devices with their start and end apart: 33, of which 18 were waited for; matrix products, arithmetic and copies ran while one was open for 1% of the time, Pallas kernels for 14%

profile of v4, /device:TPU:0, one launch (start us, length us, event | category | flops | bytes accessed | tf_op | source)
XLA Modules:
  0.0 118.6 jit_solution(10341426970604661620)
XLA Ops:
  7.2 1.1 copy-done.3
  8.4 3.1 %first_layer.1 = (f32[128,1024]{1,0:T(8,128)}, f32[128,1024]{1,0:T(8,128)S(1)}, f32[8,1,2048]{2,1,0:T(1,128)S(1)}) custom-call(bf16[128,1536]{1,0:T(8,128)(2,1)S(1)} %copy-done.3, bf16[1536,1024]{1,0:T(8,128)(2,1)} %w_hbm.1), custom_call_target="tpu_custom_call" | custom-call | flops 402653184 | bytes 3670016 | tf_op jit(solution)/shard_map/first_layer/pallas_call | solution.py:125
  11.5 14.1 %all_to_all.5.refs_0_ = f32[8,1,2048]{2,1,0:T(1,128)S(1)} all-to-all(f32[8,1,2048]{2,1,0:T(1,128)S(1)} %get-tuple-element.71), channel_id=1, replica_groups=mesh['batch'=8,'proto'=4] {'batch'}, dimensions={0} | all-to-all | bytes 131072 | tf_op jit(solution)/shard_map/all_to_all | solution.py:714
  26.0 1.3 %collective-permute-done = f32[128,256]{1,0:T(8,128)S(1)} collective-permute-done((f32[128,256]{1,0:T(8,128)S(1)}, f32[128,256]{1,0:T(8,128)S(1)}, u32[]{:S(2)}, u32[]{:S(2)}) %collective-permute-start) | collective-permute-done | bytes 131104 | tf_op jit(solution)/shard_map/ppermute | solution.py:32
  27.3 1.6 %collective-permute-start.1 = (f32[128,256]{1,0:T(8,128)S(1)}, f32[128,256]{1,0:T(8,128)S(1)}, u32[]{:S(2)}, u32[]{:S(2)}) collective-permute-start(f32[128,256]{1,0:T(8,128)S(1)} %add.9.refs_0_.refs_1_), channel_id=1, source_target_pairs={{0,2},{1,3},{2,0},{3,1},{4,6},{5,7},{6,4},{7,5},{8,10},{9,11},{10,... | collective-permute-start | bytes 393224 | tf_op jit(solution)/shard_map/ppermute | solution.py:32
  28.9 0.9 unit_rows.1.refs_1_.u_ref.refs_5_
  29.9 1.0 columns_pick.1
  30.9 2.0 %collective-permute-done.1.refs_1_.refs_2_ = f32[128,256]{1,0:T(8,128)S(1)} collective-permute-done((f32[128,256]{1,0:T(8,128)S(1)}, f32[128,256]{1,0:T(8,128)S(1)}, u32[]{:S(2)}, u32[]{:S(2)}) %collective-permute-start.1) | collective-permute-done | bytes 131104 | tf_op jit(solution)/shard_map/ppermute | solution.py:32
  33.4 1.4 %score.2 = (f32[128,4096]{1,0:T(8,128)S(1)}, f32[32,128]{1,0:T(8,128)S(1)}) custom-call(f32[128,256]{1,0:T(8,128)S(1)} %embed_rows.1.refs_0_.emb_ref, bf16[4096,256]{1,0:T(8,128)(2,1)S(1)} %unit_rows.1.refs_1_.u_ref.refs_5_), custom_call_target="tpu_custom_call" | custom-call | flops 268435456 | bytes 2097152 | tf_op jit(solution)/shard_map/score/pallas_call | solution.py:251
  34.9 2.1 %logit_sum.1 = f32[136,256]{1,0:T(8,128)S(1)} custom-call(f32[128,256]{1,0:T(8,128)S(1)} %embed_rows.1.refs_0_.emb_ref, bf16[4096,256]{1,0:T(8,128)(2,1)S(1)} %unit_rows.1.refs_1_.u_ref.refs_5_), custom_call_target="tpu_custom_call" | custom-call | flops 536870912 | bytes 2097152 | tf_op jit(solution)/shard_map/logit_sum/pallas_call | solution.py:297
  37.0 1.1 collective-permute-done.2.refs_0_
  38.1 1.5 %score.3 = (f32[128,4096]{1,0:T(8,128)S(1)}, f32[32,128]{1,0:T(8,128)S(1)}, f32[80,128]{1,0:T(8,128)S(1)}, f32[80,128]{1,0:T(8,128)S(1)}, f32[80,128]{1,0:T(8,128)S(1)}) custom-call(f32[128,256]{1,0:T(8,128)S(1)} %collective-permute-done.2.refs_0_, bf16[4096,256]{1,0:T(8,128)(2,1)S(1)} %unit_rows.1.refs_1_.u_ref.refs_5_, ...), custom_call_target="tpu_custom_call" | custom-call | flops 268435456 | bytes 2097152 | tf_op jit(solution)/shard_map/score/pallas_call | solution.py:251
  39.7 1.5 %collective-permute-start.4 = (f32[136,256]{1,0:T(8,128)S(1)}, f32[136,256]{1,0:T(8,128)S(1)}, u32[]{:S(2)}, u32[]{:S(2)}) collective-permute-start(f32[136,256]{1,0:T(8,128)S(1)} %add.10.refs_3_), channel_id=1, source_target_pairs={{0,2},{1,3},{2,0},{3,1},{4,6},{5,7},{6,4},{7,5},{8,10},{9,11},{10,... | collective-permute-start | bytes 417800 | tf_op jit(solution)/shard_map/ppermute | solution.py:32
  41.2 0.7 collective-permute-start.5
  42.3 0.7 collective-permute-start.7
  43.1 3.3 %collective-permute-start.8 = (f32[80,128]{1,0:T(8,128)S(1)}, f32[80,128]{1,0:T(8,128)S(1)}, u32[]{:S(2)}, u32[]{:S(2)}) collective-permute-start(f32[80,128]{1,0:T(8,128)S(1)} %get-tuple-element.95), channel_id=1, source_target_pairs={{0,24},{4,28},{8,16},{12,20},{16,8},{20,12},{24,0},{28,4},{1,25},{... | collective-permute-start | bytes 122888 | tf_op jit(solution)/shard_map/ppermute | solution.py:32
  46.4 1.5 %collective-permute-done.7.refs_2_ = f32[80,128]{1,0:T(8,128)S(1)} collective-permute-done((f32[80,128]{1,0:T(8,128)S(1)}, f32[80,128]{1,0:T(8,128)S(1)}, u32[]{:S(2)}, u32[]{:S(2)}) %collective-permute-start.7) | collective-permute-done | bytes 40992 | tf_op jit(solution)/shard_map/ppermute | solution.py:32
  47.9 1.0 collective-permute-done.8.refs_3_.refs_4_
  50.0 1.6 %collective-permute-start.9 = (f32[2,128]{1,0:T(2,128)S(1)}, f32[2,128]{1,0:T(2,128)S(1)}, u32[]{:S(2)}, u32[]{:S(2)}) collective-permute-start(f32[2,128]{1,0:T(2,128)S(1)} %row_pass.2.refs_0_), channel_id=1, source_target_pairs={{0,1},{1,0},{2,3},{3,2},{4,5},{5,4},{6,7},{7,6},{8,9},{9,8},{10,11... | collective-permute-start | bytes 3080 | tf_op jit(solution)/shard_map/ppermute | solution.py:32
  51.6 1.4 %collective-permute-done.10.refs_2_ = f32[2,128]{1,0:T(2,128)S(1)} collective-permute-done((f32[2,128]{1,0:T(2,128)S(1)}, f32[2,128]{1,0:T(2,128)S(1)}, u32[]{:S(2)}, u32[]{:S(2)}) %collective-permute-start.10) | collective-permute-done | bytes 1056 | tf_op jit(solution)/shard_map/ppermute | solution.py:32
  53.6 0.9 collective-permute-start.12
  54.5 3.0 %collective-permute-start.13 = (f32[80,128]{1,0:T(8,128)S(1)}, f32[80,128]{1,0:T(8,128)S(1)}, u32[]{:S(2)}, u32[]{:S(2)}) collective-permute-start(f32[80,128]{1,0:T(8,128)S(1)} %get-tuple-element.101), channel_id=1, source_target_pairs={{0,16},{4,20},{8,24},{12,28},{16,0},{20,4},{24,8},{28,12},{1,17},{... | collective-permute-start | bytes 122888 | tf_op jit(solution)/shard_map/ppermute | solution.py:32
  58.0 2.7 %collective-permute-done.12.refs_1_ = f32[80,128]{1,0:T(8,128)S(1)} collective-permute-done((f32[80,128]{1,0:T(8,128)S(1)}, f32[80,128]{1,0:T(8,128)S(1)}, u32[]{:S(2)}, u32[]{:S(2)}) %collective-permute-start.12) | collective-permute-done | bytes 40992 | tf_op jit(solution)/shard_map/ppermute | solution.py:32
  60.7 2.8 %collective-permute-done.13.refs_2_.refs_3_ = f32[80,128]{1,0:T(8,128)S(1)} collective-permute-done((f32[80,128]{1,0:T(8,128)S(1)}, f32[80,128]{1,0:T(8,128)S(1)}, u32[]{:S(2)}, u32[]{:S(2)}) %collective-permute-start.13) | collective-permute-done | bytes 40992 | tf_op jit(solution)/shard_map/ppermute | solution.py:32
  64.6 1.5 %collective-permute-start.16 = (f32[2,128]{1,0:T(2,128)S(1)}, f32[2,128]{1,0:T(2,128)S(1)}, u32[]{:S(2)}, u32[]{:S(2)}) collective-permute-start(f32[2,128]{1,0:T(2,128)S(1)} %row_pass.3.refs_0_), channel_id=1, source_target_pairs={{0,2},{1,3},{2,0},{3,1},{4,6},{5,7},{6,4},{7,5},{8,10},{9,11},{10,... | collective-permute-start | bytes 3080 | tf_op jit(solution)/shard_map/ppermute | solution.py:32
  66.5 1.8 %collective-permute-done.16.refs_2_ = f32[2,128]{1,0:T(2,128)S(1)} collective-permute-done((f32[2,128]{1,0:T(2,128)S(1)}, f32[2,128]{1,0:T(2,128)S(1)}, u32[]{:S(2)}, u32[]{:S(2)}) %collective-permute-start.16) | collective-permute-done | bytes 1056 | tf_op jit(solution)/shard_map/ppermute | solution.py:32
  68.3 0.9 collective-permute-done.17.refs_3_
  69.7 0.7 collective-permute-start.18
  70.4 3.3 %collective-permute-start.19 = (f32[32,128]{1,0:T(8,128)S(1)}, f32[32,128]{1,0:T(8,128)S(1)}, u32[]{:S(2)}, u32[]{:S(2)}) collective-permute-start(f32[32,128]{1,0:T(8,128)S(1)} %col_pass.3.refs_0_), channel_id=1, source_target_pairs={{0,8},{4,12},{8,0},{12,4},{16,24},{20,28},{24,16},{28,20},{1,9},{5... | collective-permute-start | bytes 49160 | tf_op jit(solution)/shard_map/ppermute | solution.py:32
  73.7 0.9 collective-permute-start.20
  74.6 1.5 %collective-permute-start.21 = (f32[32,128]{1,0:T(8,128)S(1)}, f32[32,128]{1,0:T(8,128)S(1)}, u32[]{:S(2)}, u32[]{:S(2)}) collective-permute-start(f32[32,128]{1,0:T(8,128)S(1)} %col_pass.3.refs_0_), channel_id=1, source_target_pairs={{0,24},{4,28},{8,16},{12,20},{16,8},{20,12},{24,0},{28,4},{1,25},{... | collective-permute-start | bytes 49160 | tf_op jit(solution)/shard_map/ppermute | solution.py:32
  76.0 1.1 collective-permute-done.18
  77.1 3.5 %collective-permute-done.20.refs_2_ = f32[32,128]{1,0:T(8,128)S(1)} collective-permute-done((f32[32,128]{1,0:T(8,128)S(1)}, f32[32,128]{1,0:T(8,128)S(1)}, u32[]{:S(2)}, u32[]{:S(2)}) %collective-permute-start.20) | collective-permute-done | bytes 16416 | tf_op jit(solution)/shard_map/ppermute | solution.py:32
  80.7 1.5 %target_sum.1 = (f32[72,256]{1,0:T(8,128)S(1)}, f32[72,256]{1,0:T(8,128)S(1)}) custom-call(f32[32,128]{1,0:T(8,128)S(1)} %col_pass.3.refs_0_, f32[32,128]{1,0:T(8,128)S(1)} %collective-permute-done.19.refs_1_, f32[32,128]{1,0:T(8,128)S(1)} %collective-permute-done.20.refs_2_, f32[32,128]{1,0:T(8,128)S(1)} %collective-permute-done.21.refs_3_, ...), custom_call_target="tpu_custom_call" | custom-call | flops 268435456 | bytes 4194304 | tf_op jit(solution)/shard_map/target_sum/pallas_call | solution.py:388
  82.8 1.3 %collective-permute-done.22 = f32[72,256]{1,0:T(8,128)S(1)} collective-permute-done((f32[72,256]{1,0:T(8,128)S(1)}, f32[72,256]{1,0:T(8,128)S(1)}, u32[]{:S(2)}, u32[]{:S(2)}) %collective-permute-start.22) | collective-permute-done | bytes 73760 | tf_op jit(solution)/shard_map/ppermute | solution.py:32
  84.1 1.2 collective-permute-start.24
  85.3 3.2 %collective-permute-done.24.refs_6_ = f32[72,256]{1,0:T(8,128)S(1)} collective-permute-done((f32[72,256]{1,0:T(8,128)S(1)}, f32[72,256]{1,0:T(8,128)S(1)}, u32[]{:S(2)}, u32[]{:S(2)}) %collective-permute-start.24) | collective-permute-done | bytes 73760 | tf_op jit(solution)/shard_map/ppermute | solution.py:32
  88.6 0.7 loss_grad.1
  89.3 1.2 %collective-permute-start.25 = (f32[64,256]{1,0:T(8,128)S(1)}, f32[64,256]{1,0:T(8,128)S(1)}, u32[]{:S(2)}, u32[]{:S(2)}) collective-permute-start(f32[64,256]{1,0:T(8,128)S(1)} %get-tuple-element.111), channel_id=1, source_target_pairs={{0,8},{4,12},{8,0},{12,4},{16,24},{20,28},{24,16},{28,20},{1,9},{5... | collective-permute-start | bytes 196616 | tf_op jit(solution)/shard_map/ppermute | solution.py:32
  90.5 0.7 collective-permute-start.26
  91.2 2.6 %collective-permute-start.27 = (f32[64,256]{1,0:T(8,128)S(1)}, f32[64,256]{1,0:T(8,128)S(1)}, u32[]{:S(2)}, u32[]{:S(2)}) collective-permute-start(f32[64,256]{1,0:T(8,128)S(1)} %get-tuple-element.111), channel_id=1, source_target_pairs={{0,24},{4,28},{8,16},{12,20},{16,8},{20,12},{24,0},{28,4},{1,25},{... | collective-permute-start | bytes 196616 | tf_op jit(solution)/shard_map/ppermute | solution.py:32
  94.4 3.7 %collective-permute-done.26 = f32[64,256]{1,0:T(8,128)S(1)} collective-permute-done((f32[64,256]{1,0:T(8,128)S(1)}, f32[64,256]{1,0:T(8,128)S(1)}, u32[]{:S(2)}, u32[]{:S(2)}) %collective-permute-start.26) | collective-permute-done | bytes 65568 | tf_op jit(solution)/shard_map/ppermute | solution.py:32
  98.1 1.4 %collective-permute-start.28 = (f32[4,64,256]{2,1,0:T(8,128)S(1)}, f32[4,64,256]{2,1,0:T(8,128)S(1)}, u32[]{:S(2)}, u32[]{:S(2)}) collective-permute-start(f32[4,64,256]{2,1,0:T(8,128)S(1)} %pad_maximum_fusion.1.refs_7_), channel_id=1, source_target_pairs={{0,4},{4,0},{8,12},{12,8},{16,20},{20,16},{24,28},{28,24},{1,5},{5... | collective-permute-start | bytes 786440 | tf_op jit(solution)/shard_map/ppermute | solution.py:32
  100.1 2.2 %copy-done.1 = f32[1024,1024]{1,0:T(8,128)S(1)} copy-done((f32[1024,1024]{1,0:T(8,128)S(1)}, f32[1024,1024]{1,0:T(8,128)}, u32[]{:S(2)}) %copy-start.1) | copy-done | bytes 4194328
  102.3 1.7 %flat_sums.1 = (f32[8,128,1024]{2,1,0:T(8,128)S(1)}, f32[192,1024]{1,0:T(8,128)S(1)}, f32[192,1]{1,0:T(8,128)S(1)}) custom-call(f32[8,128,1024]{2,1,0:T(8,128)S(1)} %bitcast.15, bf16[8,192,128]{2,1,0:T(8,128)(2,1)S(1)} %columns_all.1.cols_ref.refs_2_, f32[2,1024]{1,0:T(2,128)S(1)} %get-tuple-element.119.stats_ref.refs_3_, f32[1,1024]{1,0:T(1,128)S(1)} %bitcast.18, ...), custom_call_target="tpu_custom_call" | custom-call | flops 402653184 | bytes 4194304 | tf_op jit(solution)/shard_map/flat_sums/pallas_call | solution.py:627
  104.0 2.4 %tail_near.1 = (f32[192,1024]{1,0:T(8,128)S(1)}, f32[32,1024]{1,0:T(8,128)S(1)}, f32[2,8,1024]{2,1,0:T(8,128)S(1)}) custom-call(s32[3]{0:T(128)S(1)} %pad_add_fusion.at_ref.refs_7_.refs_0_, f32[8,128,1024]{2,1,0:T(8,128)S(1)} %get-tuple-element.120.refs_1_, bf16[8,192,128]{2,1,0:T(8,128)(2,1)S(1)} %columns_all.1.cols_ref.refs_2_, ...), custom_call_target="tpu_custom_call" | custom-call | flops 536870912 | bytes 2097152 | tf_op jit(solution)/shard_map/tail_near/pallas_call | solution.py:588
  106.9 1.5 %collective-permute-done.31.refs_8_ = f32[4,64,256]{2,1,0:T(8,128)S(1)} collective-permute-done((f32[4,64,256]{2,1,0:T(8,128)S(1)}, f32[4,64,256]{2,1,0:T(8,128)S(1)}, u32[]{:S(2)}, u32[]{:S(2)}) %collective-permute-start.31) | collective-permute-done | bytes 262176 | tf_op jit(solution)/shard_map/ppermute | solution.py:32
  108.4 3.4 %tail_far.1 = (f32[192,1024]{1,0:T(8,128)}, f32[32,1024]{1,0:T(8,128)}, f32[1,1024]{1,0:T(1,128)}, f32[1,1024]{1,0:T(1,128)}) custom-call(s32[3]{0:T(128)S(1)} %pad_add_fusion.at_ref.refs_7_.refs_0_, f32[8,128,1024]{2,1,0:T(8,128)S(1)} %get-tuple-element.120.refs_1_, bf16[8,192,128]{2,1,0:T(8,128)(2,1)S(1)} %columns_all.1.cols_ref.refs_2_, ...), custom_call_target="tpu_custom_call" | custom-call | flops 536870912 | bytes 2097152 | tf_op jit(solution)/shard_map/tail_far/pallas_call | solution.py:588
  (63 shorter events, 7.9 us)
Async XLA Ops:
  7.2 18.5 %copy-start = (bf16[1024,256]{1,0:T(8,128)(2,1)S(1)}, bf16[1024,256]{1,0:T(8,128)(2,1)}, u32[]{:S(2)}) copy-start(bf16[1024,256]{1,0:T(8,128)(2,1)} %refs_6_.3) | copy-start | bytes 1572868
  7.2 21.7 %copy-start.2 = (bf16[4096,256]{1,0:T(8,128)(2,1)S(1)}, bf16[4096,256]{1,0:T(8,128)(2,1)}, u32[]{:S(2)}) copy-start(bf16[4096,256]{1,0:T(8,128)(2,1)} %p_ref.1) | copy-start | bytes 6291460
  7.2 92.9 %all-gather.2.cloned.1.call-start = ((), (), s32[]{:S(2)}) async-start(), calls=%async_computation.1 | async-start | bytes 4718592 | tf_op jit(solution)/shard_map/all_gather | solution.py:713
  7.2 1.1 copy-start.3
  8.4 17.2 %copy-start.5 = (f32[1024]{0:T(1024)S(1)}, f32[1024]{0:T(1024)}, u32[]{:S(2)}) copy-start(f32[1024]{0:T(1024)} %param.9) | copy-start | bytes 12292
  8.4 17.2 %copy-start.6 = (f32[1024]{0:T(1024)S(1)}, f32[1024]{0:T(1024)}, u32[]{:S(2)}) copy-start(f32[1024]{0:T(1024)} %param.10) | copy-start | bytes 12292
  25.9 1.4 %collective-permute-start = (f32[128,256]{1,0:T(8,128)S(1)}, f32[128,256]{1,0:T(8,128)S(1)}, u32[]{:S(2)}, u32[]{:S(2)}) collective-permute-start(f32[128,256]{1,0:T(8,128)S(1)} %get-tuple-element.73), channel_id=1, source_target_pairs={{0,1},{1,0},{2,3},{3,2},{4,5},{5,4},{6,7},{7,6},{8,9},{9,8},{10,11... | collective-permute-start | bytes 393224 | tf_op jit(solution)/shard_map/ppermute | solution.py:32
  27.3 5.6 %collective-permute-start.1 = (f32[128,256]{1,0:T(8,128)S(1)}, f32[128,256]{1,0:T(8,128)S(1)}, u32[]{:S(2)}, u32[]{:S(2)}) collective-permute-start(f32[128,256]{1,0:T(8,128)S(1)} %add.9.refs_0_.refs_1_), channel_id=1, source_target_pairs={{0,2},{1,3},{2,0},{3,1},{4,6},{5,7},{6,4},{7,5},{8,10},{9,11},{10,... | collective-permute-start | bytes 393224 | tf_op jit(solution)/shard_map/ppermute | solution.py:32
  28.9 1.0 copy-start.4
  33.1 5.0 %collective-permute-start.2 = (f32[128,256]{1,0:T(8,128)S(1)}, f32[128,256]{1,0:T(8,128)S(1)}, u32[]{:S(2)}, u32[]{:S(2)}) collective-permute-start(f32[128,256]{1,0:T(8,128)S(1)} %embed_rows.1.refs_0_.emb_ref), channel_id=1, source_target_pairs={{0,4},{4,0},{8,12},{12,8},{16,20},{20,16},{24,28},{28,24},{1,5},{5... | collective-permute-start | bytes 393224 | tf_op jit(solution)/shard_map/ppermute | solution.py:32
  38.1 1.6 %collective-permute-start.3 = (f32[136,256]{1,0:T(8,128)S(1)}, f32[136,256]{1,0:T(8,128)S(1)}, u32[]{:S(2)}, u32[]{:S(2)}) collective-permute-start(f32[136,256]{1,0:T(8,128)S(1)} %logit_sum.1), channel_id=1, source_target_pairs={{0,1},{1,0},{2,3},{3,2},{4,5},{5,4},{6,7},{7,6},{8,9},{9,8},{10,11... | collective-permute-start | bytes 417800 | tf_op jit(solution)/shard_map/ppermute | solution.py:32
  39.7 6.7 %collective-permute-start.4 = (f32[136,256]{1,0:T(8,128)S(1)}, f32[136,256]{1,0:T(8,128)S(1)}, u32[]{:S(2)}, u32[]{:S(2)}) collective-permute-start(f32[136,256]{1,0:T(8,128)S(1)} %add.10.refs_3_), channel_id=1, source_target_pairs={{0,2},{1,3},{2,0},{3,1},{4,6},{5,7},{6,4},{7,5},{8,10},{9,11},{10,... | collective-permute-start | bytes 417800 | tf_op jit(solution)/shard_map/ppermute | solution.py:32
  41.2 5.1 %collective-permute-start.5 = (f32[4,48,128]{2,1,0:T(8,128)S(1)}, f32[4,48,128]{2,1,0:T(8,128)S(1)}, u32[]{:S(2)}, u32[]{:S(2)}) collective-permute-start(f32[4,48,128]{2,1,0:T(8,128)S(1)} %get-tuple-element.91), channel_id=1, source_target_pairs={{0,4},{4,0},{8,12},{12,8},{16,20},{20,16},{24,28},{28,24},{1,5},{5... | collective-permute-start | bytes 294920 | tf_op jit(solution)/shard_map/ppermute | solution.py:32
  42.0 4.4 %collective-permute-start.6 = (f32[80,128]{1,0:T(8,128)S(1)}, f32[80,128]{1,0:T(8,128)S(1)}, u32[]{:S(2)}, u32[]{:S(2)}) collective-permute-start(f32[80,128]{1,0:T(8,128)S(1)} %get-tuple-element.93), channel_id=1, source_target_pairs={{0,8},{4,12},{8,0},{12,4},{16,24},{20,28},{24,16},{28,20},{1,9},{5... | collective-permute-start | bytes 122888 | tf_op jit(solution)/shard_map/ppermute | solution.py:32
  42.3 5.6 %collective-permute-start.7 = (f32[80,128]{1,0:T(8,128)S(1)}, f32[80,128]{1,0:T(8,128)S(1)}, u32[]{:S(2)}, u32[]{:S(2)}) collective-permute-start(f32[80,128]{1,0:T(8,128)S(1)} %get-tuple-element.94), channel_id=1, source_target_pairs={{0,16},{4,20},{8,24},{12,28},{16,0},{20,4},{24,8},{28,12},{1,17},{... | collective-permute-start | bytes 122888 | tf_op jit(solution)/shard_map/ppermute | solution.py:32
  43.1 5.8 %collective-permute-start.8 = (f32[80,128]{1,0:T(8,128)S(1)}, f32[80,128]{1,0:T(8,128)S(1)}, u32[]{:S(2)}, u32[]{:S(2)}) collective-permute-start(f32[80,128]{1,0:T(8,128)S(1)} %get-tuple-element.95), channel_id=1, source_target_pairs={{0,24},{4,28},{8,16},{12,20},{16,8},{20,12},{24,0},{28,4},{1,25},{... | collective-permute-start | bytes 122888 | tf_op jit(solution)/shard_map/ppermute | solution.py:32
  49.4 3.6 %collective-permute-start.10 = (f32[2,128]{1,0:T(2,128)S(1)}, f32[2,128]{1,0:T(2,128)S(1)}, u32[]{:S(2)}, u32[]{:S(2)}) collective-permute-start(f32[2,128]{1,0:T(2,128)S(1)} %row_pass.2.refs_0_), channel_id=1, source_target_pairs={{0,2},{1,3},{2,0},{3,1},{4,6},{5,7},{6,4},{7,5},{8,10},{9,11},{10,... | collective-permute-start | bytes 3080 | tf_op jit(solution)/shard_map/ppermute | solution.py:32
  50.0 3.0 %collective-permute-start.11 = (f32[2,128]{1,0:T(2,128)S(1)}, f32[2,128]{1,0:T(2,128)S(1)}, u32[]{:S(2)}, u32[]{:S(2)}) collective-permute-start(f32[2,128]{1,0:T(2,128)S(1)} %row_pass.2.refs_0_), channel_id=1, source_target_pairs={{0,3},{1,2},{2,1},{3,0},{4,7},{5,6},{6,5},{7,4},{8,11},{9,10},{10,... | collective-permute-start | bytes 3080 | tf_op jit(solution)/shard_map/ppermute | solution.py:32
  50.0 3.0 %collective-permute-start.9 = (f32[2,128]{1,0:T(2,128)S(1)}, f32[2,128]{1,0:T(2,128)S(1)}, u32[]{:S(2)}, u32[]{:S(2)}) collective-permute-start(f32[2,128]{1,0:T(2,128)S(1)} %row_pass.2.refs_0_), channel_id=1, source_target_pairs={{0,1},{1,0},{2,3},{3,2},{4,5},{5,4},{6,7},{7,6},{8,9},{9,8},{10,11... | collective-permute-start | bytes 3080 | tf_op jit(solution)/shard_map/ppermute | solution.py:32
  53.6 7.2 %collective-permute-start.12 = (f32[80,128]{1,0:T(8,128)S(1)}, f32[80,128]{1,0:T(8,128)S(1)}, u32[]{:S(2)}, u32[]{:S(2)}) collective-permute-start(f32[80,128]{1,0:T(8,128)S(1)} %get-tuple-element.100), channel_id=1, source_target_pairs={{0,8},{4,12},{8,0},{12,4},{16,24},{20,28},{24,16},{28,20},{1,9},{5... | collective-permute-start | bytes 122888 | tf_op jit(solution)/shard_map/ppermute | solution.py:32
  54.5 9.0 %collective-permute-start.13 = (f32[80,128]{1,0:T(8,128)S(1)}, f32[80,128]{1,0:T(8,128)S(1)}, u32[]{:S(2)}, u32[]{:S(2)}) collective-permute-start(f32[80,128]{1,0:T(8,128)S(1)} %get-tuple-element.101), channel_id=1, source_target_pairs={{0,16},{4,20},{8,24},{12,28},{16,0},{20,4},{24,8},{28,12},{1,17},{... | collective-permute-start | bytes 122888 | tf_op jit(solution)/shard_map/ppermute | solution.py:32
  57.4 6.7 %collective-permute-start.14 = (f32[80,128]{1,0:T(8,128)S(1)}, f32[80,128]{1,0:T(8,128)S(1)}, u32[]{:S(2)}, u32[]{:S(2)}) collective-permute-start(f32[80,128]{1,0:T(8,128)S(1)} %get-tuple-element.102), channel_id=1, source_target_pairs={{0,24},{4,28},{8,16},{12,20},{16,8},{20,12},{24,0},{28,4},{1,25},{... | collective-permute-start | bytes 122888 | tf_op jit(solution)/shard_map/ppermute | solution.py:32
  64.5 16.1 %copy-start.7 = (s32[128]{0:T(128)S(1)}, s32[128]{0:T(128)}, u32[]{:S(2)}) copy-start(s32[128]{0:T(128)} %param.13) | copy-start | bytes 1540
  64.6 1.9 %collective-permute-start.15 = (f32[2,128]{1,0:T(2,128)S(1)}, f32[2,128]{1,0:T(2,128)S(1)}, u32[]{:S(2)}, u32[]{:S(2)}) collective-permute-start(f32[2,128]{1,0:T(2,128)S(1)} %row_pass.3.refs_0_), channel_id=1, source_target_pairs={{0,1},{1,0},{2,3},{3,2},{4,5},{5,4},{6,7},{7,6},{8,9},{9,8},{10,11... | collective-permute-start | bytes 3080 | tf_op jit(solution)/shard_map/ppermute | solution.py:32
  64.6 3.6 %collective-permute-start.16 = (f32[2,128]{1,0:T(2,128)S(1)}, f32[2,128]{1,0:T(2,128)S(1)}, u32[]{:S(2)}, u32[]{:S(2)}) collective-permute-start(f32[2,128]{1,0:T(2,128)S(1)} %row_pass.3.refs_0_), channel_id=1, source_target_pairs={{0,2},{1,3},{2,0},{3,1},{4,6},{5,7},{6,4},{7,5},{8,10},{9,11},{10,... | collective-permute-start | bytes 3080 | tf_op jit(solution)/shard_map/ppermute | solution.py:32
  66.1 3.0 %collective-permute-start.17 = (f32[2,128]{1,0:T(2,128)S(1)}, f32[2,128]{1,0:T(2,128)S(1)}, u32[]{:S(2)}, u32[]{:S(2)}) collective-permute-start(f32[2,128]{1,0:T(2,128)S(1)} %row_pass.3.refs_0_), channel_id=1, source_target_pairs={{0,3},{1,2},{2,1},{3,0},{4,7},{5,6},{6,5},{7,4},{8,11},{9,10},{10,... | collective-permute-start | bytes 3080 | tf_op jit(solution)/shard_map/ppermute | solution.py:32
  69.7 7.4 %collective-permute-start.18 = (f32[1,8,48,128]{3,2,1,0:T(8,128)S(1)}, f32[1,8,48,128]{3,2,1,0:T(8,128)S(1)}, u32[]{:S(2)}, u32[]{:S(2)}) collective-permute-start(f32[1,8,48,128]{3,2,1,0:T(8,128)S(1)} %columns_join.1), channel_id=1, source_target_pairs={{0,2},{1,3},{2,0},{3,1},{4,6},{5,7},{6,4},{7,5},{8,10},{9,11},{10,... | collective-permute-start | bytes 589832 | tf_op jit(solution)/shard_map/ppermute | solution.py:32
  70.4 6.8 %collective-permute-start.19 = (f32[32,128]{1,0:T(8,128)S(1)}, f32[32,128]{1,0:T(8,128)S(1)}, u32[]{:S(2)}, u32[]{:S(2)}) collective-permute-start(f32[32,128]{1,0:T(8,128)S(1)} %col_pass.3.refs_0_), channel_id=1, source_target_pairs={{0,8},{4,12},{8,0},{12,4},{16,24},{20,28},{24,16},{28,20},{1,9},{5... | collective-permute-start | bytes 49160 | tf_op jit(solution)/shard_map/ppermute | solution.py:32
  73.7 7.0 %collective-permute-start.20 = (f32[32,128]{1,0:T(8,128)S(1)}, f32[32,128]{1,0:T(8,128)S(1)}, u32[]{:S(2)}, u32[]{:S(2)}) collective-permute-start(f32[32,128]{1,0:T(8,128)S(1)} %col_pass.3.refs_0_), channel_id=1, source_target_pairs={{0,16},{4,20},{8,24},{12,28},{16,0},{20,4},{24,8},{28,12},{1,17},{... | collective-permute-start | bytes 49160 | tf_op jit(solution)/shard_map/ppermute | solution.py:32
  74.6 6.1 %collective-permute-start.21 = (f32[32,128]{1,0:T(8,128)S(1)}, f32[32,128]{1,0:T(8,128)S(1)}, u32[]{:S(2)}, u32[]{:S(2)}) collective-permute-start(f32[32,128]{1,0:T(8,128)S(1)} %col_pass.3.refs_0_), channel_id=1, source_target_pairs={{0,24},{4,28},{8,16},{12,20},{16,8},{20,12},{24,0},{28,4},{1,25},{... | collective-permute-start | bytes 49160 | tf_op jit(solution)/shard_map/ppermute | solution.py:32
  82.2 3.1 %collective-permute-start.23 = (f32[2,8,48,128]{3,2,1,0:T(8,128)S(1)}, f32[2,8,48,128]{3,2,1,0:T(8,128)S(1)}, u32[]{:S(2)}, u32[]{:S(2)}) collective-permute-start(f32[2,8,48,128]{3,2,1,0:T(8,128)S(1)} %pad_maximum_fusion.refs_0_), channel_id=1, source_target_pairs={{0,1},{1,0},{2,3},{3,2},{4,5},{5,4},{6,7},{7,6},{8,9},{9,8},{10,11... | collective-permute-start | bytes 1179656 | tf_op jit(solution)/shard_map/ppermute | solution.py:32
  82.3 1.8 %collective-permute-start.22 = (f32[72,256]{1,0:T(8,128)S(1)}, f32[72,256]{1,0:T(8,128)S(1)}, u32[]{:S(2)}, u32[]{:S(2)}) collective-permute-start(f32[72,256]{1,0:T(8,128)S(1)} %get-tuple-element.106), channel_id=1, source_target_pairs={{0,1},{1,0},{2,3},{3,2},{4,5},{5,4},{6,7},{7,6},{8,9},{9,8},{10,11... | collective-permute-start | bytes 221192 | tf_op jit(solution)/shard_map/ppermute | solution.py:32
  84.1 4.4 %collective-permute-start.24 = (f32[72,256]{1,0:T(8,128)S(1)}, f32[72,256]{1,0:T(8,128)S(1)}, u32[]{:S(2)}, u32[]{:S(2)}) collective-permute-start(f32[72,256]{1,0:T(8,128)S(1)} %add.11.refs_5_), channel_id=1, source_target_pairs={{0,2},{1,3},{2,0},{3,1},{4,6},{5,7},{6,4},{7,5},{8,10},{9,11},{10,... | collective-permute-start | bytes 221192 | tf_op jit(solution)/shard_map/ppermute | solution.py:32
  89.3 5.1 %collective-permute-start.25 = (f32[64,256]{1,0:T(8,128)S(1)}, f32[64,256]{1,0:T(8,128)S(1)}, u32[]{:S(2)}, u32[]{:S(2)}) collective-permute-start(f32[64,256]{1,0:T(8,128)S(1)} %get-tuple-element.111), channel_id=1, source_target_pairs={{0,8},{4,12},{8,0},{12,4},{16,24},{20,28},{24,16},{28,20},{1,9},{5... | collective-permute-start | bytes 196616 | tf_op jit(solution)/shard_map/ppermute | solution.py:32
  90.5 7.5 %collective-permute-start.26 = (f32[64,256]{1,0:T(8,128)S(1)}, f32[64,256]{1,0:T(8,128)S(1)}, u32[]{:S(2)}, u32[]{:S(2)}) collective-permute-start(f32[64,256]{1,0:T(8,128)S(1)} %get-tuple-element.111), channel_id=1, source_target_pairs={{0,16},{4,20},{8,24},{12,28},{16,0},{20,4},{24,8},{28,12},{1,17},{... | collective-permute-start | bytes 196616 | tf_op jit(solution)/shard_map/ppermute | solution.py:32
  91.2 6.8 %collective-permute-start.27 = (f32[64,256]{1,0:T(8,128)S(1)}, f32[64,256]{1,0:T(8,128)S(1)}, u32[]{:S(2)}, u32[]{:S(2)}) collective-permute-start(f32[64,256]{1,0:T(8,128)S(1)} %get-tuple-element.111), channel_id=1, source_target_pairs={{0,24},{4,28},{8,16},{12,20},{16,8},{20,12},{24,0},{28,4},{1,25},{... | collective-permute-start | bytes 196616 | tf_op jit(solution)/shard_map/ppermute | solution.py:32
  93.8 5.7 %collective-permute-start.29 = (f32[1,64]{1,0:T(1,128)S(1)}, f32[1,64]{1,0:T(1,128)S(1)}, u32[]{:S(2)}, u32[]{:S(2)}) collective-permute-start(f32[1,64]{1,0:T(1,128)S(1)} %get-tuple-element.112), channel_id=1, source_target_pairs={{0,1},{1,0},{2,3},{3,2},{4,5},{5,4},{6,7},{7,6},{8,9},{9,8},{10,11... | collective-permute-start | bytes 776 | tf_op jit(solution)/shard_map/ppermute | solution.py:32
  98.1 6.0 %collective-permute-start.30 = (f32[4,64,256]{2,1,0:T(8,128)S(1)}, f32[4,64,256]{2,1,0:T(8,128)S(1)}, u32[]{:S(2)}, u32[]{:S(2)}) collective-permute-start(f32[4,64,256]{2,1,0:T(8,128)S(1)} %pad_maximum_fusion.1.refs_7_), channel_id=1, source_target_pairs={{0,1},{1,0},{2,3},{3,2},{4,5},{5,4},{6,7},{7,6},{8,9},{9,8},{10,11... | collective-permute-start | bytes 786440 | tf_op jit(solution)/shard_map/ppermute | solution.py:32
  98.1 8.7 %collective-permute-start.28 = (f32[4,64,256]{2,1,0:T(8,128)S(1)}, f32[4,64,256]{2,1,0:T(8,128)S(1)}, u32[]{:S(2)}, u32[]{:S(2)}) collective-permute-start(f32[4,64,256]{2,1,0:T(8,128)S(1)} %pad_maximum_fusion.1.refs_7_), channel_id=1, source_target_pairs={{0,4},{4,0},{8,12},{12,8},{16,20},{20,16},{24,28},{28,24},{1,5},{5... | collective-permute-start | bytes 786440 | tf_op jit(solution)/shard_map/ppermute | solution.py:32
  100.1 2.2 %copy-start.1 = (f32[1024,1024]{1,0:T(8,128)S(1)}, f32[1024,1024]{1,0:T(8,128)}, u32[]{:S(2)}) copy-start(f32[1024,1024]{1,0:T(8,128)} %all-gather.2.cloned.1.call-done) | copy-start | bytes 12582916
  106.9 1.5 %collective-permute-start.31 = (f32[4,64,256]{2,1,0:T(8,128)S(1)}, f32[4,64,256]{2,1,0:T(8,128)S(1)}, u32[]{:S(2)}, u32[]{:S(2)}) collective-permute-start(f32[4,64,256]{2,1,0:T(8,128)S(1)} %collective-permute-done.28.refs_7_), channel_id=1, source_target_pairs={{0,1},{1,0},{2,3},{3,2},{4,5},{5,4},{6,7},{7,6},{8,9},{9,8},{10,11... | collective-permute-start | bytes 786440 | tf_op jit(solution)/shard_map/ppermute | solution.py:32
Sparse Core Ops, SparseCore 0:
  11.6 79.2 all-gather.1

commit v5 on v4

--- a/solution.py
+++ b/solution.py
@@ -525,7 +525,11 @@
     )(columns)
 
 
-def tail_half(refs, grads, odd, n_batch, sums_ref, grad_all, low_all, cols_all):
+def centre_of(sums, crops):
+    return [jnp.sum(sums[k], axis=0, keepdims=True) / crops for k in range(2)]
+
+
+def tail_half(refs, grads, odd, n_batch, sums_ref, centre, grad_all, low_all, cols_all, *wide):
     at_ref, pre_ref, cols_ref, stats, gain, shift, w_ref = refs
     unit, width = pre_ref.shape[1], grad_all.shape[1]
     size, n = unit // 2, n_batch // 2
@@ -533,7 +537,8 @@
     for k in range(n):
         for flip in range(2):
             place = pl.multiple_of(k * unit + (at_ref[2] ^ flip) * size, size)
-            grad_all[pl.ds(place, size), :] = grads[flip][k].astype(BF16)
+            own, rest = grads[2 * flip], grads[2 * flip + 1]
+            grad_all[pl.ds(place, size), :] = (rest[k - 1] if k else own[0]).astype(BF16)
     mine = lax.broadcasted_iota(jnp.int32, (e_rows, width), 0) + at_ref[0] * (width // n_batch)
     chosen = jnp.where(mine == lax.broadcasted_iota(jnp.int32, (e_rows, width), 1), 1.0, 0.0).astype(BF16)
     w2 = 0.0
@@ -549,34 +554,44 @@
         bn_grad = jnp.where(shifted > 0, hidden_grad, 0.0)
         sums_ref[0, pl.ds(block, 1), :] = jnp.sum(bn_grad, axis=0, keepdims=True)
         sums_ref[1, pl.ds(block, 1), :] = jnp.sum(bn_grad * normed, axis=0, keepdims=True)
-        low_all[rows, :] = bn_grad.astype(BF16)
+        if centre is None:
+            wide[0][rows, :] = bn_grad
+        else:
+            low_all[rows, :] = (bn_grad - centre[0] - normed * centre[1]).astype(BF16)
         cols_all[:, rows] = cols_ref[block]
+    if centre is None:
+        centre = centre_of(sums_ref, n * unit)
+        for k in range(n):
+            rows = slice(k * unit, (k + 1) * unit)
+            normed, _ = batch_norm(pre_ref[at_ref[0] ^ (2 * k + odd)], stats, gain, shift)
+            low_all[rows, :] = (wide[0][rows, :] - centre[0] - normed * centre[1]).astype(BF16)
     return jnp.dot(cols_all[...], low_all[...], preferred_element_type=F32), w2
 
 
 def near_kernel(n_batch, n_grads, *refs):
-    ins, refs = refs[:7], refs[7:]
-    grads, (w1_ref, w2_ref, sums_ref, *scratch) = refs[:2], refs[2:]
+    ins, grads, refs = refs[:7], refs[7 : 7 + n_grads], refs[7 + n_grads :]
+    w1_ref, w2_ref, sums_ref, wide, *scratch = refs
     sums_ref[...] = jnp.zeros_like(sums_ref)
     ins = ins[:3] + tuple(r[...] for r in ins[3:6]) + ins[6:]
-    w1_ref[...], w2_ref[...] = tail_half(ins, grads, 0, n_batch, sums_ref, *scratch)
+    w1_ref[...], w2_ref[...] = tail_half(ins, grads, 0, n_batch, sums_ref, None, *scratch, wide)
 
 
 def far_kernel(crops_all, n_batch, n_grads, *refs):
-    ins, refs = refs[:7], refs[7:]
-    grads, refs = (refs[: n_grads // 2], refs[n_grads // 2 : n_grads]), refs[n_grads:]
+    ins, grads, refs = refs[:7], refs[7 : 7 + n_grads], refs[7 + n_grads :]
     near_w1, near_w2, near_sums, flat_ref, total_ref = refs[:5]
     w1_ref, w2_ref, gain_grad_ref, shift_grad_ref, sums, *scratch = refs[5:]
     ins = ins[:3] + tuple(r[...] for r in ins[3:6]) + ins[6:]
     stats, gain = ins[3:5]
     sums[...] = near_sums[...]
-    w1, w2 = tail_half(ins, [half[0] for half in grads], 1, n_batch, sums, *scratch)
+    centre = centre_of(near_sums[...], crops_all // 2)
+    w1, w2 = tail_half(ins, grads, 1, n_batch, sums, centre, *scratch)
     w2_ref[...] = (near_w2[...] + w2)[0 : w2_ref.shape[0], :]
     shift_grad = jnp.sum(sums[0], axis=0, keepdims=True)
     gain_grad = jnp.sum(sums[1], axis=0, keepdims=True)
     shift_grad_ref[...] = shift_grad
     gain_grad_ref[...] = gain_grad
-    flat = total_ref[...] * (shift_grad / crops_all) + flat_ref[...] * (gain_grad / crops_all)
+    flat = total_ref[...] * (shift_grad / crops_all - centre[0])
+    flat = flat + flat_ref[...] * (gain_grad / crops_all - centre[1])
     w1_ref[...] = gain * stats[1:2, :] * (near_w1[...] + w1 - flat)
 
 
@@ -601,16 +616,11 @@
     )(at, pre_all, columns, stats, gain, shift, w_second, *grads, *more)
 
 
-def flat_kernel(pre_hbm, cols_ref, stats_ref, gain_ref, shift_ref, pre_ref, flat_ref, total_ref, sems):
-    n_batch = pre_ref.shape[0]
-    copies = [pltpu.make_async_copy(pre_hbm.at[k], pre_ref.at[k], sems.at[k]) for k in range(n_batch)]
-    for copy in copies:
-        copy.start()
+def flat_kernel(pre_ref, cols_ref, stats_ref, gain_ref, shift_ref, flat_ref, total_ref):
     stats, gain, shift = stats_ref[...], gain_ref[...], shift_ref[...]
     total = 0.0
-    for k in range(n_batch):
+    for k in range(pre_ref.shape[0]):
         total = total + jnp.sum(cols_ref[k].astype(F32), axis=1, keepdims=True)
-        copies[k].wait()
         normed, _ = batch_norm(pre_ref[k], stats, gain, shift)
         part = jnp.dot(cols_ref[k], normed.astype(BF16), preferred_element_type=F32)
         if k == 0:
@@ -623,17 +633,9 @@
 def flat_sums(pre_all, columns, stats, gain, shift):
     n_batch, unit, hidden = pre_all.shape
     d_cols = columns.shape[1]
-    vmem = pl.BlockSpec(memory_space=pltpu.VMEM)
     return pl.pallas_call(
         flat_kernel,
-        in_specs=[pl.BlockSpec(memory_space=pltpu.HBM)] + [vmem] * 4,
-        out_specs=[vmem] * 3,
-        out_shape=[
-            jax.ShapeDtypeStruct((n_batch, unit, hidden), F32),
-            jax.ShapeDtypeStruct((d_cols, hidden), F32),
-            jax.ShapeDtypeStruct((d_cols, 1), F32),
-        ],
-        scratch_shapes=[pltpu.SemaphoreType.DMA((n_batch,))],
+        out_shape=[jax.ShapeDtypeStruct((d_cols, hidden), F32), jax.ShapeDtypeStruct((d_cols, 1), F32)],
         compiler_params=params(20),
         cost_estimate=cost(2 * n_batch * unit * hidden * d_cols, 4 * n_batch * unit * hidden),
         name="flat_sums",
@@ -714,6 +716,7 @@
     moment_parts = [lax.all_to_all(moments, "batch", 0, 0)] if short else batch_parts(moments)
     units = unit_rows(prototypes)
     emb_part, stats = second_layer(crops_all, moment_parts, pre_again, gain, shift, w_second)
+    first, emb_part = lax.optimization_barrier((at[2] == 0, emb_part))
     raw_parts = proto_parts(emb_part)
     if short:
         keep, send = columns_pick(after(features, emb_part), at, n_batch, n_proto)
@@ -759,35 +762,38 @@
         own_half = own_half + swap(send, "proto", 1)
         columns = [columns, swap(columns, "proto", 1)]
         target_parts = proto_parts(own_half, 2)
-        target_parts[0], *columns = lax.optimization_barrier((target_parts[0], *columns))
+        columns = columns_all(*columns, at)
+        target_parts[0], columns = lax.optimization_barrier((target_parts[0], columns))
     else:
         target_parts = proto_parts(target_sum(col_parts, codes[0], units, partner[None, :], at, 1)[0])
     raw_grad, penalty = loss_grad(raw_parts, logit_parts, target_parts, at)
 
     if short:
-        columns = columns_all(*(after(c, raw_grad) for c in columns), at)
         pre_all = after(pre_all, raw_grad)
-        near = [raw_grad] + [swap(raw_grad, "batch", k) for k in (2, 4, 6)]
-        near = jnp.stack(near)
-        far = swap(near, "batch", 1)
-        other_penalty = swap(penalty, "proto", 1)
-        first = at[2] == 0
+        ins = (at, pre_all.reshape(n_batch, rows, -1), columns, stats, gain, shift, w_second)
+        e_rows, hidden = -(-e_cols // 16) * 16, w_second.shape[0]
+        table = (2, n_batch, hidden)
+        flat = flat_sums(*ins[1:-1])
+        own = raw_grad[None]
+        rest = [swap(raw_grad, "batch", k) for k in (2, 4, 6)]
+        rest = jnp.stack([rest[0]] + [after(piece, *flat) for piece in rest[1:]])
+        far_own, own_core = swap(own, "batch", 1), swap(own, "proto", 1)
+        far_own_core = swap(far_own, "proto", 1)
+        rest, far_own, own_core, far_own_core = lax.optimization_barrier((rest, far_own, own_core, far_own_core))
+        far, rest_core = swap(rest, "batch", 1), swap(rest, "proto", 1)
+        other_penalty = swap(after(penalty, rest), "proto", 1)
         penalty = jnp.concatenate(
             [jnp.where(first, penalty, other_penalty), jnp.where(first, other_penalty, penalty)], axis=1
         )
-        ins = (at, pre_all.reshape(n_batch, rows, -1), columns, stats, gain, shift, w_second)
-        e_rows, hidden = -(-e_cols // 16) * 16, w_second.shape[0]
-        table = (2, n_batch, hidden)
-        pre_near, *flat = flat_sums(*ins[1:-1])
-        ins = (at, pre_near) + ins[2:]
         half = tail_call(
-            near_kernel, [(d_cols, hidden), (e_rows, hidden), table], [], *ins, [near, swap(near, "proto", 1)], [], "tail_near"
+            near_kernel, [(d_cols, hidden), (e_rows, hidden), table], [(crops_all // 2, hidden)],
+            *ins, [own, rest, own_core, rest_core], [], "tail_near",
         )
         far, penalty, *half = lax.optimization_barrier((far, penalty, *half, *flat))
         grad_w1, grad_w2, grad_gain, grad_shift = tail_call(
             functools.partial(far_kernel, crops_all),
             [(d_cols, hidden), (e_cols, hidden), (1, hidden), (1, hidden)], [table],
-            *ins, [far, swap(far, "proto", 1)], half, "tail_far",
+            *ins, [far_own, far, far_own_core, swap(far, "proto", 1)], half, "tail_far",
         )
     else:
         by_owner = jnp.swapaxes(features.astype(F32).reshape(rows, n_batch, d_cols), 0, 1)

time: 119 us -> 119 us (level)
  blocking collectives: 14.1 us -> 0 us
  starting transfers between devices: 31.3 us -> 40.2 us
  waiting for transfers between devices: 32 us -> 37 us
    all_to_all x1 -> x0, blocking collectives: 14.1 us -> none  [body(): lax.all_to_all(moments, 'batch', 0, 0)]
    all_to_all x0 -> x1, starting transfers between devices: none -> 7.29 us  [body(): lax.all_to_all(moments, 'batch', 0, 0)]
    all_to_all x0 -> x1, waiting for transfers between devices: none -> 7.01 us  [body(): lax.all_to_all(moments, 'batch', 0, 0)]
    ppermute x32 -> x35, waiting for transfers between devices: 32 us -> 29.9 us  [swap(): return lax.ppermute(v, axis, [(i, i ^ mask) for i in range(n)])]
    ppermute x32 -> x35, starting transfers between devices: 31.2 us -> 32.8 us  [swap(): return lax.ppermute(v, axis, [(i, i ^ mask) for i in range(n)])]
    unnamed x16 -> x18, local copies, waits for them, and re-layouts: 3.35 us -> 3.36 us
  transfers between devices with their start and end apart: 33 -> 37, of which waited for: 18 -> 21; matrix products, arithmetic and copies ran while one was open for 1% -> 1% of each run, Pallas kernels for 14% -> 14%
where the time goes in v5:
time: 119 us
  starting transfers between devices  40.2 us (34%)
  waiting for transfers between devices  37 us (31%)
  Pallas kernels  23 us (19%)
  between operations  14.3 us (12%)
  local copies, waits for them, and re-layouts  3.36 us (3%)
    ppermute x35, starting transfers between devices, swap(): return lax.ppermute(v, axis, [(i, i ^ mask) for i in range(n)])  32.8 us
    ppermute x35, waiting for transfers between devices, swap(): return lax.ppermute(v, axis, [(i, i ^ mask) for i in range(n)])  29.9 us
    all_to_all x1, starting transfers between devices, body(): lax.all_to_all(moments, 'batch', 0, 0)  7.29 us
    all_to_all x1, waiting for transfers between devices, body(): lax.all_to_all(moments, 'batch', 0, 0)  7.01 us
    pallas_call x2, Pallas kernels, tail_call(): pl.pallas_call(functools.partial(kernel, n_batch, len(grads)), in_specs=[...  6.69 us
    unnamed x18, local copies, waits for them, and re-layouts  3.36 us
    pallas_call x1, Pallas kernels, first_layer(): pl.pallas_call(first_kernel, in_specs=[pl.BlockSpec(memory_space=pl.ANY)]...  3.11 us
    pallas_call x2, Pallas kernels, score(): pl.pallas_call(functools.partial(score_kernel, n), grid=(protos // blk,),...  2.98 us
  transfers between devices with their start and end apart: 37, of which 21 were waited for; matrix products, arithmetic and copies ran while one was open for 1% of the time, Pallas kernels for 14%

profile of v5, /device:TPU:0, one launch (start us, length us, event | category | flops | bytes accessed | tf_op | source)
XLA Modules:
  0.0 118.6 jit_solution(7499613614408403381)
XLA Ops:
  7.2 1.1 copy-done.4
  8.4 3.1 %first_layer.1 = (f32[128,1024]{1,0:T(8,128)}, f32[128,1024]{1,0:T(8,128)S(1)}, f32[8,1,2048]{2,1,0:T(1,128)}) custom-call(bf16[128,1536]{1,0:T(8,128)(2,1)S(1)} %copy-done.4, bf16[1536,1024]{1,0:T(8,128)(2,1)} %w_hbm.1), custom_call_target="tpu_custom_call" | custom-call | flops 402653184 | bytes 3670016 | tf_op jit(solution)/shard_map/first_layer/pallas_call | solution.py:125
  11.5 7.3 %all-to-all-start = ((f32[8,1,2048]{2,1,0:T(1,128)}), f32[8,1,2048]{2,1,0:T(1,128)S(1)}, u32[]{:S(2)}, u32[]{:S(2)}) async-start(f32[8,1,2048]{2,1,0:T(1,128)} %get-tuple-element.76), calls=%async_computation | async-start | bytes 131072 | tf_op jit(solution)/shard_map/all_to_all | solution.py:716
  18.8 7.0 %all-to-all-done.refs_0_ = f32[8,1,2048]{2,1,0:T(1,128)S(1)} async-done(((f32[8,1,2048]{2,1,0:T(1,128)}), f32[8,1,2048]{2,1,0:T(1,128)S(1)}, u32[]{:S(2)}, u32[]{:S(2)}) %all-to-all-start) | async-done | bytes 65568 | tf_op jit(solution)/shard_map/all_to_all | solution.py:716
  26.2 1.3 %collective-permute-done = f32[128,256]{1,0:T(8,128)S(1)} collective-permute-done((f32[128,256]{1,0:T(8,128)S(1)}, f32[128,256]{1,0:T(8,128)S(1)}, u32[]{:S(2)}, u32[]{:S(2)}) %collective-permute-start) | collective-permute-done | bytes 131104 | tf_op jit(solution)/shard_map/ppermute | solution.py:32
  27.6 1.6 %collective-permute-start.1 = (f32[128,256]{1,0:T(8,128)S(1)}, f32[128,256]{1,0:T(8,128)S(1)}, u32[]{:S(2)}, u32[]{:S(2)}) collective-permute-start(f32[128,256]{1,0:T(8,128)S(1)} %add.9.refs_0_.refs_1_), channel_id=1, source_target_pairs={{0,2},{1,3},{2,0},{3,1},{4,6},{5,7},{6,4},{7,5},{8,10},{9,11},{10,... | collective-permute-start | bytes 393224 | tf_op jit(solution)/shard_map/ppermute | solution.py:32
  29.1 0.9 unit_rows.1.refs_1_.u_ref.refs_5_
  30.1 1.0 columns_pick.1
  31.1 2.0 %collective-permute-done.1.refs_1_.refs_2_ = f32[128,256]{1,0:T(8,128)S(1)} collective-permute-done((f32[128,256]{1,0:T(8,128)S(1)}, f32[128,256]{1,0:T(8,128)S(1)}, u32[]{:S(2)}, u32[]{:S(2)}) %collective-permute-start.1) | collective-permute-done | bytes 131104 | tf_op jit(solution)/shard_map/ppermute | solution.py:32
  33.6 1.4 %score.2 = (f32[128,4096]{1,0:T(8,128)S(1)}, f32[32,128]{1,0:T(8,128)S(1)}) custom-call(f32[128,256]{1,0:T(8,128)S(1)} %embed_rows.1.refs_0_.emb_ref, bf16[4096,256]{1,0:T(8,128)(2,1)S(1)} %unit_rows.1.refs_1_.u_ref.refs_5_), custom_call_target="tpu_custom_call" | custom-call | flops 268435456 | bytes 2097152 | tf_op jit(solution)/shard_map/score/pallas_call | solution.py:251
  35.1 2.1 %logit_sum.1 = f32[136,256]{1,0:T(8,128)S(1)} custom-call(f32[128,256]{1,0:T(8,128)S(1)} %embed_rows.1.refs_0_.emb_ref, bf16[4096,256]{1,0:T(8,128)(2,1)S(1)} %unit_rows.1.refs_1_.u_ref.refs_5_), custom_call_target="tpu_custom_call" | custom-call | flops 536870912 | bytes 2097152 | tf_op jit(solution)/shard_map/logit_sum/pallas_call | solution.py:297
  37.2 1.1 collective-permute-done.2.refs_0_
  38.3 1.5 %score.3 = (f32[128,4096]{1,0:T(8,128)S(1)}, f32[32,128]{1,0:T(8,128)S(1)}, f32[80,128]{1,0:T(8,128)S(1)}, f32[80,128]{1,0:T(8,128)S(1)}, f32[80,128]{1,0:T(8,128)S(1)}) custom-call(f32[128,256]{1,0:T(8,128)S(1)} %collective-permute-done.2.refs_0_, bf16[4096,256]{1,0:T(8,128)(2,1)S(1)} %unit_rows.1.refs_1_.u_ref.refs_5_, ...), custom_call_target="tpu_custom_call" | custom-call | flops 268435456 | bytes 2097152 | tf_op jit(solution)/shard_map/score/pallas_call | solution.py:251
  39.9 1.6 %collective-permute-start.4 = (f32[136,256]{1,0:T(8,128)S(1)}, f32[136,256]{1,0:T(8,128)S(1)}, u32[]{:S(2)}, u32[]{:S(2)}) collective-permute-start(f32[136,256]{1,0:T(8,128)S(1)} %add.10.refs_3_), channel_id=1, source_target_pairs={{0,2},{1,3},{2,0},{3,1},{4,6},{5,7},{6,4},{7,5},{8,10},{9,11},{10,... | collective-permute-start | bytes 417800 | tf_op jit(solution)/shard_map/ppermute | solution.py:32
  41.5 0.8 collective-permute-start.5
  43.3 3.3 %collective-permute-start.8 = (f32[80,128]{1,0:T(8,128)S(1)}, f32[80,128]{1,0:T(8,128)S(1)}, u32[]{:S(2)}, u32[]{:S(2)}) collective-permute-start(f32[80,128]{1,0:T(8,128)S(1)} %get-tuple-element.101), channel_id=1, source_target_pairs={{0,24},{4,28},{8,16},{12,20},{16,8},{20,12},{24,0},{28,4},{1,25},{... | collective-permute-start | bytes 122888 | tf_op jit(solution)/shard_map/ppermute | solution.py:32
  46.6 1.5 %collective-permute-done.7.refs_2_ = f32[80,128]{1,0:T(8,128)S(1)} collective-permute-done((f32[80,128]{1,0:T(8,128)S(1)}, f32[80,128]{1,0:T(8,128)S(1)}, u32[]{:S(2)}, u32[]{:S(2)}) %collective-permute-start.7) | collective-permute-done | bytes 40992 | tf_op jit(solution)/shard_map/ppermute | solution.py:32
  48.1 1.0 collective-permute-done.8.refs_3_.refs_4_
  50.3 1.3 %collective-permute-start.11 = (f32[2,128]{1,0:T(2,128)S(1)}, f32[2,128]{1,0:T(2,128)S(1)}, u32[]{:S(2)}, u32[]{:S(2)}) collective-permute-start(f32[2,128]{1,0:T(2,128)S(1)} %row_pass.2.refs_0_), channel_id=1, source_target_pairs={{0,3},{1,2},{2,1},{3,0},{4,7},{5,6},{6,5},{7,4},{8,11},{9,10},{10,... | collective-permute-start | bytes 3080 | tf_op jit(solution)/shard_map/ppermute | solution.py:32
  51.5 1.8 %collective-permute-done.10.refs_2_ = f32[2,128]{1,0:T(2,128)S(1)} collective-permute-done((f32[2,128]{1,0:T(2,128)S(1)}, f32[2,128]{1,0:T(2,128)S(1)}, u32[]{:S(2)}, u32[]{:S(2)}) %collective-permute-start.10) | collective-permute-done | bytes 1056 | tf_op jit(solution)/shard_map/ppermute | solution.py:32
  53.8 0.9 collective-permute-start.12
  54.8 3.0 %collective-permute-start.13 = (f32[80,128]{1,0:T(8,128)S(1)}, f32[80,128]{1,0:T(8,128)S(1)}, u32[]{:S(2)}, u32[]{:S(2)}) collective-permute-start(f32[80,128]{1,0:T(8,128)S(1)} %get-tuple-element.107), channel_id=1, source_target_pairs={{0,16},{4,20},{8,24},{12,28},{16,0},{20,4},{24,8},{28,12},{1,17},{... | collective-permute-start | bytes 122888 | tf_op jit(solution)/shard_map/ppermute | solution.py:32
  58.3 2.8 %collective-permute-done.12.refs_1_ = f32[80,128]{1,0:T(8,128)S(1)} collective-permute-done((f32[80,128]{1,0:T(8,128)S(1)}, f32[80,128]{1,0:T(8,128)S(1)}, u32[]{:S(2)}, u32[]{:S(2)}) %collective-permute-start.12) | collective-permute-done | bytes 40992 | tf_op jit(solution)/shard_map/ppermute | solution.py:32
  61.1 1.7 %collective-permute-done.13.refs_2_.refs_3_ = f32[80,128]{1,0:T(8,128)S(1)} collective-permute-done((f32[80,128]{1,0:T(8,128)S(1)}, f32[80,128]{1,0:T(8,128)S(1)}, u32[]{:S(2)}, u32[]{:S(2)}) %collective-permute-start.13) | collective-permute-done | bytes 40992 | tf_op jit(solution)/shard_map/ppermute | solution.py:32
  62.8 1.7 %collective-permute-done.14.refs_3_.refs_5_ = f32[80,128]{1,0:T(8,128)S(1)} collective-permute-done((f32[80,128]{1,0:T(8,128)S(1)}, f32[80,128]{1,0:T(8,128)S(1)}, u32[]{:S(2)}, u32[]{:S(2)}) %collective-permute-start.14) | collective-permute-done | bytes 40992 | tf_op jit(solution)/shard_map/ppermute | solution.py:32
  65.0 1.5 %collective-permute-start.16 = (f32[2,128]{1,0:T(2,128)S(1)}, f32[2,128]{1,0:T(2,128)S(1)}, u32[]{:S(2)}, u32[]{:S(2)}) collective-permute-start(f32[2,128]{1,0:T(2,128)S(1)} %row_pass.3.refs_0_), channel_id=1, source_target_pairs={{0,2},{1,3},{2,0},{3,1},{4,6},{5,7},{6,4},{7,5},{8,10},{9,11},{10,... | collective-permute-start | bytes 3080 | tf_op jit(solution)/shard_map/ppermute | solution.py:32
  66.9 1.8 %collective-permute-done.16.refs_2_ = f32[2,128]{1,0:T(2,128)S(1)} collective-permute-done((f32[2,128]{1,0:T(2,128)S(1)}, f32[2,128]{1,0:T(2,128)S(1)}, u32[]{:S(2)}, u32[]{:S(2)}) %collective-permute-start.16) | collective-permute-done | bytes 1056 | tf_op jit(solution)/shard_map/ppermute | solution.py:32
  68.6 0.9 collective-permute-done.17.refs_3_
  70.8 2.8 %collective-permute-start.19 = (f32[32,128]{1,0:T(8,128)S(1)}, f32[32,128]{1,0:T(8,128)S(1)}, u32[]{:S(2)}, u32[]{:S(2)}) collective-permute-start(f32[32,128]{1,0:T(8,128)S(1)} %col_pass.3.refs_0_), channel_id=1, source_target_pairs={{0,8},{4,12},{8,0},{12,4},{16,24},{20,28},{24,16},{28,20},{1,9},{5... | collective-permute-start | bytes 49160 | tf_op jit(solution)/shard_map/ppermute | solution.py:32
  73.6 1.5 %collective-permute-start.20 = (f32[32,128]{1,0:T(8,128)S(1)}, f32[32,128]{1,0:T(8,128)S(1)}, u32[]{:S(2)}, u32[]{:S(2)}) collective-permute-start(f32[32,128]{1,0:T(8,128)S(1)} %col_pass.3.refs_0_), channel_id=1, source_target_pairs={{0,16},{4,20},{8,24},{12,28},{16,0},{20,4},{24,8},{28,12},{1,17},{... | collective-permute-start | bytes 49160 | tf_op jit(solution)/shard_map/ppermute | solution.py:32
  75.1 1.5 %collective-permute-start.21 = (f32[32,128]{1,0:T(8,128)S(1)}, f32[32,128]{1,0:T(8,128)S(1)}, u32[]{:S(2)}, u32[]{:S(2)}) collective-permute-start(f32[32,128]{1,0:T(8,128)S(1)} %col_pass.3.refs_0_), channel_id=1, source_target_pairs={{0,24},{4,28},{8,16},{12,20},{16,8},{20,12},{24,0},{28,4},{1,25},{... | collective-permute-start | bytes 49160 | tf_op jit(solution)/shard_map/ppermute | solution.py:32
  76.6 1.0 collective-permute-done.18
  77.5 2.9 %collective-permute-done.20.refs_2_ = f32[32,128]{1,0:T(8,128)S(1)} collective-permute-done((f32[32,128]{1,0:T(8,128)S(1)}, f32[32,128]{1,0:T(8,128)S(1)}, u32[]{:S(2)}, u32[]{:S(2)}) %collective-permute-start.20) | collective-permute-done | bytes 16416 | tf_op jit(solution)/shard_map/ppermute | solution.py:32
  81.0 1.5 %target_sum.1 = (f32[72,256]{1,0:T(8,128)S(1)}, f32[72,256]{1,0:T(8,128)S(1)}) custom-call(f32[32,128]{1,0:T(8,128)S(1)} %col_pass.3.refs_0_, f32[32,128]{1,0:T(8,128)S(1)} %collective-permute-done.19.refs_1_, f32[32,128]{1,0:T(8,128)S(1)} %collective-permute-done.20.refs_2_, f32[32,128]{1,0:T(8,128)S(1)} %collective-permute-done.21.refs_3_, ...), custom_call_target="tpu_custom_call" | custom-call | flops 268435456 | bytes 4194304 | tf_op jit(solution)/shard_map/target_sum/pallas_call | solution.py:388
  83.1 1.3 %collective-permute-done.22 = f32[72,256]{1,0:T(8,128)S(1)} collective-permute-done((f32[72,256]{1,0:T(8,128)S(1)}, f32[72,256]{1,0:T(8,128)S(1)}, u32[]{:S(2)}, u32[]{:S(2)}) %collective-permute-start.22) | collective-permute-done | bytes 73760 | tf_op jit(solution)/shard_map/ppermute | solution.py:32
  84.4 1.5 %collective-permute-start.24 = (f32[72,256]{1,0:T(8,128)S(1)}, f32[72,256]{1,0:T(8,128)S(1)}, u32[]{:S(2)}, u32[]{:S(2)}) collective-permute-start(f32[72,256]{1,0:T(8,128)S(1)} %add.11.refs_5_), channel_id=1, source_target_pairs={{0,2},{1,3},{2,0},{3,1},{4,6},{5,7},{6,4},{7,5},{8,10},{9,11},{10,... | collective-permute-start | bytes 221192 | tf_op jit(solution)/shard_map/ppermute | solution.py:32
  86.5 2.3 %collective-permute-done.24.refs_6_ = f32[72,256]{1,0:T(8,128)S(1)} collective-permute-done((f32[72,256]{1,0:T(8,128)S(1)}, f32[72,256]{1,0:T(8,128)S(1)}, u32[]{:S(2)}, u32[]{:S(2)}) %collective-permute-start.24) | collective-permute-done | bytes 73760 | tf_op jit(solution)/shard_map/ppermute | solution.py:32
  89.6 1.2 %collective-permute-start.28 = (f32[1,64,256]{2,1,0:T(8,128)S(1)}, f32[1,64,256]{2,1,0:T(8,128)S(1)}, u32[]{:S(2)}, u32[]{:S(2)}) collective-permute-start(f32[1,64,256]{2,1,0:T(8,128)S(1)} %bitcast.18), channel_id=1, source_target_pairs={{0,4},{4,0},{8,12},{12,8},{16,20},{20,16},{24,28},{28,24},{1,5},{5... | collective-permute-start | bytes 196616 | tf_op jit(solution)/shard_map/ppermute | solution.py:32
  90.8 1.5 %collective-permute-start.27 = (f32[64,256]{1,0:T(8,128)S(1)}, f32[64,256]{1,0:T(8,128)S(1)}, u32[]{:S(2)}, u32[]{:S(2)}) collective-permute-start(f32[64,256]{1,0:T(8,128)S(1)} %get-tuple-element.117), channel_id=1, source_target_pairs={{0,24},{4,28},{8,16},{12,20},{16,8},{20,12},{24,0},{28,4},{1,25},{... | collective-permute-start | bytes 196616 | tf_op jit(solution)/shard_map/ppermute | solution.py:32
  92.3 1.1 collective-permute-start.26
  93.3 1.8 %collective-permute-start.25 = (f32[64,256]{1,0:T(8,128)S(1)}, f32[64,256]{1,0:T(8,128)S(1)}, u32[]{:S(2)}, u32[]{:S(2)}) collective-permute-start(f32[64,256]{1,0:T(8,128)S(1)} %get-tuple-element.117), channel_id=1, source_target_pairs={{0,8},{4,12},{8,0},{12,4},{16,24},{20,28},{24,16},{28,20},{1,9},{5... | collective-permute-start | bytes 196616 | tf_op jit(solution)/shard_map/ppermute | solution.py:32
  95.7 2.2 %copy-done = f32[1024,1024]{1,0:T(8,128)S(1)} copy-done((f32[1024,1024]{1,0:T(8,128)S(1)}, f32[1024,1024]{1,0:T(8,128)}, u32[]{:S(2)}) %copy-start) | copy-done | bytes 4194328
  97.9 1.0 flat_sums.1
  99.3 0.9 collective-permute-start.31
  101.7 3.1 %tail_near.1 = (f32[192,1024]{1,0:T(8,128)S(1)}, f32[32,1024]{1,0:T(8,128)S(1)}, f32[2,8,1024]{2,1,0:T(8,128)S(1)}) custom-call(s32[3]{0:T(128)S(1)} %pad_add_fusion.at_ref.refs_7_.refs_0_, f32[8,128,1024]{2,1,0:T(8,128)S(1)} %bitcast.16, bf16[8,192,128]{2,1,0:T(8,128)(2,1)S(1)} %columns_all.1.cols_ref.refs_2_, ...), custom_call_target="tpu_custom_call" | custom-call | flops 536870912 | bytes 2097152 | tf_op jit(solution)/shard_map/tail_near/pallas_call | solution.py:603
  104.8 1.8 %collective-permute-done.31.refs_8_ = f32[3,64,256]{2,1,0:T(8,128)S(1)} collective-permute-done((f32[3,64,256]{2,1,0:T(8,128)S(1)}, f32[3,64,256]{2,1,0:T(8,128)S(1)}, u32[]{:S(2)}, u32[]{:S(2)}) %collective-permute-start.31) | collective-permute-done | bytes 196640 | tf_op jit(solution)/shard_map/ppermute | solution.py:32
  106.7 1.4 %collective-permute-done.34.refs_10_ = f32[3,64,256]{2,1,0:T(8,128)S(1)} collective-permute-done((f32[3,64,256]{2,1,0:T(8,128)S(1)}, f32[3,64,256]{2,1,0:T(8,128)S(1)}, u32[]{:S(2)}, u32[]{:S(2)}) %collective-permute-start.34) | collective-permute-done | bytes 196640 | tf_op jit(solution)/shard_map/ppermute | solution.py:32
  108.1 3.6 %tail_far.1 = (f32[192,1024]{1,0:T(8,128)}, f32[32,1024]{1,0:T(8,128)}, f32[1,1024]{1,0:T(1,128)}, f32[1,1024]{1,0:T(1,128)}) custom-call(s32[3]{0:T(128)S(1)} %pad_add_fusion.at_ref.refs_7_.refs_0_, f32[8,128,1024]{2,1,0:T(8,128)S(1)} %bitcast.17, bf16[8,192,128]{2,1,0:T(8,128)(2,1)S(1)} %columns_all.1.cols_ref.refs_2_, ...), custom_call_target="tpu_custom_call" | custom-call | flops 536870912 | bytes 2097152 | tf_op jit(solution)/shard_map/tail_far/pallas_call | solution.py:603
  (72 shorter events, 11.3 us)
Async XLA Ops:
  7.2 18.7 %copy-start.2 = (bf16[1024,256]{1,0:T(8,128)(2,1)S(1)}, bf16[1024,256]{1,0:T(8,128)(2,1)}, u32[]{:S(2)}) copy-start(bf16[1024,256]{1,0:T(8,128)(2,1)} %refs_6_.3) | copy-start | bytes 1572868
  7.2 21.9 %copy-start.3 = (bf16[4096,256]{1,0:T(8,128)(2,1)S(1)}, bf16[4096,256]{1,0:T(8,128)(2,1)}, u32[]{:S(2)}) copy-start(bf16[4096,256]{1,0:T(8,128)(2,1)} %p_ref.1) | copy-start | bytes 6291460
  7.2 88.5 %all-gather.2.cloned.1.call-start = ((), (), s32[]{:S(2)}) async-start(), calls=%async_computation.1 | async-start | bytes 4718592 | tf_op jit(solution)/shard_map/all_gather | solution.py:715
  7.2 1.1 copy-start.4
  8.4 17.5 %copy-start.6 = (f32[1024]{0:T(1024)S(1)}, f32[1024]{0:T(1024)}, u32[]{:S(2)}) copy-start(f32[1024]{0:T(1024)} %param.9) | copy-start | bytes 12292
  8.4 17.5 %copy-start.7 = (f32[1024]{0:T(1024)S(1)}, f32[1024]{0:T(1024)}, u32[]{:S(2)}) copy-start(f32[1024]{0:T(1024)} %param.10) | copy-start | bytes 12292
  11.5 14.3 %all-to-all-start = ((f32[8,1,2048]{2,1,0:T(1,128)}), f32[8,1,2048]{2,1,0:T(1,128)S(1)}, u32[]{:S(2)}, u32[]{:S(2)}) async-start(f32[8,1,2048]{2,1,0:T(1,128)} %get-tuple-element.76), calls=%async_computation | async-start | bytes 131072 | tf_op jit(solution)/shard_map/all_to_all | solution.py:716
  26.1 1.4 %collective-permute-start = (f32[128,256]{1,0:T(8,128)S(1)}, f32[128,256]{1,0:T(8,128)S(1)}, u32[]{:S(2)}, u32[]{:S(2)}) collective-permute-start(f32[128,256]{1,0:T(8,128)S(1)} %get-tuple-element.79), channel_id=1, source_target_pairs={{0,1},{1,0},{2,3},{3,2},{4,5},{5,4},{6,7},{7,6},{8,9},{9,8},{10,11... | collective-permute-start | bytes 393224 | tf_op jit(solution)/shard_map/ppermute | solution.py:32
  27.6 5.6 %collective-permute-start.1 = (f32[128,256]{1,0:T(8,128)S(1)}, f32[128,256]{1,0:T(8,128)S(1)}, u32[]{:S(2)}, u32[]{:S(2)}) collective-permute-start(f32[128,256]{1,0:T(8,128)S(1)} %add.9.refs_0_.refs_1_), channel_id=1, source_target_pairs={{0,2},{1,3},{2,0},{3,1},{4,6},{5,7},{6,4},{7,5},{8,10},{9,11},{10,... | collective-permute-start | bytes 393224 | tf_op jit(solution)/shard_map/ppermute | solution.py:32
  29.1 1.0 copy-start.5
  33.3 5.0 %collective-permute-start.2 = (f32[128,256]{1,0:T(8,128)S(1)}, f32[128,256]{1,0:T(8,128)S(1)}, u32[]{:S(2)}, u32[]{:S(2)}) collective-permute-start(f32[128,256]{1,0:T(8,128)S(1)} %embed_rows.1.refs_0_.emb_ref), channel_id=1, source_target_pairs={{0,4},{4,0},{8,12},{12,8},{16,20},{20,16},{24,28},{28,24},{1,5},{5... | collective-permute-start | bytes 393224 | tf_op jit(solution)/shard_map/ppermute | solution.py:32
  38.3 1.6 %collective-permute-start.3 = (f32[136,256]{1,0:T(8,128)S(1)}, f32[136,256]{1,0:T(8,128)S(1)}, u32[]{:S(2)}, u32[]{:S(2)}) collective-permute-start(f32[136,256]{1,0:T(8,128)S(1)} %logit_sum.1), channel_id=1, source_target_pairs={{0,1},{1,0},{2,3},{3,2},{4,5},{5,4},{6,7},{7,6},{8,9},{9,8},{10,11... | collective-permute-start | bytes 417800 | tf_op jit(solution)/shard_map/ppermute | solution.py:32
  39.9 6.7 %collective-permute-start.4 = (f32[136,256]{1,0:T(8,128)S(1)}, f32[136,256]{1,0:T(8,128)S(1)}, u32[]{:S(2)}, u32[]{:S(2)}) collective-permute-start(f32[136,256]{1,0:T(8,128)S(1)} %add.10.refs_3_), channel_id=1, source_target_pairs={{0,2},{1,3},{2,0},{3,1},{4,6},{5,7},{6,4},{7,5},{8,10},{9,11},{10,... | collective-permute-start | bytes 417800 | tf_op jit(solution)/shard_map/ppermute | solution.py:32
  41.5 5.1 %collective-permute-start.5 = (f32[4,48,128]{2,1,0:T(8,128)S(1)}, f32[4,48,128]{2,1,0:T(8,128)S(1)}, u32[]{:S(2)}, u32[]{:S(2)}) collective-permute-start(f32[4,48,128]{2,1,0:T(8,128)S(1)} %get-tuple-element.97), channel_id=1, source_target_pairs={{0,4},{4,0},{8,12},{12,8},{16,20},{20,16},{24,28},{28,24},{1,5},{5... | collective-permute-start | bytes 294920 | tf_op jit(solution)/shard_map/ppermute | solution.py:32
  42.2 4.4 %collective-permute-start.6 = (f32[80,128]{1,0:T(8,128)S(1)}, f32[80,128]{1,0:T(8,128)S(1)}, u32[]{:S(2)}, u32[]{:S(2)}) collective-permute-start(f32[80,128]{1,0:T(8,128)S(1)} %get-tuple-element.99), channel_id=1, source_target_pairs={{0,8},{4,12},{8,0},{12,4},{16,24},{20,28},{24,16},{28,20},{1,9},{5... | collective-permute-start | bytes 122888 | tf_op jit(solution)/shard_map/ppermute | solution.py:32
  42.6 5.6 %collective-permute-start.7 = (f32[80,128]{1,0:T(8,128)S(1)}, f32[80,128]{1,0:T(8,128)S(1)}, u32[]{:S(2)}, u32[]{:S(2)}) collective-permute-start(f32[80,128]{1,0:T(8,128)S(1)} %get-tuple-element.100), channel_id=1, source_target_pairs={{0,16},{4,20},{8,24},{12,28},{16,0},{20,4},{24,8},{28,12},{1,17},{... | collective-permute-start | bytes 122888 | tf_op jit(solution)/shard_map/ppermute | solution.py:32
  43.3 5.8 %collective-permute-start.8 = (f32[80,128]{1,0:T(8,128)S(1)}, f32[80,128]{1,0:T(8,128)S(1)}, u32[]{:S(2)}, u32[]{:S(2)}) collective-permute-start(f32[80,128]{1,0:T(8,128)S(1)} %get-tuple-element.101), channel_id=1, source_target_pairs={{0,24},{4,28},{8,16},{12,20},{16,8},{20,12},{24,0},{28,4},{1,25},{... | collective-permute-start | bytes 122888 | tf_op jit(solution)/shard_map/ppermute | solution.py:32
  49.6 1.9 %collective-permute-start.9 = (f32[2,128]{1,0:T(2,128)S(1)}, f32[2,128]{1,0:T(2,128)S(1)}, u32[]{:S(2)}, u32[]{:S(2)}) collective-permute-start(f32[2,128]{1,0:T(2,128)S(1)} %row_pass.2.refs_0_), channel_id=1, source_target_pairs={{0,1},{1,0},{2,3},{3,2},{4,5},{5,4},{6,7},{7,6},{8,9},{9,8},{10,11... | collective-permute-start | bytes 3080 | tf_op jit(solution)/shard_map/ppermute | solution.py:32
  49.6 3.6 %collective-permute-start.10 = (f32[2,128]{1,0:T(2,128)S(1)}, f32[2,128]{1,0:T(2,128)S(1)}, u32[]{:S(2)}, u32[]{:S(2)}) collective-permute-start(f32[2,128]{1,0:T(2,128)S(1)} %row_pass.2.refs_0_), channel_id=1, source_target_pairs={{0,2},{1,3},{2,0},{3,1},{4,6},{5,7},{6,4},{7,5},{8,10},{9,11},{10,... | collective-permute-start | bytes 3080 | tf_op jit(solution)/shard_map/ppermute | solution.py:32
  50.3 3.0 %collective-permute-start.11 = (f32[2,128]{1,0:T(2,128)S(1)}, f32[2,128]{1,0:T(2,128)S(1)}, u32[]{:S(2)}, u32[]{:S(2)}) collective-permute-start(f32[2,128]{1,0:T(2,128)S(1)} %row_pass.2.refs_0_), channel_id=1, source_target_pairs={{0,3},{1,2},{2,1},{3,0},{4,7},{5,6},{6,5},{7,4},{8,11},{9,10},{10,... | collective-permute-start | bytes 3080 | tf_op jit(solution)/shard_map/ppermute | solution.py:32
  53.8 7.2 %collective-permute-start.12 = (f32[80,128]{1,0:T(8,128)S(1)}, f32[80,128]{1,0:T(8,128)S(1)}, u32[]{:S(2)}, u32[]{:S(2)}) collective-permute-start(f32[80,128]{1,0:T(8,128)S(1)} %get-tuple-element.106), channel_id=1, source_target_pairs={{0,8},{4,12},{8,0},{12,4},{16,24},{20,28},{24,16},{28,20},{1,9},{5... | collective-permute-start | bytes 122888 | tf_op jit(solution)/shard_map/ppermute | solution.py:32
  54.8 8.0 %collective-permute-start.13 = (f32[80,128]{1,0:T(8,128)S(1)}, f32[80,128]{1,0:T(8,128)S(1)}, u32[]{:S(2)}, u32[]{:S(2)}) collective-permute-start(f32[80,128]{1,0:T(8,128)S(1)} %get-tuple-element.107), channel_id=1, source_target_pairs={{0,16},{4,20},{8,24},{12,28},{16,0},{20,4},{24,8},{28,12},{1,17},{... | collective-permute-start | bytes 122888 | tf_op jit(solution)/shard_map/ppermute | solution.py:32
  57.7 6.8 %collective-permute-start.14 = (f32[80,128]{1,0:T(8,128)S(1)}, f32[80,128]{1,0:T(8,128)S(1)}, u32[]{:S(2)}, u32[]{:S(2)}) collective-permute-start(f32[80,128]{1,0:T(8,128)S(1)} %get-tuple-element.108), channel_id=1, source_target_pairs={{0,24},{4,28},{8,16},{12,20},{16,8},{20,12},{24,0},{28,4},{1,25},{... | collective-permute-start | bytes 122888 | tf_op jit(solution)/shard_map/ppermute | solution.py:32
  64.9 16.0 %copy-start.8 = (s32[128]{0:T(128)S(1)}, s32[128]{0:T(128)}, u32[]{:S(2)}) copy-start(s32[128]{0:T(128)} %param.13) | copy-start | bytes 1540
  64.9 1.9 %collective-permute-start.15 = (f32[2,128]{1,0:T(2,128)S(1)}, f32[2,128]{1,0:T(2,128)S(1)}, u32[]{:S(2)}, u32[]{:S(2)}) collective-permute-start(f32[2,128]{1,0:T(2,128)S(1)} %row_pass.3.refs_0_), channel_id=1, source_target_pairs={{0,1},{1,0},{2,3},{3,2},{4,5},{5,4},{6,7},{7,6},{8,9},{9,8},{10,11... | collective-permute-start | bytes 3080 | tf_op jit(solution)/shard_map/ppermute | solution.py:32
  65.0 3.6 %collective-permute-start.16 = (f32[2,128]{1,0:T(2,128)S(1)}, f32[2,128]{1,0:T(2,128)S(1)}, u32[]{:S(2)}, u32[]{:S(2)}) collective-permute-start(f32[2,128]{1,0:T(2,128)S(1)} %row_pass.3.refs_0_), channel_id=1, source_target_pairs={{0,2},{1,3},{2,0},{3,1},{4,6},{5,7},{6,4},{7,5},{8,10},{9,11},{10,... | collective-permute-start | bytes 3080 | tf_op jit(solution)/shard_map/ppermute | solution.py:32
  66.5 3.0 %collective-permute-start.17 = (f32[2,128]{1,0:T(2,128)S(1)}, f32[2,128]{1,0:T(2,128)S(1)}, u32[]{:S(2)}, u32[]{:S(2)}) collective-permute-start(f32[2,128]{1,0:T(2,128)S(1)} %row_pass.3.refs_0_), channel_id=1, source_target_pairs={{0,3},{1,2},{2,1},{3,0},{4,7},{5,6},{6,5},{7,4},{8,11},{9,10},{10,... | collective-permute-start | bytes 3080 | tf_op jit(solution)/shard_map/ppermute | solution.py:32
  70.1 7.4 %collective-permute-start.18 = (f32[1,8,48,128]{3,2,1,0:T(8,128)S(1)}, f32[1,8,48,128]{3,2,1,0:T(8,128)S(1)}, u32[]{:S(2)}, u32[]{:S(2)}) collective-permute-start(f32[1,8,48,128]{3,2,1,0:T(8,128)S(1)} %columns_join.1), channel_id=1, source_target_pairs={{0,2},{1,3},{2,0},{3,1},{4,6},{5,7},{6,4},{7,5},{8,10},{9,11},{10,... | collective-permute-start | bytes 589832 | tf_op jit(solution)/shard_map/ppermute | solution.py:32
  70.8 6.8 %collective-permute-start.19 = (f32[32,128]{1,0:T(8,128)S(1)}, f32[32,128]{1,0:T(8,128)S(1)}, u32[]{:S(2)}, u32[]{:S(2)}) collective-permute-start(f32[32,128]{1,0:T(8,128)S(1)} %col_pass.3.refs_0_), channel_id=1, source_target_pairs={{0,8},{4,12},{8,0},{12,4},{16,24},{20,28},{24,16},{28,20},{1,9},{5... | collective-permute-start | bytes 49160 | tf_op jit(solution)/shard_map/ppermute | solution.py:32
  73.6 6.8 %collective-permute-start.20 = (f32[32,128]{1,0:T(8,128)S(1)}, f32[32,128]{1,0:T(8,128)S(1)}, u32[]{:S(2)}, u32[]{:S(2)}) collective-permute-start(f32[32,128]{1,0:T(8,128)S(1)} %col_pass.3.refs_0_), channel_id=1, source_target_pairs={{0,16},{4,20},{8,24},{12,28},{16,0},{20,4},{24,8},{28,12},{1,17},{... | collective-permute-start | bytes 49160 | tf_op jit(solution)/shard_map/ppermute | solution.py:32
  75.1 5.9 %collective-permute-start.21 = (f32[32,128]{1,0:T(8,128)S(1)}, f32[32,128]{1,0:T(8,128)S(1)}, u32[]{:S(2)}, u32[]{:S(2)}) collective-permute-start(f32[32,128]{1,0:T(8,128)S(1)} %col_pass.3.refs_0_), channel_id=1, source_target_pairs={{0,24},{4,28},{8,16},{12,20},{16,8},{20,12},{24,0},{28,4},{1,25},{... | collective-permute-start | bytes 49160 | tf_op jit(solution)/shard_map/ppermute | solution.py:32
  82.5 3.4 %collective-permute-start.23 = (f32[2,8,48,128]{3,2,1,0:T(8,128)S(1)}, f32[2,8,48,128]{3,2,1,0:T(8,128)S(1)}, u32[]{:S(2)}, u32[]{:S(2)}) collective-permute-start(f32[2,8,48,128]{3,2,1,0:T(8,128)S(1)} %pad_maximum_fusion.refs_0_), channel_id=1, source_target_pairs={{0,1},{1,0},{2,3},{3,2},{4,5},{5,4},{6,7},{7,6},{8,9},{9,8},{10,11... | collective-permute-start | bytes 1179656 | tf_op jit(solution)/shard_map/ppermute | solution.py:32
  82.6 1.8 %collective-permute-start.22 = (f32[72,256]{1,0:T(8,128)S(1)}, f32[72,256]{1,0:T(8,128)S(1)}, u32[]{:S(2)}, u32[]{:S(2)}) collective-permute-start(f32[72,256]{1,0:T(8,128)S(1)} %get-tuple-element.112), channel_id=1, source_target_pairs={{0,1},{1,0},{2,3},{3,2},{4,5},{5,4},{6,7},{7,6},{8,9},{9,8},{10,11... | collective-permute-start | bytes 221192 | tf_op jit(solution)/shard_map/ppermute | solution.py:32
  84.4 4.4 %collective-permute-start.24 = (f32[72,256]{1,0:T(8,128)S(1)}, f32[72,256]{1,0:T(8,128)S(1)}, u32[]{:S(2)}, u32[]{:S(2)}) collective-permute-start(f32[72,256]{1,0:T(8,128)S(1)} %add.11.refs_5_), channel_id=1, source_target_pairs={{0,2},{1,3},{2,0},{3,1},{4,6},{5,7},{6,4},{7,5},{8,10},{9,11},{10,... | collective-permute-start | bytes 221192 | tf_op jit(solution)/shard_map/ppermute | solution.py:32
  89.6 5.6 %collective-permute-start.28 = (f32[1,64,256]{2,1,0:T(8,128)S(1)}, f32[1,64,256]{2,1,0:T(8,128)S(1)}, u32[]{:S(2)}, u32[]{:S(2)}) collective-permute-start(f32[1,64,256]{2,1,0:T(8,128)S(1)} %bitcast.18), channel_id=1, source_target_pairs={{0,4},{4,0},{8,12},{12,8},{16,20},{20,16},{24,28},{28,24},{1,5},{5... | collective-permute-start | bytes 196616 | tf_op jit(solution)/shard_map/ppermute | solution.py:32
  90.8 8.1 %collective-permute-start.27 = (f32[64,256]{1,0:T(8,128)S(1)}, f32[64,256]{1,0:T(8,128)S(1)}, u32[]{:S(2)}, u32[]{:S(2)}) collective-permute-start(f32[64,256]{1,0:T(8,128)S(1)} %get-tuple-element.117), channel_id=1, source_target_pairs={{0,24},{4,28},{8,16},{12,20},{16,8},{20,12},{24,0},{28,4},{1,25},{... | collective-permute-start | bytes 196616 | tf_op jit(solution)/shard_map/ppermute | solution.py:32
  92.3 6.9 %collective-permute-start.26 = (f32[64,256]{1,0:T(8,128)S(1)}, f32[64,256]{1,0:T(8,128)S(1)}, u32[]{:S(2)}, u32[]{:S(2)}) collective-permute-start(f32[64,256]{1,0:T(8,128)S(1)} %get-tuple-element.117), channel_id=1, source_target_pairs={{0,16},{4,20},{8,24},{12,28},{16,0},{20,4},{24,8},{28,12},{1,17},{... | collective-permute-start | bytes 196616 | tf_op jit(solution)/shard_map/ppermute | solution.py:32
  93.3 5.9 %collective-permute-start.25 = (f32[64,256]{1,0:T(8,128)S(1)}, f32[64,256]{1,0:T(8,128)S(1)}, u32[]{:S(2)}, u32[]{:S(2)}) collective-permute-start(f32[64,256]{1,0:T(8,128)S(1)} %get-tuple-element.117), channel_id=1, source_target_pairs={{0,8},{4,12},{8,0},{12,4},{16,24},{20,28},{24,16},{28,20},{1,9},{5... | collective-permute-start | bytes 196616 | tf_op jit(solution)/shard_map/ppermute | solution.py:32
  95.2 4.0 %collective-permute-start.29 = (f32[1,64,256]{2,1,0:T(8,128)S(1)}, f32[1,64,256]{2,1,0:T(8,128)S(1)}, u32[]{:S(2)}, u32[]{:S(2)}) collective-permute-start(f32[1,64,256]{2,1,0:T(8,128)S(1)} %bitcast.19), channel_id=1, source_target_pairs={{0,1},{1,0},{2,3},{3,2},{4,5},{5,4},{6,7},{7,6},{8,9},{9,8},{10,11... | collective-permute-start | bytes 196616 | tf_op jit(solution)/shard_map/ppermute | solution.py:32
  95.2 4.1 %collective-permute-start.30 = (f32[1,64,256]{2,1,0:T(8,128)S(1)}, f32[1,64,256]{2,1,0:T(8,128)S(1)}, u32[]{:S(2)}, u32[]{:S(2)}) collective-permute-start(f32[1,64,256]{2,1,0:T(8,128)S(1)} %collective-permute-done.28.refs_7_), channel_id=1, source_target_pairs={{0,1},{1,0},{2,3},{3,2},{4,5},{5,4},{6,7},{7,6},{8,9},{9,8},{10,11... | collective-permute-start | bytes 196616 | tf_op jit(solution)/shard_map/ppermute | solution.py:32
  95.7 2.2 %copy-start = (f32[1024,1024]{1,0:T(8,128)S(1)}, f32[1024,1024]{1,0:T(8,128)}, u32[]{:S(2)}) copy-start(f32[1024,1024]{1,0:T(8,128)} %all-gather.2.cloned.1.call-done) | copy-start | bytes 12582916
  97.9 3.8 %copy-start.1 = (f32[1024,1024]{1,0:T(8,128)S(1)}, f32[1024,1024]{1,0:T(8,128)}, u32[]{:S(2)}) copy-start(f32[1024,1024]{1,0:T(8,128)} %all-gather.2.cloned.1.call-done) | copy-start | bytes 12582916
  99.3 1.2 %collective-permute-start.32 = (f32[1,64]{1,0:T(1,128)S(1)}, f32[1,64]{1,0:T(1,128)S(1)}, u32[]{:S(2)}, u32[]{:S(2)}) collective-permute-start(f32[1,64]{1,0:T(1,128)S(1)} %get-tuple-element.129), channel_id=1, source_target_pairs={{0,1},{1,0},{2,3},{3,2},{4,5},{5,4},{6,7},{7,6},{8,9},{9,8},{10,11... | collective-permute-start | bytes 776 | tf_op jit(solution)/shard_map/ppermute | solution.py:32
  99.3 7.3 %collective-permute-start.31 = (f32[3,64,256]{2,1,0:T(8,128)S(1)}, f32[3,64,256]{2,1,0:T(8,128)S(1)}, u32[]{:S(2)}, u32[]{:S(2)}) collective-permute-start(f32[3,64,256]{2,1,0:T(8,128)S(1)} %pad_maximum_fusion.1.refs_8_), channel_id=1, source_target_pairs={{0,4},{4,0},{8,12},{12,8},{16,20},{20,16},{24,28},{28,24},{1,5},{5... | collective-permute-start | bytes 589832 | tf_op jit(solution)/shard_map/ppermute | solution.py:32
  100.3 1.4 %collective-permute-start.33 = (f32[3,64,256]{2,1,0:T(8,128)S(1)}, f32[3,64,256]{2,1,0:T(8,128)S(1)}, u32[]{:S(2)}, u32[]{:S(2)}) collective-permute-start(f32[3,64,256]{2,1,0:T(8,128)S(1)} %pad_maximum_fusion.1.refs_8_), channel_id=1, source_target_pairs={{0,1},{1,0},{2,3},{3,2},{4,5},{5,4},{6,7},{7,6},{8,9},{9,8},{10,11... | collective-permute-start | bytes 589832 | tf_op jit(solution)/shard_map/ppermute | solution.py:32
  106.7 1.4 %collective-permute-start.34 = (f32[3,64,256]{2,1,0:T(8,128)S(1)}, f32[3,64,256]{2,1,0:T(8,128)S(1)}, u32[]{:S(2)}, u32[]{:S(2)}) collective-permute-start(f32[3,64,256]{2,1,0:T(8,128)S(1)} %collective-permute-done.31.refs_8_), channel_id=1, source_target_pairs={{0,1},{1,0},{2,3},{3,2},{4,5},{5,4},{6,7},{7,6},{8,9},{9,8},{10,11... | collective-permute-start | bytes 589832 | tf_op jit(solution)/shard_map/ppermute | solution.py:32
Sparse Core Ops, SparseCore 0:
  11.7 79.1 all-gather.1

commit v6 on v5

--- a/solution.py
+++ b/solution.py
@@ -216,43 +216,33 @@
 def score_kernel(n, *refs):
     piece, u_ref = refs[:2]
     code_ref, col_ref = refs[-2:] if n == 0 else refs[4:6]
-    j = pl.program_id(0)
-    code = jnp.exp(dot(piece[...].astype(BF16), u_ref[...], ((1,), (1,))) / balancing_epsilon)
-    code_ref[...] = code
-    put_blocks(col_ref, 0, jnp.sum(code, axis=0, keepdims=True))
+    low = piece[...].astype(BF16)
+    protos = u_ref.shape[0]
+    step = min(512, protos)
+    for j in range(protos // step):
+        at = slice(j * step, (j + 1) * step)
+        code = jnp.exp(dot(low, u_ref[at, :], ((1,), (1,))) / balancing_epsilon)
+        code_ref[:, at] = code
+        put_blocks(col_ref, j * step // 128, jnp.sum(code, axis=0, keepdims=True))
     if n:
         col_ref[...] += refs[2][...]
-        size = col_ref.shape[0]
-        at = pl.ds(pl.multiple_of(j * size, size), size)
+        lines = col_ref.shape[0]
         for k, out in enumerate(refs[6:]):
-            out[at, :] = col_ref[...]
-
-            @pl.when(j == 0)
-            def _():
-                out[out.shape[0] - refs[3].shape[1] :, :] = refs[3][k + 1]
+            out[0:lines, :] = col_ref[...]
+            out[lines:, :] = refs[3][k + 1]
 
 
 def score(piece, units, more=None):
     rows, width = piece.shape
     protos = units.shape[0]
-    blk = min(1024, protos)
-    lines, step = protos // 128, blk // 128
-    by_step = pl.BlockSpec((step, 128), lambda j: (j, 0))
-    in_specs = [whole((rows, width)), pl.BlockSpec((blk, width), lambda j: (j, 0))]
-    out_specs = [pl.BlockSpec((rows, blk), lambda j: (0, j)), by_step]
+    lines = protos // 128
+    n, extra = 0, ()
     out_shape = [jax.ShapeDtypeStruct((rows, protos), F32), jax.ShapeDtypeStruct((lines, 128), F32)]
-    n, extra = 0, ()
     if more is not None:
         n, extra = more[1].shape[0] - 1, more
-        sent = (lines + more[1].shape[1], 128)
-        in_specs += [by_step, whole(more[1].shape)]
-        out_specs += [whole(sent)] * n
-        out_shape += [jax.ShapeDtypeStruct(sent, F32)] * n
+        out_shape += [jax.ShapeDtypeStruct((lines + more[1].shape[1], 128), F32)] * n
     return pl.pallas_call(
         functools.partial(score_kernel, n),
-        grid=(protos // blk,),
-        in_specs=in_specs,
-        out_specs=out_specs,
         out_shape=out_shape,
         compiler_params=params(),
         cost_estimate=cost(2 * rows * protos * width, 4 * rows * protos, rows * protos),
@@ -272,35 +262,25 @@
     out_ref[rows : rows + 1, 0:rows] = lane_row
 
 
-def logit_kernel(emb_ref, u_ref, out_ref, total, mass):
-    j = pl.program_id(0)
-
-    @pl.when(j == 0)
-    def _():
-        total[...] = jnp.zeros_like(total)
-        mass[...] = jnp.zeros_like(mass)
-
-    units = u_ref[...]
-    logits = jnp.exp(dot(emb_ref[...].astype(BF16), units, ((1,), (1,))) / sharpness_divisor)
-    total[...] += jnp.dot(logits.astype(BF16), units, preferred_element_type=F32)
-    mass[...] += jnp.sum(logits, axis=1, keepdims=True)
-
-    @pl.when(j == pl.num_programs(0) - 1)
-    def _():
-        pack(total[...], to_lanes(mass[...]), out_ref)
+def logit_kernel(emb_ref, u_ref, out_ref):
+    low = emb_ref[...].astype(BF16)
+    protos = u_ref.shape[0]
+    step = min(512, protos)
+    total, mass = 0.0, 0.0
+    for j in range(protos // step):
+        units = u_ref[j * step : (j + 1) * step, :]
+        logits = jnp.exp(dot(low, units, ((1,), (1,))) / sharpness_divisor)
+        total = total + jnp.dot(logits.astype(BF16), units, preferred_element_type=F32)
+        mass = mass + jnp.sum(logits, axis=1, keepdims=True)
+    pack(total, to_lanes(mass), out_ref)
 
 
 def logit_sum(embedded, units):
     rows, width = embedded.shape
     protos = units.shape[0]
-    blk = min(1024, protos)
     return pl.pallas_call(
         logit_kernel,
-        grid=(protos // blk,),
-        in_specs=[whole((rows, width)), pl.BlockSpec((blk, width), lambda j: (j, 0))],
-        out_specs=whole((rows + 8, width)),
         out_shape=jax.ShapeDtypeStruct((rows + 8, width), F32),
-        scratch_shapes=[pltpu.VMEM((rows, width), F32), pltpu.VMEM((rows, 1), F32)],
         compiler_params=params(),
         cost_estimate=cost(4 * rows * protos * width, 2 * protos * width, rows * protos),
         name="logit_sum",

time: 119 us -> 119 us (level)
  waiting for transfers between devices: 37 us -> 39.3 us
  Pallas kernels: 23 us -> 21 us
    ppermute x35, waiting for transfers between devices: 29.9 us -> 32.2 us  [swap(): return lax.ppermute(v, axis, [(i, i ^ mask) for i in range(n)])]
    pallas_call x3, Pallas kernels: 5.11 us -> 3.09 us  [the longest x2 1.68 us: score(): pl.pallas_call(functools.partial(score_kernel, n), out_shape=out_shape, c...]
  transfers between devices with their start and end apart: 37 -> 37, of which waited for: 21 -> 23; matrix products, arithmetic and copies ran while one was open for 1% -> 1% of each run, Pallas kernels for 14% -> 12%
where the time goes in v6:
time: 119 us
  starting transfers between devices  39.9 us (34%)
  waiting for transfers between devices  39.3 us (33%)
  Pallas kernels  21 us (18%)
  between operations  14.3 us (12%)
  local copies, waits for them, and re-layouts  3.36 us (3%)
    ppermute x35, starting transfers between devices, swap(): return lax.ppermute(v, axis, [(i, i ^ mask) for i in range(n)])  32.6 us
    ppermute x35, waiting for transfers between devices, swap(): return lax.ppermute(v, axis, [(i, i ^ mask) for i in range(n)])  32.2 us
    all_to_all x1, starting transfers between devices, body(): lax.all_to_all(moments, 'batch', 0, 0)  7.29 us
    all_to_all x1, waiting for transfers between devices, body(): lax.all_to_all(moments, 'batch', 0, 0)  7.01 us
    pallas_call x2, Pallas kernels, tail_call(): pl.pallas_call(functools.partial(kernel, n_batch, len(grads)), in_specs=[...  6.69 us
    unnamed x18, local copies, waits for them, and re-layouts  3.36 us
    pallas_call x1, Pallas kernels, first_layer(): pl.pallas_call(first_kernel, in_specs=[pl.BlockSpec(memory_space=pl.ANY)]...  3.11 us
  transfers between devices with their start and end apart: 37, of which 23 were waited for; matrix products, arithmetic and copies ran while one was open for 1% of the time, Pallas kernels for 12%

profile of v6, /device:TPU:0, one launch (start us, length us, event | category | flops | bytes accessed | tf_op | source)
XLA Modules:
  0.0 118.6 jit_solution(4373927400789282722)
XLA Ops:
  7.2 1.1 copy-done.4
  8.4 3.1 %first_layer.1 = (f32[128,1024]{1,0:T(8,128)}, f32[128,1024]{1,0:T(8,128)S(1)}, f32[8,1,2048]{2,1,0:T(1,128)}) custom-call(bf16[128,1536]{1,0:T(8,128)(2,1)S(1)} %copy-done.4, bf16[1536,1024]{1,0:T(8,128)(2,1)} %w_hbm.1), custom_call_target="tpu_custom_call" | custom-call | flops 402653184 | bytes 3670016 | tf_op jit(solution)/shard_map/first_layer/pallas_call | solution.py:125
  11.5 7.3 %all-to-all-start = ((f32[8,1,2048]{2,1,0:T(1,128)}), f32[8,1,2048]{2,1,0:T(1,128)S(1)}, u32[]{:S(2)}, u32[]{:S(2)}) async-start(f32[8,1,2048]{2,1,0:T(1,128)} %get-tuple-element.76), calls=%async_computation | async-start | bytes 131072 | tf_op jit(solution)/shard_map/all_to_all | solution.py:696
  18.8 7.0 %all-to-all-done.refs_0_ = f32[8,1,2048]{2,1,0:T(1,128)S(1)} async-done(((f32[8,1,2048]{2,1,0:T(1,128)}), f32[8,1,2048]{2,1,0:T(1,128)S(1)}, u32[]{:S(2)}, u32[]{:S(2)}) %all-to-all-start) | async-done | bytes 65568 | tf_op jit(solution)/shard_map/all_to_all | solution.py:696
  26.2 1.3 %collective-permute-done = f32[128,256]{1,0:T(8,128)S(1)} collective-permute-done((f32[128,256]{1,0:T(8,128)S(1)}, f32[128,256]{1,0:T(8,128)S(1)}, u32[]{:S(2)}, u32[]{:S(2)}) %collective-permute-start) | collective-permute-done | bytes 131104 | tf_op jit(solution)/shard_map/ppermute | solution.py:32
  27.6 1.6 %collective-permute-start.1 = (f32[128,256]{1,0:T(8,128)S(1)}, f32[128,256]{1,0:T(8,128)S(1)}, u32[]{:S(2)}, u32[]{:S(2)}) collective-permute-start(f32[128,256]{1,0:T(8,128)S(1)} %add.9.refs_0_.refs_1_), channel_id=1, source_target_pairs={{0,2},{1,3},{2,0},{3,1},{4,6},{5,7},{6,4},{7,5},{8,10},{9,11},{10,... | collective-permute-start | bytes 393224 | tf_op jit(solution)/shard_map/ppermute | solution.py:32
  29.1 0.9 unit_rows.1.refs_1_.u_ref.refs_5_
  30.1 1.0 columns_pick.1
  31.1 2.0 %collective-permute-done.1.refs_1_.refs_2_ = f32[128,256]{1,0:T(8,128)S(1)} collective-permute-done((f32[128,256]{1,0:T(8,128)S(1)}, f32[128,256]{1,0:T(8,128)S(1)}, u32[]{:S(2)}, u32[]{:S(2)}) %collective-permute-start.1) | collective-permute-done | bytes 131104 | tf_op jit(solution)/shard_map/ppermute | solution.py:32
  33.6 0.8 score.2
  34.5 1.4 %logit_sum.1 = f32[136,256]{1,0:T(8,128)S(1)} custom-call(f32[128,256]{1,0:T(8,128)S(1)} %embed_rows.1.refs_0_.emb_ref, bf16[4096,256]{1,0:T(8,128)(2,1)S(1)} %unit_rows.1.refs_1_.u_ref.refs_5_), custom_call_target="tpu_custom_call" | custom-call | flops 536870912 | bytes 2097152 | tf_op jit(solution)/shard_map/logit_sum/pallas_call | solution.py:281
  35.9 2.4 %collective-permute-done.2.refs_0_ = f32[128,256]{1,0:T(8,128)S(1)} collective-permute-done((f32[128,256]{1,0:T(8,128)S(1)}, f32[128,256]{1,0:T(8,128)S(1)}, u32[]{:S(2)}, u32[]{:S(2)}) %collective-permute-start.2) | collective-permute-done | bytes 131104 | tf_op jit(solution)/shard_map/ppermute | solution.py:32
  38.3 0.8 score.3
  39.7 1.6 %collective-permute-start.4 = (f32[136,256]{1,0:T(8,128)S(1)}, f32[136,256]{1,0:T(8,128)S(1)}, u32[]{:S(2)}, u32[]{:S(2)}) collective-permute-start(f32[136,256]{1,0:T(8,128)S(1)} %add.10.refs_3_), channel_id=1, source_target_pairs={{0,2},{1,3},{2,0},{3,1},{4,6},{5,7},{6,4},{7,5},{8,10},{9,11},{10,... | collective-permute-start | bytes 417800 | tf_op jit(solution)/shard_map/ppermute | solution.py:32
  41.5 0.8 collective-permute-start.6
  43.1 2.8 %collective-permute-start.8 = (f32[80,128]{1,0:T(8,128)S(1)}, f32[80,128]{1,0:T(8,128)S(1)}, u32[]{:S(2)}, u32[]{:S(2)}) collective-permute-start(f32[80,128]{1,0:T(8,128)S(1)} %get-tuple-element.101), channel_id=1, source_target_pairs={{0,24},{4,28},{8,16},{12,20},{16,8},{20,12},{24,0},{28,4},{1,25},{... | collective-permute-start | bytes 122888 | tf_op jit(solution)/shard_map/ppermute | solution.py:32
  46.0 1.4 %collective-permute-done.7.refs_2_ = f32[80,128]{1,0:T(8,128)S(1)} collective-permute-done((f32[80,128]{1,0:T(8,128)S(1)}, f32[80,128]{1,0:T(8,128)S(1)}, u32[]{:S(2)}, u32[]{:S(2)}) %collective-permute-start.7) | collective-permute-done | bytes 40992 | tf_op jit(solution)/shard_map/ppermute | solution.py:32
  47.4 1.5 %collective-permute-done.8.refs_3_.refs_4_ = f32[80,128]{1,0:T(8,128)S(1)} collective-permute-done((f32[80,128]{1,0:T(8,128)S(1)}, f32[80,128]{1,0:T(8,128)S(1)}, u32[]{:S(2)}, u32[]{:S(2)}) %collective-permute-start.8) | collective-permute-done | bytes 40992 | tf_op jit(solution)/shard_map/ppermute | solution.py:32
  50.0 1.3 %collective-permute-start.11 = (f32[2,128]{1,0:T(2,128)S(1)}, f32[2,128]{1,0:T(2,128)S(1)}, u32[]{:S(2)}, u32[]{:S(2)}) collective-permute-start(f32[2,128]{1,0:T(2,128)S(1)} %row_pass.2.refs_0_), channel_id=1, source_target_pairs={{0,3},{1,2},{2,1},{3,0},{4,7},{5,6},{6,5},{7,4},{8,11},{9,10},{10,... | collective-permute-start | bytes 3080 | tf_op jit(solution)/shard_map/ppermute | solution.py:32
  51.3 1.8 %collective-permute-done.10.refs_2_ = f32[2,128]{1,0:T(2,128)S(1)} collective-permute-done((f32[2,128]{1,0:T(2,128)S(1)}, f32[2,128]{1,0:T(2,128)S(1)}, u32[]{:S(2)}, u32[]{:S(2)}) %collective-permute-start.10) | collective-permute-done | bytes 1056 | tf_op jit(solution)/shard_map/ppermute | solution.py:32
  53.7 3.4 %collective-permute-start.13 = (f32[80,128]{1,0:T(8,128)S(1)}, f32[80,128]{1,0:T(8,128)S(1)}, u32[]{:S(2)}, u32[]{:S(2)}) collective-permute-start(f32[80,128]{1,0:T(8,128)S(1)} %get-tuple-element.107), channel_id=1, source_target_pairs={{0,16},{4,20},{8,24},{12,28},{16,0},{20,4},{24,8},{28,12},{1,17},{... | collective-permute-start | bytes 122888 | tf_op jit(solution)/shard_map/ppermute | solution.py:32
  57.1 1.0 collective-permute-start.14
  58.1 2.9 %collective-permute-done.12.refs_1_ = f32[80,128]{1,0:T(8,128)S(1)} collective-permute-done((f32[80,128]{1,0:T(8,128)S(1)}, f32[80,128]{1,0:T(8,128)S(1)}, u32[]{:S(2)}, u32[]{:S(2)}) %collective-permute-start.12) | collective-permute-done | bytes 40992 | tf_op jit(solution)/shard_map/ppermute | solution.py:32
  60.9 2.3 %collective-permute-done.13.refs_2_.refs_3_ = f32[80,128]{1,0:T(8,128)S(1)} collective-permute-done((f32[80,128]{1,0:T(8,128)S(1)}, f32[80,128]{1,0:T(8,128)S(1)}, u32[]{:S(2)}, u32[]{:S(2)}) %collective-permute-start.13) | collective-permute-done | bytes 40992 | tf_op jit(solution)/shard_map/ppermute | solution.py:32
  64.3 1.5 %collective-permute-start.16 = (f32[2,128]{1,0:T(2,128)S(1)}, f32[2,128]{1,0:T(2,128)S(1)}, u32[]{:S(2)}, u32[]{:S(2)}) collective-permute-start(f32[2,128]{1,0:T(2,128)S(1)} %row_pass.3.refs_0_), channel_id=1, source_target_pairs={{0,2},{1,3},{2,0},{3,1},{4,6},{5,7},{6,4},{7,5},{8,10},{9,11},{10,... | collective-permute-start | bytes 3080 | tf_op jit(solution)/shard_map/ppermute | solution.py:32
  66.2 1.8 %collective-permute-done.16.refs_2_ = f32[2,128]{1,0:T(2,128)S(1)} collective-permute-done((f32[2,128]{1,0:T(2,128)S(1)}, f32[2,128]{1,0:T(2,128)S(1)}, u32[]{:S(2)}, u32[]{:S(2)}) %collective-permute-start.16) | collective-permute-done | bytes 1056 | tf_op jit(solution)/shard_map/ppermute | solution.py:32
  68.0 0.9 collective-permute-done.17.refs_3_
  70.1 3.3 %collective-permute-start.19 = (f32[32,128]{1,0:T(8,128)S(1)}, f32[32,128]{1,0:T(8,128)S(1)}, u32[]{:S(2)}, u32[]{:S(2)}) collective-permute-start(f32[32,128]{1,0:T(8,128)S(1)} %col_pass.3.refs_0_), channel_id=1, source_target_pairs={{0,8},{4,12},{8,0},{12,4},{16,24},{20,28},{24,16},{28,20},{1,9},{5... | collective-permute-start | bytes 49160 | tf_op jit(solution)/shard_map/ppermute | solution.py:32
  73.4 1.3 %collective-permute-start.20 = (f32[32,128]{1,0:T(8,128)S(1)}, f32[32,128]{1,0:T(8,128)S(1)}, u32[]{:S(2)}, u32[]{:S(2)}) collective-permute-start(f32[32,128]{1,0:T(8,128)S(1)} %col_pass.3.refs_0_), channel_id=1, source_target_pairs={{0,16},{4,20},{8,24},{12,28},{16,0},{20,4},{24,8},{28,12},{1,17},{... | collective-permute-start | bytes 49160 | tf_op jit(solution)/shard_map/ppermute | solution.py:32
  74.6 1.5 %collective-permute-start.21 = (f32[32,128]{1,0:T(8,128)S(1)}, f32[32,128]{1,0:T(8,128)S(1)}, u32[]{:S(2)}, u32[]{:S(2)}) collective-permute-start(f32[32,128]{1,0:T(8,128)S(1)} %col_pass.3.refs_0_), channel_id=1, source_target_pairs={{0,24},{4,28},{8,16},{12,20},{16,8},{20,12},{24,0},{28,4},{1,25},{... | collective-permute-start | bytes 49160 | tf_op jit(solution)/shard_map/ppermute | solution.py:32
  76.1 0.8 collective-permute-done.18
  76.9 1.8 %collective-permute-done.20.refs_2_ = f32[32,128]{1,0:T(8,128)S(1)} collective-permute-done((f32[32,128]{1,0:T(8,128)S(1)}, f32[32,128]{1,0:T(8,128)S(1)}, u32[]{:S(2)}, u32[]{:S(2)}) %collective-permute-start.20) | collective-permute-done | bytes 16416 | tf_op jit(solution)/shard_map/ppermute | solution.py:32
  78.7 1.8 %collective-permute-done.21.refs_3_ = f32[32,128]{1,0:T(8,128)S(1)} collective-permute-done((f32[32,128]{1,0:T(8,128)S(1)}, f32[32,128]{1,0:T(8,128)S(1)}, u32[]{:S(2)}, u32[]{:S(2)}) %collective-permute-start.21) | collective-permute-done | bytes 16416 | tf_op jit(solution)/shard_map/ppermute | solution.py:32
  80.5 1.5 %target_sum.1 = (f32[72,256]{1,0:T(8,128)S(1)}, f32[72,256]{1,0:T(8,128)S(1)}) custom-call(f32[32,128]{1,0:T(8,128)S(1)} %col_pass.3.refs_0_, f32[32,128]{1,0:T(8,128)S(1)} %collective-permute-done.19.refs_1_, f32[32,128]{1,0:T(8,128)S(1)} %collective-permute-done.20.refs_2_, f32[32,128]{1,0:T(8,128)S(1)} %collective-permute-done.21.refs_3_, ...), custom_call_target="tpu_custom_call" | custom-call | flops 268435456 | bytes 4194304 | tf_op jit(solution)/shard_map/target_sum/pallas_call | solution.py:368
  82.6 1.3 %collective-permute-done.22 = f32[72,256]{1,0:T(8,128)S(1)} collective-permute-done((f32[72,256]{1,0:T(8,128)S(1)}, f32[72,256]{1,0:T(8,128)S(1)}, u32[]{:S(2)}, u32[]{:S(2)}) %collective-permute-start.22) | collective-permute-done | bytes 73760 | tf_op jit(solution)/shard_map/ppermute | solution.py:32
  84.0 1.5 %collective-permute-start.24 = (f32[72,256]{1,0:T(8,128)S(1)}, f32[72,256]{1,0:T(8,128)S(1)}, u32[]{:S(2)}, u32[]{:S(2)}) collective-permute-start(f32[72,256]{1,0:T(8,128)S(1)} %add.11.refs_5_), channel_id=1, source_target_pairs={{0,2},{1,3},{2,0},{3,1},{4,6},{5,7},{6,4},{7,5},{8,10},{9,11},{10,... | collective-permute-start | bytes 221192 | tf_op jit(solution)/shard_map/ppermute | solution.py:32
  86.1 2.3 %collective-permute-done.24.refs_6_ = f32[72,256]{1,0:T(8,128)S(1)} collective-permute-done((f32[72,256]{1,0:T(8,128)S(1)}, f32[72,256]{1,0:T(8,128)S(1)}, u32[]{:S(2)}, u32[]{:S(2)}) %collective-permute-start.24) | collective-permute-done | bytes 73760 | tf_op jit(solution)/shard_map/ppermute | solution.py:32
  88.4 0.8 loss_grad.1
  89.1 1.7 %collective-permute-start.28 = (f32[1,64,256]{2,1,0:T(8,128)S(1)}, f32[1,64,256]{2,1,0:T(8,128)S(1)}, u32[]{:S(2)}, u32[]{:S(2)}) collective-permute-start(f32[1,64,256]{2,1,0:T(8,128)S(1)} %bitcast.18), channel_id=1, source_target_pairs={{0,4},{4,0},{8,12},{12,8},{16,20},{20,16},{24,28},{28,24},{1,5},{5... | collective-permute-start | bytes 196616 | tf_op jit(solution)/shard_map/ppermute | solution.py:32
  90.8 1.3 %collective-permute-start.27 = (f32[64,256]{1,0:T(8,128)S(1)}, f32[64,256]{1,0:T(8,128)S(1)}, u32[]{:S(2)}, u32[]{:S(2)}) collective-permute-start(f32[64,256]{1,0:T(8,128)S(1)} %get-tuple-element.117), channel_id=1, source_target_pairs={{0,24},{4,28},{8,16},{12,20},{16,8},{20,12},{24,0},{28,4},{1,25},{... | collective-permute-start | bytes 196616 | tf_op jit(solution)/shard_map/ppermute | solution.py:32
  92.2 1.3 %collective-permute-start.26 = (f32[64,256]{1,0:T(8,128)S(1)}, f32[64,256]{1,0:T(8,128)S(1)}, u32[]{:S(2)}, u32[]{:S(2)}) collective-permute-start(f32[64,256]{1,0:T(8,128)S(1)} %get-tuple-element.117), channel_id=1, source_target_pairs={{0,16},{4,20},{8,24},{12,28},{16,0},{20,4},{24,8},{28,12},{1,17},{... | collective-permute-start | bytes 196616 | tf_op jit(solution)/shard_map/ppermute | solution.py:32
  93.4 1.8 %collective-permute-start.25 = (f32[64,256]{1,0:T(8,128)S(1)}, f32[64,256]{1,0:T(8,128)S(1)}, u32[]{:S(2)}, u32[]{:S(2)}) collective-permute-start(f32[64,256]{1,0:T(8,128)S(1)} %get-tuple-element.117), channel_id=1, source_target_pairs={{0,8},{4,12},{8,0},{12,4},{16,24},{20,28},{24,16},{28,20},{1,9},{5... | collective-permute-start | bytes 196616 | tf_op jit(solution)/shard_map/ppermute | solution.py:32
  95.7 2.2 %copy-done = f32[1024,1024]{1,0:T(8,128)S(1)} copy-done((f32[1024,1024]{1,0:T(8,128)S(1)}, f32[1024,1024]{1,0:T(8,128)}, u32[]{:S(2)}) %copy-start) | copy-done | bytes 4194328
  97.9 1.0 flat_sums.1
  101.3 3.1 %tail_near.1 = (f32[192,1024]{1,0:T(8,128)S(1)}, f32[32,1024]{1,0:T(8,128)S(1)}, f32[2,8,1024]{2,1,0:T(8,128)S(1)}) custom-call(s32[3]{0:T(128)S(1)} %pad_add_fusion.at_ref.refs_7_.refs_0_, f32[8,128,1024]{2,1,0:T(8,128)S(1)} %bitcast.16, bf16[8,192,128]{2,1,0:T(8,128)(2,1)S(1)} %columns_all.1.cols_ref.refs_2_, ...), custom_call_target="tpu_custom_call" | custom-call | flops 536870912 | bytes 2097152 | tf_op jit(solution)/shard_map/tail_near/pallas_call | solution.py:583
  104.3 2.3 %collective-permute-done.31.refs_8_ = f32[3,64,256]{2,1,0:T(8,128)S(1)} collective-permute-done((f32[3,64,256]{2,1,0:T(8,128)S(1)}, f32[3,64,256]{2,1,0:T(8,128)S(1)}, u32[]{:S(2)}, u32[]{:S(2)}) %collective-permute-start.31) | collective-permute-done | bytes 196640 | tf_op jit(solution)/shard_map/ppermute | solution.py:32
  106.7 1.4 %collective-permute-done.34.refs_10_ = f32[3,64,256]{2,1,0:T(8,128)S(1)} collective-permute-done((f32[3,64,256]{2,1,0:T(8,128)S(1)}, f32[3,64,256]{2,1,0:T(8,128)S(1)}, u32[]{:S(2)}, u32[]{:S(2)}) %collective-permute-start.34) | collective-permute-done | bytes 196640 | tf_op jit(solution)/shard_map/ppermute | solution.py:32
  108.1 3.6 %tail_far.1 = (f32[192,1024]{1,0:T(8,128)}, f32[32,1024]{1,0:T(8,128)}, f32[1,1024]{1,0:T(1,128)}, f32[1,1024]{1,0:T(1,128)}) custom-call(s32[3]{0:T(128)S(1)} %pad_add_fusion.at_ref.refs_7_.refs_0_, f32[8,128,1024]{2,1,0:T(8,128)S(1)} %bitcast.17, bf16[8,192,128]{2,1,0:T(8,128)(2,1)S(1)} %columns_all.1.cols_ref.refs_2_, ...), custom_call_target="tpu_custom_call" | custom-call | flops 536870912 | bytes 2097152 | tf_op jit(solution)/shard_map/tail_far/pallas_call | solution.py:583
  (72 shorter events, 11.0 us)
Async XLA Ops:
  7.2 18.7 %copy-start.2 = (bf16[1024,256]{1,0:T(8,128)(2,1)S(1)}, bf16[1024,256]{1,0:T(8,128)(2,1)}, u32[]{:S(2)}) copy-start(bf16[1024,256]{1,0:T(8,128)(2,1)} %refs_6_.3) | copy-start | bytes 1572868
  7.2 21.9 %copy-start.3 = (bf16[4096,256]{1,0:T(8,128)(2,1)S(1)}, bf16[4096,256]{1,0:T(8,128)(2,1)}, u32[]{:S(2)}) copy-start(bf16[4096,256]{1,0:T(8,128)(2,1)} %p_ref.1) | copy-start | bytes 6291460
  7.2 88.5 %all-gather.2.cloned.1.call-start = ((), (), s32[]{:S(2)}) async-start(), calls=%async_computation.1 | async-start | bytes 4718592 | tf_op jit(solution)/shard_map/all_gather | solution.py:695
  7.2 1.1 copy-start.4
  8.4 17.5 %copy-start.6 = (f32[1024]{0:T(1024)S(1)}, f32[1024]{0:T(1024)}, u32[]{:S(2)}) copy-start(f32[1024]{0:T(1024)} %param.9) | copy-start | bytes 12292
  8.4 17.5 %copy-start.7 = (f32[1024]{0:T(1024)S(1)}, f32[1024]{0:T(1024)}, u32[]{:S(2)}) copy-start(f32[1024]{0:T(1024)} %param.10) | copy-start | bytes 12292
  11.5 14.3 %all-to-all-start = ((f32[8,1,2048]{2,1,0:T(1,128)}), f32[8,1,2048]{2,1,0:T(1,128)S(1)}, u32[]{:S(2)}, u32[]{:S(2)}) async-start(f32[8,1,2048]{2,1,0:T(1,128)} %get-tuple-element.76), calls=%async_computation | async-start | bytes 131072 | tf_op jit(solution)/shard_map/all_to_all | solution.py:696
  26.1 1.4 %collective-permute-start = (f32[128,256]{1,0:T(8,128)S(1)}, f32[128,256]{1,0:T(8,128)S(1)}, u32[]{:S(2)}, u32[]{:S(2)}) collective-permute-start(f32[128,256]{1,0:T(8,128)S(1)} %get-tuple-element.79), channel_id=1, source_target_pairs={{0,1},{1,0},{2,3},{3,2},{4,5},{5,4},{6,7},{7,6},{8,9},{9,8},{10,11... | collective-permute-start | bytes 393224 | tf_op jit(solution)/shard_map/ppermute | solution.py:32
  27.6 5.6 %collective-permute-start.1 = (f32[128,256]{1,0:T(8,128)S(1)}, f32[128,256]{1,0:T(8,128)S(1)}, u32[]{:S(2)}, u32[]{:S(2)}) collective-permute-start(f32[128,256]{1,0:T(8,128)S(1)} %add.9.refs_0_.refs_1_), channel_id=1, source_target_pairs={{0,2},{1,3},{2,0},{3,1},{4,6},{5,7},{6,4},{7,5},{8,10},{9,11},{10,... | collective-permute-start | bytes 393224 | tf_op jit(solution)/shard_map/ppermute | solution.py:32
  29.1 1.0 copy-start.5
  33.3 5.0 %collective-permute-start.2 = (f32[128,256]{1,0:T(8,128)S(1)}, f32[128,256]{1,0:T(8,128)S(1)}, u32[]{:S(2)}, u32[]{:S(2)}) collective-permute-start(f32[128,256]{1,0:T(8,128)S(1)} %embed_rows.1.refs_0_.emb_ref), channel_id=1, source_target_pairs={{0,4},{4,0},{8,12},{12,8},{16,20},{20,16},{24,28},{28,24},{1,5},{5... | collective-permute-start | bytes 393224 | tf_op jit(solution)/shard_map/ppermute | solution.py:32
  38.3 1.4 %collective-permute-start.3 = (f32[136,256]{1,0:T(8,128)S(1)}, f32[136,256]{1,0:T(8,128)S(1)}, u32[]{:S(2)}, u32[]{:S(2)}) collective-permute-start(f32[136,256]{1,0:T(8,128)S(1)} %logit_sum.1), channel_id=1, source_target_pairs={{0,1},{1,0},{2,3},{3,2},{4,5},{5,4},{6,7},{7,6},{8,9},{9,8},{10,11... | collective-permute-start | bytes 417800 | tf_op jit(solution)/shard_map/ppermute | solution.py:32
  39.7 6.2 %collective-permute-start.4 = (f32[136,256]{1,0:T(8,128)S(1)}, f32[136,256]{1,0:T(8,128)S(1)}, u32[]{:S(2)}, u32[]{:S(2)}) collective-permute-start(f32[136,256]{1,0:T(8,128)S(1)} %add.10.refs_3_), channel_id=1, source_target_pairs={{0,2},{1,3},{2,0},{3,1},{4,6},{5,7},{6,4},{7,5},{8,10},{9,11},{10,... | collective-permute-start | bytes 417800 | tf_op jit(solution)/shard_map/ppermute | solution.py:32
  41.2 4.7 %collective-permute-start.5 = (f32[4,48,128]{2,1,0:T(8,128)S(1)}, f32[4,48,128]{2,1,0:T(8,128)S(1)}, u32[]{:S(2)}, u32[]{:S(2)}) collective-permute-start(f32[4,48,128]{2,1,0:T(8,128)S(1)} %get-tuple-element.97), channel_id=1, source_target_pairs={{0,4},{4,0},{8,12},{12,8},{16,20},{20,16},{24,28},{28,24},{1,5},{5... | collective-permute-start | bytes 294920 | tf_op jit(solution)/shard_map/ppermute | solution.py:32
  41.5 4.4 %collective-permute-start.6 = (f32[80,128]{1,0:T(8,128)S(1)}, f32[80,128]{1,0:T(8,128)S(1)}, u32[]{:S(2)}, u32[]{:S(2)}) collective-permute-start(f32[80,128]{1,0:T(8,128)S(1)} %get-tuple-element.99), channel_id=1, source_target_pairs={{0,8},{4,12},{8,0},{12,4},{16,24},{20,28},{24,16},{28,20},{1,9},{5... | collective-permute-start | bytes 122888 | tf_op jit(solution)/shard_map/ppermute | solution.py:32
  42.4 5.0 %collective-permute-start.7 = (f32[80,128]{1,0:T(8,128)S(1)}, f32[80,128]{1,0:T(8,128)S(1)}, u32[]{:S(2)}, u32[]{:S(2)}) collective-permute-start(f32[80,128]{1,0:T(8,128)S(1)} %get-tuple-element.100), channel_id=1, source_target_pairs={{0,16},{4,20},{8,24},{12,28},{16,0},{20,4},{24,8},{28,12},{1,17},{... | collective-permute-start | bytes 122888 | tf_op jit(solution)/shard_map/ppermute | solution.py:32
  43.1 5.8 %collective-permute-start.8 = (f32[80,128]{1,0:T(8,128)S(1)}, f32[80,128]{1,0:T(8,128)S(1)}, u32[]{:S(2)}, u32[]{:S(2)}) collective-permute-start(f32[80,128]{1,0:T(8,128)S(1)} %get-tuple-element.101), channel_id=1, source_target_pairs={{0,24},{4,28},{8,16},{12,20},{16,8},{20,12},{24,0},{28,4},{1,25},{... | collective-permute-start | bytes 122888 | tf_op jit(solution)/shard_map/ppermute | solution.py:32
  49.3 1.9 %collective-permute-start.9 = (f32[2,128]{1,0:T(2,128)S(1)}, f32[2,128]{1,0:T(2,128)S(1)}, u32[]{:S(2)}, u32[]{:S(2)}) collective-permute-start(f32[2,128]{1,0:T(2,128)S(1)} %row_pass.2.refs_0_), channel_id=1, source_target_pairs={{0,1},{1,0},{2,3},{3,2},{4,5},{5,4},{6,7},{7,6},{8,9},{9,8},{10,11... | collective-permute-start | bytes 3080 | tf_op jit(solution)/shard_map/ppermute | solution.py:32
  49.4 3.6 %collective-permute-start.10 = (f32[2,128]{1,0:T(2,128)S(1)}, f32[2,128]{1,0:T(2,128)S(1)}, u32[]{:S(2)}, u32[]{:S(2)}) collective-permute-start(f32[2,128]{1,0:T(2,128)S(1)} %row_pass.2.refs_0_), channel_id=1, source_target_pairs={{0,2},{1,3},{2,0},{3,1},{4,6},{5,7},{6,4},{7,5},{8,10},{9,11},{10,... | collective-permute-start | bytes 3080 | tf_op jit(solution)/shard_map/ppermute | solution.py:32
  50.0 3.0 %collective-permute-start.11 = (f32[2,128]{1,0:T(2,128)S(1)}, f32[2,128]{1,0:T(2,128)S(1)}, u32[]{:S(2)}, u32[]{:S(2)}) collective-permute-start(f32[2,128]{1,0:T(2,128)S(1)} %row_pass.2.refs_0_), channel_id=1, source_target_pairs={{0,3},{1,2},{2,1},{3,0},{4,7},{5,6},{6,5},{7,4},{8,11},{9,10},{10,... | collective-permute-start | bytes 3080 | tf_op jit(solution)/shard_map/ppermute | solution.py:32
  53.6 7.3 %collective-permute-start.12 = (f32[80,128]{1,0:T(8,128)S(1)}, f32[80,128]{1,0:T(8,128)S(1)}, u32[]{:S(2)}, u32[]{:S(2)}) collective-permute-start(f32[80,128]{1,0:T(8,128)S(1)} %get-tuple-element.106), channel_id=1, source_target_pairs={{0,8},{4,12},{8,0},{12,4},{16,24},{20,28},{24,16},{28,20},{1,9},{5... | collective-permute-start | bytes 122888 | tf_op jit(solution)/shard_map/ppermute | solution.py:32
  53.7 9.6 %collective-permute-start.13 = (f32[80,128]{1,0:T(8,128)S(1)}, f32[80,128]{1,0:T(8,128)S(1)}, u32[]{:S(2)}, u32[]{:S(2)}) collective-permute-start(f32[80,128]{1,0:T(8,128)S(1)} %get-tuple-element.107), channel_id=1, source_target_pairs={{0,16},{4,20},{8,24},{12,28},{16,0},{20,4},{24,8},{28,12},{1,17},{... | collective-permute-start | bytes 122888 | tf_op jit(solution)/shard_map/ppermute | solution.py:32
  57.1 6.8 %collective-permute-start.14 = (f32[80,128]{1,0:T(8,128)S(1)}, f32[80,128]{1,0:T(8,128)S(1)}, u32[]{:S(2)}, u32[]{:S(2)}) collective-permute-start(f32[80,128]{1,0:T(8,128)S(1)} %get-tuple-element.108), channel_id=1, source_target_pairs={{0,24},{4,28},{8,16},{12,20},{16,8},{20,12},{24,0},{28,4},{1,25},{... | collective-permute-start | bytes 122888 | tf_op jit(solution)/shard_map/ppermute | solution.py:32
  64.3 16.2 %copy-start.8 = (s32[128]{0:T(128)S(1)}, s32[128]{0:T(128)}, u32[]{:S(2)}) copy-start(s32[128]{0:T(128)} %param.13) | copy-start | bytes 1540
  64.3 1.9 %collective-permute-start.15 = (f32[2,128]{1,0:T(2,128)S(1)}, f32[2,128]{1,0:T(2,128)S(1)}, u32[]{:S(2)}, u32[]{:S(2)}) collective-permute-start(f32[2,128]{1,0:T(2,128)S(1)} %row_pass.3.refs_0_), channel_id=1, source_target_pairs={{0,1},{1,0},{2,3},{3,2},{4,5},{5,4},{6,7},{7,6},{8,9},{9,8},{10,11... | collective-permute-start | bytes 3080 | tf_op jit(solution)/shard_map/ppermute | solution.py:32
  64.3 3.6 %collective-permute-start.16 = (f32[2,128]{1,0:T(2,128)S(1)}, f32[2,128]{1,0:T(2,128)S(1)}, u32[]{:S(2)}, u32[]{:S(2)}) collective-permute-start(f32[2,128]{1,0:T(2,128)S(1)} %row_pass.3.refs_0_), channel_id=1, source_target_pairs={{0,2},{1,3},{2,0},{3,1},{4,6},{5,7},{6,4},{7,5},{8,10},{9,11},{10,... | collective-permute-start | bytes 3080 | tf_op jit(solution)/shard_map/ppermute | solution.py:32
  65.9 3.0 %collective-permute-start.17 = (f32[2,128]{1,0:T(2,128)S(1)}, f32[2,128]{1,0:T(2,128)S(1)}, u32[]{:S(2)}, u32[]{:S(2)}) collective-permute-start(f32[2,128]{1,0:T(2,128)S(1)} %row_pass.3.refs_0_), channel_id=1, source_target_pairs={{0,3},{1,2},{2,1},{3,0},{4,7},{5,6},{6,5},{7,4},{8,11},{9,10},{10,... | collective-permute-start | bytes 3080 | tf_op jit(solution)/shard_map/ppermute | solution.py:32
  69.4 7.4 %collective-permute-start.18 = (f32[1,8,48,128]{3,2,1,0:T(8,128)S(1)}, f32[1,8,48,128]{3,2,1,0:T(8,128)S(1)}, u32[]{:S(2)}, u32[]{:S(2)}) collective-permute-start(f32[1,8,48,128]{3,2,1,0:T(8,128)S(1)} %columns_join.1), channel_id=1, source_target_pairs={{0,2},{1,3},{2,0},{3,1},{4,6},{5,7},{6,4},{7,5},{8,10},{9,11},{10,... | collective-permute-start | bytes 589832 | tf_op jit(solution)/shard_map/ppermute | solution.py:32
  70.1 6.8 %collective-permute-start.19 = (f32[32,128]{1,0:T(8,128)S(1)}, f32[32,128]{1,0:T(8,128)S(1)}, u32[]{:S(2)}, u32[]{:S(2)}) collective-permute-start(f32[32,128]{1,0:T(8,128)S(1)} %col_pass.3.refs_0_), channel_id=1, source_target_pairs={{0,8},{4,12},{8,0},{12,4},{16,24},{20,28},{24,16},{28,20},{1,9},{5... | collective-permute-start | bytes 49160 | tf_op jit(solution)/shard_map/ppermute | solution.py:32
  73.4 5.3 %collective-permute-start.20 = (f32[32,128]{1,0:T(8,128)S(1)}, f32[32,128]{1,0:T(8,128)S(1)}, u32[]{:S(2)}, u32[]{:S(2)}) collective-permute-start(f32[32,128]{1,0:T(8,128)S(1)} %col_pass.3.refs_0_), channel_id=1, source_target_pairs={{0,16},{4,20},{8,24},{12,28},{16,0},{20,4},{24,8},{28,12},{1,17},{... | collective-permute-start | bytes 49160 | tf_op jit(solution)/shard_map/ppermute | solution.py:32
  74.6 5.9 %collective-permute-start.21 = (f32[32,128]{1,0:T(8,128)S(1)}, f32[32,128]{1,0:T(8,128)S(1)}, u32[]{:S(2)}, u32[]{:S(2)}) collective-permute-start(f32[32,128]{1,0:T(8,128)S(1)} %col_pass.3.refs_0_), channel_id=1, source_target_pairs={{0,24},{4,28},{8,16},{12,20},{16,8},{20,12},{24,0},{28,4},{1,25},{... | collective-permute-start | bytes 49160 | tf_op jit(solution)/shard_map/ppermute | solution.py:32
  82.0 3.4 %collective-permute-start.23 = (f32[2,8,48,128]{3,2,1,0:T(8,128)S(1)}, f32[2,8,48,128]{3,2,1,0:T(8,128)S(1)}, u32[]{:S(2)}, u32[]{:S(2)}) collective-permute-start(f32[2,8,48,128]{3,2,1,0:T(8,128)S(1)} %pad_maximum_fusion.refs_0_), channel_id=1, source_target_pairs={{0,1},{1,0},{2,3},{3,2},{4,5},{5,4},{6,7},{7,6},{8,9},{9,8},{10,11... | collective-permute-start | bytes 1179656 | tf_op jit(solution)/shard_map/ppermute | solution.py:32
  82.1 1.8 %collective-permute-start.22 = (f32[72,256]{1,0:T(8,128)S(1)}, f32[72,256]{1,0:T(8,128)S(1)}, u32[]{:S(2)}, u32[]{:S(2)}) collective-permute-start(f32[72,256]{1,0:T(8,128)S(1)} %get-tuple-element.112), channel_id=1, source_target_pairs={{0,1},{1,0},{2,3},{3,2},{4,5},{5,4},{6,7},{7,6},{8,9},{9,8},{10,11... | collective-permute-start | bytes 221192 | tf_op jit(solution)/shard_map/ppermute | solution.py:32
  84.0 4.4 %collective-permute-start.24 = (f32[72,256]{1,0:T(8,128)S(1)}, f32[72,256]{1,0:T(8,128)S(1)}, u32[]{:S(2)}, u32[]{:S(2)}) collective-permute-start(f32[72,256]{1,0:T(8,128)S(1)} %add.11.refs_5_), channel_id=1, source_target_pairs={{0,2},{1,3},{2,0},{3,1},{4,6},{5,7},{6,4},{7,5},{8,10},{9,11},{10,... | collective-permute-start | bytes 221192 | tf_op jit(solution)/shard_map/ppermute | solution.py:32
  89.1 6.1 %collective-permute-start.28 = (f32[1,64,256]{2,1,0:T(8,128)S(1)}, f32[1,64,256]{2,1,0:T(8,128)S(1)}, u32[]{:S(2)}, u32[]{:S(2)}) collective-permute-start(f32[1,64,256]{2,1,0:T(8,128)S(1)} %bitcast.18), channel_id=1, source_target_pairs={{0,4},{4,0},{8,12},{12,8},{16,20},{20,16},{24,28},{28,24},{1,5},{5... | collective-permute-start | bytes 196616 | tf_op jit(solution)/shard_map/ppermute | solution.py:32
  90.8 8.1 %collective-permute-start.27 = (f32[64,256]{1,0:T(8,128)S(1)}, f32[64,256]{1,0:T(8,128)S(1)}, u32[]{:S(2)}, u32[]{:S(2)}) collective-permute-start(f32[64,256]{1,0:T(8,128)S(1)} %get-tuple-element.117), channel_id=1, source_target_pairs={{0,24},{4,28},{8,16},{12,20},{16,8},{20,12},{24,0},{28,4},{1,25},{... | collective-permute-start | bytes 196616 | tf_op jit(solution)/shard_map/ppermute | solution.py:32
  92.2 7.1 %collective-permute-start.26 = (f32[64,256]{1,0:T(8,128)S(1)}, f32[64,256]{1,0:T(8,128)S(1)}, u32[]{:S(2)}, u32[]{:S(2)}) collective-permute-start(f32[64,256]{1,0:T(8,128)S(1)} %get-tuple-element.117), channel_id=1, source_target_pairs={{0,16},{4,20},{8,24},{12,28},{16,0},{20,4},{24,8},{28,12},{1,17},{... | collective-permute-start | bytes 196616 | tf_op jit(solution)/shard_map/ppermute | solution.py:32
  93.4 5.8 %collective-permute-start.25 = (f32[64,256]{1,0:T(8,128)S(1)}, f32[64,256]{1,0:T(8,128)S(1)}, u32[]{:S(2)}, u32[]{:S(2)}) collective-permute-start(f32[64,256]{1,0:T(8,128)S(1)} %get-tuple-element.117), channel_id=1, source_target_pairs={{0,8},{4,12},{8,0},{12,4},{16,24},{20,28},{24,16},{28,20},{1,9},{5... | collective-permute-start | bytes 196616 | tf_op jit(solution)/shard_map/ppermute | solution.py:32
  95.2 4.0 %collective-permute-start.29 = (f32[1,64,256]{2,1,0:T(8,128)S(1)}, f32[1,64,256]{2,1,0:T(8,128)S(1)}, u32[]{:S(2)}, u32[]{:S(2)}) collective-permute-start(f32[1,64,256]{2,1,0:T(8,128)S(1)} %bitcast.19), channel_id=1, source_target_pairs={{0,1},{1,0},{2,3},{3,2},{4,5},{5,4},{6,7},{7,6},{8,9},{9,8},{10,11... | collective-permute-start | bytes 196616 | tf_op jit(solution)/shard_map/ppermute | solution.py:32
  95.2 4.1 %collective-permute-start.30 = (f32[1,64,256]{2,1,0:T(8,128)S(1)}, f32[1,64,256]{2,1,0:T(8,128)S(1)}, u32[]{:S(2)}, u32[]{:S(2)}) collective-permute-start(f32[1,64,256]{2,1,0:T(8,128)S(1)} %collective-permute-done.28.refs_7_), channel_id=1, source_target_pairs={{0,1},{1,0},{2,3},{3,2},{4,5},{5,4},{6,7},{7,6},{8,9},{9,8},{10,11... | collective-permute-start | bytes 196616 | tf_op jit(solution)/shard_map/ppermute | solution.py:32
  95.7 2.2 %copy-start = (f32[1024,1024]{1,0:T(8,128)S(1)}, f32[1024,1024]{1,0:T(8,128)}, u32[]{:S(2)}) copy-start(f32[1024,1024]{1,0:T(8,128)} %all-gather.2.cloned.1.call-done) | copy-start | bytes 12582916
  97.9 3.4 %copy-start.1 = (f32[1024,1024]{1,0:T(8,128)S(1)}, f32[1024,1024]{1,0:T(8,128)}, u32[]{:S(2)}) copy-start(f32[1024,1024]{1,0:T(8,128)} %all-gather.2.cloned.1.call-done) | copy-start | bytes 12582916
  99.3 1.2 %collective-permute-start.32 = (f32[1,64]{1,0:T(1,128)S(1)}, f32[1,64]{1,0:T(1,128)S(1)}, u32[]{:S(2)}, u32[]{:S(2)}) collective-permute-start(f32[1,64]{1,0:T(1,128)S(1)} %get-tuple-element.129), channel_id=1, source_target_pairs={{0,1},{1,0},{2,3},{3,2},{4,5},{5,4},{6,7},{7,6},{8,9},{9,8},{10,11... | collective-permute-start | bytes 776 | tf_op jit(solution)/shard_map/ppermute | solution.py:32
  99.4 7.3 %collective-permute-start.31 = (f32[3,64,256]{2,1,0:T(8,128)S(1)}, f32[3,64,256]{2,1,0:T(8,128)S(1)}, u32[]{:S(2)}, u32[]{:S(2)}) collective-permute-start(f32[3,64,256]{2,1,0:T(8,128)S(1)} %pad_maximum_fusion.1.refs_8_), channel_id=1, source_target_pairs={{0,4},{4,0},{8,12},{12,8},{16,20},{20,16},{24,28},{28,24},{1,5},{5... | collective-permute-start | bytes 589832 | tf_op jit(solution)/shard_map/ppermute | solution.py:32
  99.8 1.4 %collective-permute-start.33 = (f32[3,64,256]{2,1,0:T(8,128)S(1)}, f32[3,64,256]{2,1,0:T(8,128)S(1)}, u32[]{:S(2)}, u32[]{:S(2)}) collective-permute-start(f32[3,64,256]{2,1,0:T(8,128)S(1)} %pad_maximum_fusion.1.refs_8_), channel_id=1, source_target_pairs={{0,1},{1,0},{2,3},{3,2},{4,5},{5,4},{6,7},{7,6},{8,9},{9,8},{10,11... | collective-permute-start | bytes 589832 | tf_op jit(solution)/shard_map/ppermute | solution.py:32
  106.7 1.4 %collective-permute-start.34 = (f32[3,64,256]{2,1,0:T(8,128)S(1)}, f32[3,64,256]{2,1,0:T(8,128)S(1)}, u32[]{:S(2)}, u32[]{:S(2)}) collective-permute-start(f32[3,64,256]{2,1,0:T(8,128)S(1)} %collective-permute-done.31.refs_8_), channel_id=1, source_target_pairs={{0,1},{1,0},{2,3},{3,2},{4,5},{5,4},{6,7},{7,6},{8,9},{9,8},{10,11... | collective-permute-start | bytes 589832 | tf_op jit(solution)/shard_map/ppermute | solution.py:32
Sparse Core Ops, SparseCore 0:
  11.7 79.3 all-gather.1

commit v7 on v6

--- a/solution.py
+++ b/solution.py
@@ -345,13 +345,17 @@
     outs, table_all, mass_all, low = refs[n_parts + 4 : -3], refs[-3], refs[-2], refs[-1]
     rows = codes_ref.shape[0]
     scale = col_scale(parts)
-    total = 0.0
-    for j in range(scale.shape[0]):
-        weighted = codes_ref[:, j * 128 : (j + 1) * 128] * scale[j : j + 1, :]
-        low[:, j * 128 : (j + 1) * 128] = weighted.astype(BF16)
-        total = total + weighted
+    total, table = 0.0, 0.0
+    lines = scale.shape[0]
+    step = min(8, lines)
+    for i in range(lines // step):
+        for j in range(i * step, (i + 1) * step):
+            weighted = codes_ref[:, j * 128 : (j + 1) * 128] * scale[j : j + 1, :]
+            low[:, j * 128 : (j + 1) * 128] = weighted.astype(BF16)
+            total = total + weighted
+        at = slice(i * step * 128, (i + 1) * step * 128)
+        table = table + jnp.dot(low[:, at], u_ref[at, :], preferred_element_type=F32)
     mass = jnp.sum(total, axis=1, keepdims=True)
-    table = jnp.dot(low[...], u_ref[...], preferred_element_type=F32)
     chosen = partner_ref[...] == lax.broadcasted_iota(jnp.int32, (rows, rows), 0)
     table_all[...] = dot(jnp.where(chosen, 1.0, 0.0).astype(F32), table, ((1,), (0,)), HIGHEST)
     mass_all[...] = jnp.sum(jnp.where(chosen, to_lanes(mass), 0.0), axis=1, keepdims=True)

time: 119 us -> 119 us (level)
  no operation moved by 1% of the time
where the time goes in v7:
time: 119 us
  starting transfers between devices  39.9 us (34%)
  waiting for transfers between devices  39.3 us (33%)
  Pallas kernels  21 us (18%)
  between operations  14.3 us (12%)
  local copies, waits for them, and re-layouts  3.36 us (3%)
    ppermute x35, starting transfers between devices, swap(): return lax.ppermute(v, axis, [(i, i ^ mask) for i in range(n)])  32.6 us
    ppermute x35, waiting for transfers between devices, swap(): return lax.ppermute(v, axis, [(i, i ^ mask) for i in range(n)])  32.2 us
    all_to_all x1, starting transfers between devices, body(): lax.all_to_all(moments, 'batch', 0, 0)  7.29 us
    all_to_all x1, waiting for transfers between devices, body(): lax.all_to_all(moments, 'batch', 0, 0)  7.01 us
    pallas_call x2, Pallas kernels, tail_call(): pl.pallas_call(functools.partial(kernel, n_batch, len(grads)), in_specs=[...  6.69 us
    unnamed x18, local copies, waits for them, and re-layouts  3.36 us
    pallas_call x1, Pallas kernels, first_layer(): pl.pallas_call(first_kernel, in_specs=[pl.BlockSpec(memory_space=pl.ANY)]...  3.11 us
  transfers between devices with their start and end apart: 37, of which 23 were waited for; matrix products, arithmetic and copies ran while one was open for 1% of the time, Pallas kernels for 12%

profile of v7, /device:TPU:0, one launch (start us, length us, event | category | flops | bytes accessed | tf_op | source)
XLA Modules:
  0.0 118.6 jit_solution(7263243104100074442)
XLA Ops:
  7.2 1.1 copy-done.4
  8.4 3.1 %first_layer.1 = (f32[128,1024]{1,0:T(8,128)}, f32[128,1024]{1,0:T(8,128)S(1)}, f32[8,1,2048]{2,1,0:T(1,128)}) custom-call(bf16[128,1536]{1,0:T(8,128)(2,1)S(1)} %copy-done.4, bf16[1536,1024]{1,0:T(8,128)(2,1)} %w_hbm.1), custom_call_target="tpu_custom_call" | custom-call | flops 402653184 | bytes 3670016 | tf_op jit(solution)/shard_map/first_layer/pallas_call | solution.py:125
  11.5 7.3 %all-to-all-start = ((f32[8,1,2048]{2,1,0:T(1,128)}), f32[8,1,2048]{2,1,0:T(1,128)S(1)}, u32[]{:S(2)}, u32[]{:S(2)}) async-start(f32[8,1,2048]{2,1,0:T(1,128)} %get-tuple-element.76), calls=%async_computation | async-start | bytes 131072 | tf_op jit(solution)/shard_map/all_to_all | solution.py:700
  18.8 7.0 %all-to-all-done.refs_0_ = f32[8,1,2048]{2,1,0:T(1,128)S(1)} async-done(((f32[8,1,2048]{2,1,0:T(1,128)}), f32[8,1,2048]{2,1,0:T(1,128)S(1)}, u32[]{:S(2)}, u32[]{:S(2)}) %all-to-all-start) | async-done | bytes 65568 | tf_op jit(solution)/shard_map/all_to_all | solution.py:700
  26.2 1.3 %collective-permute-done = f32[128,256]{1,0:T(8,128)S(1)} collective-permute-done((f32[128,256]{1,0:T(8,128)S(1)}, f32[128,256]{1,0:T(8,128)S(1)}, u32[]{:S(2)}, u32[]{:S(2)}) %collective-permute-start) | collective-permute-done | bytes 131104 | tf_op jit(solution)/shard_map/ppermute | solution.py:32
  27.6 1.6 %collective-permute-start.1 = (f32[128,256]{1,0:T(8,128)S(1)}, f32[128,256]{1,0:T(8,128)S(1)}, u32[]{:S(2)}, u32[]{:S(2)}) collective-permute-start(f32[128,256]{1,0:T(8,128)S(1)} %add.9.refs_0_.refs_1_), channel_id=1, source_target_pairs={{0,2},{1,3},{2,0},{3,1},{4,6},{5,7},{6,4},{7,5},{8,10},{9,11},{10,... | collective-permute-start | bytes 393224 | tf_op jit(solution)/shard_map/ppermute | solution.py:32
  29.1 0.9 unit_rows.1.refs_1_.u_ref.refs_5_
  30.1 1.0 columns_pick.1
  31.1 2.0 %collective-permute-done.1.refs_1_.refs_2_ = f32[128,256]{1,0:T(8,128)S(1)} collective-permute-done((f32[128,256]{1,0:T(8,128)S(1)}, f32[128,256]{1,0:T(8,128)S(1)}, u32[]{:S(2)}, u32[]{:S(2)}) %collective-permute-start.1) | collective-permute-done | bytes 131104 | tf_op jit(solution)/shard_map/ppermute | solution.py:32
  33.6 0.8 score.2
  34.5 1.4 %logit_sum.1 = f32[136,256]{1,0:T(8,128)S(1)} custom-call(f32[128,256]{1,0:T(8,128)S(1)} %embed_rows.1.refs_0_.emb_ref, bf16[4096,256]{1,0:T(8,128)(2,1)S(1)} %unit_rows.1.refs_1_.u_ref.refs_5_), custom_call_target="tpu_custom_call" | custom-call | flops 536870912 | bytes 2097152 | tf_op jit(solution)/shard_map/logit_sum/pallas_call | solution.py:281
  35.9 2.4 %collective-permute-done.2.refs_0_ = f32[128,256]{1,0:T(8,128)S(1)} collective-permute-done((f32[128,256]{1,0:T(8,128)S(1)}, f32[128,256]{1,0:T(8,128)S(1)}, u32[]{:S(2)}, u32[]{:S(2)}) %collective-permute-start.2) | collective-permute-done | bytes 131104 | tf_op jit(solution)/shard_map/ppermute | solution.py:32
  38.3 0.8 score.3
  39.7 1.6 %collective-permute-start.4 = (f32[136,256]{1,0:T(8,128)S(1)}, f32[136,256]{1,0:T(8,128)S(1)}, u32[]{:S(2)}, u32[]{:S(2)}) collective-permute-start(f32[136,256]{1,0:T(8,128)S(1)} %add.10.refs_3_), channel_id=1, source_target_pairs={{0,2},{1,3},{2,0},{3,1},{4,6},{5,7},{6,4},{7,5},{8,10},{9,11},{10,... | collective-permute-start | bytes 417800 | tf_op jit(solution)/shard_map/ppermute | solution.py:32
  41.5 0.8 collective-permute-start.6
  43.1 2.8 %collective-permute-start.8 = (f32[80,128]{1,0:T(8,128)S(1)}, f32[80,128]{1,0:T(8,128)S(1)}, u32[]{:S(2)}, u32[]{:S(2)}) collective-permute-start(f32[80,128]{1,0:T(8,128)S(1)} %get-tuple-element.101), channel_id=1, source_target_pairs={{0,24},{4,28},{8,16},{12,20},{16,8},{20,12},{24,0},{28,4},{1,25},{... | collective-permute-start | bytes 122888 | tf_op jit(solution)/shard_map/ppermute | solution.py:32
  46.0 1.4 %collective-permute-done.7.refs_2_ = f32[80,128]{1,0:T(8,128)S(1)} collective-permute-done((f32[80,128]{1,0:T(8,128)S(1)}, f32[80,128]{1,0:T(8,128)S(1)}, u32[]{:S(2)}, u32[]{:S(2)}) %collective-permute-start.7) | collective-permute-done | bytes 40992 | tf_op jit(solution)/shard_map/ppermute | solution.py:32
  47.4 1.5 %collective-permute-done.8.refs_3_.refs_4_ = f32[80,128]{1,0:T(8,128)S(1)} collective-permute-done((f32[80,128]{1,0:T(8,128)S(1)}, f32[80,128]{1,0:T(8,128)S(1)}, u32[]{:S(2)}, u32[]{:S(2)}) %collective-permute-start.8) | collective-permute-done | bytes 40992 | tf_op jit(solution)/shard_map/ppermute | solution.py:32
  50.0 1.3 %collective-permute-start.11 = (f32[2,128]{1,0:T(2,128)S(1)}, f32[2,128]{1,0:T(2,128)S(1)}, u32[]{:S(2)}, u32[]{:S(2)}) collective-permute-start(f32[2,128]{1,0:T(2,128)S(1)} %row_pass.2.refs_0_), channel_id=1, source_target_pairs={{0,3},{1,2},{2,1},{3,0},{4,7},{5,6},{6,5},{7,4},{8,11},{9,10},{10,... | collective-permute-start | bytes 3080 | tf_op jit(solution)/shard_map/ppermute | solution.py:32
  51.3 1.8 %collective-permute-done.10.refs_2_ = f32[2,128]{1,0:T(2,128)S(1)} collective-permute-done((f32[2,128]{1,0:T(2,128)S(1)}, f32[2,128]{1,0:T(2,128)S(1)}, u32[]{:S(2)}, u32[]{:S(2)}) %collective-permute-start.10) | collective-permute-done | bytes 1056 | tf_op jit(solution)/shard_map/ppermute | solution.py:32
  53.7 3.4 %collective-permute-start.13 = (f32[80,128]{1,0:T(8,128)S(1)}, f32[80,128]{1,0:T(8,128)S(1)}, u32[]{:S(2)}, u32[]{:S(2)}) collective-permute-start(f32[80,128]{1,0:T(8,128)S(1)} %get-tuple-element.107), channel_id=1, source_target_pairs={{0,16},{4,20},{8,24},{12,28},{16,0},{20,4},{24,8},{28,12},{1,17},{... | collective-permute-start | bytes 122888 | tf_op jit(solution)/shard_map/ppermute | solution.py:32
  57.1 1.0 collective-permute-start.14
  58.1 2.9 %collective-permute-done.12.refs_1_ = f32[80,128]{1,0:T(8,128)S(1)} collective-permute-done((f32[80,128]{1,0:T(8,128)S(1)}, f32[80,128]{1,0:T(8,128)S(1)}, u32[]{:S(2)}, u32[]{:S(2)}) %collective-permute-start.12) | collective-permute-done | bytes 40992 | tf_op jit(solution)/shard_map/ppermute | solution.py:32
  60.9 2.3 %collective-permute-done.13.refs_2_.refs_3_ = f32[80,128]{1,0:T(8,128)S(1)} collective-permute-done((f32[80,128]{1,0:T(8,128)S(1)}, f32[80,128]{1,0:T(8,128)S(1)}, u32[]{:S(2)}, u32[]{:S(2)}) %collective-permute-start.13) | collective-permute-done | bytes 40992 | tf_op jit(solution)/shard_map/ppermute | solution.py:32
  64.3 1.5 %collective-permute-start.16 = (f32[2,128]{1,0:T(2,128)S(1)}, f32[2,128]{1,0:T(2,128)S(1)}, u32[]{:S(2)}, u32[]{:S(2)}) collective-permute-start(f32[2,128]{1,0:T(2,128)S(1)} %row_pass.3.refs_0_), channel_id=1, source_target_pairs={{0,2},{1,3},{2,0},{3,1},{4,6},{5,7},{6,4},{7,5},{8,10},{9,11},{10,... | collective-permute-start | bytes 3080 | tf_op jit(solution)/shard_map/ppermute | solution.py:32
  66.2 1.8 %collective-permute-done.16.refs_2_ = f32[2,128]{1,0:T(2,128)S(1)} collective-permute-done((f32[2,128]{1,0:T(2,128)S(1)}, f32[2,128]{1,0:T(2,128)S(1)}, u32[]{:S(2)}, u32[]{:S(2)}) %collective-permute-start.16) | collective-permute-done | bytes 1056 | tf_op jit(solution)/shard_map/ppermute | solution.py:32
  68.0 0.9 collective-permute-done.17.refs_3_
  70.1 3.3 %collective-permute-start.19 = (f32[32,128]{1,0:T(8,128)S(1)}, f32[32,128]{1,0:T(8,128)S(1)}, u32[]{:S(2)}, u32[]{:S(2)}) collective-permute-start(f32[32,128]{1,0:T(8,128)S(1)} %col_pass.3.refs_0_), channel_id=1, source_target_pairs={{0,8},{4,12},{8,0},{12,4},{16,24},{20,28},{24,16},{28,20},{1,9},{5... | collective-permute-start | bytes 49160 | tf_op jit(solution)/shard_map/ppermute | solution.py:32
  73.4 1.3 %collective-permute-start.20 = (f32[32,128]{1,0:T(8,128)S(1)}, f32[32,128]{1,0:T(8,128)S(1)}, u32[]{:S(2)}, u32[]{:S(2)}) collective-permute-start(f32[32,128]{1,0:T(8,128)S(1)} %col_pass.3.refs_0_), channel_id=1, source_target_pairs={{0,16},{4,20},{8,24},{12,28},{16,0},{20,4},{24,8},{28,12},{1,17},{... | collective-permute-start | bytes 49160 | tf_op jit(solution)/shard_map/ppermute | solution.py:32
  74.6 1.5 %collective-permute-start.21 = (f32[32,128]{1,0:T(8,128)S(1)}, f32[32,128]{1,0:T(8,128)S(1)}, u32[]{:S(2)}, u32[]{:S(2)}) collective-permute-start(f32[32,128]{1,0:T(8,128)S(1)} %col_pass.3.refs_0_), channel_id=1, source_target_pairs={{0,24},{4,28},{8,16},{12,20},{16,8},{20,12},{24,0},{28,4},{1,25},{... | collective-permute-start | bytes 49160 | tf_op jit(solution)/shard_map/ppermute | solution.py:32
  76.1 0.8 collective-permute-done.18
  76.9 1.8 %collective-permute-done.20.refs_2_ = f32[32,128]{1,0:T(8,128)S(1)} collective-permute-done((f32[32,128]{1,0:T(8,128)S(1)}, f32[32,128]{1,0:T(8,128)S(1)}, u32[]{:S(2)}, u32[]{:S(2)}) %collective-permute-start.20) | collective-permute-done | bytes 16416 | tf_op jit(solution)/shard_map/ppermute | solution.py:32
  78.7 1.8 %collective-permute-done.21.refs_3_ = f32[32,128]{1,0:T(8,128)S(1)} collective-permute-done((f32[32,128]{1,0:T(8,128)S(1)}, f32[32,128]{1,0:T(8,128)S(1)}, u32[]{:S(2)}, u32[]{:S(2)}) %collective-permute-start.21) | collective-permute-done | bytes 16416 | tf_op jit(solution)/shard_map/ppermute | solution.py:32
  80.5 1.5 %target_sum.1 = (f32[72,256]{1,0:T(8,128)S(1)}, f32[72,256]{1,0:T(8,128)S(1)}) custom-call(f32[32,128]{1,0:T(8,128)S(1)} %col_pass.3.refs_0_, f32[32,128]{1,0:T(8,128)S(1)} %collective-permute-done.19.refs_1_, f32[32,128]{1,0:T(8,128)S(1)} %collective-permute-done.20.refs_2_, f32[32,128]{1,0:T(8,128)S(1)} %collective-permute-done.21.refs_3_, ...), custom_call_target="tpu_custom_call" | custom-call | flops 268435456 | bytes 4194304 | tf_op jit(solution)/shard_map/target_sum/pallas_call | solution.py:372
  82.6 1.3 %collective-permute-done.22 = f32[72,256]{1,0:T(8,128)S(1)} collective-permute-done((f32[72,256]{1,0:T(8,128)S(1)}, f32[72,256]{1,0:T(8,128)S(1)}, u32[]{:S(2)}, u32[]{:S(2)}) %collective-permute-start.22) | collective-permute-done | bytes 73760 | tf_op jit(solution)/shard_map/ppermute | solution.py:32
  84.0 1.5 %collective-permute-start.24 = (f32[72,256]{1,0:T(8,128)S(1)}, f32[72,256]{1,0:T(8,128)S(1)}, u32[]{:S(2)}, u32[]{:S(2)}) collective-permute-start(f32[72,256]{1,0:T(8,128)S(1)} %add.11.refs_5_), channel_id=1, source_target_pairs={{0,2},{1,3},{2,0},{3,1},{4,6},{5,7},{6,4},{7,5},{8,10},{9,11},{10,... | collective-permute-start | bytes 221192 | tf_op jit(solution)/shard_map/ppermute | solution.py:32
  86.1 2.3 %collective-permute-done.24.refs_6_ = f32[72,256]{1,0:T(8,128)S(1)} collective-permute-done((f32[72,256]{1,0:T(8,128)S(1)}, f32[72,256]{1,0:T(8,128)S(1)}, u32[]{:S(2)}, u32[]{:S(2)}) %collective-permute-start.24) | collective-permute-done | bytes 73760 | tf_op jit(solution)/shard_map/ppermute | solution.py:32
  88.4 0.8 loss_grad.1
  89.1 1.7 %collective-permute-start.28 = (f32[1,64,256]{2,1,0:T(8,128)S(1)}, f32[1,64,256]{2,1,0:T(8,128)S(1)}, u32[]{:S(2)}, u32[]{:S(2)}) collective-permute-start(f32[1,64,256]{2,1,0:T(8,128)S(1)} %bitcast.18), channel_id=1, source_target_pairs={{0,4},{4,0},{8,12},{12,8},{16,20},{20,16},{24,28},{28,24},{1,5},{5... | collective-permute-start | bytes 196616 | tf_op jit(solution)/shard_map/ppermute | solution.py:32
  90.8 1.3 %collective-permute-start.27 = (f32[64,256]{1,0:T(8,128)S(1)}, f32[64,256]{1,0:T(8,128)S(1)}, u32[]{:S(2)}, u32[]{:S(2)}) collective-permute-start(f32[64,256]{1,0:T(8,128)S(1)} %get-tuple-element.117), channel_id=1, source_target_pairs={{0,24},{4,28},{8,16},{12,20},{16,8},{20,12},{24,0},{28,4},{1,25},{... | collective-permute-start | bytes 196616 | tf_op jit(solution)/shard_map/ppermute | solution.py:32
  92.2 1.3 %collective-permute-start.26 = (f32[64,256]{1,0:T(8,128)S(1)}, f32[64,256]{1,0:T(8,128)S(1)}, u32[]{:S(2)}, u32[]{:S(2)}) collective-permute-start(f32[64,256]{1,0:T(8,128)S(1)} %get-tuple-element.117), channel_id=1, source_target_pairs={{0,16},{4,20},{8,24},{12,28},{16,0},{20,4},{24,8},{28,12},{1,17},{... | collective-permute-start | bytes 196616 | tf_op jit(solution)/shard_map/ppermute | solution.py:32
  93.5 1.8 %collective-permute-start.25 = (f32[64,256]{1,0:T(8,128)S(1)}, f32[64,256]{1,0:T(8,128)S(1)}, u32[]{:S(2)}, u32[]{:S(2)}) collective-permute-start(f32[64,256]{1,0:T(8,128)S(1)} %get-tuple-element.117), channel_id=1, source_target_pairs={{0,8},{4,12},{8,0},{12,4},{16,24},{20,28},{24,16},{28,20},{1,9},{5... | collective-permute-start | bytes 196616 | tf_op jit(solution)/shard_map/ppermute | solution.py:32
  95.7 2.2 %copy-done = f32[1024,1024]{1,0:T(8,128)S(1)} copy-done((f32[1024,1024]{1,0:T(8,128)S(1)}, f32[1024,1024]{1,0:T(8,128)}, u32[]{:S(2)}) %copy-start) | copy-done | bytes 4194328
  97.9 1.0 flat_sums.1
  101.3 3.1 %tail_near.1 = (f32[192,1024]{1,0:T(8,128)S(1)}, f32[32,1024]{1,0:T(8,128)S(1)}, f32[2,8,1024]{2,1,0:T(8,128)S(1)}) custom-call(s32[3]{0:T(128)S(1)} %pad_add_fusion.at_ref.refs_7_.refs_0_, f32[8,128,1024]{2,1,0:T(8,128)S(1)} %bitcast.16, bf16[8,192,128]{2,1,0:T(8,128)(2,1)S(1)} %columns_all.1.cols_ref.refs_2_, ...), custom_call_target="tpu_custom_call" | custom-call | flops 536870912 | bytes 2097152 | tf_op jit(solution)/shard_map/tail_near/pallas_call | solution.py:587
  104.4 2.3 %collective-permute-done.31.refs_8_ = f32[3,64,256]{2,1,0:T(8,128)S(1)} collective-permute-done((f32[3,64,256]{2,1,0:T(8,128)S(1)}, f32[3,64,256]{2,1,0:T(8,128)S(1)}, u32[]{:S(2)}, u32[]{:S(2)}) %collective-permute-start.31) | collective-permute-done | bytes 196640 | tf_op jit(solution)/shard_map/ppermute | solution.py:32
  106.7 1.4 %collective-permute-done.34.refs_10_ = f32[3,64,256]{2,1,0:T(8,128)S(1)} collective-permute-done((f32[3,64,256]{2,1,0:T(8,128)S(1)}, f32[3,64,256]{2,1,0:T(8,128)S(1)}, u32[]{:S(2)}, u32[]{:S(2)}) %collective-permute-start.34) | collective-permute-done | bytes 196640 | tf_op jit(solution)/shard_map/ppermute | solution.py:32
  108.1 3.6 %tail_far.1 = (f32[192,1024]{1,0:T(8,128)}, f32[32,1024]{1,0:T(8,128)}, f32[1,1024]{1,0:T(1,128)}, f32[1,1024]{1,0:T(1,128)}) custom-call(s32[3]{0:T(128)S(1)} %pad_add_fusion.at_ref.refs_7_.refs_0_, f32[8,128,1024]{2,1,0:T(8,128)S(1)} %bitcast.17, bf16[8,192,128]{2,1,0:T(8,128)(2,1)S(1)} %columns_all.1.cols_ref.refs_2_, ...), custom_call_target="tpu_custom_call" | custom-call | flops 536870912 | bytes 2097152 | tf_op jit(solution)/shard_map/tail_far/pallas_call | solution.py:587
  (72 shorter events, 11.0 us)
Async XLA Ops:
  7.2 18.7 %copy-start.2 = (bf16[1024,256]{1,0:T(8,128)(2,1)S(1)}, bf16[1024,256]{1,0:T(8,128)(2,1)}, u32[]{:S(2)}) copy-start(bf16[1024,256]{1,0:T(8,128)(2,1)} %refs_6_.3) | copy-start | bytes 1572868
  7.2 21.9 %copy-start.3 = (bf16[4096,256]{1,0:T(8,128)(2,1)S(1)}, bf16[4096,256]{1,0:T(8,128)(2,1)}, u32[]{:S(2)}) copy-start(bf16[4096,256]{1,0:T(8,128)(2,1)} %p_ref.1) | copy-start | bytes 6291460
  7.2 88.5 %all-gather.2.cloned.1.call-start = ((), (), s32[]{:S(2)}) async-start(), calls=%async_computation.1 | async-start | bytes 4718592 | tf_op jit(solution)/shard_map/all_gather | solution.py:699
  7.2 1.1 copy-start.4
  8.4 17.5 %copy-start.6 = (f32[1024]{0:T(1024)S(1)}, f32[1024]{0:T(1024)}, u32[]{:S(2)}) copy-start(f32[1024]{0:T(1024)} %param.9) | copy-start | bytes 12292
  8.4 17.5 %copy-start.7 = (f32[1024]{0:T(1024)S(1)}, f32[1024]{0:T(1024)}, u32[]{:S(2)}) copy-start(f32[1024]{0:T(1024)} %param.10) | copy-start | bytes 12292
  11.5 14.3 %all-to-all-start = ((f32[8,1,2048]{2,1,0:T(1,128)}), f32[8,1,2048]{2,1,0:T(1,128)S(1)}, u32[]{:S(2)}, u32[]{:S(2)}) async-start(f32[8,1,2048]{2,1,0:T(1,128)} %get-tuple-element.76), calls=%async_computation | async-start | bytes 131072 | tf_op jit(solution)/shard_map/all_to_all | solution.py:700
  26.1 1.4 %collective-permute-start = (f32[128,256]{1,0:T(8,128)S(1)}, f32[128,256]{1,0:T(8,128)S(1)}, u32[]{:S(2)}, u32[]{:S(2)}) collective-permute-start(f32[128,256]{1,0:T(8,128)S(1)} %get-tuple-element.79), channel_id=1, source_target_pairs={{0,1},{1,0},{2,3},{3,2},{4,5},{5,4},{6,7},{7,6},{8,9},{9,8},{10,11... | collective-permute-start | bytes 393224 | tf_op jit(solution)/shard_map/ppermute | solution.py:32
  27.6 5.6 %collective-permute-start.1 = (f32[128,256]{1,0:T(8,128)S(1)}, f32[128,256]{1,0:T(8,128)S(1)}, u32[]{:S(2)}, u32[]{:S(2)}) collective-permute-start(f32[128,256]{1,0:T(8,128)S(1)} %add.9.refs_0_.refs_1_), channel_id=1, source_target_pairs={{0,2},{1,3},{2,0},{3,1},{4,6},{5,7},{6,4},{7,5},{8,10},{9,11},{10,... | collective-permute-start | bytes 393224 | tf_op jit(solution)/shard_map/ppermute | solution.py:32
  29.1 1.0 copy-start.5
  33.3 5.0 %collective-permute-start.2 = (f32[128,256]{1,0:T(8,128)S(1)}, f32[128,256]{1,0:T(8,128)S(1)}, u32[]{:S(2)}, u32[]{:S(2)}) collective-permute-start(f32[128,256]{1,0:T(8,128)S(1)} %embed_rows.1.refs_0_.emb_ref), channel_id=1, source_target_pairs={{0,4},{4,0},{8,12},{12,8},{16,20},{20,16},{24,28},{28,24},{1,5},{5... | collective-permute-start | bytes 393224 | tf_op jit(solution)/shard_map/ppermute | solution.py:32
  38.3 1.4 %collective-permute-start.3 = (f32[136,256]{1,0:T(8,128)S(1)}, f32[136,256]{1,0:T(8,128)S(1)}, u32[]{:S(2)}, u32[]{:S(2)}) collective-permute-start(f32[136,256]{1,0:T(8,128)S(1)} %logit_sum.1), channel_id=1, source_target_pairs={{0,1},{1,0},{2,3},{3,2},{4,5},{5,4},{6,7},{7,6},{8,9},{9,8},{10,11... | collective-permute-start | bytes 417800 | tf_op jit(solution)/shard_map/ppermute | solution.py:32
  39.7 6.2 %collective-permute-start.4 = (f32[136,256]{1,0:T(8,128)S(1)}, f32[136,256]{1,0:T(8,128)S(1)}, u32[]{:S(2)}, u32[]{:S(2)}) collective-permute-start(f32[136,256]{1,0:T(8,128)S(1)} %add.10.refs_3_), channel_id=1, source_target_pairs={{0,2},{1,3},{2,0},{3,1},{4,6},{5,7},{6,4},{7,5},{8,10},{9,11},{10,... | collective-permute-start | bytes 417800 | tf_op jit(solution)/shard_map/ppermute | solution.py:32
  41.2 4.7 %collective-permute-start.5 = (f32[4,48,128]{2,1,0:T(8,128)S(1)}, f32[4,48,128]{2,1,0:T(8,128)S(1)}, u32[]{:S(2)}, u32[]{:S(2)}) collective-permute-start(f32[4,48,128]{2,1,0:T(8,128)S(1)} %get-tuple-element.97), channel_id=1, source_target_pairs={{0,4},{4,0},{8,12},{12,8},{16,20},{20,16},{24,28},{28,24},{1,5},{5... | collective-permute-start | bytes 294920 | tf_op jit(solution)/shard_map/ppermute | solution.py:32
  41.5 4.4 %collective-permute-start.6 = (f32[80,128]{1,0:T(8,128)S(1)}, f32[80,128]{1,0:T(8,128)S(1)}, u32[]{:S(2)}, u32[]{:S(2)}) collective-permute-start(f32[80,128]{1,0:T(8,128)S(1)} %get-tuple-element.99), channel_id=1, source_target_pairs={{0,8},{4,12},{8,0},{12,4},{16,24},{20,28},{24,16},{28,20},{1,9},{5... | collective-permute-start | bytes 122888 | tf_op jit(solution)/shard_map/ppermute | solution.py:32
  42.4 5.0 %collective-permute-start.7 = (f32[80,128]{1,0:T(8,128)S(1)}, f32[80,128]{1,0:T(8,128)S(1)}, u32[]{:S(2)}, u32[]{:S(2)}) collective-permute-start(f32[80,128]{1,0:T(8,128)S(1)} %get-tuple-element.100), channel_id=1, source_target_pairs={{0,16},{4,20},{8,24},{12,28},{16,0},{20,4},{24,8},{28,12},{1,17},{... | collective-permute-start | bytes 122888 | tf_op jit(solution)/shard_map/ppermute | solution.py:32
  43.1 5.8 %collective-permute-start.8 = (f32[80,128]{1,0:T(8,128)S(1)}, f32[80,128]{1,0:T(8,128)S(1)}, u32[]{:S(2)}, u32[]{:S(2)}) collective-permute-start(f32[80,128]{1,0:T(8,128)S(1)} %get-tuple-element.101), channel_id=1, source_target_pairs={{0,24},{4,28},{8,16},{12,20},{16,8},{20,12},{24,0},{28,4},{1,25},{... | collective-permute-start | bytes 122888 | tf_op jit(solution)/shard_map/ppermute | solution.py:32
  49.3 1.9 %collective-permute-start.9 = (f32[2,128]{1,0:T(2,128)S(1)}, f32[2,128]{1,0:T(2,128)S(1)}, u32[]{:S(2)}, u32[]{:S(2)}) collective-permute-start(f32[2,128]{1,0:T(2,128)S(1)} %row_pass.2.refs_0_), channel_id=1, source_target_pairs={{0,1},{1,0},{2,3},{3,2},{4,5},{5,4},{6,7},{7,6},{8,9},{9,8},{10,11... | collective-permute-start | bytes 3080 | tf_op jit(solution)/shard_map/ppermute | solution.py:32
  49.4 3.6 %collective-permute-start.10 = (f32[2,128]{1,0:T(2,128)S(1)}, f32[2,128]{1,0:T(2,128)S(1)}, u32[]{:S(2)}, u32[]{:S(2)}) collective-permute-start(f32[2,128]{1,0:T(2,128)S(1)} %row_pass.2.refs_0_), channel_id=1, source_target_pairs={{0,2},{1,3},{2,0},{3,1},{4,6},{5,7},{6,4},{7,5},{8,10},{9,11},{10,... | collective-permute-start | bytes 3080 | tf_op jit(solution)/shard_map/ppermute | solution.py:32
  50.0 3.0 %collective-permute-start.11 = (f32[2,128]{1,0:T(2,128)S(1)}, f32[2,128]{1,0:T(2,128)S(1)}, u32[]{:S(2)}, u32[]{:S(2)}) collective-permute-start(f32[2,128]{1,0:T(2,128)S(1)} %row_pass.2.refs_0_), channel_id=1, source_target_pairs={{0,3},{1,2},{2,1},{3,0},{4,7},{5,6},{6,5},{7,4},{8,11},{9,10},{10,... | collective-permute-start | bytes 3080 | tf_op jit(solution)/shard_map/ppermute | solution.py:32
  53.6 7.3 %collective-permute-start.12 = (f32[80,128]{1,0:T(8,128)S(1)}, f32[80,128]{1,0:T(8,128)S(1)}, u32[]{:S(2)}, u32[]{:S(2)}) collective-permute-start(f32[80,128]{1,0:T(8,128)S(1)} %get-tuple-element.106), channel_id=1, source_target_pairs={{0,8},{4,12},{8,0},{12,4},{16,24},{20,28},{24,16},{28,20},{1,9},{5... | collective-permute-start | bytes 122888 | tf_op jit(solution)/shard_map/ppermute | solution.py:32
  53.7 9.6 %collective-permute-start.13 = (f32[80,128]{1,0:T(8,128)S(1)}, f32[80,128]{1,0:T(8,128)S(1)}, u32[]{:S(2)}, u32[]{:S(2)}) collective-permute-start(f32[80,128]{1,0:T(8,128)S(1)} %get-tuple-element.107), channel_id=1, source_target_pairs={{0,16},{4,20},{8,24},{12,28},{16,0},{20,4},{24,8},{28,12},{1,17},{... | collective-permute-start | bytes 122888 | tf_op jit(solution)/shard_map/ppermute | solution.py:32
  57.1 6.8 %collective-permute-start.14 = (f32[80,128]{1,0:T(8,128)S(1)}, f32[80,128]{1,0:T(8,128)S(1)}, u32[]{:S(2)}, u32[]{:S(2)}) collective-permute-start(f32[80,128]{1,0:T(8,128)S(1)} %get-tuple-element.108), channel_id=1, source_target_pairs={{0,24},{4,28},{8,16},{12,20},{16,8},{20,12},{24,0},{28,4},{1,25},{... | collective-permute-start | bytes 122888 | tf_op jit(solution)/shard_map/ppermute | solution.py:32
  64.3 16.2 %copy-start.8 = (s32[128]{0:T(128)S(1)}, s32[128]{0:T(128)}, u32[]{:S(2)}) copy-start(s32[128]{0:T(128)} %param.13) | copy-start | bytes 1540
  64.3 1.9 %collective-permute-start.15 = (f32[2,128]{1,0:T(2,128)S(1)}, f32[2,128]{1,0:T(2,128)S(1)}, u32[]{:S(2)}, u32[]{:S(2)}) collective-permute-start(f32[2,128]{1,0:T(2,128)S(1)} %row_pass.3.refs_0_), channel_id=1, source_target_pairs={{0,1},{1,0},{2,3},{3,2},{4,5},{5,4},{6,7},{7,6},{8,9},{9,8},{10,11... | collective-permute-start | bytes 3080 | tf_op jit(solution)/shard_map/ppermute | solution.py:32
  64.3 3.6 %collective-permute-start.16 = (f32[2,128]{1,0:T(2,128)S(1)}, f32[2,128]{1,0:T(2,128)S(1)}, u32[]{:S(2)}, u32[]{:S(2)}) collective-permute-start(f32[2,128]{1,0:T(2,128)S(1)} %row_pass.3.refs_0_), channel_id=1, source_target_pairs={{0,2},{1,3},{2,0},{3,1},{4,6},{5,7},{6,4},{7,5},{8,10},{9,11},{10,... | collective-permute-start | bytes 3080 | tf_op jit(solution)/shard_map/ppermute | solution.py:32
  65.9 3.0 %collective-permute-start.17 = (f32[2,128]{1,0:T(2,128)S(1)}, f32[2,128]{1,0:T(2,128)S(1)}, u32[]{:S(2)}, u32[]{:S(2)}) collective-permute-start(f32[2,128]{1,0:T(2,128)S(1)} %row_pass.3.refs_0_), channel_id=1, source_target_pairs={{0,3},{1,2},{2,1},{3,0},{4,7},{5,6},{6,5},{7,4},{8,11},{9,10},{10,... | collective-permute-start | bytes 3080 | tf_op jit(solution)/shard_map/ppermute | solution.py:32
  69.4 7.4 %collective-permute-start.18 = (f32[1,8,48,128]{3,2,1,0:T(8,128)S(1)}, f32[1,8,48,128]{3,2,1,0:T(8,128)S(1)}, u32[]{:S(2)}, u32[]{:S(2)}) collective-permute-start(f32[1,8,48,128]{3,2,1,0:T(8,128)S(1)} %columns_join.1), channel_id=1, source_target_pairs={{0,2},{1,3},{2,0},{3,1},{4,6},{5,7},{6,4},{7,5},{8,10},{9,11},{10,... | collective-permute-start | bytes 589832 | tf_op jit(solution)/shard_map/ppermute | solution.py:32
  70.1 6.8 %collective-permute-start.19 = (f32[32,128]{1,0:T(8,128)S(1)}, f32[32,128]{1,0:T(8,128)S(1)}, u32[]{:S(2)}, u32[]{:S(2)}) collective-permute-start(f32[32,128]{1,0:T(8,128)S(1)} %col_pass.3.refs_0_), channel_id=1, source_target_pairs={{0,8},{4,12},{8,0},{12,4},{16,24},{20,28},{24,16},{28,20},{1,9},{5... | collective-permute-start | bytes 49160 | tf_op jit(solution)/shard_map/ppermute | solution.py:32
  73.4 5.3 %collective-permute-start.20 = (f32[32,128]{1,0:T(8,128)S(1)}, f32[32,128]{1,0:T(8,128)S(1)}, u32[]{:S(2)}, u32[]{:S(2)}) collective-permute-start(f32[32,128]{1,0:T(8,128)S(1)} %col_pass.3.refs_0_), channel_id=1, source_target_pairs={{0,16},{4,20},{8,24},{12,28},{16,0},{20,4},{24,8},{28,12},{1,17},{... | collective-permute-start | bytes 49160 | tf_op jit(solution)/shard_map/ppermute | solution.py:32
  74.6 5.9 %collective-permute-start.21 = (f32[32,128]{1,0:T(8,128)S(1)}, f32[32,128]{1,0:T(8,128)S(1)}, u32[]{:S(2)}, u32[]{:S(2)}) collective-permute-start(f32[32,128]{1,0:T(8,128)S(1)} %col_pass.3.refs_0_), channel_id=1, source_target_pairs={{0,24},{4,28},{8,16},{12,20},{16,8},{20,12},{24,0},{28,4},{1,25},{... | collective-permute-start | bytes 49160 | tf_op jit(solution)/shard_map/ppermute | solution.py:32
  82.0 3.4 %collective-permute-start.23 = (f32[2,8,48,128]{3,2,1,0:T(8,128)S(1)}, f32[2,8,48,128]{3,2,1,0:T(8,128)S(1)}, u32[]{:S(2)}, u32[]{:S(2)}) collective-permute-start(f32[2,8,48,128]{3,2,1,0:T(8,128)S(1)} %pad_maximum_fusion.refs_0_), channel_id=1, source_target_pairs={{0,1},{1,0},{2,3},{3,2},{4,5},{5,4},{6,7},{7,6},{8,9},{9,8},{10,11... | collective-permute-start | bytes 1179656 | tf_op jit(solution)/shard_map/ppermute | solution.py:32
  82.1 1.8 %collective-permute-start.22 = (f32[72,256]{1,0:T(8,128)S(1)}, f32[72,256]{1,0:T(8,128)S(1)}, u32[]{:S(2)}, u32[]{:S(2)}) collective-permute-start(f32[72,256]{1,0:T(8,128)S(1)} %get-tuple-element.112), channel_id=1, source_target_pairs={{0,1},{1,0},{2,3},{3,2},{4,5},{5,4},{6,7},{7,6},{8,9},{9,8},{10,11... | collective-permute-start | bytes 221192 | tf_op jit(solution)/shard_map/ppermute | solution.py:32
  84.0 4.4 %collective-permute-start.24 = (f32[72,256]{1,0:T(8,128)S(1)}, f32[72,256]{1,0:T(8,128)S(1)}, u32[]{:S(2)}, u32[]{:S(2)}) collective-permute-start(f32[72,256]{1,0:T(8,128)S(1)} %add.11.refs_5_), channel_id=1, source_target_pairs={{0,2},{1,3},{2,0},{3,1},{4,6},{5,7},{6,4},{7,5},{8,10},{9,11},{10,... | collective-permute-start | bytes 221192 | tf_op jit(solution)/shard_map/ppermute | solution.py:32
  89.1 6.1 %collective-permute-start.28 = (f32[1,64,256]{2,1,0:T(8,128)S(1)}, f32[1,64,256]{2,1,0:T(8,128)S(1)}, u32[]{:S(2)}, u32[]{:S(2)}) collective-permute-start(f32[1,64,256]{2,1,0:T(8,128)S(1)} %bitcast.18), channel_id=1, source_target_pairs={{0,4},{4,0},{8,12},{12,8},{16,20},{20,16},{24,28},{28,24},{1,5},{5... | collective-permute-start | bytes 196616 | tf_op jit(solution)/shard_map/ppermute | solution.py:32
  90.8 8.1 %collective-permute-start.27 = (f32[64,256]{1,0:T(8,128)S(1)}, f32[64,256]{1,0:T(8,128)S(1)}, u32[]{:S(2)}, u32[]{:S(2)}) collective-permute-start(f32[64,256]{1,0:T(8,128)S(1)} %get-tuple-element.117), channel_id=1, source_target_pairs={{0,24},{4,28},{8,16},{12,20},{16,8},{20,12},{24,0},{28,4},{1,25},{... | collective-permute-start | bytes 196616 | tf_op jit(solution)/shard_map/ppermute | solution.py:32
  92.2 7.1 %collective-permute-start.26 = (f32[64,256]{1,0:T(8,128)S(1)}, f32[64,256]{1,0:T(8,128)S(1)}, u32[]{:S(2)}, u32[]{:S(2)}) collective-permute-start(f32[64,256]{1,0:T(8,128)S(1)} %get-tuple-element.117), channel_id=1, source_target_pairs={{0,16},{4,20},{8,24},{12,28},{16,0},{20,4},{24,8},{28,12},{1,17},{... | collective-permute-start | bytes 196616 | tf_op jit(solution)/shard_map/ppermute | solution.py:32
  93.5 5.8 %collective-permute-start.25 = (f32[64,256]{1,0:T(8,128)S(1)}, f32[64,256]{1,0:T(8,128)S(1)}, u32[]{:S(2)}, u32[]{:S(2)}) collective-permute-start(f32[64,256]{1,0:T(8,128)S(1)} %get-tuple-element.117), channel_id=1, source_target_pairs={{0,8},{4,12},{8,0},{12,4},{16,24},{20,28},{24,16},{28,20},{1,9},{5... | collective-permute-start | bytes 196616 | tf_op jit(solution)/shard_map/ppermute | solution.py:32
  95.2 4.0 %collective-permute-start.29 = (f32[1,64,256]{2,1,0:T(8,128)S(1)}, f32[1,64,256]{2,1,0:T(8,128)S(1)}, u32[]{:S(2)}, u32[]{:S(2)}) collective-permute-start(f32[1,64,256]{2,1,0:T(8,128)S(1)} %bitcast.19), channel_id=1, source_target_pairs={{0,1},{1,0},{2,3},{3,2},{4,5},{5,4},{6,7},{7,6},{8,9},{9,8},{10,11... | collective-permute-start | bytes 196616 | tf_op jit(solution)/shard_map/ppermute | solution.py:32
  95.2 4.1 %collective-permute-start.30 = (f32[1,64,256]{2,1,0:T(8,128)S(1)}, f32[1,64,256]{2,1,0:T(8,128)S(1)}, u32[]{:S(2)}, u32[]{:S(2)}) collective-permute-start(f32[1,64,256]{2,1,0:T(8,128)S(1)} %collective-permute-done.28.refs_7_), channel_id=1, source_target_pairs={{0,1},{1,0},{2,3},{3,2},{4,5},{5,4},{6,7},{7,6},{8,9},{9,8},{10,11... | collective-permute-start | bytes 196616 | tf_op jit(solution)/shard_map/ppermute | solution.py:32
  95.7 2.2 %copy-start = (f32[1024,1024]{1,0:T(8,128)S(1)}, f32[1024,1024]{1,0:T(8,128)}, u32[]{:S(2)}) copy-start(f32[1024,1024]{1,0:T(8,128)} %all-gather.2.cloned.1.call-done) | copy-start | bytes 12582916
  97.9 3.4 %copy-start.1 = (f32[1024,1024]{1,0:T(8,128)S(1)}, f32[1024,1024]{1,0:T(8,128)}, u32[]{:S(2)}) copy-start(f32[1024,1024]{1,0:T(8,128)} %all-gather.2.cloned.1.call-done) | copy-start | bytes 12582916
  99.3 1.2 %collective-permute-start.32 = (f32[1,64]{1,0:T(1,128)S(1)}, f32[1,64]{1,0:T(1,128)S(1)}, u32[]{:S(2)}, u32[]{:S(2)}) collective-permute-start(f32[1,64]{1,0:T(1,128)S(1)} %get-tuple-element.129), channel_id=1, source_target_pairs={{0,1},{1,0},{2,3},{3,2},{4,5},{5,4},{6,7},{7,6},{8,9},{9,8},{10,11... | collective-permute-start | bytes 776 | tf_op jit(solution)/shard_map/ppermute | solution.py:32
  99.4 7.3 %collective-permute-start.31 = (f32[3,64,256]{2,1,0:T(8,128)S(1)}, f32[3,64,256]{2,1,0:T(8,128)S(1)}, u32[]{:S(2)}, u32[]{:S(2)}) collective-permute-start(f32[3,64,256]{2,1,0:T(8,128)S(1)} %pad_maximum_fusion.1.refs_8_), channel_id=1, source_target_pairs={{0,4},{4,0},{8,12},{12,8},{16,20},{20,16},{24,28},{28,24},{1,5},{5... | collective-permute-start | bytes 589832 | tf_op jit(solution)/shard_map/ppermute | solution.py:32
  99.8 1.4 %collective-permute-start.33 = (f32[3,64,256]{2,1,0:T(8,128)S(1)}, f32[3,64,256]{2,1,0:T(8,128)S(1)}, u32[]{:S(2)}, u32[]{:S(2)}) collective-permute-start(f32[3,64,256]{2,1,0:T(8,128)S(1)} %pad_maximum_fusion.1.refs_8_), channel_id=1, source_target_pairs={{0,1},{1,0},{2,3},{3,2},{4,5},{5,4},{6,7},{7,6},{8,9},{9,8},{10,11... | collective-permute-start | bytes 589832 | tf_op jit(solution)/shard_map/ppermute | solution.py:32
  106.7 1.4 %collective-permute-start.34 = (f32[3,64,256]{2,1,0:T(8,128)S(1)}, f32[3,64,256]{2,1,0:T(8,128)S(1)}, u32[]{:S(2)}, u32[]{:S(2)}) collective-permute-start(f32[3,64,256]{2,1,0:T(8,128)S(1)} %collective-permute-done.31.refs_8_), channel_id=1, source_target_pairs={{0,1},{1,0},{2,3},{3,2},{4,5},{5,4},{6,7},{7,6},{8,9},{9,8},{10,11... | collective-permute-start | bytes 589832 | tf_op jit(solution)/shard_map/ppermute | solution.py:32
Sparse Core Ops, SparseCore 0:
  11.7 79.3 all-gather.1
